TPU v7x, 256 devices: a whole 4x4x8 slice. The times are simulated.
256 devices in a mesh: src: 32 (over z, x), tgt: 8 (over y, core).
Axes of the slice: x: 4, y: 4, z: 8, core: 2. Of those that a mesh axis runs over, the one named last changes fastest.
Arguments:
- src_points: float32 [50, 524288], P(None, 'src')
- tgt_points: float32 [50, 196608], P(None, 'tgt')
- tiles: int32 [32, 8, 2, 32], P('src', 'tgt'), may hold values from 0 to 95, as said below
- counts: int32 [32, 8], P('src', 'tgt'), may hold values from 8 to 32, as said below
Outputs:
- source_potential: float32 [524288], P('src')
- target_potential: float32 [196608], P('tgt')
Inputs may be any that keep to these rules, and one draw needn't show every extreme that they name: tiles[i, j, 0, k] is a row block below 64 and tiles[i, j, 1, k] a column block below 96; the pairs of the live slots of one device are distinct; each source block of src index i is in a live slot of some device (i, j), each target block of tgt index j in a live slot of some device (i, j). The live slots of device (i, j) are its first counts[i, j] slots.
All inputs are finite; a program needn't handle non-finite values.
Results may differ from a plain program's by a relative error of at most 0.0003.
Values sent between devices are 32-bit elements; how exact they have to be, the bound alone decides.
No kernel may reach another device: no remote copies, remote signals or barrier semaphores. Data moves between devices by JAX's collectives and lax.ppermute only.
A program may use at most 128 MiB of HBM per device.

v0:
```python
import jax
import jax.numpy as jnp
from jax import lax
from jax.sharding import PartitionSpec as P

TILE = 256
ITERS = 3


EPS = 0.05
FLOOR = -1e30


def joined(shard, axis, combine):
    everything = jax.tree.map(lambda part: lax.all_gather(part, axis), shard)
    first = jax.tree.map(lambda part: part[0], everything)

    def hop(k, so_far):
        return combine(so_far, jax.tree.map(lambda part: part[k], everything))

    return lax.fori_loop(1, lax.axis_size(axis), hop, first)


def combine(first, second):
    top = jnp.maximum(first[0], second[0])
    return (top, first[1] * jnp.exp(first[0] - top) + second[1] * jnp.exp(second[0] - top))


def block_partial(scores, axis_num, live, blocks, num_blocks):
    peak = jnp.max(scores, axis=axis_num)
    total = jnp.sum(jnp.exp(scores - jnp.expand_dims(peak, axis_num)), axis=axis_num)
    peak = jnp.where(live[:, None], peak, FLOOR)
    total = jnp.where(live[:, None], total, 0.0)
    select = blocks[:, None] == jnp.arange(num_blocks, dtype=jnp.int32)[None, :]
    top = jnp.max(jnp.where(select[:, :, None], peak[:, None, :], FLOOR), axis=0)
    gap = jnp.where(select[:, :, None], peak[:, None, :] - top[None], FLOOR)
    summed = jnp.sum(jnp.exp(gap) * total[:, None, :], axis=0)
    return (top.reshape(-1), summed.reshape(-1))


def body(src_points, tgt_points, tiles, counts):
    rows = tiles[0, 0, 0]
    cols = tiles[0, 0, 1]
    live = jnp.arange(rows.shape[0], dtype=jnp.int32) < counts[0, 0]
    width = src_points.shape[0]
    row_blocks = src_points.shape[1] // TILE
    col_blocks = tgt_points.shape[1] // TILE
    src_cells = src_points.shape[1] * lax.axis_size("src")
    tgt_cells = tgt_points.shape[1] * lax.axis_size("tgt")
    src_tiles = jnp.take(src_points.reshape(width, row_blocks, TILE), rows, axis=1)
    tgt_tiles = jnp.take(tgt_points.reshape(width, col_blocks, TILE), cols, axis=1)
    src_square = jnp.sum(src_tiles * src_tiles, axis=0)
    tgt_square = jnp.sum(tgt_tiles * tgt_tiles, axis=0)

    def tile_costs():
        cross = jnp.einsum("pka,pkb->kab", src_tiles, tgt_tiles, precision=lax.Precision.HIGHEST)
        return src_square[:, :, None] + tgt_square[:, None, :] - 2.0 * cross

    stored = None

    def current_costs():
        return tile_costs()

    source_potential = jnp.zeros((src_points.shape[1],), jnp.float32)
    target_potential = jnp.zeros((tgt_points.shape[1],), jnp.float32)
    for sweep in range(ITERS):
        cost = current_costs()
        picked = jnp.take(target_potential.reshape(col_blocks, TILE), cols, axis=0)
        partial_top, partial_sum = block_partial(
            (picked[:, None, :] - cost) / EPS, 2, live, rows, row_blocks
        )
        top, summed = joined((partial_top, partial_sum), "tgt", combine)
        source_potential = EPS * jnp.log(1.0 / src_cells) - EPS * (top + jnp.log(summed))
        cost = current_costs()
        picked = jnp.take(source_potential.reshape(row_blocks, TILE), rows, axis=0)
        partial_top, partial_sum = block_partial(
            (picked[:, :, None] - cost) / EPS, 1, live, cols, col_blocks
        )
        top, summed = joined((partial_top, partial_sum), "src", combine)
        target_potential = EPS * jnp.log(1.0 / tgt_cells) - EPS * (top + jnp.log(summed))
    return (source_potential, target_potential)


def solution(mesh):
    in_specs = (P(None, "src"), P(None, "tgt"), P("src", "tgt", None, None), P("src", "tgt"))
    out_specs = (P("src"), P("tgt"))
    return jax.shard_map(body, mesh=mesh, in_specs=in_specs, out_specs=out_specs, check_vma=False)
```

profile of v0, /device:TPU:2, one launch (start us, length us, event | category | flops | bytes accessed | tf_op | source)
XLA Modules:
  0.0 816.1 jit_solution(1427796269251093200)
XLA Ops:
  9.5 4.2 copy.25
  14.2 5.3 copy.11
  21.0 3.8 copy.10
  29.4 4.0 gather_fusion
  35.6 10.9 %fusion = (f32[32,256]{1,0:T(8,128)S(1)}, f32[32,256,256]{2,1,0:T(8,128)S(1)}) fusion(f32[32,256]{1,0:T(8,128)S(1)} %broadcast_select_fusion.5, f32[32,50,256]{2,1,0:T(8,128)S(1)} %gather_fusion.1, pred[32]{0:T(512)(128)(4,1)S(1)} %get-tuple-element.904, f32[32,50,256]{2,1,0:T(8,128)S(1)} %copy-done.2, pred[32]{0:T(512)(128)(4,1)S(1)} %get-tuple-element.886, ...), kind=kOutput, calls=%fused_computation.39 | convolution fusion | flops 1271685120 | bytes 11796544 | tf_op jit(solution)/shard_map/pka,pkb->kab/dot_general | solution.py:56
  50.3 13.6 %all-gather = f32[8,1,16384]{2,1,0:T(1,128)S(1)} all-gather(f32[1,1,16384]{2,1,0:T(1,128)S(1)} %reshape.424), channel_id=1, replica_groups=mesh['src'=32,'tgt'=8] {'tgt'}, dimensions={0}, use_global_device_ids=true | all-gather | bytes 589824 | tf_op jit(solution)/shard_map/all_gather | solution.py:15
  64.9 13.1 %all-gather.1 = f32[8,1,16384]{2,1,0:T(1,128)S(1)} all-gather(f32[1,1,16384]{2,1,0:T(1,128)S(1)} %reshape.426), channel_id=1, replica_groups=mesh['src'=32,'tgt'=8] {'tgt'}, dimensions={0}, use_global_device_ids=true | all-gather | bytes 589824 | tf_op jit(solution)/shard_map/all_gather | solution.py:15
  80.5 4.3 fusion.1
  92.0 79.1 %all-gather.19.cloned.1.call-done = f32[32,1,24576]{2,1,0:T(1,128)} async-done(((f32[1,1,24576]{2,1,0:T(1,128)}), f32[32,1,24576]{2,1,0:T(1,128)}) %all-gather.19.cloned.1.call-update) | async-done | bytes 3145744 | tf_op jit(solution)/shard_map/all_gather | solution.py:15
  174.8 75.4 %all-gather.21.cloned.1.call-done = f32[32,1,24576]{2,1,0:T(1,128)} async-done(((f32[1,1,24576]{2,1,0:T(1,128)}), f32[32,1,24576]{2,1,0:T(1,128)}) %all-gather.21.cloned.1.call-update) | async-done | bytes 3145744 | tf_op jit(solution)/shard_map/all_gather | solution.py:15
  250.3 5.5 copy.42
  255.8 43.2 %while.103 = (s32[]{:T(128)}, f32[24576]{0:T(1024)S(1)}, f32[24576]{0:T(1024)S(1)}, f32[32,24576]{1,0:T(8,128)S(1)}, f32[32,24576]{1,0:T(8,128)}, /*index=5*/s32[]{:T(128)}, s32[]{:T(128)}, s32[]{:T(128)}) while((s32[]{:T(128)}, f32[24576]{0:T(1024)S(1)}, f32[24576]{0:T(1024)S(1)}, f32[32,24576]{1,0:T(8,128)S(1)}, f32[32,24576]{1,0:T(8,128)}, ...), condition=%wide.region_13.16_spmd, body=%wide.region_12.15_spmd.sunk | while | flops 147461 | bytes 983171 | solution.py:21
  299.8 4.5 fusion.2
  304.3 4.8 exponential_reduce_fusion.3
  309.6 13.4 %all-gather.4 = f32[8,1,16384]{2,1,0:T(1,128)S(1)} all-gather(f32[1,1,16384]{2,1,0:T(1,128)S(1)} %reshape.432), channel_id=1, replica_groups=mesh['src'=32,'tgt'=8] {'tgt'}, dimensions={0}, use_global_device_ids=true | all-gather | bytes 589824 | tf_op jit(solution)/shard_map/all_gather | solution.py:15
  324.1 13.1 %all-gather.5 = f32[8,1,16384]{2,1,0:T(1,128)S(1)} all-gather(f32[1,1,16384]{2,1,0:T(1,128)S(1)} %reshape.434), channel_id=1, replica_groups=mesh['src'=32,'tgt'=8] {'tgt'}, dimensions={0}, use_global_device_ids=true | all-gather | bytes 589824 | tf_op jit(solution)/shard_map/all_gather | solution.py:15
  339.7 4.1 fusion.3
  343.8 4.5 exponential_reduce_fusion.2
  351.9 73.9 %all-gather.23.cloned.1.call-done = f32[32,1,24576]{2,1,0:T(1,128)} async-done(((f32[1,1,24576]{2,1,0:T(1,128)}), f32[32,1,24576]{2,1,0:T(1,128)}) %all-gather.23.cloned.1.call-update) | async-done | bytes 3145744 | tf_op jit(solution)/shard_map/all_gather | solution.py:15
  429.6 75.3 %all-gather.25.cloned.1.call-done = f32[32,1,24576]{2,1,0:T(1,128)} async-done(((f32[1,1,24576]{2,1,0:T(1,128)}), f32[32,1,24576]{2,1,0:T(1,128)}) %all-gather.25.cloned.1.call-update) | async-done | bytes 3145744 | tf_op jit(solution)/shard_map/all_gather | solution.py:15
  504.9 5.5 copy.40
  510.4 43.2 %while.105 = (s32[]{:T(128)}, f32[24576]{0:T(1024)S(1)}, f32[24576]{0:T(1024)S(1)}, f32[32,24576]{1,0:T(8,128)S(1)}, f32[32,24576]{1,0:T(8,128)}, /*index=5*/s32[]{:T(128)}, s32[]{:T(128)}, s32[]{:T(128)}) while((s32[]{:T(128)}, f32[24576]{0:T(1024)S(1)}, f32[24576]{0:T(1024)S(1)}, f32[32,24576]{1,0:T(8,128)S(1)}, f32[32,24576]{1,0:T(8,128)}, ...), condition=%wide.region_25.28_spmd, body=%wide.region_24.27_spmd.sunk | while | flops 147461 | bytes 983171 | solution.py:21
  554.4 4.5 fusion.4
  558.9 4.8 exponential_reduce_fusion.1
  564.3 13.4 %all-gather.8 = f32[8,1,16384]{2,1,0:T(1,128)S(1)} all-gather(f32[1,1,16384]{2,1,0:T(1,128)S(1)} %reshape.440), channel_id=1, replica_groups=mesh['src'=32,'tgt'=8] {'tgt'}, dimensions={0}, use_global_device_ids=true | all-gather | bytes 589824 | tf_op jit(solution)/shard_map/all_gather | solution.py:15
  578.8 13.3 %all-gather.9 = f32[8,1,16384]{2,1,0:T(1,128)S(1)} all-gather(f32[1,1,16384]{2,1,0:T(1,128)S(1)} %reshape.442), channel_id=1, replica_groups=mesh['src'=32,'tgt'=8] {'tgt'}, dimensions={0}, use_global_device_ids=true | all-gather | bytes 589824 | tf_op jit(solution)/shard_map/all_gather | solution.py:15
  594.5 4.1 fusion.5
  598.6 4.5 exponential_reduce_fusion
  606.3 74.4 %all-gather.27.cloned.1.call-done = f32[32,1,24576]{2,1,0:T(1,128)} async-done(((f32[1,1,24576]{2,1,0:T(1,128)}), f32[32,1,24576]{2,1,0:T(1,128)}) %all-gather.27.cloned.1.call-update) | async-done | bytes 3145744 | tf_op jit(solution)/shard_map/all_gather | solution.py:15
  684.4 75.3 %all-gather.29.cloned.1.call-done = f32[32,1,24576]{2,1,0:T(1,128)} async-done(((f32[1,1,24576]{2,1,0:T(1,128)}), f32[32,1,24576]{2,1,0:T(1,128)}) %all-gather.29.cloned.1.call-update) | async-done | bytes 3145744 | tf_op jit(solution)/shard_map/all_gather | solution.py:15
  759.7 5.4 copy.38
  765.2 43.2 %while.107 = (s32[]{:T(128)}, f32[24576]{0:T(1024)S(1)}, f32[24576]{0:T(1024)S(1)}, f32[32,24576]{1,0:T(8,128)S(1)}, f32[32,24576]{1,0:T(8,128)}, /*index=5*/s32[]{:T(128)}, s32[]{:T(128)}, s32[]{:T(128)}) while((s32[]{:T(128)}, f32[24576]{0:T(1024)S(1)}, f32[24576]{0:T(1024)S(1)}, f32[32,24576]{1,0:T(8,128)S(1)}, f32[32,24576]{1,0:T(8,128)}, ...), condition=%wide.region_37.40_spmd, body=%wide.region_36.39_spmd.sunk | while | flops 147461 | bytes 983171 | solution.py:21
  (350 shorter events, 183.3 us)
Async XLA Ops:
  7.2 163.9 %all-gather.19.cloned.1.call-start = ((), (), s32[]{:S(2)}) async-start(), calls=%async_computation | async-start | bytes 3244032 | tf_op jit(solution)/shard_map/all_gather | solution.py:15
  14.2 5.3 copy-start.3
  33.4 2.2 copy-start.2
  46.6 3.2 copy-start
  80.5 5.8 copy-start.1
  90.0 160.2 %all-gather.21.cloned.1.call-start = ((), (), s32[]{:S(2)}) async-start(), calls=%async_computation.1 | async-start | bytes 3244032 | tf_op jit(solution)/shard_map/all_gather | solution.py:15
  91.7 334.1 %all-gather.23.cloned.1.call-start = ((), (), s32[]{:S(2)}) async-start(), calls=%async_computation.2 | async-start | bytes 3244032 | tf_op jit(solution)/shard_map/all_gather | solution.py:15
  250.2 5.5 slice-start
  250.3 5.5 slice-start.3
  349.8 155.1 %all-gather.25.cloned.1.call-start = ((), (), s32[]{:S(2)}) async-start(), calls=%async_computation.3 | async-start | bytes 3244032 | tf_op jit(solution)/shard_map/all_gather | solution.py:15
  351.9 328.8 %all-gather.27.cloned.1.call-start = ((), (), s32[]{:S(2)}) async-start(), calls=%async_computation.4 | async-start | bytes 3244032 | tf_op jit(solution)/shard_map/all_gather | solution.py:15
  504.9 5.5 slice-start.1
  504.9 5.5 slice-start.4
  593.8 4.9 copy-start.4
  604.6 155.1 %all-gather.29.cloned.1.call-start = ((), (), s32[]{:S(2)}) async-start(), calls=%async_computation.5 | async-start | bytes 3244032 | tf_op jit(solution)/shard_map/all_gather | solution.py:15
  759.7 5.5 slice-start.2
  759.7 5.5 slice-start.5
Sparse Core Ops, SparseCore 0:
  90.1 80.9 all-gather.18
  173.7 76.5 all-gather.20
  349.9 75.9 all-gather.22
  428.3 76.5 all-gather.24
  604.7 75.9 all-gather.26
  683.1 76.5 all-gather.28
where the time goes:
time: 829 us; the launch traced here: 816 us
  waiting for transfers between devices  454 us (55%)
  local copies, waits for them, and re-layouts  184 us (22%)
  blocking collectives  80 us (10%)
  other arithmetic  68.5 us (8%)
  between operations  15.5 us (2%)
  matrix products  10.9 us (1%)
    all_gather x6, waiting for transfers between devices, joined(): everything = jax.tree.map(lambda part: lax.all_gather(part, axis), shard)  453 us
    dynamic_slice x114, local copies, waits for them, and re-layouts, hop(): return combine(so_far, jax.tree.map(lambda part: part[k], everything))  121 us
    all_gather x6, blocking collectives, joined(): everything = jax.tree.map(lambda part: lax.all_gather(part, axis), shard)  80 us
    unnamed x36, local copies, waits for them, and re-layouts  41.4 us
    reduce_sum x6, other arithmetic, block_partial(): jnp.sum(jnp.exp(scores - jnp.expand_dims(peak, axis_num)), axis=axis_num)  23.9 us
    reduce_max x5, other arithmetic, block_partial(): peak = jnp.max(scores, axis=axis_num)  21.6 us
  transfers between devices with their start and end apart: 6, of which 6 were waited for; matrix products, arithmetic and copies ran while one was open for 2% of the time, Pallas kernels for 0%

commit v1 on v0

v1 whole, which is shorter than its diff:
```python
import functools
import math

import jax
import jax.numpy as jnp
from jax import lax
from jax.experimental import pallas as pl
from jax.experimental.pallas import tpu as pltpu
from jax.sharding import PartitionSpec as P

TILE = 256
HALF = 128
ROWS = 8
ITERS = 3
EPS = 0.05
FLOOR = -1e30
SCALE = 1.0 / (EPS * math.log(2.0))
DEPTH = 64
VMEM_LIMIT = 16 * 1024 * 1024


def lse2(first, second):
    top = jnp.maximum(first, second)
    return top + jnp.log2(1.0 + jnp.exp2(jnp.minimum(first, second) - top))


def lse2_many(parts):
    top = functools.reduce(jnp.maximum, parts)
    return top + jnp.log2(functools.reduce(jnp.add, [jnp.exp2(p - top) for p in parts]))


def split(value):
    high = value.astype(jnp.bfloat16)
    rest = value - high.astype(jnp.float32)
    middle = rest.astype(jnp.bfloat16)
    low = (rest - middle.astype(jnp.float32)).astype(jnp.bfloat16)
    return high, middle, low


def cost_kernel(tiles, counts, src, tgt, cost_ab, cost_ba, xs, ys, ext, left, right, xsem, ysem):
    live = counts[0]
    width = src.shape[0]

    def copies(k):
        row = pl.multiple_of(tiles[0, k] * TILE, TILE)
        col = pl.multiple_of(tiles[1, k] * TILE, TILE)
        return (
            pltpu.make_async_copy(src.at[:, pl.ds(row, TILE)], xs.at[k], xsem.at[k]),
            pltpu.make_async_copy(tgt.at[:, pl.ds(col, TILE)], ys.at[k], ysem.at[k]),
        )

    def begin(k, carry):
        one, two = copies(k)
        one.start()
        two.start()
        return carry

    lax.fori_loop(0, live, begin, 0)
    ext[...] = jnp.zeros_like(ext)

    def step(k, carry):
        one, two = copies(k)
        one.wait()
        two.wait()
        x = xs[k]
        y = ys[k]
        ext[0, pl.ds(0, width), :] = x * (-2.0 * SCALE)
        ext[0, pl.ds(width, 1), :] = jnp.sum(x * x, axis=0, keepdims=True) * SCALE
        ext[0, pl.ds(width + 1, 1), :] = jnp.full((1, TILE), SCALE, jnp.float32)
        ext[1, pl.ds(0, width), :] = y
        ext[1, pl.ds(width, 1), :] = jnp.ones((1, TILE), jnp.float32)
        ext[1, pl.ds(width + 1, 1), :] = jnp.sum(y * y, axis=0, keepdims=True)
        xh, xm, xl = split(ext[0])
        yh, ym, yl = split(ext[1])
        for n, part in enumerate((xh, xh, xm, xm, xh, xl)):
            left[pl.ds(n * DEPTH, DEPTH), :] = part
        for n, part in enumerate((yh, ym, yh, ym, yl, yh)):
            right[pl.ds(n * DEPTH, DEPTH), :] = part
        dims = (((0,), (0,)), ((), ()))
        cost_ab[k] = lax.dot_general(left[...], right[...], dims, preferred_element_type=jnp.float32)
        cost_ba[k] = lax.dot_general(right[...], left[...], dims, preferred_element_type=jnp.float32)
        return carry

    lax.fori_loop(0, live, step, 0)


def sweep_kernel(offset, scale, inner, outer, blocks_in, blocks_out, tiles, counts, cost, *refs):
    parts = refs[:-5]
    out, result, spread, top, total = refs[-5:]
    live = counts[0]
    if parts:
        potential = offset - lse2_many([part[...] for part in parts])
        result[...] = potential * scale
        padded = potential
        if blocks_in < HALF:
            padded = jnp.concatenate(
                [potential, jnp.zeros((HALF - blocks_in, TILE), jnp.float32)], axis=0
            )
        spread[...] = padded.T
    else:
        result[...] = jnp.zeros_like(result)
    top[...] = jnp.full_like(top, FLOOR)
    total[...] = jnp.zeros_like(total)

    def column(k):
        if not parts:
            return jnp.zeros((TILE, HALF), jnp.float32)
        index = jnp.full((TILE, HALF), tiles[inner, k], jnp.int32)
        return jnp.take_along_axis(spread[...], index, axis=1, mode="promise_in_bounds")

    def scores(k, pot, h):
        return pot - cost[k, :, pl.ds(h * HALF, HALF)]

    def peaks(k, carry):
        pot = column(k)
        block = tiles[outer, k]
        for h in range(2):
            lanes = pl.ds(h * HALF, HALF)
            peak = jnp.max(scores(k, pot, h), axis=0, keepdims=True)
            top[block, :, lanes] = jnp.maximum(top[block, :, lanes], peak)
        return carry

    lax.fori_loop(0, live, peaks, 0)

    def sums(k, carry):
        pot = column(k)
        block = tiles[outer, k]
        for h in range(2):
            lanes = pl.ds(h * HALF, HALF)
            shift = top[block, pl.ds(0, 1), lanes]
            terms = jnp.exp2(scores(k, pot, h) - shift)
            part = jnp.sum(terms.reshape(TILE // ROWS, ROWS, HALF), axis=0)
            total[block, :, lanes] = total[block, :, lanes] + part
        return carry

    lax.fori_loop(0, live, sums, 0)
    summed = jnp.sum(total[...], axis=1)
    found = summed > 0.0
    out[...] = jnp.where(found, jnp.max(top[...], axis=1) + jnp.log2(jnp.where(found, summed, 1.0)), FLOOR)


def vmem_spec():
    return pl.BlockSpec(memory_space=pltpu.VMEM)


def smem_spec():
    return pl.BlockSpec(memory_space=pltpu.SMEM)


def costs(tiles, counts, src, tgt):
    slots = tiles.shape[1]
    width = src.shape[0]
    shape = pltpu.VMEM((slots, TILE, TILE), jnp.float32)
    return pl.pallas_call(
        cost_kernel,
        out_shape=(shape, shape),
        in_specs=[smem_spec(), smem_spec(), pl.BlockSpec(memory_space=pl.ANY), pl.BlockSpec(memory_space=pl.ANY)],
        out_specs=(vmem_spec(), vmem_spec()),
        scratch_shapes=[
            pltpu.VMEM((slots, width, TILE), jnp.float32),
            pltpu.VMEM((slots, width, TILE), jnp.float32),
            pltpu.VMEM((2, DEPTH, TILE), jnp.float32),
            pltpu.VMEM((6 * DEPTH, TILE), jnp.bfloat16),
            pltpu.VMEM((6 * DEPTH, TILE), jnp.bfloat16),
            pltpu.SemaphoreType.DMA((slots,)),
            pltpu.SemaphoreType.DMA((slots,)),
        ],
        compiler_params=pltpu.CompilerParams(vmem_limit_bytes=VMEM_LIMIT),
    )(tiles, counts, src, tgt)


def sweep(tiles, counts, cost, parts, cells, inner, outer, blocks_in, blocks_out):
    kernel = functools.partial(
        sweep_kernel, math.log2(1.0 / cells), 1.0 / SCALE, inner, outer, blocks_in, blocks_out
    )
    return pl.pallas_call(
        kernel,
        out_shape=(
            jax.ShapeDtypeStruct((blocks_out, TILE), jnp.float32),
            jax.ShapeDtypeStruct((blocks_in, TILE), jnp.float32),
        ),
        in_specs=[smem_spec(), smem_spec()] + [vmem_spec()] * (1 + len(parts)),
        out_specs=(vmem_spec(), vmem_spec()),
        scratch_shapes=[
            pltpu.VMEM((TILE, HALF), jnp.float32),
            pltpu.VMEM((blocks_out, ROWS, TILE), jnp.float32),
            pltpu.VMEM((blocks_out, ROWS, TILE), jnp.float32),
        ],
        compiler_params=pltpu.CompilerParams(vmem_limit_bytes=VMEM_LIMIT),
    )(tiles, counts, cost, *parts)


def fan(value, axis, size, stride, count):
    got = [value]
    for turn in range(1, count):
        pairs = []
        for k in range(size):
            place = (k // stride) % count
            pairs.append((k, k + ((place ^ turn) - place) * stride))
        got.append(lax.ppermute(value, axis, pairs))
    return got


def pair(value, axis, size, flip):
    return [value, lax.ppermute(value, axis, [(k, flip(k)) for k in range(size)])]


def over_tgt(value):
    size = lax.axis_size("tgt")
    value = lse2_many(pair(value, "tgt", size, lambda k: k ^ 1))
    return fan(value, "tgt", size, 2, size // 2)


def over_src(value):
    size = lax.axis_size("src")
    value = lse2_many(fan(value, "src", size, 1, 4))
    value = lse2_many(pair(value, "src", size, lambda k: k ^ 4))
    value = lse2_many(pair(value, "src", size, lambda k: k ^ 12))
    return pair(value, "src", size, lambda k: k ^ 28)


def body(src_points, tgt_points, tiles, counts):
    tiles = tiles[0, 0]
    counts = counts[0]
    row_blocks = src_points.shape[1] // TILE
    col_blocks = tgt_points.shape[1] // TILE
    src_cells = src_points.shape[1] * lax.axis_size("src")
    tgt_cells = tgt_points.shape[1] * lax.axis_size("tgt")
    cost_ab, cost_ba = costs(tiles, counts, src_points, tgt_points)
    parts = []
    for _ in range(ITERS):
        rows, _ = sweep(tiles, counts, cost_ba, parts, tgt_cells, 1, 0, col_blocks, row_blocks)
        parts = over_tgt(rows)
        cols, source = sweep(tiles, counts, cost_ab, parts, src_cells, 0, 1, row_blocks, col_blocks)
        parts = over_src(cols)
    target = (math.log2(1.0 / tgt_cells) - lse2_many(parts)) / SCALE
    return (source.reshape(-1), target.reshape(-1))


def solution(mesh):
    in_specs = (P(None, "src"), P(None, "tgt"), P("src", "tgt", None, None), P("src", "tgt"))
    out_specs = (P("src"), P("tgt"))
    return jax.shard_map(body, mesh=mesh, in_specs=in_specs, out_specs=out_specs, check_vma=False)
```

time: 829 us -> 178 us (0.21); the launches traced: 816 us -> 175 us
  waiting for transfers between devices: 454 us -> 58.7 us
  local copies, waits for them, and re-layouts: 184 us -> 6.63 us
  starting transfers between devices: 0.86 us -> 83.6 us
  blocking collectives: 80 us -> 0 us
  other arithmetic: 68.5 us -> 0.86 us
  Pallas kernels: 0 us -> 24.2 us
  between operations: 15.5 us -> 1.38 us
  matrix products: 10.9 us -> 0 us
    all_gather x6 -> x0, waiting for transfers between devices: 453 us -> none  [joined(): everything = jax.tree.map(lambda part: lax.all_gather(part, axis), shard)]
    dynamic_slice x114 -> x0, local copies, waits for them, and re-layouts: 121 us -> none  [hop(): return combine(so_far, jax.tree.map(lambda part: part[k], everything))]
    ppermute x0 -> x30, starting transfers between devices: none -> 83.6 us  [the longest x18 47.7 us: fan(): got.append(lax.ppermute(value, axis, pairs))]
    all_gather x6 -> x0, blocking collectives: 80 us -> none  [joined(): everything = jax.tree.map(lambda part: lax.all_gather(part, axis), shard)]
    ppermute x0 -> x30, waiting for transfers between devices: none -> 58.7 us  [the longest x12 32.6 us: pair(): lax.ppermute(value, axis, [(k, flip(k)) for k in range(size)])]
    unnamed x36 -> x8, local copies, waits for them, and re-layouts: 41.4 us -> 6.63 us
    reduce_sum x13 -> x0, other arithmetic: 30.7 us -> none  [the longest x6 23.9 us: block_partial(): jnp.sum(jnp.exp(scores - jnp.expand_dims(peak, axis_num)), axis=axis_num)]
    reduce_max x11 -> x0, other arithmetic: 24.3 us -> none  [the longest x5 21.6 us: block_partial(): peak = jnp.max(scores, axis=axis_num)]
  transfers between devices with their start and end apart: 6 -> 30, of which waited for: 6 -> 27; matrix products, arithmetic and copies ran while one was open for 2% -> 0% of each run, Pallas kernels for 0% -> 0%
where the time goes in v1:
time: 178 us; the launch traced here: 175 us
  starting transfers between devices  83.6 us (47%)
  waiting for transfers between devices  58.7 us (33%)
  Pallas kernels  24.2 us (14%)
  local copies, waits for them, and re-layouts  6.63 us (4%)
    ppermute x18, starting transfers between devices, fan(): got.append(lax.ppermute(value, axis, pairs))  47.7 us
    ppermute x12, starting transfers between devices, pair(): lax.ppermute(value, axis, [(k, flip(k)) for k in range(size)])  35.9 us
    ppermute x12, waiting for transfers between devices, pair(): lax.ppermute(value, axis, [(k, flip(k)) for k in range(size)])  32.6 us
    ppermute x18, waiting for transfers between devices, fan(): got.append(lax.ppermute(value, axis, pairs))  26 us
    pallas_call x6, Pallas kernels, sweep(): pl.pallas_call(kernel, out_shape=(jax.ShapeDtypeStruct((blocks_out, TILE)...  19.5 us
    unnamed x8, local copies, waits for them, and re-layouts  6.63 us
    pallas_call x1, Pallas kernels, costs(): pl.pallas_call(cost_kernel, out_shape=(shape, shape), in_specs=[smem_spec...  4.75 us
  transfers between devices with their start and end apart: 30, of which 27 were waited for; matrix products, arithmetic and copies ran while one was open for 0% of the time, Pallas kernels for 0%

profile of v1, /device:TPU:2, one launch (start us, length us, event | category | flops | bytes accessed | tf_op | source)
XLA Modules:
  0.0 175.4 jit_solution(2542424749769102775)
XLA Ops:
  1.3 2.6 %copy-done = f32[50,24576]{1,0:T(8,128)S(1)} copy-done((f32[50,24576]{1,0:T(8,128)S(1)}, f32[50,24576]{1,0:T(8,128)}, u32[]{:S(2)}) %copy-start) | copy-done | bytes 4915224
  6.6 4.8 %shard_map.59 = (f32[32,256,256]{2,1,0:T(8,128)S(1)}, f32[32,256,256]{2,1,0:T(8,128)S(1)}) custom-call(s32[2,32]{1,0:T(2,128)S(1)} %bitcast.15, s32[1]{0:T(128)} %bitcast.7.counts, f32[50,16384]{1,0:T(8,128)S(1)} %copy-done.1, f32[50,24576]{1,0:T(8,128)S(1)} %copy-done), custom_call_target="tpu_custom_call" | custom-call | tf_op jit(solution)/shard_map/pallas_call | solution.py:154
  14.7 5.1 %collective-permute-start.3 = (f32[64,256]{1,0:T(8,128)S(1)}, f32[64,256]{1,0:T(8,128)S(1)}, u32[]{:S(2)}, u32[]{:S(2)}) collective-permute-start(f32[64,256]{1,0:T(8,128)S(1)} %multiply_add_fusion.11.refs_0_), channel_id=1, source_target_pairs={{0,6},{1,7},{2,4},{3,5},{4,2},{5,3},{6,0},{7,1},{8,14},{9,15},{10,... | collective-permute-start | bytes 196616 | tf_op jit(solution)/shard_map/ppermute | solution.py:200
  19.8 10.0 %collective-permute-start.2 = (f32[64,256]{1,0:T(8,128)S(1)}, f32[64,256]{1,0:T(8,128)S(1)}, u32[]{:S(2)}, u32[]{:S(2)}) collective-permute-start(f32[64,256]{1,0:T(8,128)S(1)} %multiply_add_fusion.11.refs_0_), channel_id=1, source_target_pairs={{0,4},{1,5},{2,6},{3,7},{4,0},{5,1},{6,2},{7,3},{8,12},{9,13},{10,... | collective-permute-start | bytes 196616 | tf_op jit(solution)/shard_map/ppermute | solution.py:200
  34.1 3.5 %shard_map.61 = (f32[96,256]{1,0:T(8,128)S(1)}, f32[64,256]{1,0:T(8,128)}) custom-call(s32[2,32]{1,0:T(2,128)S(1)} %bitcast.17, s32[1]{0:T(128)} %bitcast.9.counts, f32[32,256,256]{2,1,0:T(8,128)S(1)} %get-tuple-element.11.cost, f32[64,256]{1,0:T(8,128)S(1)} %multiply_add_fusion.11.refs_0_, f32[64,256]{1,0:T(8,128)S(1)} %collective-permute-done.1.refs_1_, ...), custom_call_target="tpu_custom_call" | custom-call | tf_op jit(solution)/shard_map/pallas_call | solution.py:176
  42.8 2.7 %collective-permute-done.5 = f32[96,256]{1,0:T(8,128)S(1)} collective-permute-done((f32[96,256]{1,0:T(8,128)S(1)}, f32[96,256]{1,0:T(8,128)S(1)}, u32[]{:S(2)}, u32[]{:S(2)}) %collective-permute-start.5) | collective-permute-done | bytes 98336 | tf_op jit(solution)/shard_map/ppermute | solution.py:200
  46.8 3.4 %collective-permute-start.7 = (f32[96,256]{1,0:T(8,128)S(1)}, f32[96,256]{1,0:T(8,128)S(1)}, u32[]{:S(2)}, u32[]{:S(2)}) collective-permute-start(f32[96,256]{1,0:T(8,128)S(1)} %multiply_add_fusion.8), channel_id=1, source_target_pairs={{0,32},{8,40},{16,48},{24,56},{32,0},{40,8},{48,16},{56,24},{64,96... | collective-permute-start | bytes 294920 | tf_op jit(solution)/shard_map/ppermute | solution.py:205
  50.2 2.6 %collective-permute-done.7 = f32[96,256]{1,0:T(8,128)S(1)} collective-permute-done((f32[96,256]{1,0:T(8,128)S(1)}, f32[96,256]{1,0:T(8,128)S(1)}, u32[]{:S(2)}, u32[]{:S(2)}) %collective-permute-start.7) | collective-permute-done | bytes 98336 | tf_op jit(solution)/shard_map/ppermute | solution.py:205
  52.9 2.8 %collective-permute-start.8 = (f32[96,256]{1,0:T(8,128)S(1)}, f32[96,256]{1,0:T(8,128)S(1)}, u32[]{:S(2)}, u32[]{:S(2)}) collective-permute-start(f32[96,256]{1,0:T(8,128)S(1)} %multiply_add_fusion.7), channel_id=1, source_target_pairs={{0,96},{8,104},{16,112},{24,120},{32,64},{40,72},{48,80},{56,88},{... | collective-permute-start | bytes 294920 | tf_op jit(solution)/shard_map/ppermute | solution.py:205
  55.6 3.8 %collective-permute-done.8 = f32[96,256]{1,0:T(8,128)S(1)} collective-permute-done((f32[96,256]{1,0:T(8,128)S(1)}, f32[96,256]{1,0:T(8,128)S(1)}, u32[]{:S(2)}, u32[]{:S(2)}) %collective-permute-start.8) | collective-permute-done | bytes 98336 | tf_op jit(solution)/shard_map/ppermute | solution.py:205
  59.5 7.3 %collective-permute-start.9 = (f32[96,256]{1,0:T(8,128)S(1)}, f32[96,256]{1,0:T(8,128)S(1)}, u32[]{:S(2)}, u32[]{:S(2)}) collective-permute-start(f32[96,256]{1,0:T(8,128)S(1)} %multiply_add_fusion.6.refs_0_), channel_id=1, source_target_pairs={{0,224},{8,232},{16,240},{24,248},{32,192},{40,200},{48,208},{56,2... | collective-permute-start | bytes 294920 | tf_op jit(solution)/shard_map/ppermute | solution.py:205
  66.8 2.6 %collective-permute-done.9.refs_1_ = f32[96,256]{1,0:T(8,128)S(1)} collective-permute-done((f32[96,256]{1,0:T(8,128)S(1)}, f32[96,256]{1,0:T(8,128)S(1)}, u32[]{:S(2)}, u32[]{:S(2)}) %collective-permute-start.9) | collective-permute-done | bytes 98336 | tf_op jit(solution)/shard_map/ppermute | solution.py:205
  69.4 3.5 %shard_map.62 = (f32[64,256]{1,0:T(8,128)S(1)}, f32[96,256]{1,0:T(8,128)}) custom-call(s32[2,32]{1,0:T(2,128)S(1)} %bitcast.18, s32[1]{0:T(128)} %bitcast.10.counts, f32[32,256,256]{2,1,0:T(8,128)S(1)} %get-tuple-element.12.cost, f32[96,256]{1,0:T(8,128)S(1)} %multiply_add_fusion.6.refs_0_, f32[96,256]{1,0:T(8,128)S(1)} %collective-permute-done.9.refs_1_), custom_call_target="tpu_custom_call" | custom-call | tf_op jit(solution)/shard_map/pallas_call | solution.py:176
  74.2 5.5 %collective-permute-start.13 = (f32[64,256]{1,0:T(8,128)S(1)}, f32[64,256]{1,0:T(8,128)S(1)}, u32[]{:S(2)}, u32[]{:S(2)}) collective-permute-start(f32[64,256]{1,0:T(8,128)S(1)} %multiply_add_fusion.10.refs_0_), channel_id=1, source_target_pairs={{0,6},{1,7},{2,4},{3,5},{4,2},{5,3},{6,0},{7,1},{8,14},{9,15},{10,... | collective-permute-start | bytes 196616 | tf_op jit(solution)/shard_map/ppermute | solution.py:200
  79.7 4.2 %collective-permute-start.12 = (f32[64,256]{1,0:T(8,128)S(1)}, f32[64,256]{1,0:T(8,128)S(1)}, u32[]{:S(2)}, u32[]{:S(2)}) collective-permute-start(f32[64,256]{1,0:T(8,128)S(1)} %multiply_add_fusion.10.refs_0_), channel_id=1, source_target_pairs={{0,4},{1,5},{2,6},{3,7},{4,0},{5,1},{6,2},{7,3},{8,12},{9,13},{10,... | collective-permute-start | bytes 196616 | tf_op jit(solution)/shard_map/ppermute | solution.py:200
  88.1 3.5 %shard_map.63 = (f32[96,256]{1,0:T(8,128)S(1)}, f32[64,256]{1,0:T(8,128)}) custom-call(s32[2,32]{1,0:T(2,128)S(1)} %bitcast.19, s32[1]{0:T(128)} %bitcast.11.counts, f32[32,256,256]{2,1,0:T(8,128)S(1)} %get-tuple-element.11.cost, f32[64,256]{1,0:T(8,128)S(1)} %multiply_add_fusion.10.refs_0_, f32[64,256]{1,0:T(8,128)S(1)} %collective-permute-done.11.refs_1_, ...), custom_call_target="tpu_custom_call" | custom-call | tf_op jit(solution)/shard_map/pallas_call | solution.py:176
  92.7 3.1 %collective-permute-start.14 = (f32[96,256]{1,0:T(8,128)S(1)}, f32[96,256]{1,0:T(8,128)S(1)}, u32[]{:S(2)}, u32[]{:S(2)}) collective-permute-start(f32[96,256]{1,0:T(8,128)S(1)} %get-tuple-element.16), channel_id=1, source_target_pairs={{0,8},{8,0},{16,24},{24,16},{32,40},{40,32},{48,56},{56,48},{64,72... | collective-permute-start | bytes 294920 | tf_op jit(solution)/shard_map/ppermute | solution.py:200
  96.3 2.6 %collective-permute-done.15 = f32[96,256]{1,0:T(8,128)S(1)} collective-permute-done((f32[96,256]{1,0:T(8,128)S(1)}, f32[96,256]{1,0:T(8,128)S(1)}, u32[]{:S(2)}, u32[]{:S(2)}) %collective-permute-start.15) | collective-permute-done | bytes 98336 | tf_op jit(solution)/shard_map/ppermute | solution.py:200
  101.5 3.6 %collective-permute-done.17 = f32[96,256]{1,0:T(8,128)S(1)} collective-permute-done((f32[96,256]{1,0:T(8,128)S(1)}, f32[96,256]{1,0:T(8,128)S(1)}, u32[]{:S(2)}, u32[]{:S(2)}) %collective-permute-start.17) | collective-permute-done | bytes 98336 | tf_op jit(solution)/shard_map/ppermute | solution.py:205
  105.1 3.2 %collective-permute-start.18 = (f32[96,256]{1,0:T(8,128)S(1)}, f32[96,256]{1,0:T(8,128)S(1)}, u32[]{:S(2)}, u32[]{:S(2)}) collective-permute-start(f32[96,256]{1,0:T(8,128)S(1)} %multiply_add_fusion.4), channel_id=1, source_target_pairs={{0,96},{8,104},{16,112},{24,120},{32,64},{40,72},{48,80},{56,88},{... | collective-permute-start | bytes 294920 | tf_op jit(solution)/shard_map/ppermute | solution.py:205
  108.3 3.4 %collective-permute-done.18 = f32[96,256]{1,0:T(8,128)S(1)} collective-permute-done((f32[96,256]{1,0:T(8,128)S(1)}, f32[96,256]{1,0:T(8,128)S(1)}, u32[]{:S(2)}, u32[]{:S(2)}) %collective-permute-start.18) | collective-permute-done | bytes 98336 | tf_op jit(solution)/shard_map/ppermute | solution.py:205
  111.8 8.1 %collective-permute-start.19 = (f32[96,256]{1,0:T(8,128)S(1)}, f32[96,256]{1,0:T(8,128)S(1)}, u32[]{:S(2)}, u32[]{:S(2)}) collective-permute-start(f32[96,256]{1,0:T(8,128)S(1)} %multiply_add_fusion.3.refs_0_), channel_id=1, source_target_pairs={{0,224},{8,232},{16,240},{24,248},{32,192},{40,200},{48,208},{56,2... | collective-permute-start | bytes 294920 | tf_op jit(solution)/shard_map/ppermute | solution.py:205
  119.8 2.6 %collective-permute-done.19.refs_1_ = f32[96,256]{1,0:T(8,128)S(1)} collective-permute-done((f32[96,256]{1,0:T(8,128)S(1)}, f32[96,256]{1,0:T(8,128)S(1)}, u32[]{:S(2)}, u32[]{:S(2)}) %collective-permute-start.19) | collective-permute-done | bytes 98336 | tf_op jit(solution)/shard_map/ppermute | solution.py:205
  122.4 3.5 %shard_map.64 = (f32[64,256]{1,0:T(8,128)S(1)}, f32[96,256]{1,0:T(8,128)}) custom-call(s32[2,32]{1,0:T(2,128)S(1)} %bitcast.20, s32[1]{0:T(128)} %bitcast.12.counts, f32[32,256,256]{2,1,0:T(8,128)S(1)} %get-tuple-element.12.cost, f32[96,256]{1,0:T(8,128)S(1)} %multiply_add_fusion.3.refs_0_, f32[96,256]{1,0:T(8,128)S(1)} %collective-permute-done.19.refs_1_), custom_call_target="tpu_custom_call" | custom-call | tf_op jit(solution)/shard_map/pallas_call | solution.py:176
  127.2 4.5 %collective-permute-start.23 = (f32[64,256]{1,0:T(8,128)S(1)}, f32[64,256]{1,0:T(8,128)S(1)}, u32[]{:S(2)}, u32[]{:S(2)}) collective-permute-start(f32[64,256]{1,0:T(8,128)S(1)} %multiply_add_fusion.9.refs_0_), channel_id=1, source_target_pairs={{0,6},{1,7},{2,4},{3,5},{4,2},{5,3},{6,0},{7,1},{8,14},{9,15},{10,... | collective-permute-start | bytes 196616 | tf_op jit(solution)/shard_map/ppermute | solution.py:200
  131.7 6.2 %collective-permute-start.22 = (f32[64,256]{1,0:T(8,128)S(1)}, f32[64,256]{1,0:T(8,128)S(1)}, u32[]{:S(2)}, u32[]{:S(2)}) collective-permute-start(f32[64,256]{1,0:T(8,128)S(1)} %multiply_add_fusion.9.refs_0_), channel_id=1, source_target_pairs={{0,4},{1,5},{2,6},{3,7},{4,0},{5,1},{6,2},{7,3},{8,12},{9,13},{10,... | collective-permute-start | bytes 196616 | tf_op jit(solution)/shard_map/ppermute | solution.py:200
  142.2 3.3 %shard_map.65 = (f32[96,256]{1,0:T(8,128)S(1)}, f32[64,256]{1,0:T(8,128)S(1)}) custom-call(s32[2,32]{1,0:T(2,128)S(1)} %bitcast.21, s32[1]{0:T(128)} %bitcast.13.counts, f32[32,256,256]{2,1,0:T(8,128)S(1)} %get-tuple-element.11.cost, f32[64,256]{1,0:T(8,128)S(1)} %multiply_add_fusion.9.refs_0_, f32[64,256]{1,0:T(8,128)S(1)} %collective-permute-done.21.refs_1_, ...), custom_call_target="tpu_custom_call" | custom-call | tf_op jit(solution)/shard_map/pallas_call | solution.py:176
  145.7 4.0 %collective-permute-start.24 = (f32[96,256]{1,0:T(8,128)S(1)}, f32[96,256]{1,0:T(8,128)S(1)}, u32[]{:S(2)}, u32[]{:S(2)}) collective-permute-start(f32[96,256]{1,0:T(8,128)S(1)} %get-tuple-element.19), channel_id=1, source_target_pairs={{0,8},{8,0},{16,24},{24,16},{32,40},{40,32},{48,56},{56,48},{64,72... | collective-permute-start | bytes 294920 | tf_op jit(solution)/shard_map/ppermute | solution.py:200
  153.5 4.6 %collective-permute-done.27 = f32[96,256]{1,0:T(8,128)S(1)} collective-permute-done((f32[96,256]{1,0:T(8,128)S(1)}, f32[96,256]{1,0:T(8,128)S(1)}, u32[]{:S(2)}, u32[]{:S(2)}) %collective-permute-start.27) | collective-permute-done | bytes 98336 | tf_op jit(solution)/shard_map/ppermute | solution.py:205
  158.2 2.9 %collective-permute-start.28 = (f32[96,256]{1,0:T(8,128)S(1)}, f32[96,256]{1,0:T(8,128)S(1)}, u32[]{:S(2)}, u32[]{:S(2)}) collective-permute-start(f32[96,256]{1,0:T(8,128)S(1)} %multiply_add_fusion.1), channel_id=1, source_target_pairs={{0,96},{8,104},{16,112},{24,120},{32,64},{40,72},{48,80},{56,88},{... | collective-permute-start | bytes 294920 | tf_op jit(solution)/shard_map/ppermute | solution.py:205
  161.1 3.7 %collective-permute-done.28 = f32[96,256]{1,0:T(8,128)S(1)} collective-permute-done((f32[96,256]{1,0:T(8,128)S(1)}, f32[96,256]{1,0:T(8,128)S(1)}, u32[]{:S(2)}, u32[]{:S(2)}) %collective-permute-start.28) | collective-permute-done | bytes 98336 | tf_op jit(solution)/shard_map/ppermute | solution.py:205
  164.9 7.2 %collective-permute-start.29 = (f32[96,256]{1,0:T(8,128)S(1)}, f32[96,256]{1,0:T(8,128)S(1)}, u32[]{:S(2)}, u32[]{:S(2)}) collective-permute-start(f32[96,256]{1,0:T(8,128)S(1)} %multiply_add_fusion), channel_id=1, source_target_pairs={{0,224},{8,232},{16,240},{24,248},{32,192},{40,200},{48,208},{56,2... | collective-permute-start | bytes 294920 | tf_op jit(solution)/shard_map/ppermute | solution.py:205
  (56 shorter events, 39.9 us)
Async XLA Ops:
  1.3 2.6 %copy-start = (f32[50,24576]{1,0:T(8,128)S(1)}, f32[50,24576]{1,0:T(8,128)}, u32[]{:S(2)}) copy-start(f32[50,24576]{1,0:T(8,128)} %tgt.1) | copy-start | bytes 14745604
  3.8 2.0 %copy-start.1 = (f32[50,16384]{1,0:T(8,128)S(1)}, f32[50,16384]{1,0:T(8,128)}, u32[]{:S(2)}) copy-start(f32[50,16384]{1,0:T(8,128)} %src.1) | copy-start | bytes 9830404
  13.4 1.3 collective-permute-start
  14.7 15.1 %collective-permute-start.3 = (f32[64,256]{1,0:T(8,128)S(1)}, f32[64,256]{1,0:T(8,128)S(1)}, u32[]{:S(2)}, u32[]{:S(2)}) collective-permute-start(f32[64,256]{1,0:T(8,128)S(1)} %multiply_add_fusion.11.refs_0_), channel_id=1, source_target_pairs={{0,6},{1,7},{2,4},{3,5},{4,2},{5,3},{6,0},{7,1},{8,14},{9,15},{10,... | collective-permute-start | bytes 196616 | tf_op jit(solution)/shard_map/ppermute | solution.py:200
  19.8 12.2 %collective-permute-start.2 = (f32[64,256]{1,0:T(8,128)S(1)}, f32[64,256]{1,0:T(8,128)S(1)}, u32[]{:S(2)}, u32[]{:S(2)}) collective-permute-start(f32[64,256]{1,0:T(8,128)S(1)} %multiply_add_fusion.11.refs_0_), channel_id=1, source_target_pairs={{0,4},{1,5},{2,6},{3,7},{4,0},{5,1},{6,2},{7,3},{8,12},{9,13},{10,... | collective-permute-start | bytes 196616 | tf_op jit(solution)/shard_map/ppermute | solution.py:200
  29.8 4.3 %collective-permute-start.1 = (f32[64,256]{1,0:T(8,128)S(1)}, f32[64,256]{1,0:T(8,128)S(1)}, u32[]{:S(2)}, u32[]{:S(2)}) collective-permute-start(f32[64,256]{1,0:T(8,128)S(1)} %multiply_add_fusion.11.refs_0_), channel_id=1, source_target_pairs={{0,2},{1,3},{2,0},{3,1},{4,6},{5,7},{6,4},{7,5},{8,10},{9,11},{10,... | collective-permute-start | bytes 196616 | tf_op jit(solution)/shard_map/ppermute | solution.py:200
  37.6 5.2 %collective-permute-start.6 = (f32[96,256]{1,0:T(8,128)S(1)}, f32[96,256]{1,0:T(8,128)S(1)}, u32[]{:S(2)}, u32[]{:S(2)}) collective-permute-start(f32[96,256]{1,0:T(8,128)S(1)} %get-tuple-element.14), channel_id=1, source_target_pairs={{0,24},{8,16},{16,8},{24,0},{32,56},{40,48},{48,40},{56,32},{64,88... | collective-permute-start | bytes 294920 | tf_op jit(solution)/shard_map/ppermute | solution.py:200
  38.5 7.1 %collective-permute-start.5 = (f32[96,256]{1,0:T(8,128)S(1)}, f32[96,256]{1,0:T(8,128)S(1)}, u32[]{:S(2)}, u32[]{:S(2)}) collective-permute-start(f32[96,256]{1,0:T(8,128)S(1)} %get-tuple-element.14), channel_id=1, source_target_pairs={{0,16},{8,24},{16,0},{24,8},{32,48},{40,56},{48,32},{56,40},{64,80... | collective-permute-start | bytes 294920 | tf_op jit(solution)/shard_map/ppermute | solution.py:200
  39.5 7.2 %collective-permute-start.4 = (f32[96,256]{1,0:T(8,128)S(1)}, f32[96,256]{1,0:T(8,128)S(1)}, u32[]{:S(2)}, u32[]{:S(2)}) collective-permute-start(f32[96,256]{1,0:T(8,128)S(1)} %get-tuple-element.14), channel_id=1, source_target_pairs={{0,8},{8,0},{16,24},{24,16},{32,40},{40,32},{48,56},{56,48},{64,72... | collective-permute-start | bytes 294920 | tf_op jit(solution)/shard_map/ppermute | solution.py:200
  46.8 6.0 %collective-permute-start.7 = (f32[96,256]{1,0:T(8,128)S(1)}, f32[96,256]{1,0:T(8,128)S(1)}, u32[]{:S(2)}, u32[]{:S(2)}) collective-permute-start(f32[96,256]{1,0:T(8,128)S(1)} %multiply_add_fusion.8), channel_id=1, source_target_pairs={{0,32},{8,40},{16,48},{24,56},{32,0},{40,8},{48,16},{56,24},{64,96... | collective-permute-start | bytes 294920 | tf_op jit(solution)/shard_map/ppermute | solution.py:205
  52.9 6.6 %collective-permute-start.8 = (f32[96,256]{1,0:T(8,128)S(1)}, f32[96,256]{1,0:T(8,128)S(1)}, u32[]{:S(2)}, u32[]{:S(2)}) collective-permute-start(f32[96,256]{1,0:T(8,128)S(1)} %multiply_add_fusion.7), channel_id=1, source_target_pairs={{0,96},{8,104},{16,112},{24,120},{32,64},{40,72},{48,80},{56,88},{... | collective-permute-start | bytes 294920 | tf_op jit(solution)/shard_map/ppermute | solution.py:205
  59.5 9.9 %collective-permute-start.9 = (f32[96,256]{1,0:T(8,128)S(1)}, f32[96,256]{1,0:T(8,128)S(1)}, u32[]{:S(2)}, u32[]{:S(2)}) collective-permute-start(f32[96,256]{1,0:T(8,128)S(1)} %multiply_add_fusion.6.refs_0_), channel_id=1, source_target_pairs={{0,224},{8,232},{16,240},{24,248},{32,192},{40,200},{48,208},{56,2... | collective-permute-start | bytes 294920 | tf_op jit(solution)/shard_map/ppermute | solution.py:205
  72.9 1.3 collective-permute-start.10
  74.2 9.6 %collective-permute-start.13 = (f32[64,256]{1,0:T(8,128)S(1)}, f32[64,256]{1,0:T(8,128)S(1)}, u32[]{:S(2)}, u32[]{:S(2)}) collective-permute-start(f32[64,256]{1,0:T(8,128)S(1)} %multiply_add_fusion.10.refs_0_), channel_id=1, source_target_pairs={{0,6},{1,7},{2,4},{3,5},{4,2},{5,3},{6,0},{7,1},{8,14},{9,15},{10,... | collective-permute-start | bytes 196616 | tf_op jit(solution)/shard_map/ppermute | solution.py:200
  79.7 6.4 %collective-permute-start.12 = (f32[64,256]{1,0:T(8,128)S(1)}, f32[64,256]{1,0:T(8,128)S(1)}, u32[]{:S(2)}, u32[]{:S(2)}) collective-permute-start(f32[64,256]{1,0:T(8,128)S(1)} %multiply_add_fusion.10.refs_0_), channel_id=1, source_target_pairs={{0,4},{1,5},{2,6},{3,7},{4,0},{5,1},{6,2},{7,3},{8,12},{9,13},{10,... | collective-permute-start | bytes 196616 | tf_op jit(solution)/shard_map/ppermute | solution.py:200
  83.9 4.3 %collective-permute-start.11 = (f32[64,256]{1,0:T(8,128)S(1)}, f32[64,256]{1,0:T(8,128)S(1)}, u32[]{:S(2)}, u32[]{:S(2)}) collective-permute-start(f32[64,256]{1,0:T(8,128)S(1)} %multiply_add_fusion.10.refs_0_), channel_id=1, source_target_pairs={{0,2},{1,3},{2,0},{3,1},{4,6},{5,7},{6,4},{7,5},{8,10},{9,11},{10,... | collective-permute-start | bytes 196616 | tf_op jit(solution)/shard_map/ppermute | solution.py:200
  91.6 4.6 %collective-permute-start.16 = (f32[96,256]{1,0:T(8,128)S(1)}, f32[96,256]{1,0:T(8,128)S(1)}, u32[]{:S(2)}, u32[]{:S(2)}) collective-permute-start(f32[96,256]{1,0:T(8,128)S(1)} %get-tuple-element.16), channel_id=1, source_target_pairs={{0,24},{8,16},{16,8},{24,0},{32,56},{40,48},{48,40},{56,32},{64,88... | collective-permute-start | bytes 294920 | tf_op jit(solution)/shard_map/ppermute | solution.py:200
  91.6 7.2 %collective-permute-start.15 = (f32[96,256]{1,0:T(8,128)S(1)}, f32[96,256]{1,0:T(8,128)S(1)}, u32[]{:S(2)}, u32[]{:S(2)}) collective-permute-start(f32[96,256]{1,0:T(8,128)S(1)} %get-tuple-element.16), channel_id=1, source_target_pairs={{0,16},{8,24},{16,0},{24,8},{32,48},{40,56},{48,32},{56,40},{64,80... | collective-permute-start | bytes 294920 | tf_op jit(solution)/shard_map/ppermute | solution.py:200
  92.7 7.6 %collective-permute-start.14 = (f32[96,256]{1,0:T(8,128)S(1)}, f32[96,256]{1,0:T(8,128)S(1)}, u32[]{:S(2)}, u32[]{:S(2)}) collective-permute-start(f32[96,256]{1,0:T(8,128)S(1)} %get-tuple-element.16), channel_id=1, source_target_pairs={{0,8},{8,0},{16,24},{24,16},{32,40},{40,32},{48,56},{56,48},{64,72... | collective-permute-start | bytes 294920 | tf_op jit(solution)/shard_map/ppermute | solution.py:200
  100.4 4.7 %collective-permute-start.17 = (f32[96,256]{1,0:T(8,128)S(1)}, f32[96,256]{1,0:T(8,128)S(1)}, u32[]{:S(2)}, u32[]{:S(2)}) collective-permute-start(f32[96,256]{1,0:T(8,128)S(1)} %multiply_add_fusion.5), channel_id=1, source_target_pairs={{0,32},{8,40},{16,48},{24,56},{32,0},{40,8},{48,16},{56,24},{64,96... | collective-permute-start | bytes 294920 | tf_op jit(solution)/shard_map/ppermute | solution.py:205
  105.1 6.6 %collective-permute-start.18 = (f32[96,256]{1,0:T(8,128)S(1)}, f32[96,256]{1,0:T(8,128)S(1)}, u32[]{:S(2)}, u32[]{:S(2)}) collective-permute-start(f32[96,256]{1,0:T(8,128)S(1)} %multiply_add_fusion.4), channel_id=1, source_target_pairs={{0,96},{8,104},{16,112},{24,120},{32,64},{40,72},{48,80},{56,88},{... | collective-permute-start | bytes 294920 | tf_op jit(solution)/shard_map/ppermute | solution.py:205
  111.8 10.7 %collective-permute-start.19 = (f32[96,256]{1,0:T(8,128)S(1)}, f32[96,256]{1,0:T(8,128)S(1)}, u32[]{:S(2)}, u32[]{:S(2)}) collective-permute-start(f32[96,256]{1,0:T(8,128)S(1)} %multiply_add_fusion.3.refs_0_), channel_id=1, source_target_pairs={{0,224},{8,232},{16,240},{24,248},{32,192},{40,200},{48,208},{56,2... | collective-permute-start | bytes 294920 | tf_op jit(solution)/shard_map/ppermute | solution.py:205
  125.9 1.3 collective-permute-start.20
  127.2 10.7 %collective-permute-start.23 = (f32[64,256]{1,0:T(8,128)S(1)}, f32[64,256]{1,0:T(8,128)S(1)}, u32[]{:S(2)}, u32[]{:S(2)}) collective-permute-start(f32[64,256]{1,0:T(8,128)S(1)} %multiply_add_fusion.9.refs_0_), channel_id=1, source_target_pairs={{0,6},{1,7},{2,4},{3,5},{4,2},{5,3},{6,0},{7,1},{8,14},{9,15},{10,... | collective-permute-start | bytes 196616 | tf_op jit(solution)/shard_map/ppermute | solution.py:200
  131.7 8.4 %collective-permute-start.22 = (f32[64,256]{1,0:T(8,128)S(1)}, f32[64,256]{1,0:T(8,128)S(1)}, u32[]{:S(2)}, u32[]{:S(2)}) collective-permute-start(f32[64,256]{1,0:T(8,128)S(1)} %multiply_add_fusion.9.refs_0_), channel_id=1, source_target_pairs={{0,4},{1,5},{2,6},{3,7},{4,0},{5,1},{6,2},{7,3},{8,12},{9,13},{10,... | collective-permute-start | bytes 196616 | tf_op jit(solution)/shard_map/ppermute | solution.py:200
  137.9 4.3 %collective-permute-start.21 = (f32[64,256]{1,0:T(8,128)S(1)}, f32[64,256]{1,0:T(8,128)S(1)}, u32[]{:S(2)}, u32[]{:S(2)}) collective-permute-start(f32[64,256]{1,0:T(8,128)S(1)} %multiply_add_fusion.9.refs_0_), channel_id=1, source_target_pairs={{0,2},{1,3},{2,0},{3,1},{4,6},{5,7},{6,4},{7,5},{8,10},{9,11},{10,... | collective-permute-start | bytes 196616 | tf_op jit(solution)/shard_map/ppermute | solution.py:200
  145.5 6.2 %collective-permute-start.26 = (f32[96,256]{1,0:T(8,128)S(1)}, f32[96,256]{1,0:T(8,128)S(1)}, u32[]{:S(2)}, u32[]{:S(2)}) collective-permute-start(f32[96,256]{1,0:T(8,128)S(1)} %get-tuple-element.19), channel_id=1, source_target_pairs={{0,24},{8,16},{16,8},{24,0},{32,56},{40,48},{48,40},{56,32},{64,88... | collective-permute-start | bytes 294920 | tf_op jit(solution)/shard_map/ppermute | solution.py:200
  145.6 6.9 %collective-permute-start.25 = (f32[96,256]{1,0:T(8,128)S(1)}, f32[96,256]{1,0:T(8,128)S(1)}, u32[]{:S(2)}, u32[]{:S(2)}) collective-permute-start(f32[96,256]{1,0:T(8,128)S(1)} %get-tuple-element.19), channel_id=1, source_target_pairs={{0,16},{8,24},{16,0},{24,8},{32,48},{40,56},{48,32},{56,40},{64,80... | collective-permute-start | bytes 294920 | tf_op jit(solution)/shard_map/ppermute | solution.py:200
  145.7 7.6 %collective-permute-start.24 = (f32[96,256]{1,0:T(8,128)S(1)}, f32[96,256]{1,0:T(8,128)S(1)}, u32[]{:S(2)}, u32[]{:S(2)}) collective-permute-start(f32[96,256]{1,0:T(8,128)S(1)} %get-tuple-element.19), channel_id=1, source_target_pairs={{0,8},{8,0},{16,24},{24,16},{32,40},{40,32},{48,56},{56,48},{64,72... | collective-permute-start | bytes 294920 | tf_op jit(solution)/shard_map/ppermute | solution.py:200
  153.4 4.7 %collective-permute-start.27 = (f32[96,256]{1,0:T(8,128)S(1)}, f32[96,256]{1,0:T(8,128)S(1)}, u32[]{:S(2)}, u32[]{:S(2)}) collective-permute-start(f32[96,256]{1,0:T(8,128)S(1)} %multiply_add_fusion.2), channel_id=1, source_target_pairs={{0,32},{8,40},{16,48},{24,56},{32,0},{40,8},{48,16},{56,24},{64,96... | collective-permute-start | bytes 294920 | tf_op jit(solution)/shard_map/ppermute | solution.py:205
  158.2 6.6 %collective-permute-start.28 = (f32[96,256]{1,0:T(8,128)S(1)}, f32[96,256]{1,0:T(8,128)S(1)}, u32[]{:S(2)}, u32[]{:S(2)}) collective-permute-start(f32[96,256]{1,0:T(8,128)S(1)} %multiply_add_fusion.1), channel_id=1, source_target_pairs={{0,96},{8,104},{16,112},{24,120},{32,64},{40,72},{48,80},{56,88},{... | collective-permute-start | bytes 294920 | tf_op jit(solution)/shard_map/ppermute | solution.py:205
  164.9 9.8 %collective-permute-start.29 = (f32[96,256]{1,0:T(8,128)S(1)}, f32[96,256]{1,0:T(8,128)S(1)}, u32[]{:S(2)}, u32[]{:S(2)}) collective-permute-start(f32[96,256]{1,0:T(8,128)S(1)} %multiply_add_fusion), channel_id=1, source_target_pairs={{0,224},{8,232},{16,240},{24,248},{32,192},{40,200},{48,208},{56,2... | collective-permute-start | bytes 294920 | tf_op jit(solution)/shard_map/ppermute | solution.py:205
  (1 other events, 0.7 us)

commit v2 on v1

v2 whole, which is shorter than its diff:
```python
import functools
import math

import jax
import jax.numpy as jnp
from jax import lax
from jax.experimental import pallas as pl
from jax.experimental.pallas import tpu as pltpu
from jax.sharding import PartitionSpec as P

TILE = 256
HALF = 128
ROWS = 8
GROUP = 8
ITERS = 3
EPS = 0.05
FLOOR = -1e30
SCALE = 1.0 / (EPS * math.log(2.0))
DEPTH = 64
LEAST = 2.0**-80
MOST = 2.0**100
VMEM_LIMIT = 16 * 1024 * 1024


def lse2_many(parts):
    top = functools.reduce(jnp.maximum, parts)
    return top + jnp.log2(functools.reduce(jnp.add, [jnp.exp2(p - top) for p in parts]))


def split(value):
    high = value.astype(jnp.bfloat16)
    rest = value - high.astype(jnp.float32)
    middle = rest.astype(jnp.bfloat16)
    low = (rest - middle.astype(jnp.float32)).astype(jnp.bfloat16)
    return high, middle, low


def halves():
    return [(h, pl.ds(h * HALF, HALF)) for h in range(2)]


def block(tiles, side, k, blocks):
    return jnp.minimum(tiles[side, k], blocks - 1)


def sums(k, cost, potential, shift):
    found = []
    for h, lanes in halves():
        kept = None
        for g, cells in halves():
            score = cost[k, cells, lanes]
            score = (0.0 - score if potential is None else potential[g] - score) - shift[h]
            part = jnp.sum(jnp.exp2(score).reshape(HALF // ROWS, ROWS, HALF), axis=0)
            kept = part if kept is None else kept + part
        found.append(jnp.sum(kept, axis=0, keepdims=True))
    return found


def peaks(k, cost, potential):
    found = []
    for h, lanes in halves():
        kept = None
        for g, cells in halves():
            score = cost[k, cells, lanes]
            score = 0.0 - score if potential is None else potential[g] - score
            part = jnp.max(score, axis=0, keepdims=True)
            kept = part if kept is None else jnp.maximum(kept, part)
        found.append(kept)
    return found


def spread(held, index):
    return [jnp.broadcast_to(held[g, pl.ds(index, 1), :], (HALF, HALF)).T for g in range(2)]


def add_up(live, tiles, outer, blocks_out, cost, potential_of, top, total):
    def group(q, carry):
        least, most = carry
        ready = []
        for u in range(GROUP):
            k = q * GROUP + u
            out = block(tiles, outer, k, blocks_out)
            shift = [top[h, pl.ds(out, 1), :] for h in range(2)]
            ready.append((k < live, out, sums(k, cost, potential_of(k), shift)))
        for on, out, found in ready:
            for h in range(2):
                total[h, pl.ds(out, 1), :] = total[h, pl.ds(out, 1), :] + jnp.where(on, found[h], 0.0)
                least = jnp.minimum(least, jnp.where(on, found[h], 1.0))
                most = jnp.maximum(most, jnp.where(on, found[h], 1.0))
        return least, most

    one = jnp.ones((1, HALF), jnp.float32)
    return lax.fori_loop(0, (live + GROUP - 1) // GROUP, group, (one, one))


def finish(out, top, total):
    for h, lanes in halves():
        found = total[h] > 0.0
        out[:, lanes] = jnp.where(found, top[h] + jnp.log2(jnp.where(found, total[h], 1.0)), FLOOR)


def cost_kernel(
    blocks_in, blocks_out, tiles, counts, src, tgt, cost_ab, cost_ba, out,
    xs, ys, ext, top, total, xsem, ysem
):
    live = counts[0]
    width = src.shape[0]

    def copies(k):
        row = pl.multiple_of(block(tiles, 0, k, blocks_out) * TILE, TILE)
        col = pl.multiple_of(block(tiles, 1, k, blocks_in) * TILE, TILE)
        return (
            pltpu.make_async_copy(src.at[:, pl.ds(row, TILE)], xs.at[k], xsem.at[k]),
            pltpu.make_async_copy(tgt.at[:, pl.ds(col, TILE)], ys.at[k], ysem.at[k]),
        )

    def begin(k, carry):
        for one in copies(k):
            one.start()
        return carry

    def end(k, carry):
        for one in copies(k):
            one.wait()
        return carry

    lax.fori_loop(0, live, begin, 0)
    ext[...] = jnp.zeros_like(ext)
    top[...] = jnp.full_like(top, FLOOR)
    total[...] = jnp.zeros_like(total)
    dims = (((0,), (0,)), ((), ()))

    def group(q, carry):
        lax.fori_loop(q * GROUP, jnp.minimum(live, q * GROUP + GROUP), end, 0)
        ready = []
        for u in range(GROUP):
            k = q * GROUP + u
            x = xs[k]
            y = ys[k]
            ext[u, 0, pl.ds(0, width), :] = x * (-2.0 * SCALE)
            ext[u, 0, pl.ds(width, 1), :] = jnp.sum(x * x, axis=0, keepdims=True) * SCALE
            ext[u, 0, pl.ds(width + 1, 1), :] = jnp.full((1, TILE), SCALE, jnp.float32)
            ext[u, 1, pl.ds(0, width), :] = y
            ext[u, 1, pl.ds(width, 1), :] = jnp.ones((1, TILE), jnp.float32)
            ext[u, 1, pl.ds(width + 1, 1), :] = jnp.sum(y * y, axis=0, keepdims=True)
            xh, xm, xl = split(ext[u, 0])
            yh, ym, yl = split(ext[u, 1])
            left = jnp.concatenate((xh, xh, xm, xm, xh, xl), axis=0)
            right = jnp.concatenate((yh, ym, yh, ym, yl, yh), axis=0)
            cost_ab[k] = lax.dot_general(left, right, dims, preferred_element_type=jnp.float32)
            value = lax.dot_general(right, left, dims, preferred_element_type=jnp.float32)
            cost_ba[k] = value
            peak = 0.0 - jnp.min(value, axis=0, keepdims=True)
            ready.append((k < live, block(tiles, 0, k, blocks_out), peak))
        for on, index, peak in ready:
            for h, lanes in halves():
                new = jnp.where(on, peak[:, h * HALF : (h + 1) * HALF], FLOOR)
                top[h, pl.ds(index, 1), :] = jnp.maximum(top[h, pl.ds(index, 1), :], new)
        return carry

    lax.fori_loop(0, (live + GROUP - 1) // GROUP, group, 0)
    add_up(live, tiles, 0, blocks_out, cost_ba, lambda k: None, top, total)
    finish(out, top, total)


def sweep_kernel(offset, far, scale, inner, outer, blocks_in, blocks_out, tiles, counts, cost, *refs):
    parts = refs[:-5]
    out, result, held, top, total = refs[-5:]
    live = counts[0]
    before = None
    if far is not None:
        before, parts = parts[0], parts[1:]
    potential = offset - lse2_many([part[...] for part in parts])
    result[...] = potential * scale
    for h, lanes in halves():
        held[h] = potential[:, h * HALF : (h + 1) * HALF]
        if before is None:
            top[h] = jnp.full((blocks_out, HALF), offset, jnp.float32)
        else:
            top[h] = far - before[:, lanes]
    total[...] = jnp.zeros_like(total)

    def potential_of(k):
        return spread(held, block(tiles, inner, k, blocks_in))

    least, most = add_up(live, tiles, outer, blocks_out, cost, potential_of, top, total)
    finish(out, top, total)
    exact = (jnp.min(least) >= LEAST) & (jnp.max(most) <= MOST)

    @pl.when(jnp.logical_not(exact))
    def _():
        top[...] = jnp.full_like(top, FLOOR)
        total[...] = jnp.zeros_like(total)

        def step(k, carry):
            index = block(tiles, outer, k, blocks_out)
            found = peaks(k, cost, potential_of(k))
            for h in range(2):
                top[h, pl.ds(index, 1), :] = jnp.maximum(top[h, pl.ds(index, 1), :], found[h])
            return carry

        lax.fori_loop(0, live, step, 0)
        add_up(live, tiles, outer, blocks_out, cost, potential_of, top, total)
        finish(out, top, total)


def vmem_spec():
    return pl.BlockSpec(memory_space=pltpu.VMEM)


def smem_spec():
    return pl.BlockSpec(memory_space=pltpu.SMEM)


def hbm_spec():
    return pl.BlockSpec(memory_space=pltpu.HBM)


def costs(tiles, counts, src, tgt, blocks_in, blocks_out):
    slots = tiles.shape[1]
    width = src.shape[0]
    shape = pltpu.VMEM((slots, TILE, TILE), jnp.float32)
    src = pltpu.with_memory_space_constraint(src, pltpu.HBM)
    tgt = pltpu.with_memory_space_constraint(tgt, pltpu.HBM)
    return pl.pallas_call(
        functools.partial(cost_kernel, blocks_in, blocks_out),
        out_shape=(shape, shape, jax.ShapeDtypeStruct((blocks_out, TILE), jnp.float32)),
        in_specs=[smem_spec(), smem_spec(), hbm_spec(), hbm_spec()],
        out_specs=(vmem_spec(), vmem_spec(), vmem_spec()),
        scratch_shapes=[
            pltpu.VMEM((slots, width, TILE), jnp.float32),
            pltpu.VMEM((slots, width, TILE), jnp.float32),
            pltpu.VMEM((GROUP, 2, DEPTH, TILE), jnp.float32),
            pltpu.VMEM((2, blocks_out, HALF), jnp.float32),
            pltpu.VMEM((2, blocks_out, HALF), jnp.float32),
            pltpu.SemaphoreType.DMA((slots,)),
            pltpu.SemaphoreType.DMA((slots,)),
        ],
        compiler_params=pltpu.CompilerParams(vmem_limit_bytes=VMEM_LIMIT),
    )(tiles, counts, src, tgt)


def sweep(tiles, counts, cost, before, parts, cells, far_cells, inner, outer, blocks_in, blocks_out, scale):
    far = None if before is None else math.log2(1.0 / far_cells)
    operands = list(parts) if before is None else [before, *parts]
    kernel = functools.partial(
        sweep_kernel, math.log2(1.0 / cells), far, scale, inner, outer, blocks_in, blocks_out
    )
    return pl.pallas_call(
        kernel,
        out_shape=(
            jax.ShapeDtypeStruct((blocks_out, TILE), jnp.float32),
            jax.ShapeDtypeStruct((blocks_in, TILE), jnp.float32),
        ),
        in_specs=[smem_spec(), smem_spec()] + [vmem_spec()] * (1 + len(operands)),
        out_specs=(vmem_spec(), vmem_spec()),
        scratch_shapes=[
            pltpu.VMEM((2, blocks_in, HALF), jnp.float32),
            pltpu.VMEM((2, blocks_out, HALF), jnp.float32),
            pltpu.VMEM((2, blocks_out, HALF), jnp.float32),
        ],
        compiler_params=pltpu.CompilerParams(vmem_limit_bytes=VMEM_LIMIT),
    )(tiles, counts, cost, *operands)


def fan(value, axis, size, stride, count):
    got = [value]
    for turn in range(1, count):
        pairs = []
        for k in range(size):
            place = (k // stride) % count
            pairs.append((k, k + ((place ^ turn) - place) * stride))
        got.append(lax.ppermute(value, axis, pairs))
    return got


def pair(value, axis, size, flip):
    return [value, lax.ppermute(value, axis, [(k, flip(k)) for k in range(size)])]


def over_tgt(value):
    size = lax.axis_size("tgt")
    value = lse2_many(pair(value, "tgt", size, lambda k: k ^ 1))
    return fan(value, "tgt", size, 2, size // 2)


def over_src(value):
    size = lax.axis_size("src")
    value = lse2_many(fan(value, "src", size, 1, 4))
    value = lse2_many(pair(value, "src", size, lambda k: k ^ 4))
    value = lse2_many(pair(value, "src", size, lambda k: k ^ 12))
    return pair(value, "src", size, lambda k: k ^ 28)


def body(src_points, tgt_points, tiles, counts):
    tiles = tiles[0, 0]
    counts = counts[0]
    row_blocks = src_points.shape[1] // TILE
    col_blocks = tgt_points.shape[1] // TILE
    src_cells = src_points.shape[1] * lax.axis_size("src")
    tgt_cells = tgt_points.shape[1] * lax.axis_size("tgt")
    cost_ab, cost_ba, rows = costs(tiles, counts, src_points, tgt_points, col_blocks, row_blocks)
    target = None
    for turn in range(ITERS):
        last = turn == ITERS - 1
        cols, source = sweep(
            tiles, counts, cost_ab, target, over_tgt(rows), src_cells, tgt_cells, 0, 1,
            row_blocks, col_blocks, 1.0 / SCALE if last else 1.0,
        )
        parts = over_src(cols)
        if last:
            target = (math.log2(1.0 / tgt_cells) - lse2_many(parts)) / SCALE
        else:
            rows, target = sweep(
                tiles, counts, cost_ba, source, parts, tgt_cells, src_cells, 1, 0,
                col_blocks, row_blocks, 1.0,
            )
    return (source.reshape(-1), target.reshape(-1))


def solution(mesh):
    in_specs = (P(None, "src"), P(None, "tgt"), P("src", "tgt", None, None), P("src", "tgt"))
    out_specs = (P("src"), P("tgt"))
    return jax.shard_map(body, mesh=mesh, in_specs=in_specs, out_specs=out_specs, check_vma=False)
```

time: 178 us -> 157 us (0.88); the launches traced: 175 us -> 158 us
  Pallas kernels: 24.2 us -> 13.7 us
  local copies, waits for them, and re-layouts: 6.63 us -> 2.03 us
  waiting for transfers between devices: 58.7 us -> 56.6 us
    ppermute x18, starting transfers between devices: 47.7 us -> 35.7 us  [fan(): got.append(lax.ppermute(value, axis, pairs))]
    ppermute x12, starting transfers between devices: 35.9 us -> 47.5 us  [pair(): lax.ppermute(value, axis, [(k, flip(k)) for k in range(size)])]
    pallas_call x6 -> x5, Pallas kernels: 19.5 us -> 9.75 us  [sweep(): pl.pallas_call(kernel, out_shape=(jax.ShapeDtypeStruct((blocks_out, TILE)...]
    unnamed x8 -> x6, local copies, waits for them, and re-layouts: 6.63 us -> 2.03 us
    ppermute x12, waiting for transfers between devices: 32.6 us -> 30.2 us  [pair(): lax.ppermute(value, axis, [(k, flip(k)) for k in range(size)])]
  transfers between devices with their start and end apart: 30 -> 30, of which waited for: 27 -> 25; matrix products, arithmetic and copies ran while one was open for 0% -> 0% of each run, Pallas kernels for 0% -> 0%
where the time goes in v2:
time: 157 us; the launch traced here: 158 us
  starting transfers between devices  83.2 us (53%)
  waiting for transfers between devices  56.6 us (36%)
  Pallas kernels  13.7 us (9%)
  local copies, waits for them, and re-layouts  2.03 us (1%)
    ppermute x12, starting transfers between devices, pair(): lax.ppermute(value, axis, [(k, flip(k)) for k in range(size)])  47.5 us
    ppermute x18, starting transfers between devices, fan(): got.append(lax.ppermute(value, axis, pairs))  35.7 us
    ppermute x12, waiting for transfers between devices, pair(): lax.ppermute(value, axis, [(k, flip(k)) for k in range(size)])  30.2 us
    ppermute x18, waiting for transfers between devices, fan(): got.append(lax.ppermute(value, axis, pairs))  26.4 us
    pallas_call x5, Pallas kernels, sweep(): pl.pallas_call(kernel, out_shape=(jax.ShapeDtypeStruct((blocks_out, TILE)...  9.75 us
    pallas_call x1, Pallas kernels, costs(): pl.pallas_call(functools.partial(cost_kernel, blocks_in, blocks_out), out...  3.99 us
  transfers between devices with their start and end apart: 30, of which 25 were waited for; matrix products, arithmetic and copies ran while one was open for 0% of the time, Pallas kernels for 0%

profile of v2, /device:TPU:2, one launch (start us, length us, event | category | flops | bytes accessed | tf_op | source)
XLA Modules:
  0.0 157.8 jit_solution(682629528409594842)
XLA Ops:
  2.0 4.0 %shard_map.59 = (f32[32,256,256]{2,1,0:T(8,128)S(1)}, f32[32,256,256]{2,1,0:T(8,128)S(1)}, f32[64,256]{1,0:T(8,128)S(1)}) custom-call(s32[2,32]{1,0:T(2,128)S(1)} %bitcast.14, s32[1]{0:T(128)} %bitcast.7.counts, f32[50,16384]{1,0:T(8,128)} %src.1, f32[50,24576]{1,0:T(8,128)} %tgt.1), custom_call_target="tpu_custom_call" | custom-call | tf_op jit(solution)/shard_map/pallas_call | solution.py:225
  7.4 3.1 %collective-permute-start.3 = (f32[64,256]{1,0:T(8,128)S(1)}, f32[64,256]{1,0:T(8,128)S(1)}, u32[]{:S(2)}, u32[]{:S(2)}) collective-permute-start(f32[64,256]{1,0:T(8,128)S(1)} %multiply_add_fusion.11.refs_0_), channel_id=1, source_target_pairs={{0,6},{1,7},{2,4},{3,5},{4,2},{5,3},{6,0},{7,1},{8,14},{9,15},{10,... | collective-permute-start | bytes 196616 | tf_op jit(solution)/shard_map/ppermute | solution.py:273
  13.7 2.5 %collective-permute-done.2.refs_2_ = f32[64,256]{1,0:T(8,128)S(1)} collective-permute-done((f32[64,256]{1,0:T(8,128)S(1)}, f32[64,256]{1,0:T(8,128)S(1)}, u32[]{:S(2)}, u32[]{:S(2)}) %collective-permute-start.2) | collective-permute-done | bytes 65568 | tf_op jit(solution)/shard_map/ppermute | solution.py:273
  17.0 2.5 %shard_map.60 = (f32[96,256]{1,0:T(8,128)S(1)}, f32[64,256]{1,0:T(8,128)S(1)}) custom-call(s32[2,32]{1,0:T(2,128)S(1)} %bitcast.15, s32[1]{0:T(128)} %bitcast.8.counts, f32[32,256,256]{2,1,0:T(8,128)S(1)} %get-tuple-element.15.cost, f32[64,256]{1,0:T(8,128)S(1)} %multiply_add_fusion.11.refs_0_, f32[64,256]{1,0:T(8,128)S(1)} %collective-permute-done.1.refs_1_, ...), custom_call_target="tpu_custom_call" | custom-call | tf_op jit(solution)/shard_map/pallas_call | solution.py:249
  19.5 5.8 %collective-permute-start.6 = (f32[96,256]{1,0:T(8,128)S(1)}, f32[96,256]{1,0:T(8,128)S(1)}, u32[]{:S(2)}, u32[]{:S(2)}) collective-permute-start(f32[96,256]{1,0:T(8,128)S(1)} %get-tuple-element.19), channel_id=1, source_target_pairs={{0,24},{8,16},{16,8},{24,0},{32,56},{40,48},{48,40},{56,32},{64,88... | collective-permute-start | bytes 294920 | tf_op jit(solution)/shard_map/ppermute | solution.py:273
  29.0 2.5 %collective-permute-done.5 = f32[96,256]{1,0:T(8,128)S(1)} collective-permute-done((f32[96,256]{1,0:T(8,128)S(1)}, f32[96,256]{1,0:T(8,128)S(1)}, u32[]{:S(2)}, u32[]{:S(2)}) %collective-permute-start.5) | collective-permute-done | bytes 98336 | tf_op jit(solution)/shard_map/ppermute | solution.py:273
  31.6 6.2 %collective-permute-start.7 = (f32[96,256]{1,0:T(8,128)S(1)}, f32[96,256]{1,0:T(8,128)S(1)}, u32[]{:S(2)}, u32[]{:S(2)}) collective-permute-start(f32[96,256]{1,0:T(8,128)S(1)} %multiply_add_fusion.8), channel_id=1, source_target_pairs={{0,32},{8,40},{16,48},{24,56},{32,0},{40,8},{48,16},{56,24},{64,96... | collective-permute-start | bytes 294920 | tf_op jit(solution)/shard_map/ppermute | solution.py:278
  37.7 2.6 %collective-permute-done.7 = f32[96,256]{1,0:T(8,128)S(1)} collective-permute-done((f32[96,256]{1,0:T(8,128)S(1)}, f32[96,256]{1,0:T(8,128)S(1)}, u32[]{:S(2)}, u32[]{:S(2)}) %collective-permute-start.7) | collective-permute-done | bytes 98336 | tf_op jit(solution)/shard_map/ppermute | solution.py:278
  40.4 3.7 %collective-permute-start.8 = (f32[96,256]{1,0:T(8,128)S(1)}, f32[96,256]{1,0:T(8,128)S(1)}, u32[]{:S(2)}, u32[]{:S(2)}) collective-permute-start(f32[96,256]{1,0:T(8,128)S(1)} %multiply_add_fusion.7), channel_id=1, source_target_pairs={{0,96},{8,104},{16,112},{24,120},{32,64},{40,72},{48,80},{56,88},{... | collective-permute-start | bytes 294920 | tf_op jit(solution)/shard_map/ppermute | solution.py:278
  44.1 2.9 %collective-permute-done.8 = f32[96,256]{1,0:T(8,128)S(1)} collective-permute-done((f32[96,256]{1,0:T(8,128)S(1)}, f32[96,256]{1,0:T(8,128)S(1)}, u32[]{:S(2)}, u32[]{:S(2)}) %collective-permute-start.8) | collective-permute-done | bytes 98336 | tf_op jit(solution)/shard_map/ppermute | solution.py:278
  47.1 4.9 %collective-permute-start.9 = (f32[96,256]{1,0:T(8,128)S(1)}, f32[96,256]{1,0:T(8,128)S(1)}, u32[]{:S(2)}, u32[]{:S(2)}) collective-permute-start(f32[96,256]{1,0:T(8,128)S(1)} %multiply_add_fusion.6.refs_1_), channel_id=1, source_target_pairs={{0,224},{8,232},{16,240},{24,248},{32,192},{40,200},{48,208},{56,2... | collective-permute-start | bytes 294920 | tf_op jit(solution)/shard_map/ppermute | solution.py:278
  51.9 3.6 %collective-permute-done.9.refs_2_ = f32[96,256]{1,0:T(8,128)S(1)} collective-permute-done((f32[96,256]{1,0:T(8,128)S(1)}, f32[96,256]{1,0:T(8,128)S(1)}, u32[]{:S(2)}, u32[]{:S(2)}) %collective-permute-start.9) | collective-permute-done | bytes 98336 | tf_op jit(solution)/shard_map/ppermute | solution.py:278
  58.1 3.6 %collective-permute-start.13 = (f32[64,256]{1,0:T(8,128)S(1)}, f32[64,256]{1,0:T(8,128)S(1)}, u32[]{:S(2)}, u32[]{:S(2)}) collective-permute-start(f32[64,256]{1,0:T(8,128)S(1)} %multiply_add_fusion.10.refs_1_), channel_id=1, source_target_pairs={{0,6},{1,7},{2,4},{3,5},{4,2},{5,3},{6,0},{7,1},{8,14},{9,15},{10,... | collective-permute-start | bytes 196616 | tf_op jit(solution)/shard_map/ppermute | solution.py:273
  64.8 3.0 %collective-permute-done.12.refs_3_ = f32[64,256]{1,0:T(8,128)S(1)} collective-permute-done((f32[64,256]{1,0:T(8,128)S(1)}, f32[64,256]{1,0:T(8,128)S(1)}, u32[]{:S(2)}, u32[]{:S(2)}) %collective-permute-start.12) | collective-permute-done | bytes 65568 | tf_op jit(solution)/shard_map/ppermute | solution.py:273
  67.8 2.6 %shard_map.62 = (f32[96,256]{1,0:T(8,128)S(1)}, f32[64,256]{1,0:T(8,128)S(1)}) custom-call(s32[2,32]{1,0:T(2,128)S(1)} %bitcast.17, s32[1]{0:T(128)} %bitcast.10.counts, f32[32,256,256]{2,1,0:T(8,128)S(1)} %get-tuple-element.15.cost, f32[96,256]{1,0:T(8,128)S(1)} %get-tuple-element.20.refs_0_, f32[64,256]{1,0:T(8,128)S(1)} %multiply_add_fusion.10.refs_1_, ...), custom_call_target="tpu_custom_call" | custom-call | tf_op jit(solution)/shard_map/pallas_call | solution.py:249
  70.5 3.8 %collective-permute-start.16 = (f32[96,256]{1,0:T(8,128)S(1)}, f32[96,256]{1,0:T(8,128)S(1)}, u32[]{:S(2)}, u32[]{:S(2)}) collective-permute-start(f32[96,256]{1,0:T(8,128)S(1)} %get-tuple-element.23), channel_id=1, source_target_pairs={{0,24},{8,16},{16,8},{24,0},{32,56},{40,48},{48,40},{56,32},{64,88... | collective-permute-start | bytes 294920 | tf_op jit(solution)/shard_map/ppermute | solution.py:273
  77.8 2.6 %collective-permute-done.15 = f32[96,256]{1,0:T(8,128)S(1)} collective-permute-done((f32[96,256]{1,0:T(8,128)S(1)}, f32[96,256]{1,0:T(8,128)S(1)}, u32[]{:S(2)}, u32[]{:S(2)}) %collective-permute-start.15) | collective-permute-done | bytes 98336 | tf_op jit(solution)/shard_map/ppermute | solution.py:273
  80.5 9.1 %collective-permute-start.17 = (f32[96,256]{1,0:T(8,128)S(1)}, f32[96,256]{1,0:T(8,128)S(1)}, u32[]{:S(2)}, u32[]{:S(2)}) collective-permute-start(f32[96,256]{1,0:T(8,128)S(1)} %multiply_add_fusion.5), channel_id=1, source_target_pairs={{0,32},{8,40},{16,48},{24,56},{32,0},{40,8},{48,16},{56,24},{64,96... | collective-permute-start | bytes 294920 | tf_op jit(solution)/shard_map/ppermute | solution.py:278
  89.6 2.6 %collective-permute-done.17 = f32[96,256]{1,0:T(8,128)S(1)} collective-permute-done((f32[96,256]{1,0:T(8,128)S(1)}, f32[96,256]{1,0:T(8,128)S(1)}, u32[]{:S(2)}, u32[]{:S(2)}) %collective-permute-start.17) | collective-permute-done | bytes 98336 | tf_op jit(solution)/shard_map/ppermute | solution.py:278
  93.9 5.0 %collective-permute-done.18 = f32[96,256]{1,0:T(8,128)S(1)} collective-permute-done((f32[96,256]{1,0:T(8,128)S(1)}, f32[96,256]{1,0:T(8,128)S(1)}, u32[]{:S(2)}, u32[]{:S(2)}) %collective-permute-start.18) | collective-permute-done | bytes 98336 | tf_op jit(solution)/shard_map/ppermute | solution.py:278
  98.9 3.3 %collective-permute-start.19 = (f32[96,256]{1,0:T(8,128)S(1)}, f32[96,256]{1,0:T(8,128)S(1)}, u32[]{:S(2)}, u32[]{:S(2)}) collective-permute-start(f32[96,256]{1,0:T(8,128)S(1)} %multiply_add_fusion.3.refs_1_), channel_id=1, source_target_pairs={{0,224},{8,232},{16,240},{24,248},{32,192},{40,200},{48,208},{56,2... | collective-permute-start | bytes 294920 | tf_op jit(solution)/shard_map/ppermute | solution.py:278
  102.2 2.6 %collective-permute-done.19.refs_2_ = f32[96,256]{1,0:T(8,128)S(1)} collective-permute-done((f32[96,256]{1,0:T(8,128)S(1)}, f32[96,256]{1,0:T(8,128)S(1)}, u32[]{:S(2)}, u32[]{:S(2)}) %collective-permute-start.19) | collective-permute-done | bytes 98336 | tf_op jit(solution)/shard_map/ppermute | solution.py:278
  107.3 5.8 %collective-permute-start.23 = (f32[64,256]{1,0:T(8,128)S(1)}, f32[64,256]{1,0:T(8,128)S(1)}, u32[]{:S(2)}, u32[]{:S(2)}) collective-permute-start(f32[64,256]{1,0:T(8,128)S(1)} %multiply_add_fusion.9.refs_1_), channel_id=1, source_target_pairs={{0,6},{1,7},{2,4},{3,5},{4,2},{5,3},{6,0},{7,1},{8,14},{9,15},{10,... | collective-permute-start | bytes 196616 | tf_op jit(solution)/shard_map/ppermute | solution.py:273
  116.3 3.0 %collective-permute-done.22.refs_3_ = f32[64,256]{1,0:T(8,128)S(1)} collective-permute-done((f32[64,256]{1,0:T(8,128)S(1)}, f32[64,256]{1,0:T(8,128)S(1)}, u32[]{:S(2)}, u32[]{:S(2)}) %collective-permute-start.22) | collective-permute-done | bytes 65568 | tf_op jit(solution)/shard_map/ppermute | solution.py:273
  119.2 2.5 %shard_map.64 = (f32[96,256]{1,0:T(8,128)S(1)}, f32[64,256]{1,0:T(8,128)S(1)}) custom-call(s32[2,32]{1,0:T(2,128)S(1)} %bitcast.19, s32[1]{0:T(128)} %bitcast.12.counts, f32[32,256,256]{2,1,0:T(8,128)S(1)} %get-tuple-element.15.cost, f32[96,256]{1,0:T(8,128)S(1)} %get-tuple-element.24.refs_0_, f32[64,256]{1,0:T(8,128)S(1)} %multiply_add_fusion.9.refs_1_, ...), custom_call_target="tpu_custom_call" | custom-call | tf_op jit(solution)/shard_map/pallas_call | solution.py:249
  121.7 2.8 %collective-permute-start.26 = (f32[96,256]{1,0:T(8,128)S(1)}, f32[96,256]{1,0:T(8,128)S(1)}, u32[]{:S(2)}, u32[]{:S(2)}) collective-permute-start(f32[96,256]{1,0:T(8,128)S(1)} %get-tuple-element.27), channel_id=1, source_target_pairs={{0,24},{8,16},{16,8},{24,0},{32,56},{40,48},{48,40},{56,32},{64,88... | collective-permute-start | bytes 294920 | tf_op jit(solution)/shard_map/ppermute | solution.py:273
  128.0 2.6 %collective-permute-done.25 = f32[96,256]{1,0:T(8,128)S(1)} collective-permute-done((f32[96,256]{1,0:T(8,128)S(1)}, f32[96,256]{1,0:T(8,128)S(1)}, u32[]{:S(2)}, u32[]{:S(2)}) %collective-permute-start.25) | collective-permute-done | bytes 98336 | tf_op jit(solution)/shard_map/ppermute | solution.py:273
  130.7 5.0 %collective-permute-start.27 = (f32[96,256]{1,0:T(8,128)S(1)}, f32[96,256]{1,0:T(8,128)S(1)}, u32[]{:S(2)}, u32[]{:S(2)}) collective-permute-start(f32[96,256]{1,0:T(8,128)S(1)} %multiply_add_fusion.2), channel_id=1, source_target_pairs={{0,32},{8,40},{16,48},{24,56},{32,0},{40,8},{48,16},{56,24},{64,96... | collective-permute-start | bytes 294920 | tf_op jit(solution)/shard_map/ppermute | solution.py:278
  135.7 2.6 %collective-permute-done.27 = f32[96,256]{1,0:T(8,128)S(1)} collective-permute-done((f32[96,256]{1,0:T(8,128)S(1)}, f32[96,256]{1,0:T(8,128)S(1)}, u32[]{:S(2)}, u32[]{:S(2)}) %collective-permute-start.27) | collective-permute-done | bytes 98336 | tf_op jit(solution)/shard_map/ppermute | solution.py:278
  138.4 5.4 %collective-permute-start.28 = (f32[96,256]{1,0:T(8,128)S(1)}, f32[96,256]{1,0:T(8,128)S(1)}, u32[]{:S(2)}, u32[]{:S(2)}) collective-permute-start(f32[96,256]{1,0:T(8,128)S(1)} %multiply_add_fusion.1), channel_id=1, source_target_pairs={{0,96},{8,104},{16,112},{24,120},{32,64},{40,72},{48,80},{56,88},{... | collective-permute-start | bytes 294920 | tf_op jit(solution)/shard_map/ppermute | solution.py:278
  143.8 2.6 %collective-permute-done.28 = f32[96,256]{1,0:T(8,128)S(1)} collective-permute-done((f32[96,256]{1,0:T(8,128)S(1)}, f32[96,256]{1,0:T(8,128)S(1)}, u32[]{:S(2)}, u32[]{:S(2)}) %collective-permute-start.28) | collective-permute-done | bytes 98336 | tf_op jit(solution)/shard_map/ppermute | solution.py:278
  146.5 8.0 %collective-permute-start.29 = (f32[96,256]{1,0:T(8,128)S(1)}, f32[96,256]{1,0:T(8,128)S(1)}, u32[]{:S(2)}, u32[]{:S(2)}) collective-permute-start(f32[96,256]{1,0:T(8,128)S(1)} %multiply_add_fusion), channel_id=1, source_target_pairs={{0,224},{8,232},{16,240},{24,248},{32,192},{40,200},{48,208},{56,2... | collective-permute-start | bytes 294920 | tf_op jit(solution)/shard_map/ppermute | solution.py:278
  (53 shorter events, 33.6 us)
Async XLA Ops:
  0.6 16.4 %copy-start.1 = (s32[1,1,2,32]{3,2,1,0:T(2,128)S(1)}, s32[1,1,2,32]{3,2,1,0:T(2,128)}, u32[]{:S(2)}) copy-start(s32[1,1,2,32]{3,2,1,0:T(2,128)} %param.6) | copy-start | bytes 772
  1.3 0.7 copy-start
  6.0 1.3 collective-permute-start
  7.4 6.3 %collective-permute-start.3 = (f32[64,256]{1,0:T(8,128)S(1)}, f32[64,256]{1,0:T(8,128)S(1)}, u32[]{:S(2)}, u32[]{:S(2)}) collective-permute-start(f32[64,256]{1,0:T(8,128)S(1)} %multiply_add_fusion.11.refs_0_), channel_id=1, source_target_pairs={{0,6},{1,7},{2,4},{3,5},{4,2},{5,3},{6,0},{7,1},{8,14},{9,15},{10,... | collective-permute-start | bytes 196616 | tf_op jit(solution)/shard_map/ppermute | solution.py:273
  10.5 5.8 %collective-permute-start.2 = (f32[64,256]{1,0:T(8,128)S(1)}, f32[64,256]{1,0:T(8,128)S(1)}, u32[]{:S(2)}, u32[]{:S(2)}) collective-permute-start(f32[64,256]{1,0:T(8,128)S(1)} %multiply_add_fusion.11.refs_0_), channel_id=1, source_target_pairs={{0,4},{1,5},{2,6},{3,7},{4,0},{5,1},{6,2},{7,3},{8,12},{9,13},{10,... | collective-permute-start | bytes 196616 | tf_op jit(solution)/shard_map/ppermute | solution.py:273
  12.8 4.3 %collective-permute-start.1 = (f32[64,256]{1,0:T(8,128)S(1)}, f32[64,256]{1,0:T(8,128)S(1)}, u32[]{:S(2)}, u32[]{:S(2)}) collective-permute-start(f32[64,256]{1,0:T(8,128)S(1)} %multiply_add_fusion.11.refs_0_), channel_id=1, source_target_pairs={{0,2},{1,3},{2,0},{3,1},{4,6},{5,7},{6,4},{7,5},{8,10},{9,11},{10,... | collective-permute-start | bytes 196616 | tf_op jit(solution)/shard_map/ppermute | solution.py:273
  19.5 9.5 %collective-permute-start.6 = (f32[96,256]{1,0:T(8,128)S(1)}, f32[96,256]{1,0:T(8,128)S(1)}, u32[]{:S(2)}, u32[]{:S(2)}) collective-permute-start(f32[96,256]{1,0:T(8,128)S(1)} %get-tuple-element.19), channel_id=1, source_target_pairs={{0,24},{8,16},{16,8},{24,0},{32,56},{40,48},{48,40},{56,32},{64,88... | collective-permute-start | bytes 294920 | tf_op jit(solution)/shard_map/ppermute | solution.py:273
  25.3 6.1 %collective-permute-start.5 = (f32[96,256]{1,0:T(8,128)S(1)}, f32[96,256]{1,0:T(8,128)S(1)}, u32[]{:S(2)}, u32[]{:S(2)}) collective-permute-start(f32[96,256]{1,0:T(8,128)S(1)} %get-tuple-element.19), channel_id=1, source_target_pairs={{0,16},{8,24},{16,0},{24,8},{32,48},{40,56},{48,32},{56,40},{64,80... | collective-permute-start | bytes 294920 | tf_op jit(solution)/shard_map/ppermute | solution.py:273
  25.4 6.1 %collective-permute-start.4 = (f32[96,256]{1,0:T(8,128)S(1)}, f32[96,256]{1,0:T(8,128)S(1)}, u32[]{:S(2)}, u32[]{:S(2)}) collective-permute-start(f32[96,256]{1,0:T(8,128)S(1)} %get-tuple-element.19), channel_id=1, source_target_pairs={{0,8},{8,0},{16,24},{24,16},{32,40},{40,32},{48,56},{56,48},{64,72... | collective-permute-start | bytes 294920 | tf_op jit(solution)/shard_map/ppermute | solution.py:273
  31.6 8.8 %collective-permute-start.7 = (f32[96,256]{1,0:T(8,128)S(1)}, f32[96,256]{1,0:T(8,128)S(1)}, u32[]{:S(2)}, u32[]{:S(2)}) collective-permute-start(f32[96,256]{1,0:T(8,128)S(1)} %multiply_add_fusion.8), channel_id=1, source_target_pairs={{0,32},{8,40},{16,48},{24,56},{32,0},{40,8},{48,16},{56,24},{64,96... | collective-permute-start | bytes 294920 | tf_op jit(solution)/shard_map/ppermute | solution.py:278
  40.4 6.6 %collective-permute-start.8 = (f32[96,256]{1,0:T(8,128)S(1)}, f32[96,256]{1,0:T(8,128)S(1)}, u32[]{:S(2)}, u32[]{:S(2)}) collective-permute-start(f32[96,256]{1,0:T(8,128)S(1)} %multiply_add_fusion.7), channel_id=1, source_target_pairs={{0,96},{8,104},{16,112},{24,120},{32,64},{40,72},{48,80},{56,88},{... | collective-permute-start | bytes 294920 | tf_op jit(solution)/shard_map/ppermute | solution.py:278
  47.1 8.5 %collective-permute-start.9 = (f32[96,256]{1,0:T(8,128)S(1)}, f32[96,256]{1,0:T(8,128)S(1)}, u32[]{:S(2)}, u32[]{:S(2)}) collective-permute-start(f32[96,256]{1,0:T(8,128)S(1)} %multiply_add_fusion.6.refs_1_), channel_id=1, source_target_pairs={{0,224},{8,232},{16,240},{24,248},{32,192},{40,200},{48,208},{56,2... | collective-permute-start | bytes 294920 | tf_op jit(solution)/shard_map/ppermute | solution.py:278
  56.7 1.3 collective-permute-start.10
  58.1 6.8 %collective-permute-start.13 = (f32[64,256]{1,0:T(8,128)S(1)}, f32[64,256]{1,0:T(8,128)S(1)}, u32[]{:S(2)}, u32[]{:S(2)}) collective-permute-start(f32[64,256]{1,0:T(8,128)S(1)} %multiply_add_fusion.10.refs_1_), channel_id=1, source_target_pairs={{0,6},{1,7},{2,4},{3,5},{4,2},{5,3},{6,0},{7,1},{8,14},{9,15},{10,... | collective-permute-start | bytes 196616 | tf_op jit(solution)/shard_map/ppermute | solution.py:273
  61.7 6.1 %collective-permute-start.12 = (f32[64,256]{1,0:T(8,128)S(1)}, f32[64,256]{1,0:T(8,128)S(1)}, u32[]{:S(2)}, u32[]{:S(2)}) collective-permute-start(f32[64,256]{1,0:T(8,128)S(1)} %multiply_add_fusion.10.refs_1_), channel_id=1, source_target_pairs={{0,4},{1,5},{2,6},{3,7},{4,0},{5,1},{6,2},{7,3},{8,12},{9,13},{10,... | collective-permute-start | bytes 196616 | tf_op jit(solution)/shard_map/ppermute | solution.py:273
  61.7 6.1 %collective-permute-start.11 = (f32[64,256]{1,0:T(8,128)S(1)}, f32[64,256]{1,0:T(8,128)S(1)}, u32[]{:S(2)}, u32[]{:S(2)}) collective-permute-start(f32[64,256]{1,0:T(8,128)S(1)} %multiply_add_fusion.10.refs_1_), channel_id=1, source_target_pairs={{0,2},{1,3},{2,0},{3,1},{4,6},{5,7},{6,4},{7,5},{8,10},{9,11},{10,... | collective-permute-start | bytes 196616 | tf_op jit(solution)/shard_map/ppermute | solution.py:273
  70.5 7.3 %collective-permute-start.16 = (f32[96,256]{1,0:T(8,128)S(1)}, f32[96,256]{1,0:T(8,128)S(1)}, u32[]{:S(2)}, u32[]{:S(2)}) collective-permute-start(f32[96,256]{1,0:T(8,128)S(1)} %get-tuple-element.23), channel_id=1, source_target_pairs={{0,24},{8,16},{16,8},{24,0},{32,56},{40,48},{48,40},{56,32},{64,88... | collective-permute-start | bytes 294920 | tf_op jit(solution)/shard_map/ppermute | solution.py:273
  74.3 6.1 %collective-permute-start.15 = (f32[96,256]{1,0:T(8,128)S(1)}, f32[96,256]{1,0:T(8,128)S(1)}, u32[]{:S(2)}, u32[]{:S(2)}) collective-permute-start(f32[96,256]{1,0:T(8,128)S(1)} %get-tuple-element.23), channel_id=1, source_target_pairs={{0,16},{8,24},{16,0},{24,8},{32,48},{40,56},{48,32},{56,40},{64,80... | collective-permute-start | bytes 294920 | tf_op jit(solution)/shard_map/ppermute | solution.py:273
  74.3 6.1 %collective-permute-start.14 = (f32[96,256]{1,0:T(8,128)S(1)}, f32[96,256]{1,0:T(8,128)S(1)}, u32[]{:S(2)}, u32[]{:S(2)}) collective-permute-start(f32[96,256]{1,0:T(8,128)S(1)} %get-tuple-element.23), channel_id=1, source_target_pairs={{0,8},{8,0},{16,24},{24,16},{32,40},{40,32},{48,56},{56,48},{64,72... | collective-permute-start | bytes 294920 | tf_op jit(solution)/shard_map/ppermute | solution.py:273
  80.5 11.7 %collective-permute-start.17 = (f32[96,256]{1,0:T(8,128)S(1)}, f32[96,256]{1,0:T(8,128)S(1)}, u32[]{:S(2)}, u32[]{:S(2)}) collective-permute-start(f32[96,256]{1,0:T(8,128)S(1)} %multiply_add_fusion.5), channel_id=1, source_target_pairs={{0,32},{8,40},{16,48},{24,56},{32,0},{40,8},{48,16},{56,24},{64,96... | collective-permute-start | bytes 294920 | tf_op jit(solution)/shard_map/ppermute | solution.py:278
  92.3 6.6 %collective-permute-start.18 = (f32[96,256]{1,0:T(8,128)S(1)}, f32[96,256]{1,0:T(8,128)S(1)}, u32[]{:S(2)}, u32[]{:S(2)}) collective-permute-start(f32[96,256]{1,0:T(8,128)S(1)} %multiply_add_fusion.4), channel_id=1, source_target_pairs={{0,96},{8,104},{16,112},{24,120},{32,64},{40,72},{48,80},{56,88},{... | collective-permute-start | bytes 294920 | tf_op jit(solution)/shard_map/ppermute | solution.py:278
  98.9 5.9 %collective-permute-start.19 = (f32[96,256]{1,0:T(8,128)S(1)}, f32[96,256]{1,0:T(8,128)S(1)}, u32[]{:S(2)}, u32[]{:S(2)}) collective-permute-start(f32[96,256]{1,0:T(8,128)S(1)} %multiply_add_fusion.3.refs_1_), channel_id=1, source_target_pairs={{0,224},{8,232},{16,240},{24,248},{32,192},{40,200},{48,208},{56,2... | collective-permute-start | bytes 294920 | tf_op jit(solution)/shard_map/ppermute | solution.py:278
  105.9 1.3 collective-permute-start.20
  107.3 8.9 %collective-permute-start.23 = (f32[64,256]{1,0:T(8,128)S(1)}, f32[64,256]{1,0:T(8,128)S(1)}, u32[]{:S(2)}, u32[]{:S(2)}) collective-permute-start(f32[64,256]{1,0:T(8,128)S(1)} %multiply_add_fusion.9.refs_1_), channel_id=1, source_target_pairs={{0,6},{1,7},{2,4},{3,5},{4,2},{5,3},{6,0},{7,1},{8,14},{9,15},{10,... | collective-permute-start | bytes 196616 | tf_op jit(solution)/shard_map/ppermute | solution.py:273
  113.1 6.1 %collective-permute-start.22 = (f32[64,256]{1,0:T(8,128)S(1)}, f32[64,256]{1,0:T(8,128)S(1)}, u32[]{:S(2)}, u32[]{:S(2)}) collective-permute-start(f32[64,256]{1,0:T(8,128)S(1)} %multiply_add_fusion.9.refs_1_), channel_id=1, source_target_pairs={{0,4},{1,5},{2,6},{3,7},{4,0},{5,1},{6,2},{7,3},{8,12},{9,13},{10,... | collective-permute-start | bytes 196616 | tf_op jit(solution)/shard_map/ppermute | solution.py:273
  113.1 6.1 %collective-permute-start.21 = (f32[64,256]{1,0:T(8,128)S(1)}, f32[64,256]{1,0:T(8,128)S(1)}, u32[]{:S(2)}, u32[]{:S(2)}) collective-permute-start(f32[64,256]{1,0:T(8,128)S(1)} %multiply_add_fusion.9.refs_1_), channel_id=1, source_target_pairs={{0,2},{1,3},{2,0},{3,1},{4,6},{5,7},{6,4},{7,5},{8,10},{9,11},{10,... | collective-permute-start | bytes 196616 | tf_op jit(solution)/shard_map/ppermute | solution.py:273
  121.7 6.3 %collective-permute-start.26 = (f32[96,256]{1,0:T(8,128)S(1)}, f32[96,256]{1,0:T(8,128)S(1)}, u32[]{:S(2)}, u32[]{:S(2)}) collective-permute-start(f32[96,256]{1,0:T(8,128)S(1)} %get-tuple-element.27), channel_id=1, source_target_pairs={{0,24},{8,16},{16,8},{24,0},{32,56},{40,48},{48,40},{56,32},{64,88... | collective-permute-start | bytes 294920 | tf_op jit(solution)/shard_map/ppermute | solution.py:273
  124.5 6.1 %collective-permute-start.25 = (f32[96,256]{1,0:T(8,128)S(1)}, f32[96,256]{1,0:T(8,128)S(1)}, u32[]{:S(2)}, u32[]{:S(2)}) collective-permute-start(f32[96,256]{1,0:T(8,128)S(1)} %get-tuple-element.27), channel_id=1, source_target_pairs={{0,16},{8,24},{16,0},{24,8},{32,48},{40,56},{48,32},{56,40},{64,80... | collective-permute-start | bytes 294920 | tf_op jit(solution)/shard_map/ppermute | solution.py:273
  124.5 6.1 %collective-permute-start.24 = (f32[96,256]{1,0:T(8,128)S(1)}, f32[96,256]{1,0:T(8,128)S(1)}, u32[]{:S(2)}, u32[]{:S(2)}) collective-permute-start(f32[96,256]{1,0:T(8,128)S(1)} %get-tuple-element.27), channel_id=1, source_target_pairs={{0,8},{8,0},{16,24},{24,16},{32,40},{40,32},{48,56},{56,48},{64,72... | collective-permute-start | bytes 294920 | tf_op jit(solution)/shard_map/ppermute | solution.py:273
  130.7 7.6 %collective-permute-start.27 = (f32[96,256]{1,0:T(8,128)S(1)}, f32[96,256]{1,0:T(8,128)S(1)}, u32[]{:S(2)}, u32[]{:S(2)}) collective-permute-start(f32[96,256]{1,0:T(8,128)S(1)} %multiply_add_fusion.2), channel_id=1, source_target_pairs={{0,32},{8,40},{16,48},{24,56},{32,0},{40,8},{48,16},{56,24},{64,96... | collective-permute-start | bytes 294920 | tf_op jit(solution)/shard_map/ppermute | solution.py:278
  138.4 8.0 %collective-permute-start.28 = (f32[96,256]{1,0:T(8,128)S(1)}, f32[96,256]{1,0:T(8,128)S(1)}, u32[]{:S(2)}, u32[]{:S(2)}) collective-permute-start(f32[96,256]{1,0:T(8,128)S(1)} %multiply_add_fusion.1), channel_id=1, source_target_pairs={{0,96},{8,104},{16,112},{24,120},{32,64},{40,72},{48,80},{56,88},{... | collective-permute-start | bytes 294920 | tf_op jit(solution)/shard_map/ppermute | solution.py:278
  146.5 10.6 %collective-permute-start.29 = (f32[96,256]{1,0:T(8,128)S(1)}, f32[96,256]{1,0:T(8,128)S(1)}, u32[]{:S(2)}, u32[]{:S(2)}) collective-permute-start(f32[96,256]{1,0:T(8,128)S(1)} %multiply_add_fusion), channel_id=1, source_target_pairs={{0,224},{8,232},{16,240},{24,248},{32,192},{40,200},{48,208},{56,2... | collective-permute-start | bytes 294920 | tf_op jit(solution)/shard_map/ppermute | solution.py:278

commit v3 on v2

--- a/solution.py
+++ b/solution.py
@@ -29,14 +29,15 @@
 
 def split(value):
     high = value.astype(jnp.bfloat16)
-    rest = value - high.astype(jnp.float32)
-    middle = rest.astype(jnp.bfloat16)
-    low = (rest - middle.astype(jnp.float32)).astype(jnp.bfloat16)
-    return high, middle, low
+    return high, (value - high.astype(jnp.float32)).astype(jnp.bfloat16)
 
 
 def halves():
     return [(h, pl.ds(h * HALF, HALF)) for h in range(2)]
+
+
+def row(index, h):
+    return pl.ds(2 * index + h, 1)
 
 
 def block(tiles, side, k, blocks):
@@ -70,7 +71,7 @@
 
 
 def spread(held, index):
-    return [jnp.broadcast_to(held[g, pl.ds(index, 1), :], (HALF, HALF)).T for g in range(2)]
+    return [jnp.broadcast_to(held[row(index, g), :], (HALF, HALF)).T for g in range(2)]
 
 
 def add_up(live, tiles, outer, blocks_out, cost, potential_of, top, total):
@@ -80,11 +81,11 @@
         for u in range(GROUP):
             k = q * GROUP + u
             out = block(tiles, outer, k, blocks_out)
-            shift = [top[h, pl.ds(out, 1), :] for h in range(2)]
+            shift = [top[row(out, h), :] for h in range(2)]
             ready.append((k < live, out, sums(k, cost, potential_of(k), shift)))
         for on, out, found in ready:
             for h in range(2):
-                total[h, pl.ds(out, 1), :] = total[h, pl.ds(out, 1), :] + jnp.where(on, found[h], 0.0)
+                total[row(out, h), :] = total[row(out, h), :] + jnp.where(on, found[h], 0.0)
                 least = jnp.minimum(least, jnp.where(on, found[h], 1.0))
                 most = jnp.maximum(most, jnp.where(on, found[h], 1.0))
         return least, most
@@ -94,24 +95,30 @@
 
 
 def finish(out, top, total):
-    for h, lanes in halves():
-        found = total[h] > 0.0
-        out[:, lanes] = jnp.where(found, top[h] + jnp.log2(jnp.where(found, total[h], 1.0)), FLOOR)
+    found = total[...] > 0.0
+    out[...] = jnp.where(found, top[...] + jnp.log2(jnp.where(found, total[...], 1.0)), FLOOR)
+
+
+def table_scratch(slots):
+    return [pltpu.SMEM((2, slots), jnp.int32), pltpu.SemaphoreType.DMA(())]
 
 
 def cost_kernel(
-    blocks_in, blocks_out, tiles, counts, src, tgt, cost_ab, cost_ba, out,
-    xs, ys, ext, top, total, xsem, ysem
+    blocks_in, blocks_out, tiles_in, counts, src, tgt, cost_ab, cost_ba, out,
+    tiles, tsem, xs, ys, ext, top, total, xsem, ysem
 ):
-    live = counts[0]
+    table = pltpu.make_async_copy(tiles_in, tiles, tsem)
+    table.start()
+    table.wait()
+    live = counts[0, 0]
     width = src.shape[0]
 
     def copies(k):
-        row = pl.multiple_of(block(tiles, 0, k, blocks_out) * TILE, TILE)
-        col = pl.multiple_of(block(tiles, 1, k, blocks_in) * TILE, TILE)
+        first = pl.multiple_of(block(tiles, 0, k, blocks_out) * TILE, TILE)
+        second = pl.multiple_of(block(tiles, 1, k, blocks_in) * TILE, TILE)
         return (
-            pltpu.make_async_copy(src.at[:, pl.ds(row, TILE)], xs.at[k], xsem.at[k]),
-            pltpu.make_async_copy(tgt.at[:, pl.ds(col, TILE)], ys.at[k], ysem.at[k]),
+            pltpu.make_async_copy(src.at[:, pl.ds(first, TILE)], xs.at[k], xsem.at[k]),
+            pltpu.make_async_copy(tgt.at[:, pl.ds(second, TILE)], ys.at[k], ysem.at[k]),
         )
 
     def begin(k, carry):
@@ -126,36 +133,45 @@
 
     lax.fori_loop(0, live, begin, 0)
     ext[...] = jnp.zeros_like(ext)
+    for u in range(GROUP):
+        for side, place in ((0, 1), (0, 3), (1, 0), (1, 2)):
+            ext[u, side, pl.ds(width + place, 1), :] = jnp.ones((1, TILE), jnp.float32)
     top[...] = jnp.full_like(top, FLOOR)
     total[...] = jnp.zeros_like(total)
-    dims = (((0,), (0,)), ((), ()))
+
+    def extend(u, side, points, scale):
+        square = jnp.sum(points * points, axis=0, keepdims=True) * SCALE
+        high, middle = split(square)
+        ext[u, side, pl.ds(0, width), :] = points * scale
+        ext[u, side, pl.ds(width + side, 1), :] = square
+        rest = square - high.astype(jnp.float32) - middle.astype(jnp.float32)
+        ext[u, side, pl.ds(width + side + 2, 1), :] = rest
+        return split(ext[u, side])
+
+    def product(first, second):
+        turned = jnp.concatenate(first, axis=0).T
+        turned = jnp.concatenate((turned, turned), axis=1)
+        high, middle = second
+        other = jnp.concatenate((high, high, middle, middle), axis=0)
+        return jnp.dot(turned, other, preferred_element_type=jnp.float32)
 
     def group(q, carry):
         lax.fori_loop(q * GROUP, jnp.minimum(live, q * GROUP + GROUP), end, 0)
         ready = []
         for u in range(GROUP):
             k = q * GROUP + u
-            x = xs[k]
-            y = ys[k]
-            ext[u, 0, pl.ds(0, width), :] = x * (-2.0 * SCALE)
-            ext[u, 0, pl.ds(width, 1), :] = jnp.sum(x * x, axis=0, keepdims=True) * SCALE
-            ext[u, 0, pl.ds(width + 1, 1), :] = jnp.full((1, TILE), SCALE, jnp.float32)
-            ext[u, 1, pl.ds(0, width), :] = y
-            ext[u, 1, pl.ds(width, 1), :] = jnp.ones((1, TILE), jnp.float32)
-            ext[u, 1, pl.ds(width + 1, 1), :] = jnp.sum(y * y, axis=0, keepdims=True)
-            xh, xm, xl = split(ext[u, 0])
-            yh, ym, yl = split(ext[u, 1])
-            left = jnp.concatenate((xh, xh, xm, xm, xh, xl), axis=0)
-            right = jnp.concatenate((yh, ym, yh, ym, yl, yh), axis=0)
-            cost_ab[k] = lax.dot_general(left, right, dims, preferred_element_type=jnp.float32)
-            value = lax.dot_general(right, left, dims, preferred_element_type=jnp.float32)
+            centre = ys[k, :, pl.ds(0, 1)]
+            left = extend(u, 0, xs[k] - centre, -2.0 * SCALE)
+            right = extend(u, 1, ys[k] - centre, 1.0)
+            cost_ab[k] = product(left, right)
+            value = product(right, left)
             cost_ba[k] = value
             peak = 0.0 - jnp.min(value, axis=0, keepdims=True)
             ready.append((k < live, block(tiles, 0, k, blocks_out), peak))
         for on, index, peak in ready:
-            for h, lanes in halves():
+            for h in range(2):
                 new = jnp.where(on, peak[:, h * HALF : (h + 1) * HALF], FLOOR)
-                top[h, pl.ds(index, 1), :] = jnp.maximum(top[h, pl.ds(index, 1), :], new)
+                top[row(index, h), :] = jnp.maximum(top[row(index, h), :], new)
         return carry
 
     lax.fori_loop(0, (live + GROUP - 1) // GROUP, group, 0)
@@ -163,22 +179,22 @@
     finish(out, top, total)
 
 
-def sweep_kernel(offset, far, scale, inner, outer, blocks_in, blocks_out, tiles, counts, cost, *refs):
-    parts = refs[:-5]
-    out, result, held, top, total = refs[-5:]
-    live = counts[0]
-    before = None
-    if far is not None:
-        before, parts = parts[0], parts[1:]
+def sweep_kernel(offset, far, scale, inner, outer, blocks_in, blocks_out, tiles_in, counts, cost, *refs):
+    parts = refs[:-7]
+    out, result, tiles, tsem, held, top, total = refs[-7:]
+    table = pltpu.make_async_copy(tiles_in, tiles, tsem)
+    table.start()
+    if far is None:
+        top[...] = jnp.full_like(top, offset)
+    else:
+        top[...] = far - parts[0][...]
+        parts = parts[1:]
     potential = offset - lse2_many([part[...] for part in parts])
     result[...] = potential * scale
-    for h, lanes in halves():
-        held[h] = potential[:, h * HALF : (h + 1) * HALF]
-        if before is None:
-            top[h] = jnp.full((blocks_out, HALF), offset, jnp.float32)
-        else:
-            top[h] = far - before[:, lanes]
+    held[...] = potential
     total[...] = jnp.zeros_like(total)
+    table.wait()
+    live = counts[0, 0]
 
     def potential_of(k):
         return spread(held, block(tiles, inner, k, blocks_in))
@@ -196,7 +212,7 @@
             index = block(tiles, outer, k, blocks_out)
             found = peaks(k, cost, potential_of(k))
             for h in range(2):
-                top[h, pl.ds(index, 1), :] = jnp.maximum(top[h, pl.ds(index, 1), :], found[h])
+                top[row(index, h), :] = jnp.maximum(top[row(index, h), :], found[h])
             return carry
 
         lax.fori_loop(0, live, step, 0)
@@ -220,19 +236,18 @@
     slots = tiles.shape[1]
     width = src.shape[0]
     shape = pltpu.VMEM((slots, TILE, TILE), jnp.float32)
-    src = pltpu.with_memory_space_constraint(src, pltpu.HBM)
-    tgt = pltpu.with_memory_space_constraint(tgt, pltpu.HBM)
     return pl.pallas_call(
         functools.partial(cost_kernel, blocks_in, blocks_out),
-        out_shape=(shape, shape, jax.ShapeDtypeStruct((blocks_out, TILE), jnp.float32)),
-        in_specs=[smem_spec(), smem_spec(), hbm_spec(), hbm_spec()],
+        out_shape=(shape, shape, jax.ShapeDtypeStruct((2 * blocks_out, HALF), jnp.float32)),
+        in_specs=[hbm_spec(), smem_spec(), hbm_spec(), hbm_spec()],
         out_specs=(vmem_spec(), vmem_spec(), vmem_spec()),
         scratch_shapes=[
+            *table_scratch(slots),
             pltpu.VMEM((slots, width, TILE), jnp.float32),
             pltpu.VMEM((slots, width, TILE), jnp.float32),
             pltpu.VMEM((GROUP, 2, DEPTH, TILE), jnp.float32),
-            pltpu.VMEM((2, blocks_out, HALF), jnp.float32),
-            pltpu.VMEM((2, blocks_out, HALF), jnp.float32),
+            pltpu.VMEM((2 * blocks_out, HALF), jnp.float32),
+            pltpu.VMEM((2 * blocks_out, HALF), jnp.float32),
             pltpu.SemaphoreType.DMA((slots,)),
             pltpu.SemaphoreType.DMA((slots,)),
         ],
@@ -249,15 +264,16 @@
     return pl.pallas_call(
         kernel,
         out_shape=(
-            jax.ShapeDtypeStruct((blocks_out, TILE), jnp.float32),
-            jax.ShapeDtypeStruct((blocks_in, TILE), jnp.float32),
+            jax.ShapeDtypeStruct((2 * blocks_out, HALF), jnp.float32),
+            jax.ShapeDtypeStruct((2 * blocks_in, HALF), jnp.float32),
         ),
-        in_specs=[smem_spec(), smem_spec()] + [vmem_spec()] * (1 + len(operands)),
+        in_specs=[hbm_spec(), smem_spec()] + [vmem_spec()] * (1 + len(operands)),
         out_specs=(vmem_spec(), vmem_spec()),
         scratch_shapes=[
-            pltpu.VMEM((2, blocks_in, HALF), jnp.float32),
-            pltpu.VMEM((2, blocks_out, HALF), jnp.float32),
-            pltpu.VMEM((2, blocks_out, HALF), jnp.float32),
+            *table_scratch(tiles.shape[1]),
+            pltpu.VMEM((2 * blocks_in, HALF), jnp.float32),
+            pltpu.VMEM((2 * blocks_out, HALF), jnp.float32),
+            pltpu.VMEM((2 * blocks_out, HALF), jnp.float32),
         ],
         compiler_params=pltpu.CompilerParams(vmem_limit_bytes=VMEM_LIMIT),
     )(tiles, counts, cost, *operands)
@@ -293,8 +309,10 @@
 
 
 def body(src_points, tgt_points, tiles, counts):
-    tiles = tiles[0, 0]
-    counts = counts[0]
+    tiles, src_points, tgt_points = (
+        pltpu.with_memory_space_constraint(each, pltpu.HBM)
+        for each in (tiles[0, 0], src_points, tgt_points)
+    )
     row_blocks = src_points.shape[1] // TILE
     col_blocks = tgt_points.shape[1] // TILE
     src_cells = src_points.shape[1] * lax.axis_size("src")

time: 157 us -> 155 us (0.987)
  the two profiles are of different devices: /device:TPU:2 before, /device:TPU:8 now
where the time goes in v3:
time: 155 us; the launch traced here: 157 us
  starting transfers between devices  77.9 us (50%)
  waiting for transfers between devices  61.3 us (40%)
  Pallas kernels  14.5 us (9%)
    ppermute x12, starting transfers between devices, pair(): lax.ppermute(value, axis, [(k, flip(k)) for k in range(size)])  45.7 us
    ppermute x12, waiting for transfers between devices, pair(): lax.ppermute(value, axis, [(k, flip(k)) for k in range(size)])  35.4 us
    ppermute x18, starting transfers between devices, fan(): got.append(lax.ppermute(value, axis, pairs))  32.3 us
    ppermute x18, waiting for transfers between devices, fan(): got.append(lax.ppermute(value, axis, pairs))  25.9 us
    pallas_call x5, Pallas kernels, sweep(): pl.pallas_call(kernel, out_shape=(jax.ShapeDtypeStruct((2 * blocks_out, H...  10.9 us
    pallas_call x1, Pallas kernels, costs(): pl.pallas_call(functools.partial(cost_kernel, blocks_in, blocks_out), out...  3.69 us
  transfers between devices with their start and end apart: 30, of which 26 were waited for; matrix products, arithmetic and copies ran while one was open for 0% of the time, Pallas kernels for 0%

profile of v3, /device:TPU:8, one launch (start us, length us, event | category | flops | bytes accessed | tf_op | source)
XLA Modules:
  0.0 156.7 jit_solution(14734864558989532520)
XLA Ops:
  1.3 3.7 %shard_map.59 = (f32[32,256,256]{2,1,0:T(8,128)S(1)}, f32[32,256,256]{2,1,0:T(8,128)S(1)}, f32[128,128]{1,0:T(8,128)S(1)}) custom-call(s32[2,32]{1,0:T(2,128)} %bitcast.4, s32[1,1]{1,0:T(1,128)S(6)} %copy.6.counts, f32[50,16384]{1,0:T(8,128)} %src.1, f32[50,24576]{1,0:T(8,128)} %tgt.1), custom_call_target="tpu_custom_call" | custom-call | tf_op jit(solution)/shard_map/pallas_call | solution.py:239
  6.4 4.1 %collective-permute-start.3 = (f32[128,128]{1,0:T(8,128)S(1)}, f32[128,128]{1,0:T(8,128)S(1)}, u32[]{:S(2)}, u32[]{:S(2)}) collective-permute-start(f32[128,128]{1,0:T(8,128)S(1)} %multiply_add_fusion.11.refs_0_), channel_id=1, source_target_pairs={{0,6},{1,7},{2,4},{3,5},{4,2},{5,3},{6,0},{7,1},{8,14},{9,15},{10,... | collective-permute-start | bytes 196616 | tf_op jit(solution)/shard_map/ppermute | solution.py:289
  12.9 3.7 %collective-permute-done.2.refs_2_ = f32[128,128]{1,0:T(8,128)S(1)} collective-permute-done((f32[128,128]{1,0:T(8,128)S(1)}, f32[128,128]{1,0:T(8,128)S(1)}, u32[]{:S(2)}, u32[]{:S(2)}) %collective-permute-start.2) | collective-permute-done | bytes 65568 | tf_op jit(solution)/shard_map/ppermute | solution.py:289
  16.6 2.5 %shard_map.60 = (f32[192,128]{1,0:T(8,128)S(1)}, f32[128,128]{1,0:T(8,128)S(1)}) custom-call(s32[2,32]{1,0:T(2,128)} %bitcast.5, s32[1,1]{1,0:T(1,128)S(6)} %copy.6.counts, f32[32,256,256]{2,1,0:T(8,128)S(1)} %get-tuple-element.15.cost, f32[128,128]{1,0:T(8,128)S(1)} %multiply_add_fusion.11.refs_0_, f32[128,128]{1,0:T(8,128)S(1)} %collective-permute-done.1.refs_1_, ...), custom_call_target="tpu_custom_call" | custom-call | tf_op jit(solution)/shard_map/pallas_call | solution.py:264
  19.2 3.0 %collective-permute-start.6 = (f32[192,128]{1,0:T(8,128)S(1)}, f32[192,128]{1,0:T(8,128)S(1)}, u32[]{:S(2)}, u32[]{:S(2)}) collective-permute-start(f32[192,128]{1,0:T(8,128)S(1)} %get-tuple-element.19), channel_id=1, source_target_pairs={{0,24},{8,16},{16,8},{24,0},{32,56},{40,48},{48,40},{56,32},{64,88... | collective-permute-start | bytes 294920 | tf_op jit(solution)/shard_map/ppermute | solution.py:289
  22.2 2.7 %collective-permute-start.5 = (f32[192,128]{1,0:T(8,128)S(1)}, f32[192,128]{1,0:T(8,128)S(1)}, u32[]{:S(2)}, u32[]{:S(2)}) collective-permute-start(f32[192,128]{1,0:T(8,128)S(1)} %get-tuple-element.19), channel_id=1, source_target_pairs={{0,16},{8,24},{16,0},{24,8},{32,48},{40,56},{48,32},{56,40},{64,80... | collective-permute-start | bytes 294920 | tf_op jit(solution)/shard_map/ppermute | solution.py:289
  26.1 3.2 %collective-permute-done.5 = f32[192,128]{1,0:T(8,128)S(1)} collective-permute-done((f32[192,128]{1,0:T(8,128)S(1)}, f32[192,128]{1,0:T(8,128)S(1)}, u32[]{:S(2)}, u32[]{:S(2)}) %collective-permute-start.5) | collective-permute-done | bytes 98336 | tf_op jit(solution)/shard_map/ppermute | solution.py:289
  29.5 6.7 %collective-permute-start.7 = (f32[192,128]{1,0:T(8,128)S(1)}, f32[192,128]{1,0:T(8,128)S(1)}, u32[]{:S(2)}, u32[]{:S(2)}) collective-permute-start(f32[192,128]{1,0:T(8,128)S(1)} %multiply_add_fusion.8), channel_id=1, source_target_pairs={{0,32},{8,40},{16,48},{24,56},{32,0},{40,8},{48,16},{56,24},{64,96... | collective-permute-start | bytes 294920 | tf_op jit(solution)/shard_map/ppermute | solution.py:294
  36.3 2.6 %collective-permute-done.7 = f32[192,128]{1,0:T(8,128)S(1)} collective-permute-done((f32[192,128]{1,0:T(8,128)S(1)}, f32[192,128]{1,0:T(8,128)S(1)}, u32[]{:S(2)}, u32[]{:S(2)}) %collective-permute-start.7) | collective-permute-done | bytes 98336 | tf_op jit(solution)/shard_map/ppermute | solution.py:294
  38.9 3.4 %collective-permute-start.8 = (f32[192,128]{1,0:T(8,128)S(1)}, f32[192,128]{1,0:T(8,128)S(1)}, u32[]{:S(2)}, u32[]{:S(2)}) collective-permute-start(f32[192,128]{1,0:T(8,128)S(1)} %multiply_add_fusion.7), channel_id=1, source_target_pairs={{0,96},{8,104},{16,112},{24,120},{32,64},{40,72},{48,80},{56,88},{... | collective-permute-start | bytes 294920 | tf_op jit(solution)/shard_map/ppermute | solution.py:294
  42.3 3.2 %collective-permute-done.8 = f32[192,128]{1,0:T(8,128)S(1)} collective-permute-done((f32[192,128]{1,0:T(8,128)S(1)}, f32[192,128]{1,0:T(8,128)S(1)}, u32[]{:S(2)}, u32[]{:S(2)}) %collective-permute-start.8) | collective-permute-done | bytes 98336 | tf_op jit(solution)/shard_map/ppermute | solution.py:294
  45.6 4.3 %collective-permute-start.9 = (f32[192,128]{1,0:T(8,128)S(1)}, f32[192,128]{1,0:T(8,128)S(1)}, u32[]{:S(2)}, u32[]{:S(2)}) collective-permute-start(f32[192,128]{1,0:T(8,128)S(1)} %multiply_add_fusion.6.refs_1_), channel_id=1, source_target_pairs={{0,224},{8,232},{16,240},{24,248},{32,192},{40,200},{48,208},{56,2... | collective-permute-start | bytes 294920 | tf_op jit(solution)/shard_map/ppermute | solution.py:294
  49.9 3.6 %collective-permute-done.9.refs_2_ = f32[192,128]{1,0:T(8,128)S(1)} collective-permute-done((f32[192,128]{1,0:T(8,128)S(1)}, f32[192,128]{1,0:T(8,128)S(1)}, u32[]{:S(2)}, u32[]{:S(2)}) %collective-permute-start.9) | collective-permute-done | bytes 98336 | tf_op jit(solution)/shard_map/ppermute | solution.py:294
  60.5 3.6 %collective-permute-done.12.refs_3_ = f32[128,128]{1,0:T(8,128)S(1)} collective-permute-done((f32[128,128]{1,0:T(8,128)S(1)}, f32[128,128]{1,0:T(8,128)S(1)}, u32[]{:S(2)}, u32[]{:S(2)}) %collective-permute-start.12) | collective-permute-done | bytes 65568 | tf_op jit(solution)/shard_map/ppermute | solution.py:289
  64.2 2.7 %shard_map.62 = (f32[192,128]{1,0:T(8,128)S(1)}, f32[128,128]{1,0:T(8,128)S(1)}) custom-call(s32[2,32]{1,0:T(2,128)} %bitcast.7, s32[1,1]{1,0:T(1,128)S(6)} %copy.6.counts, f32[32,256,256]{2,1,0:T(8,128)S(1)} %get-tuple-element.15.cost, f32[192,128]{1,0:T(8,128)S(1)} %get-tuple-element.20.refs_0_, f32[128,128]{1,0:T(8,128)S(1)} %multiply_add_fusion.10.refs_1_, ...), custom_call_target="tpu_custom_call" | custom-call | tf_op jit(solution)/shard_map/pallas_call | solution.py:264
  66.9 5.2 %collective-permute-start.16 = (f32[192,128]{1,0:T(8,128)S(1)}, f32[192,128]{1,0:T(8,128)S(1)}, u32[]{:S(2)}, u32[]{:S(2)}) collective-permute-start(f32[192,128]{1,0:T(8,128)S(1)} %get-tuple-element.23), channel_id=1, source_target_pairs={{0,24},{8,16},{16,8},{24,0},{32,56},{40,48},{48,40},{56,32},{64,88... | collective-permute-start | bytes 294920 | tf_op jit(solution)/shard_map/ppermute | solution.py:289
  73.0 2.7 %collective-permute-done.16 = f32[192,128]{1,0:T(8,128)S(1)} collective-permute-done((f32[192,128]{1,0:T(8,128)S(1)}, f32[192,128]{1,0:T(8,128)S(1)}, u32[]{:S(2)}, u32[]{:S(2)}) %collective-permute-start.16) | collective-permute-done | bytes 98336 | tf_op jit(solution)/shard_map/ppermute | solution.py:289
  78.3 4.0 %collective-permute-start.17 = (f32[192,128]{1,0:T(8,128)S(1)}, f32[192,128]{1,0:T(8,128)S(1)}, u32[]{:S(2)}, u32[]{:S(2)}) collective-permute-start(f32[192,128]{1,0:T(8,128)S(1)} %multiply_add_fusion.5), channel_id=1, source_target_pairs={{0,32},{8,40},{16,48},{24,56},{32,0},{40,8},{48,16},{56,24},{64,96... | collective-permute-start | bytes 294920 | tf_op jit(solution)/shard_map/ppermute | solution.py:294
  82.3 2.6 %collective-permute-done.17 = f32[192,128]{1,0:T(8,128)S(1)} collective-permute-done((f32[192,128]{1,0:T(8,128)S(1)}, f32[192,128]{1,0:T(8,128)S(1)}, u32[]{:S(2)}, u32[]{:S(2)}) %collective-permute-start.17) | collective-permute-done | bytes 98336 | tf_op jit(solution)/shard_map/ppermute | solution.py:294
  84.9 2.7 %collective-permute-start.18 = (f32[192,128]{1,0:T(8,128)S(1)}, f32[192,128]{1,0:T(8,128)S(1)}, u32[]{:S(2)}, u32[]{:S(2)}) collective-permute-start(f32[192,128]{1,0:T(8,128)S(1)} %multiply_add_fusion.4), channel_id=1, source_target_pairs={{0,96},{8,104},{16,112},{24,120},{32,64},{40,72},{48,80},{56,88},{... | collective-permute-start | bytes 294920 | tf_op jit(solution)/shard_map/ppermute | solution.py:294
  87.6 3.9 %collective-permute-done.18 = f32[192,128]{1,0:T(8,128)S(1)} collective-permute-done((f32[192,128]{1,0:T(8,128)S(1)}, f32[192,128]{1,0:T(8,128)S(1)}, u32[]{:S(2)}, u32[]{:S(2)}) %collective-permute-start.18) | collective-permute-done | bytes 98336 | tf_op jit(solution)/shard_map/ppermute | solution.py:294
  91.6 9.4 %collective-permute-start.19 = (f32[192,128]{1,0:T(8,128)S(1)}, f32[192,128]{1,0:T(8,128)S(1)}, u32[]{:S(2)}, u32[]{:S(2)}) collective-permute-start(f32[192,128]{1,0:T(8,128)S(1)} %multiply_add_fusion.3.refs_1_), channel_id=1, source_target_pairs={{0,224},{8,232},{16,240},{24,248},{32,192},{40,200},{48,208},{56,2... | collective-permute-start | bytes 294920 | tf_op jit(solution)/shard_map/ppermute | solution.py:294
  101.0 2.6 %collective-permute-done.19.refs_2_ = f32[192,128]{1,0:T(8,128)S(1)} collective-permute-done((f32[192,128]{1,0:T(8,128)S(1)}, f32[192,128]{1,0:T(8,128)S(1)}, u32[]{:S(2)}, u32[]{:S(2)}) %collective-permute-start.19) | collective-permute-done | bytes 98336 | tf_op jit(solution)/shard_map/ppermute | solution.py:294
  106.3 3.0 %collective-permute-start.22 = (f32[128,128]{1,0:T(8,128)S(1)}, f32[128,128]{1,0:T(8,128)S(1)}, u32[]{:S(2)}, u32[]{:S(2)}) collective-permute-start(f32[128,128]{1,0:T(8,128)S(1)} %multiply_add_fusion.9.refs_1_), channel_id=1, source_target_pairs={{0,4},{1,5},{2,6},{3,7},{4,0},{5,1},{6,2},{7,3},{8,12},{9,13},{10,... | collective-permute-start | bytes 196616 | tf_op jit(solution)/shard_map/ppermute | solution.py:289
  113.7 3.2 %shard_map.64 = (f32[192,128]{1,0:T(8,128)S(1)}, f32[128,128]{1,0:T(8,128)}) custom-call(s32[2,32]{1,0:T(2,128)} %bitcast.9, s32[1,1]{1,0:T(1,128)S(6)} %copy.6.counts, f32[32,256,256]{2,1,0:T(8,128)S(1)} %get-tuple-element.15.cost, f32[192,128]{1,0:T(8,128)S(1)} %get-tuple-element.24.refs_0_, f32[128,128]{1,0:T(8,128)S(1)} %multiply_add_fusion.9.refs_1_, ...), custom_call_target="tpu_custom_call" | custom-call | tf_op jit(solution)/shard_map/pallas_call | solution.py:264
  116.8 4.8 %collective-permute-start.26 = (f32[192,128]{1,0:T(8,128)S(1)}, f32[192,128]{1,0:T(8,128)S(1)}, u32[]{:S(2)}, u32[]{:S(2)}) collective-permute-start(f32[192,128]{1,0:T(8,128)S(1)} %get-tuple-element.27), channel_id=1, source_target_pairs={{0,24},{8,16},{16,8},{24,0},{32,56},{40,48},{48,40},{56,32},{64,88... | collective-permute-start | bytes 294920 | tf_op jit(solution)/shard_map/ppermute | solution.py:289
  122.6 2.7 %collective-permute-done.26 = f32[192,128]{1,0:T(8,128)S(1)} collective-permute-done((f32[192,128]{1,0:T(8,128)S(1)}, f32[192,128]{1,0:T(8,128)S(1)}, u32[]{:S(2)}, u32[]{:S(2)}) %collective-permute-start.26) | collective-permute-done | bytes 98336 | tf_op jit(solution)/shard_map/ppermute | solution.py:289
  127.9 5.4 %collective-permute-start.27 = (f32[192,128]{1,0:T(8,128)S(1)}, f32[192,128]{1,0:T(8,128)S(1)}, u32[]{:S(2)}, u32[]{:S(2)}) collective-permute-start(f32[192,128]{1,0:T(8,128)S(1)} %multiply_add_fusion.2), channel_id=1, source_target_pairs={{0,32},{8,40},{16,48},{24,56},{32,0},{40,8},{48,16},{56,24},{64,96... | collective-permute-start | bytes 294920 | tf_op jit(solution)/shard_map/ppermute | solution.py:294
  133.2 3.6 %collective-permute-done.27 = f32[192,128]{1,0:T(8,128)S(1)} collective-permute-done((f32[192,128]{1,0:T(8,128)S(1)}, f32[192,128]{1,0:T(8,128)S(1)}, u32[]{:S(2)}, u32[]{:S(2)}) %collective-permute-start.27) | collective-permute-done | bytes 98336 | tf_op jit(solution)/shard_map/ppermute | solution.py:294
  137.8 5.8 %collective-permute-done.28 = f32[192,128]{1,0:T(8,128)S(1)} collective-permute-done((f32[192,128]{1,0:T(8,128)S(1)}, f32[192,128]{1,0:T(8,128)S(1)}, u32[]{:S(2)}, u32[]{:S(2)}) %collective-permute-start.28) | collective-permute-done | bytes 98336 | tf_op jit(solution)/shard_map/ppermute | solution.py:294
  143.6 8.7 %collective-permute-start.29 = (f32[192,128]{1,0:T(8,128)S(1)}, f32[192,128]{1,0:T(8,128)S(1)}, u32[]{:S(2)}, u32[]{:S(2)}) collective-permute-start(f32[192,128]{1,0:T(8,128)S(1)} %multiply_add_fusion), channel_id=1, source_target_pairs={{0,224},{8,232},{16,240},{24,248},{32,192},{40,200},{48,208},{56,2... | collective-permute-start | bytes 294920 | tf_op jit(solution)/shard_map/ppermute | solution.py:294
  152.3 3.6 %collective-permute-done.29 = f32[192,128]{1,0:T(8,128)S(1)} collective-permute-done((f32[192,128]{1,0:T(8,128)S(1)}, f32[192,128]{1,0:T(8,128)S(1)}, u32[]{:S(2)}, u32[]{:S(2)}) %collective-permute-start.29) | collective-permute-done | bytes 98336 | tf_op jit(solution)/shard_map/ppermute | solution.py:294
  (47 shorter events, 28.2 us)
Async XLA Ops:
  5.0 1.3 collective-permute-start
  6.4 6.6 %collective-permute-start.3 = (f32[128,128]{1,0:T(8,128)S(1)}, f32[128,128]{1,0:T(8,128)S(1)}, u32[]{:S(2)}, u32[]{:S(2)}) collective-permute-start(f32[128,128]{1,0:T(8,128)S(1)} %multiply_add_fusion.11.refs_0_), channel_id=1, source_target_pairs={{0,6},{1,7},{2,4},{3,5},{4,2},{5,3},{6,0},{7,1},{8,14},{9,15},{10,... | collective-permute-start | bytes 196616 | tf_op jit(solution)/shard_map/ppermute | solution.py:289
  10.5 6.1 %collective-permute-start.2 = (f32[128,128]{1,0:T(8,128)S(1)}, f32[128,128]{1,0:T(8,128)S(1)}, u32[]{:S(2)}, u32[]{:S(2)}) collective-permute-start(f32[128,128]{1,0:T(8,128)S(1)} %multiply_add_fusion.11.refs_0_), channel_id=1, source_target_pairs={{0,4},{1,5},{2,6},{3,7},{4,0},{5,1},{6,2},{7,3},{8,12},{9,13},{10,... | collective-permute-start | bytes 196616 | tf_op jit(solution)/shard_map/ppermute | solution.py:289
  10.7 5.9 %collective-permute-start.1 = (f32[128,128]{1,0:T(8,128)S(1)}, f32[128,128]{1,0:T(8,128)S(1)}, u32[]{:S(2)}, u32[]{:S(2)}) collective-permute-start(f32[128,128]{1,0:T(8,128)S(1)} %multiply_add_fusion.11.refs_0_), channel_id=1, source_target_pairs={{0,2},{1,3},{2,0},{3,1},{4,6},{5,7},{6,4},{7,5},{8,10},{9,11},{10,... | collective-permute-start | bytes 196616 | tf_op jit(solution)/shard_map/ppermute | solution.py:289
  19.2 7.0 %collective-permute-start.6 = (f32[192,128]{1,0:T(8,128)S(1)}, f32[192,128]{1,0:T(8,128)S(1)}, u32[]{:S(2)}, u32[]{:S(2)}) collective-permute-start(f32[192,128]{1,0:T(8,128)S(1)} %get-tuple-element.19), channel_id=1, source_target_pairs={{0,24},{8,16},{16,8},{24,0},{32,56},{40,48},{48,40},{56,32},{64,88... | collective-permute-start | bytes 294920 | tf_op jit(solution)/shard_map/ppermute | solution.py:289
  22.2 7.1 %collective-permute-start.5 = (f32[192,128]{1,0:T(8,128)S(1)}, f32[192,128]{1,0:T(8,128)S(1)}, u32[]{:S(2)}, u32[]{:S(2)}) collective-permute-start(f32[192,128]{1,0:T(8,128)S(1)} %get-tuple-element.19), channel_id=1, source_target_pairs={{0,16},{8,24},{16,0},{24,8},{32,48},{40,56},{48,32},{56,40},{64,80... | collective-permute-start | bytes 294920 | tf_op jit(solution)/shard_map/ppermute | solution.py:289
  24.8 4.6 %collective-permute-start.4 = (f32[192,128]{1,0:T(8,128)S(1)}, f32[192,128]{1,0:T(8,128)S(1)}, u32[]{:S(2)}, u32[]{:S(2)}) collective-permute-start(f32[192,128]{1,0:T(8,128)S(1)} %get-tuple-element.19), channel_id=1, source_target_pairs={{0,8},{8,0},{16,24},{24,16},{32,40},{40,32},{48,56},{56,48},{64,72... | collective-permute-start | bytes 294920 | tf_op jit(solution)/shard_map/ppermute | solution.py:289
  29.5 9.3 %collective-permute-start.7 = (f32[192,128]{1,0:T(8,128)S(1)}, f32[192,128]{1,0:T(8,128)S(1)}, u32[]{:S(2)}, u32[]{:S(2)}) collective-permute-start(f32[192,128]{1,0:T(8,128)S(1)} %multiply_add_fusion.8), channel_id=1, source_target_pairs={{0,32},{8,40},{16,48},{24,56},{32,0},{40,8},{48,16},{56,24},{64,96... | collective-permute-start | bytes 294920 | tf_op jit(solution)/shard_map/ppermute | solution.py:294
  38.9 6.6 %collective-permute-start.8 = (f32[192,128]{1,0:T(8,128)S(1)}, f32[192,128]{1,0:T(8,128)S(1)}, u32[]{:S(2)}, u32[]{:S(2)}) collective-permute-start(f32[192,128]{1,0:T(8,128)S(1)} %multiply_add_fusion.7), channel_id=1, source_target_pairs={{0,96},{8,104},{16,112},{24,120},{32,64},{40,72},{48,80},{56,88},{... | collective-permute-start | bytes 294920 | tf_op jit(solution)/shard_map/ppermute | solution.py:294
  45.6 8.0 %collective-permute-start.9 = (f32[192,128]{1,0:T(8,128)S(1)}, f32[192,128]{1,0:T(8,128)S(1)}, u32[]{:S(2)}, u32[]{:S(2)}) collective-permute-start(f32[192,128]{1,0:T(8,128)S(1)} %multiply_add_fusion.6.refs_1_), channel_id=1, source_target_pairs={{0,224},{8,232},{16,240},{24,248},{32,192},{40,200},{48,208},{56,2... | collective-permute-start | bytes 294920 | tf_op jit(solution)/shard_map/ppermute | solution.py:294
  54.8 1.3 collective-permute-start.10
  56.2 4.4 %collective-permute-start.13 = (f32[128,128]{1,0:T(8,128)S(1)}, f32[128,128]{1,0:T(8,128)S(1)}, u32[]{:S(2)}, u32[]{:S(2)}) collective-permute-start(f32[128,128]{1,0:T(8,128)S(1)} %multiply_add_fusion.10.refs_1_), channel_id=1, source_target_pairs={{0,6},{1,7},{2,4},{3,5},{4,2},{5,3},{6,0},{7,1},{8,14},{9,15},{10,... | collective-permute-start | bytes 196616 | tf_op jit(solution)/shard_map/ppermute | solution.py:289
  58.1 6.1 %collective-permute-start.12 = (f32[128,128]{1,0:T(8,128)S(1)}, f32[128,128]{1,0:T(8,128)S(1)}, u32[]{:S(2)}, u32[]{:S(2)}) collective-permute-start(f32[128,128]{1,0:T(8,128)S(1)} %multiply_add_fusion.10.refs_1_), channel_id=1, source_target_pairs={{0,4},{1,5},{2,6},{3,7},{4,0},{5,1},{6,2},{7,3},{8,12},{9,13},{10,... | collective-permute-start | bytes 196616 | tf_op jit(solution)/shard_map/ppermute | solution.py:289
  58.3 5.9 %collective-permute-start.11 = (f32[128,128]{1,0:T(8,128)S(1)}, f32[128,128]{1,0:T(8,128)S(1)}, u32[]{:S(2)}, u32[]{:S(2)}) collective-permute-start(f32[128,128]{1,0:T(8,128)S(1)} %multiply_add_fusion.10.refs_1_), channel_id=1, source_target_pairs={{0,2},{1,3},{2,0},{3,1},{4,6},{5,7},{6,4},{7,5},{8,10},{9,11},{10,... | collective-permute-start | bytes 196616 | tf_op jit(solution)/shard_map/ppermute | solution.py:289
  66.9 8.8 %collective-permute-start.16 = (f32[192,128]{1,0:T(8,128)S(1)}, f32[192,128]{1,0:T(8,128)S(1)}, u32[]{:S(2)}, u32[]{:S(2)}) collective-permute-start(f32[192,128]{1,0:T(8,128)S(1)} %get-tuple-element.23), channel_id=1, source_target_pairs={{0,24},{8,16},{16,8},{24,0},{32,56},{40,48},{48,40},{56,32},{64,88... | collective-permute-start | bytes 294920 | tf_op jit(solution)/shard_map/ppermute | solution.py:289
  72.1 6.1 %collective-permute-start.15 = (f32[192,128]{1,0:T(8,128)S(1)}, f32[192,128]{1,0:T(8,128)S(1)}, u32[]{:S(2)}, u32[]{:S(2)}) collective-permute-start(f32[192,128]{1,0:T(8,128)S(1)} %get-tuple-element.23), channel_id=1, source_target_pairs={{0,16},{8,24},{16,0},{24,8},{32,48},{40,56},{48,32},{56,40},{64,80... | collective-permute-start | bytes 294920 | tf_op jit(solution)/shard_map/ppermute | solution.py:289
  72.1 6.1 %collective-permute-start.14 = (f32[192,128]{1,0:T(8,128)S(1)}, f32[192,128]{1,0:T(8,128)S(1)}, u32[]{:S(2)}, u32[]{:S(2)}) collective-permute-start(f32[192,128]{1,0:T(8,128)S(1)} %get-tuple-element.23), channel_id=1, source_target_pairs={{0,8},{8,0},{16,24},{24,16},{32,40},{40,32},{48,56},{56,48},{64,72... | collective-permute-start | bytes 294920 | tf_op jit(solution)/shard_map/ppermute | solution.py:289
  78.3 6.6 %collective-permute-start.17 = (f32[192,128]{1,0:T(8,128)S(1)}, f32[192,128]{1,0:T(8,128)S(1)}, u32[]{:S(2)}, u32[]{:S(2)}) collective-permute-start(f32[192,128]{1,0:T(8,128)S(1)} %multiply_add_fusion.5), channel_id=1, source_target_pairs={{0,32},{8,40},{16,48},{24,56},{32,0},{40,8},{48,16},{56,24},{64,96... | collective-permute-start | bytes 294920 | tf_op jit(solution)/shard_map/ppermute | solution.py:294
  84.9 6.6 %collective-permute-start.18 = (f32[192,128]{1,0:T(8,128)S(1)}, f32[192,128]{1,0:T(8,128)S(1)}, u32[]{:S(2)}, u32[]{:S(2)}) collective-permute-start(f32[192,128]{1,0:T(8,128)S(1)} %multiply_add_fusion.4), channel_id=1, source_target_pairs={{0,96},{8,104},{16,112},{24,120},{32,64},{40,72},{48,80},{56,88},{... | collective-permute-start | bytes 294920 | tf_op jit(solution)/shard_map/ppermute | solution.py:294
  91.6 12.0 %collective-permute-start.19 = (f32[192,128]{1,0:T(8,128)S(1)}, f32[192,128]{1,0:T(8,128)S(1)}, u32[]{:S(2)}, u32[]{:S(2)}) collective-permute-start(f32[192,128]{1,0:T(8,128)S(1)} %multiply_add_fusion.3.refs_1_), channel_id=1, source_target_pairs={{0,224},{8,232},{16,240},{24,248},{32,192},{40,200},{48,208},{56,2... | collective-permute-start | bytes 294920 | tf_op jit(solution)/shard_map/ppermute | solution.py:294
  104.8 1.3 collective-permute-start.20
  106.2 4.4 %collective-permute-start.23 = (f32[128,128]{1,0:T(8,128)S(1)}, f32[128,128]{1,0:T(8,128)S(1)}, u32[]{:S(2)}, u32[]{:S(2)}) collective-permute-start(f32[128,128]{1,0:T(8,128)S(1)} %multiply_add_fusion.9.refs_1_), channel_id=1, source_target_pairs={{0,6},{1,7},{2,4},{3,5},{4,2},{5,3},{6,0},{7,1},{8,14},{9,15},{10,... | collective-permute-start | bytes 196616 | tf_op jit(solution)/shard_map/ppermute | solution.py:289
  106.3 6.4 %collective-permute-start.22 = (f32[128,128]{1,0:T(8,128)S(1)}, f32[128,128]{1,0:T(8,128)S(1)}, u32[]{:S(2)}, u32[]{:S(2)}) collective-permute-start(f32[128,128]{1,0:T(8,128)S(1)} %multiply_add_fusion.9.refs_1_), channel_id=1, source_target_pairs={{0,4},{1,5},{2,6},{3,7},{4,0},{5,1},{6,2},{7,3},{8,12},{9,13},{10,... | collective-permute-start | bytes 196616 | tf_op jit(solution)/shard_map/ppermute | solution.py:289
  109.3 4.3 %collective-permute-start.21 = (f32[128,128]{1,0:T(8,128)S(1)}, f32[128,128]{1,0:T(8,128)S(1)}, u32[]{:S(2)}, u32[]{:S(2)}) collective-permute-start(f32[128,128]{1,0:T(8,128)S(1)} %multiply_add_fusion.9.refs_1_), channel_id=1, source_target_pairs={{0,2},{1,3},{2,0},{3,1},{4,6},{5,7},{6,4},{7,5},{8,10},{9,11},{10,... | collective-permute-start | bytes 196616 | tf_op jit(solution)/shard_map/ppermute | solution.py:289
  116.8 8.5 %collective-permute-start.26 = (f32[192,128]{1,0:T(8,128)S(1)}, f32[192,128]{1,0:T(8,128)S(1)}, u32[]{:S(2)}, u32[]{:S(2)}) collective-permute-start(f32[192,128]{1,0:T(8,128)S(1)} %get-tuple-element.27), channel_id=1, source_target_pairs={{0,24},{8,16},{16,8},{24,0},{32,56},{40,48},{48,40},{56,32},{64,88... | collective-permute-start | bytes 294920 | tf_op jit(solution)/shard_map/ppermute | solution.py:289
  121.7 6.1 %collective-permute-start.25 = (f32[192,128]{1,0:T(8,128)S(1)}, f32[192,128]{1,0:T(8,128)S(1)}, u32[]{:S(2)}, u32[]{:S(2)}) collective-permute-start(f32[192,128]{1,0:T(8,128)S(1)} %get-tuple-element.27), channel_id=1, source_target_pairs={{0,16},{8,24},{16,0},{24,8},{32,48},{40,56},{48,32},{56,40},{64,80... | collective-permute-start | bytes 294920 | tf_op jit(solution)/shard_map/ppermute | solution.py:289
  121.7 6.1 %collective-permute-start.24 = (f32[192,128]{1,0:T(8,128)S(1)}, f32[192,128]{1,0:T(8,128)S(1)}, u32[]{:S(2)}, u32[]{:S(2)}) collective-permute-start(f32[192,128]{1,0:T(8,128)S(1)} %get-tuple-element.27), channel_id=1, source_target_pairs={{0,8},{8,0},{16,24},{24,16},{32,40},{40,32},{48,56},{56,48},{64,72... | collective-permute-start | bytes 294920 | tf_op jit(solution)/shard_map/ppermute | solution.py:289
  127.9 9.0 %collective-permute-start.27 = (f32[192,128]{1,0:T(8,128)S(1)}, f32[192,128]{1,0:T(8,128)S(1)}, u32[]{:S(2)}, u32[]{:S(2)}) collective-permute-start(f32[192,128]{1,0:T(8,128)S(1)} %multiply_add_fusion.2), channel_id=1, source_target_pairs={{0,32},{8,40},{16,48},{24,56},{32,0},{40,8},{48,16},{56,24},{64,96... | collective-permute-start | bytes 294920 | tf_op jit(solution)/shard_map/ppermute | solution.py:294
  137.0 6.6 %collective-permute-start.28 = (f32[192,128]{1,0:T(8,128)S(1)}, f32[192,128]{1,0:T(8,128)S(1)}, u32[]{:S(2)}, u32[]{:S(2)}) collective-permute-start(f32[192,128]{1,0:T(8,128)S(1)} %multiply_add_fusion.1), channel_id=1, source_target_pairs={{0,96},{8,104},{16,112},{24,120},{32,64},{40,72},{48,80},{56,88},{... | collective-permute-start | bytes 294920 | tf_op jit(solution)/shard_map/ppermute | solution.py:294
  143.6 12.3 %collective-permute-start.29 = (f32[192,128]{1,0:T(8,128)S(1)}, f32[192,128]{1,0:T(8,128)S(1)}, u32[]{:S(2)}, u32[]{:S(2)}) collective-permute-start(f32[192,128]{1,0:T(8,128)S(1)} %multiply_add_fusion), channel_id=1, source_target_pairs={{0,224},{8,232},{16,240},{24,248},{32,192},{40,200},{48,208},{56,2... | collective-permute-start | bytes 294920 | tf_op jit(solution)/shard_map/ppermute | solution.py:294

commit v4 on v3

--- a/solution.py
+++ b/solution.py
@@ -12,6 +12,7 @@
 HALF = 128
 ROWS = 8
 GROUP = 8
+WIDE = 16
 ITERS = 3
 EPS = 0.05
 FLOOR = -1e30
@@ -71,15 +72,15 @@
 
 
 def spread(held, index):
-    return [jnp.broadcast_to(held[row(index, g), :], (HALF, HALF)).T for g in range(2)]
-
-
-def add_up(live, tiles, outer, blocks_out, cost, potential_of, top, total):
+    return [jnp.broadcast_to(held[0, row(index, g), :], (HALF, HALF)).T for g in range(2)]
+
+
+def add_up(size, live, tiles, outer, blocks_out, cost, potential_of, top, total):
     def group(q, carry):
         least, most = carry
         ready = []
-        for u in range(GROUP):
-            k = q * GROUP + u
+        for u in range(size):
+            k = q * size + u
             out = block(tiles, outer, k, blocks_out)
             shift = [top[row(out, h), :] for h in range(2)]
             ready.append((k < live, out, sums(k, cost, potential_of(k), shift)))
@@ -91,7 +92,7 @@
         return least, most
 
     one = jnp.ones((1, HALF), jnp.float32)
-    return lax.fori_loop(0, (live + GROUP - 1) // GROUP, group, (one, one))
+    return lax.fori_loop(0, (live + size - 1) // size, group, (one, one))
 
 
 def finish(out, top, total):
@@ -99,13 +100,17 @@
     out[...] = jnp.where(found, top[...] + jnp.log2(jnp.where(found, total[...], 1.0)), FLOOR)
 
 
-def table_scratch(slots):
-    return [pltpu.SMEM((2, slots), jnp.int32), pltpu.SemaphoreType.DMA(())]
+def product(first, second):
+    turned = first.T
+    turned = jnp.concatenate((turned, turned), axis=1)
+    high, middle = second[:DEPTH], second[DEPTH:]
+    other = jnp.concatenate((high, high, middle, middle), axis=0)
+    return jnp.dot(turned, other, preferred_element_type=jnp.float32)
 
 
 def cost_kernel(
-    blocks_in, blocks_out, tiles_in, counts, src, tgt, cost_ab, cost_ba, out,
-    tiles, tsem, xs, ys, ext, top, total, xsem, ysem
+    blocks_in, blocks_out, tiles_in, counts, src, tgt, cost, out, lefts, rights, tiles,
+    tsem, xs, ys, ext, top, total, xsem, ysem
 ):
     table = pltpu.make_async_copy(tiles_in, tiles, tsem)
     table.start()
@@ -146,14 +151,7 @@
         ext[u, side, pl.ds(width + side, 1), :] = square
         rest = square - high.astype(jnp.float32) - middle.astype(jnp.float32)
         ext[u, side, pl.ds(width + side + 2, 1), :] = rest
-        return split(ext[u, side])
-
-    def product(first, second):
-        turned = jnp.concatenate(first, axis=0).T
-        turned = jnp.concatenate((turned, turned), axis=1)
-        high, middle = second
-        other = jnp.concatenate((high, high, middle, middle), axis=0)
-        return jnp.dot(turned, other, preferred_element_type=jnp.float32)
+        return jnp.concatenate(split(ext[u, side]), axis=0)
 
     def group(q, carry):
         lax.fori_loop(q * GROUP, jnp.minimum(live, q * GROUP + GROUP), end, 0)
@@ -163,9 +161,10 @@
             centre = ys[k, :, pl.ds(0, 1)]
             left = extend(u, 0, xs[k] - centre, -2.0 * SCALE)
             right = extend(u, 1, ys[k] - centre, 1.0)
-            cost_ab[k] = product(left, right)
+            lefts[k] = left
+            rights[k] = right
             value = product(right, left)
-            cost_ba[k] = value
+            cost[k] = value
             peak = 0.0 - jnp.min(value, axis=0, keepdims=True)
             ready.append((k < live, block(tiles, 0, k, blocks_out), peak))
         for on, index, peak in ready:
@@ -175,31 +174,45 @@
         return carry
 
     lax.fori_loop(0, (live + GROUP - 1) // GROUP, group, 0)
-    add_up(live, tiles, 0, blocks_out, cost_ba, lambda k: None, top, total)
+    add_up(GROUP, live, tiles, 0, blocks_out, cost, lambda k: None, top, total)
     finish(out, top, total)
 
 
-def sweep_kernel(offset, far, scale, inner, outer, blocks_in, blocks_out, tiles_in, counts, cost, *refs):
-    parts = refs[:-7]
-    out, result, tiles, tsem, held, top, total = refs[-7:]
-    table = pltpu.make_async_copy(tiles_in, tiles, tsem)
-    table.start()
+def turn_kernel(counts, lefts, rights, cost):
+    live = counts[0, 0]
+
+    def group(q, carry):
+        for u in range(GROUP):
+            k = q * GROUP + u
+            cost[k] = product(lefts[k], rights[k])
+        return carry
+
+    lax.fori_loop(0, (live + GROUP - 1) // GROUP, group, 0)
+
+
+def sweep_kernel(offset, far, last, inner, outer, blocks_in, blocks_out, tiles, counts, cost, *refs):
+    parts = refs[:-6]
+    out, result, held, top, total, rsem = refs[-6:]
     if far is None:
         top[...] = jnp.full_like(top, offset)
     else:
         top[...] = far - parts[0][...]
         parts = parts[1:]
     potential = offset - lse2_many([part[...] for part in parts])
-    result[...] = potential * scale
-    held[...] = potential
+    held[0] = potential
+    if last:
+        held[1] = potential / SCALE
+        leave = pltpu.make_async_copy(held.at[1], result, rsem)
+        leave.start()
+    else:
+        result[...] = potential
     total[...] = jnp.zeros_like(total)
-    table.wait()
     live = counts[0, 0]
 
     def potential_of(k):
         return spread(held, block(tiles, inner, k, blocks_in))
 
-    least, most = add_up(live, tiles, outer, blocks_out, cost, potential_of, top, total)
+    least, most = add_up(WIDE, live, tiles, outer, blocks_out, cost, potential_of, top, total)
     finish(out, top, total)
     exact = (jnp.min(least) >= LEAST) & (jnp.max(most) <= MOST)
 
@@ -216,8 +229,11 @@
             return carry
 
         lax.fori_loop(0, live, step, 0)
-        add_up(live, tiles, outer, blocks_out, cost, potential_of, top, total)
+        add_up(2, live, tiles, outer, blocks_out, cost, potential_of, top, total)
         finish(out, top, total)
+
+    if last:
+        leave.wait()
 
 
 def vmem_spec():
@@ -235,14 +251,20 @@
 def costs(tiles, counts, src, tgt, blocks_in, blocks_out):
     slots = tiles.shape[1]
     width = src.shape[0]
-    shape = pltpu.VMEM((slots, TILE, TILE), jnp.float32)
+    part = pltpu.VMEM((slots, 2 * DEPTH, TILE), jnp.bfloat16)
     return pl.pallas_call(
         functools.partial(cost_kernel, blocks_in, blocks_out),
-        out_shape=(shape, shape, jax.ShapeDtypeStruct((2 * blocks_out, HALF), jnp.float32)),
+        out_shape=(
+            pltpu.VMEM((slots, TILE, TILE), jnp.float32),
+            jax.ShapeDtypeStruct((2 * blocks_out, HALF), jnp.float32),
+            part,
+            part,
+            pltpu.SMEM(tiles.shape, jnp.int32),
+        ),
         in_specs=[hbm_spec(), smem_spec(), hbm_spec(), hbm_spec()],
-        out_specs=(vmem_spec(), vmem_spec(), vmem_spec()),
+        out_specs=(vmem_spec(), vmem_spec(), vmem_spec(), vmem_spec(), smem_spec()),
         scratch_shapes=[
-            *table_scratch(slots),
+            pltpu.SemaphoreType.DMA(()),
             pltpu.VMEM((slots, width, TILE), jnp.float32),
             pltpu.VMEM((slots, width, TILE), jnp.float32),
             pltpu.VMEM((GROUP, 2, DEPTH, TILE), jnp.float32),
@@ -255,11 +277,25 @@
     )(tiles, counts, src, tgt)
 
 
-def sweep(tiles, counts, cost, before, parts, cells, far_cells, inner, outer, blocks_in, blocks_out, scale):
+def turned(counts, lefts, rights):
+    slots = lefts.shape[0]
+    return pl.pallas_call(
+        turn_kernel,
+        out_shape=pltpu.VMEM((slots, TILE, TILE), jnp.float32),
+        in_specs=[smem_spec(), vmem_spec(), vmem_spec()],
+        out_specs=vmem_spec(),
+        compiler_params=pltpu.CompilerParams(vmem_limit_bytes=VMEM_LIMIT),
+        cost_estimate=pl.CostEstimate(
+            flops=slots * 8 * DEPTH * TILE * TILE, bytes_accessed=slots * 8 * TILE * TILE, transcendentals=0
+        ),
+    )(counts, lefts, rights)
+
+
+def sweep(tiles, counts, cost, before, parts, cells, far_cells, inner, outer, blocks_in, blocks_out, last):
     far = None if before is None else math.log2(1.0 / far_cells)
     operands = list(parts) if before is None else [before, *parts]
     kernel = functools.partial(
-        sweep_kernel, math.log2(1.0 / cells), far, scale, inner, outer, blocks_in, blocks_out
+        sweep_kernel, math.log2(1.0 / cells), far, last, inner, outer, blocks_in, blocks_out
     )
     return pl.pallas_call(
         kernel,
@@ -267,13 +303,13 @@
             jax.ShapeDtypeStruct((2 * blocks_out, HALF), jnp.float32),
             jax.ShapeDtypeStruct((2 * blocks_in, HALF), jnp.float32),
         ),
-        in_specs=[hbm_spec(), smem_spec()] + [vmem_spec()] * (1 + len(operands)),
-        out_specs=(vmem_spec(), vmem_spec()),
+        in_specs=[smem_spec(), smem_spec()] + [vmem_spec()] * (1 + len(operands)),
+        out_specs=(vmem_spec(), hbm_spec() if last else vmem_spec()),
         scratch_shapes=[
-            *table_scratch(tiles.shape[1]),
-            pltpu.VMEM((2 * blocks_in, HALF), jnp.float32),
+            pltpu.VMEM((2, 2 * blocks_in, HALF), jnp.float32),
             pltpu.VMEM((2 * blocks_out, HALF), jnp.float32),
             pltpu.VMEM((2 * blocks_out, HALF), jnp.float32),
+            pltpu.SemaphoreType.DMA(()),
         ],
         compiler_params=pltpu.CompilerParams(vmem_limit_bytes=VMEM_LIMIT),
     )(tiles, counts, cost, *operands)
@@ -294,17 +330,20 @@
     return [value, lax.ppermute(value, axis, [(k, flip(k)) for k in range(size)])]
 
 
-def over_tgt(value):
+def over_core(value):
     size = lax.axis_size("tgt")
-    value = lse2_many(pair(value, "tgt", size, lambda k: k ^ 1))
+    return lse2_many(pair(value, "tgt", size, lambda k: k ^ 1))
+
+
+def over_y(value):
+    size = lax.axis_size("tgt")
     return fan(value, "tgt", size, 2, size // 2)
 
 
 def over_src(value):
     size = lax.axis_size("src")
     value = lse2_many(fan(value, "src", size, 1, 4))
-    value = lse2_many(pair(value, "src", size, lambda k: k ^ 4))
-    value = lse2_many(pair(value, "src", size, lambda k: k ^ 12))
+    value = lse2_many(fan(value, "src", size, 4, 4))
     return pair(value, "src", size, lambda k: k ^ 28)
 
 
@@ -317,13 +356,19 @@
     col_blocks = tgt_points.shape[1] // TILE
     src_cells = src_points.shape[1] * lax.axis_size("src")
     tgt_cells = tgt_points.shape[1] * lax.axis_size("tgt")
-    cost_ab, cost_ba, rows = costs(tiles, counts, src_points, tgt_points, col_blocks, row_blocks)
+    cost_ba, rows, lefts, rights, tiles = costs(
+        tiles, counts, src_points, tgt_points, col_blocks, row_blocks
+    )
     target = None
     for turn in range(ITERS):
         last = turn == ITERS - 1
+        rows = over_core(rows)
+        if turn == 0:
+            rows, lefts = lax.optimization_barrier((rows, lefts))
+            cost_ab = turned(counts, lefts, rights)
         cols, source = sweep(
-            tiles, counts, cost_ab, target, over_tgt(rows), src_cells, tgt_cells, 0, 1,
-            row_blocks, col_blocks, 1.0 / SCALE if last else 1.0,
+            tiles, counts, cost_ab, target, over_y(rows), src_cells, tgt_cells, 0, 1,
+            row_blocks, col_blocks, last,
         )
         parts = over_src(cols)
         if last:
@@ -331,7 +376,7 @@
         else:
             rows, target = sweep(
                 tiles, counts, cost_ba, source, parts, tgt_cells, src_cells, 1, 0,
-                col_blocks, row_blocks, 1.0,
+                col_blocks, row_blocks, False,
             )
     return (source.reshape(-1), target.reshape(-1))
 

time: 155 us -> 154 us (level)
  the two profiles are of different devices: /device:TPU:8 before, /device:TPU:2 now
where the time goes in v4:
time: 154 us; the launch traced here: 151 us
  starting transfers between devices  66.9 us (43%)
  waiting for transfers between devices  65.7 us (43%)
  Pallas kernels  15.6 us (10%)
    ppermute x27, starting transfers between devices, fan(): got.append(lax.ppermute(value, axis, pairs))  58.8 us
    ppermute x27, waiting for transfers between devices, fan(): got.append(lax.ppermute(value, axis, pairs))  49.3 us
    ppermute x6, waiting for transfers between devices, pair(): lax.ppermute(value, axis, [(k, flip(k)) for k in range(size)])  16.4 us
    pallas_call x5, Pallas kernels, sweep(): pl.pallas_call(kernel, out_shape=(jax.ShapeDtypeStruct((2 * blocks_out, H...  9.96 us
    ppermute x6, starting transfers between devices, pair(): lax.ppermute(value, axis, [(k, flip(k)) for k in range(size)])  8.09 us
    pallas_call x1, Pallas kernels, costs(): pl.pallas_call(functools.partial(cost_kernel, blocks_in, blocks_out), out...  4.68 us
  transfers between devices with their start and end apart: 33, of which 24 were waited for; matrix products, arithmetic and copies ran while one was open for 0% of the time, Pallas kernels for 1%

profile of v4, /device:TPU:2, one launch (start us, length us, event | category | flops | bytes accessed | tf_op | source)
XLA Modules:
  0.0 151.0 jit_solution(11397601584179524654)
XLA Ops:
  1.3 4.7 %shard_map.59 = (f32[32,256,256]{2,1,0:T(8,128)S(1)}, f32[128,128]{1,0:T(8,128)S(1)}, bf16[32,128,256]{2,1,0:T(8,128)(2,1)S(1)}, bf16[32,128,256]{2,1,0:T(8,128)(2,1)S(1)}, s32[2,32]{1,0:T(2,128)S(4)}) custom-call(s32[2,32]{1,0:T(2,128)} %bitcast.4, s32[1,1]{1,0:T(1,128)S(6)} %copy.6.counts, f32[50,16384]{1,0:T(8,128)} %src.1, f32[50,24576]{1,0:T(8,128)} %tgt.1), custom_call_target="tpu_custom_call" | custom-call | tf_op jit(solution)/shard_map/pallas_call | solution.py:255
  7.9 5.2 %collective-permute-start.2 = (f32[128,128]{1,0:T(8,128)S(1)}, f32[128,128]{1,0:T(8,128)S(1)}, u32[]{:S(2)}, u32[]{:S(2)}) collective-permute-start(f32[128,128]{1,0:T(8,128)S(1)} %multiply_add_fusion.8.refs_0_), channel_id=1, source_target_pairs={{0,4},{1,5},{2,6},{3,7},{4,0},{5,1},{6,2},{7,3},{8,12},{9,13},{10,... | collective-permute-start | bytes 196616 | tf_op jit(solution)/shard_map/ppermute | solution.py:325
  14.0 2.6 %collective-permute-done.2.refs_2_ = f32[128,128]{1,0:T(8,128)S(1)} collective-permute-done((f32[128,128]{1,0:T(8,128)S(1)}, f32[128,128]{1,0:T(8,128)S(1)}, u32[]{:S(2)}, u32[]{:S(2)}) %collective-permute-start.2) | collective-permute-done | bytes 65568 | tf_op jit(solution)/shard_map/ppermute | solution.py:325
  16.6 1.9 %collective-permute-done.3.refs_3_ = f32[128,128]{1,0:T(8,128)S(1)} collective-permute-done((f32[128,128]{1,0:T(8,128)S(1)}, f32[128,128]{1,0:T(8,128)S(1)}, u32[]{:S(2)}, u32[]{:S(2)}) %collective-permute-start.3) | collective-permute-done | bytes 65568 | tf_op jit(solution)/shard_map/ppermute | solution.py:325
  18.6 2.7 %shard_map.61 = (f32[192,128]{1,0:T(8,128)S(1)}, f32[128,128]{1,0:T(8,128)S(1)}) custom-call(s32[2,32]{1,0:T(2,128)S(4)} %get-tuple-element.19.tiles, s32[1,1]{1,0:T(1,128)S(6)} %copy.6.counts, f32[32,256,256]{2,1,0:T(8,128)S(1)} %shard_map.60.cost, f32[128,128]{1,0:T(8,128)S(1)} %multiply_add_fusion.8.refs_0_, ...), custom_call_target="tpu_custom_call" | custom-call | tf_op jit(solution)/shard_map/pallas_call | solution.py:300
  21.4 5.6 %collective-permute-start.5 = (f32[192,128]{1,0:T(8,128)S(1)}, f32[192,128]{1,0:T(8,128)S(1)}, u32[]{:S(2)}, u32[]{:S(2)}) collective-permute-start(f32[192,128]{1,0:T(8,128)S(1)} %get-tuple-element.27), channel_id=1, source_target_pairs={{0,16},{8,24},{16,0},{24,8},{32,48},{40,56},{48,32},{56,40},{64,80... | collective-permute-start | bytes 294920 | tf_op jit(solution)/shard_map/ppermute | solution.py:325
  27.5 3.1 %collective-permute-done.5 = f32[192,128]{1,0:T(8,128)S(1)} collective-permute-done((f32[192,128]{1,0:T(8,128)S(1)}, f32[192,128]{1,0:T(8,128)S(1)}, u32[]{:S(2)}, u32[]{:S(2)}) %collective-permute-start.5) | collective-permute-done | bytes 98336 | tf_op jit(solution)/shard_map/ppermute | solution.py:325
  31.8 2.6 %collective-permute-start.7 = (f32[192,128]{1,0:T(8,128)S(1)}, f32[192,128]{1,0:T(8,128)S(1)}, u32[]{:S(2)}, u32[]{:S(2)}) collective-permute-start(f32[192,128]{1,0:T(8,128)S(1)} %multiply_add_fusion.5), channel_id=1, source_target_pairs={{0,32},{8,40},{16,48},{24,56},{32,0},{40,8},{48,16},{56,24},{64,96... | collective-permute-start | bytes 294920 | tf_op jit(solution)/shard_map/ppermute | solution.py:325
  34.4 3.5 %collective-permute-start.8 = (f32[192,128]{1,0:T(8,128)S(1)}, f32[192,128]{1,0:T(8,128)S(1)}, u32[]{:S(2)}, u32[]{:S(2)}) collective-permute-start(f32[192,128]{1,0:T(8,128)S(1)} %multiply_add_fusion.5), channel_id=1, source_target_pairs={{0,64},{8,72},{16,80},{24,88},{32,96},{40,104},{48,112},{56,120},{... | collective-permute-start | bytes 294920 | tf_op jit(solution)/shard_map/ppermute | solution.py:325
  37.9 4.6 %collective-permute-done.8 = f32[192,128]{1,0:T(8,128)S(1)} collective-permute-done((f32[192,128]{1,0:T(8,128)S(1)}, f32[192,128]{1,0:T(8,128)S(1)}, u32[]{:S(2)}, u32[]{:S(2)}) %collective-permute-start.8) | collective-permute-done | bytes 98336 | tf_op jit(solution)/shard_map/ppermute | solution.py:325
  42.5 1.9 %collective-permute-done.9 = f32[192,128]{1,0:T(8,128)S(1)} collective-permute-done((f32[192,128]{1,0:T(8,128)S(1)}, f32[192,128]{1,0:T(8,128)S(1)}, u32[]{:S(2)}, u32[]{:S(2)}) %collective-permute-start.9) | collective-permute-done | bytes 98336 | tf_op jit(solution)/shard_map/ppermute | solution.py:325
  44.5 4.4 %collective-permute-start.10 = (f32[192,128]{1,0:T(8,128)S(1)}, f32[192,128]{1,0:T(8,128)S(1)}, u32[]{:S(2)}, u32[]{:S(2)}) collective-permute-start(f32[192,128]{1,0:T(8,128)S(1)} %multiply_add_fusion.4.refs_1_), channel_id=1, source_target_pairs={{0,224},{8,232},{16,240},{24,248},{32,192},{40,200},{48,208},{56,2... | collective-permute-start | bytes 294920 | tf_op jit(solution)/shard_map/ppermute | solution.py:330
  48.9 2.9 %collective-permute-done.10.refs_2_ = f32[192,128]{1,0:T(8,128)S(1)} collective-permute-done((f32[192,128]{1,0:T(8,128)S(1)}, f32[192,128]{1,0:T(8,128)S(1)}, u32[]{:S(2)}, u32[]{:S(2)}) %collective-permute-start.10) | collective-permute-done | bytes 98336 | tf_op jit(solution)/shard_map/ppermute | solution.py:330
  54.0 4.3 %collective-permute-start.12 = (f32[128,128]{1,0:T(8,128)S(1)}, f32[128,128]{1,0:T(8,128)S(1)}, u32[]{:S(2)}, u32[]{:S(2)}) collective-permute-start(f32[128,128]{1,0:T(8,128)S(1)} %multiply_add_fusion.7.refs_1_), channel_id=1, source_target_pairs={{0,2},{1,3},{2,0},{3,1},{4,6},{5,7},{6,4},{7,5},{8,10},{9,11},{10,... | collective-permute-start | bytes 196616 | tf_op jit(solution)/shard_map/ppermute | solution.py:325
  61.1 3.0 %collective-permute-done.13.refs_3_ = f32[128,128]{1,0:T(8,128)S(1)} collective-permute-done((f32[128,128]{1,0:T(8,128)S(1)}, f32[128,128]{1,0:T(8,128)S(1)}, u32[]{:S(2)}, u32[]{:S(2)}) %collective-permute-start.13) | collective-permute-done | bytes 65568 | tf_op jit(solution)/shard_map/ppermute | solution.py:325
  65.5 2.7 %shard_map.63 = (f32[192,128]{1,0:T(8,128)S(1)}, f32[128,128]{1,0:T(8,128)S(1)}) custom-call(s32[2,32]{1,0:T(2,128)S(4)} %get-tuple-element.19.tiles, s32[1,1]{1,0:T(1,128)S(6)} %copy.6.counts, f32[32,256,256]{2,1,0:T(8,128)S(1)} %shard_map.60.cost, f32[192,128]{1,0:T(8,128)S(1)} %get-tuple-element.28.refs_0_, f32[128,128]{1,0:T(8,128)S(1)} %multiply_add_fusion.7.refs_1_, ...), custom_call_target="tpu_custom_call" | custom-call | tf_op jit(solution)/shard_map/pallas_call | solution.py:300
  68.3 4.1 %collective-permute-start.15 = (f32[192,128]{1,0:T(8,128)S(1)}, f32[192,128]{1,0:T(8,128)S(1)}, u32[]{:S(2)}, u32[]{:S(2)}) collective-permute-start(f32[192,128]{1,0:T(8,128)S(1)} %get-tuple-element.31), channel_id=1, source_target_pairs={{0,8},{8,0},{16,24},{24,16},{32,40},{40,32},{48,56},{56,48},{64,72... | collective-permute-start | bytes 294920 | tf_op jit(solution)/shard_map/ppermute | solution.py:325
  75.1 3.4 %collective-permute-done.16 = f32[192,128]{1,0:T(8,128)S(1)} collective-permute-done((f32[192,128]{1,0:T(8,128)S(1)}, f32[192,128]{1,0:T(8,128)S(1)}, u32[]{:S(2)}, u32[]{:S(2)}) %collective-permute-start.16) | collective-permute-done | bytes 98336 | tf_op jit(solution)/shard_map/ppermute | solution.py:325
  79.6 3.7 %collective-permute-start.18 = (f32[192,128]{1,0:T(8,128)S(1)}, f32[192,128]{1,0:T(8,128)S(1)}, u32[]{:S(2)}, u32[]{:S(2)}) collective-permute-start(f32[192,128]{1,0:T(8,128)S(1)} %multiply_add_fusion.3), channel_id=1, source_target_pairs={{0,32},{8,40},{16,48},{24,56},{32,0},{40,8},{48,16},{56,24},{64,96... | collective-permute-start | bytes 294920 | tf_op jit(solution)/shard_map/ppermute | solution.py:325
  86.0 7.7 %collective-permute-done.19 = f32[192,128]{1,0:T(8,128)S(1)} collective-permute-done((f32[192,128]{1,0:T(8,128)S(1)}, f32[192,128]{1,0:T(8,128)S(1)}, u32[]{:S(2)}, u32[]{:S(2)}) %collective-permute-start.19) | collective-permute-done | bytes 98336 | tf_op jit(solution)/shard_map/ppermute | solution.py:325
  93.8 2.4 %collective-permute-start.21 = (f32[192,128]{1,0:T(8,128)S(1)}, f32[192,128]{1,0:T(8,128)S(1)}, u32[]{:S(2)}, u32[]{:S(2)}) collective-permute-start(f32[192,128]{1,0:T(8,128)S(1)} %multiply_add_fusion.2.refs_1_), channel_id=1, source_target_pairs={{0,224},{8,232},{16,240},{24,248},{32,192},{40,200},{48,208},{56,2... | collective-permute-start | bytes 294920 | tf_op jit(solution)/shard_map/ppermute | solution.py:330
  96.2 4.3 %collective-permute-done.21.refs_2_ = f32[192,128]{1,0:T(8,128)S(1)} collective-permute-done((f32[192,128]{1,0:T(8,128)S(1)}, f32[192,128]{1,0:T(8,128)S(1)}, u32[]{:S(2)}, u32[]{:S(2)}) %collective-permute-start.21) | collective-permute-done | bytes 98336 | tf_op jit(solution)/shard_map/ppermute | solution.py:330
  102.8 2.2 %collective-permute-start.23 = (f32[128,128]{1,0:T(8,128)S(1)}, f32[128,128]{1,0:T(8,128)S(1)}, u32[]{:S(2)}, u32[]{:S(2)}) collective-permute-start(f32[128,128]{1,0:T(8,128)S(1)} %multiply_add_fusion.6.refs_1_), channel_id=1, source_target_pairs={{0,2},{1,3},{2,0},{3,1},{4,6},{5,7},{6,4},{7,5},{8,10},{9,11},{10,... | collective-permute-start | bytes 196616 | tf_op jit(solution)/shard_map/ppermute | solution.py:325
  105.0 3.0 %collective-permute-start.24 = (f32[128,128]{1,0:T(8,128)S(1)}, f32[128,128]{1,0:T(8,128)S(1)}, u32[]{:S(2)}, u32[]{:S(2)}) collective-permute-start(f32[128,128]{1,0:T(8,128)S(1)} %multiply_add_fusion.6.refs_1_), channel_id=1, source_target_pairs={{0,4},{1,5},{2,6},{3,7},{4,0},{5,1},{6,2},{7,3},{8,12},{9,13},{10,... | collective-permute-start | bytes 196616 | tf_op jit(solution)/shard_map/ppermute | solution.py:325
  108.4 3.2 %collective-permute-done.24.refs_3_ = f32[128,128]{1,0:T(8,128)S(1)} collective-permute-done((f32[128,128]{1,0:T(8,128)S(1)}, f32[128,128]{1,0:T(8,128)S(1)}, u32[]{:S(2)}, u32[]{:S(2)}) %collective-permute-start.24) | collective-permute-done | bytes 65568 | tf_op jit(solution)/shard_map/ppermute | solution.py:325
  113.4 2.7 %shard_map.65 = (f32[192,128]{1,0:T(8,128)S(1)}, f32[128,128]{1,0:T(8,128)}) custom-call(s32[2,32]{1,0:T(2,128)S(4)} %get-tuple-element.19.tiles, s32[1,1]{1,0:T(1,128)S(6)} %copy.6.counts, f32[32,256,256]{2,1,0:T(8,128)S(1)} %shard_map.60.cost, f32[192,128]{1,0:T(8,128)S(1)} %get-tuple-element.32.refs_0_, f32[128,128]{1,0:T(8,128)S(1)} %multiply_add_fusion.6.refs_1_, ...), custom_call_target="tpu_custom_call" | custom-call | tf_op jit(solution)/shard_map/pallas_call | solution.py:300
  116.2 2.7 %collective-permute-start.26 = (f32[192,128]{1,0:T(8,128)S(1)}, f32[192,128]{1,0:T(8,128)S(1)}, u32[]{:S(2)}, u32[]{:S(2)}) collective-permute-start(f32[192,128]{1,0:T(8,128)S(1)} %get-tuple-element.35), channel_id=1, source_target_pairs={{0,8},{8,0},{16,24},{24,16},{32,40},{40,32},{48,56},{56,48},{64,72... | collective-permute-start | bytes 294920 | tf_op jit(solution)/shard_map/ppermute | solution.py:325
  118.9 5.3 %collective-permute-start.27 = (f32[192,128]{1,0:T(8,128)S(1)}, f32[192,128]{1,0:T(8,128)S(1)}, u32[]{:S(2)}, u32[]{:S(2)}) collective-permute-start(f32[192,128]{1,0:T(8,128)S(1)} %get-tuple-element.35), channel_id=1, source_target_pairs={{0,16},{8,24},{16,0},{24,8},{32,48},{40,56},{48,32},{56,40},{64,80... | collective-permute-start | bytes 294920 | tf_op jit(solution)/shard_map/ppermute | solution.py:325
  124.7 3.1 %collective-permute-done.27 = f32[192,128]{1,0:T(8,128)S(1)} collective-permute-done((f32[192,128]{1,0:T(8,128)S(1)}, f32[192,128]{1,0:T(8,128)S(1)}, u32[]{:S(2)}, u32[]{:S(2)}) %collective-permute-start.27) | collective-permute-done | bytes 98336 | tf_op jit(solution)/shard_map/ppermute | solution.py:325
  128.9 4.3 %collective-permute-start.29 = (f32[192,128]{1,0:T(8,128)S(1)}, f32[192,128]{1,0:T(8,128)S(1)}, u32[]{:S(2)}, u32[]{:S(2)}) collective-permute-start(f32[192,128]{1,0:T(8,128)S(1)} %multiply_add_fusion.1), channel_id=1, source_target_pairs={{0,32},{8,40},{16,48},{24,56},{32,0},{40,8},{48,16},{56,24},{64,96... | collective-permute-start | bytes 294920 | tf_op jit(solution)/shard_map/ppermute | solution.py:325
  135.9 7.8 %collective-permute-done.30 = f32[192,128]{1,0:T(8,128)S(1)} collective-permute-done((f32[192,128]{1,0:T(8,128)S(1)}, f32[192,128]{1,0:T(8,128)S(1)}, u32[]{:S(2)}, u32[]{:S(2)}) %collective-permute-start.30) | collective-permute-done | bytes 98336 | tf_op jit(solution)/shard_map/ppermute | solution.py:325
  144.8 5.5 %collective-permute-done.32 = f32[192,128]{1,0:T(8,128)S(1)} collective-permute-done((f32[192,128]{1,0:T(8,128)S(1)}, f32[192,128]{1,0:T(8,128)S(1)}, u32[]{:S(2)}, u32[]{:S(2)}) %collective-permute-start.32) | collective-permute-done | bytes 98336 | tf_op jit(solution)/shard_map/ppermute | solution.py:330
  (51 shorter events, 28.2 us)
Async XLA Ops:
  6.0 1.3 collective-permute-start
  7.4 6.7 %collective-permute-start.1 = (f32[128,128]{1,0:T(8,128)S(1)}, f32[128,128]{1,0:T(8,128)S(1)}, u32[]{:S(2)}, u32[]{:S(2)}) collective-permute-start(f32[128,128]{1,0:T(8,128)S(1)} %multiply_add_fusion.8.refs_0_), channel_id=1, source_target_pairs={{0,2},{1,3},{2,0},{3,1},{4,6},{5,7},{6,4},{7,5},{8,10},{9,11},{10,... | collective-permute-start | bytes 196616 | tf_op jit(solution)/shard_map/ppermute | solution.py:325
  7.9 8.7 %collective-permute-start.2 = (f32[128,128]{1,0:T(8,128)S(1)}, f32[128,128]{1,0:T(8,128)S(1)}, u32[]{:S(2)}, u32[]{:S(2)}) collective-permute-start(f32[128,128]{1,0:T(8,128)S(1)} %multiply_add_fusion.8.refs_0_), channel_id=1, source_target_pairs={{0,4},{1,5},{2,6},{3,7},{4,0},{5,1},{6,2},{7,3},{8,12},{9,13},{10,... | collective-permute-start | bytes 196616 | tf_op jit(solution)/shard_map/ppermute | solution.py:325
  13.1 5.5 %collective-permute-start.3 = (f32[128,128]{1,0:T(8,128)S(1)}, f32[128,128]{1,0:T(8,128)S(1)}, u32[]{:S(2)}, u32[]{:S(2)}) collective-permute-start(f32[128,128]{1,0:T(8,128)S(1)} %multiply_add_fusion.8.refs_0_), channel_id=1, source_target_pairs={{0,6},{1,7},{2,4},{3,5},{4,2},{5,3},{6,0},{7,1},{8,14},{9,15},{10,... | collective-permute-start | bytes 196616 | tf_op jit(solution)/shard_map/ppermute | solution.py:325
  21.3 6.2 %collective-permute-start.4 = (f32[192,128]{1,0:T(8,128)S(1)}, f32[192,128]{1,0:T(8,128)S(1)}, u32[]{:S(2)}, u32[]{:S(2)}) collective-permute-start(f32[192,128]{1,0:T(8,128)S(1)} %get-tuple-element.27), channel_id=1, source_target_pairs={{0,8},{8,0},{16,24},{24,16},{32,40},{40,32},{48,56},{56,48},{64,72... | collective-permute-start | bytes 294920 | tf_op jit(solution)/shard_map/ppermute | solution.py:325
  21.4 9.2 %collective-permute-start.5 = (f32[192,128]{1,0:T(8,128)S(1)}, f32[192,128]{1,0:T(8,128)S(1)}, u32[]{:S(2)}, u32[]{:S(2)}) collective-permute-start(f32[192,128]{1,0:T(8,128)S(1)} %get-tuple-element.27), channel_id=1, source_target_pairs={{0,16},{8,24},{16,0},{24,8},{32,48},{40,56},{48,32},{56,40},{64,80... | collective-permute-start | bytes 294920 | tf_op jit(solution)/shard_map/ppermute | solution.py:325
  27.0 4.6 %collective-permute-start.6 = (f32[192,128]{1,0:T(8,128)S(1)}, f32[192,128]{1,0:T(8,128)S(1)}, u32[]{:S(2)}, u32[]{:S(2)}) collective-permute-start(f32[192,128]{1,0:T(8,128)S(1)} %get-tuple-element.27), channel_id=1, source_target_pairs={{0,24},{8,16},{16,8},{24,0},{32,56},{40,48},{48,40},{56,32},{64,88... | collective-permute-start | bytes 294920 | tf_op jit(solution)/shard_map/ppermute | solution.py:325
  31.8 6.1 %collective-permute-start.7 = (f32[192,128]{1,0:T(8,128)S(1)}, f32[192,128]{1,0:T(8,128)S(1)}, u32[]{:S(2)}, u32[]{:S(2)}) collective-permute-start(f32[192,128]{1,0:T(8,128)S(1)} %multiply_add_fusion.5), channel_id=1, source_target_pairs={{0,32},{8,40},{16,48},{24,56},{32,0},{40,8},{48,16},{56,24},{64,96... | collective-permute-start | bytes 294920 | tf_op jit(solution)/shard_map/ppermute | solution.py:325
  34.4 8.1 %collective-permute-start.8 = (f32[192,128]{1,0:T(8,128)S(1)}, f32[192,128]{1,0:T(8,128)S(1)}, u32[]{:S(2)}, u32[]{:S(2)}) collective-permute-start(f32[192,128]{1,0:T(8,128)S(1)} %multiply_add_fusion.5), channel_id=1, source_target_pairs={{0,64},{8,72},{16,80},{24,88},{32,96},{40,104},{48,112},{56,120},{... | collective-permute-start | bytes 294920 | tf_op jit(solution)/shard_map/ppermute | solution.py:325
  37.8 6.5 %collective-permute-start.9 = (f32[192,128]{1,0:T(8,128)S(1)}, f32[192,128]{1,0:T(8,128)S(1)}, u32[]{:S(2)}, u32[]{:S(2)}) collective-permute-start(f32[192,128]{1,0:T(8,128)S(1)} %multiply_add_fusion.5), channel_id=1, source_target_pairs={{0,96},{8,104},{16,112},{24,120},{32,64},{40,72},{48,80},{56,88},{... | collective-permute-start | bytes 294920 | tf_op jit(solution)/shard_map/ppermute | solution.py:325
  44.5 7.3 %collective-permute-start.10 = (f32[192,128]{1,0:T(8,128)S(1)}, f32[192,128]{1,0:T(8,128)S(1)}, u32[]{:S(2)}, u32[]{:S(2)}) collective-permute-start(f32[192,128]{1,0:T(8,128)S(1)} %multiply_add_fusion.4.refs_1_), channel_id=1, source_target_pairs={{0,224},{8,232},{16,240},{24,248},{32,192},{40,200},{48,208},{56,2... | collective-permute-start | bytes 294920 | tf_op jit(solution)/shard_map/ppermute | solution.py:330
  52.6 1.3 collective-permute-start.11
  54.0 7.1 %collective-permute-start.12 = (f32[128,128]{1,0:T(8,128)S(1)}, f32[128,128]{1,0:T(8,128)S(1)}, u32[]{:S(2)}, u32[]{:S(2)}) collective-permute-start(f32[128,128]{1,0:T(8,128)S(1)} %multiply_add_fusion.7.refs_1_), channel_id=1, source_target_pairs={{0,2},{1,3},{2,0},{3,1},{4,6},{5,7},{6,4},{7,5},{8,10},{9,11},{10,... | collective-permute-start | bytes 196616 | tf_op jit(solution)/shard_map/ppermute | solution.py:325
  58.4 5.8 %collective-permute-start.13 = (f32[128,128]{1,0:T(8,128)S(1)}, f32[128,128]{1,0:T(8,128)S(1)}, u32[]{:S(2)}, u32[]{:S(2)}) collective-permute-start(f32[128,128]{1,0:T(8,128)S(1)} %multiply_add_fusion.7.refs_1_), channel_id=1, source_target_pairs={{0,4},{1,5},{2,6},{3,7},{4,0},{5,1},{6,2},{7,3},{8,12},{9,13},{10,... | collective-permute-start | bytes 196616 | tf_op jit(solution)/shard_map/ppermute | solution.py:325
  59.9 5.7 %collective-permute-start.14 = (f32[128,128]{1,0:T(8,128)S(1)}, f32[128,128]{1,0:T(8,128)S(1)}, u32[]{:S(2)}, u32[]{:S(2)}) collective-permute-start(f32[128,128]{1,0:T(8,128)S(1)} %multiply_add_fusion.7.refs_1_), channel_id=1, source_target_pairs={{0,6},{1,7},{2,4},{3,5},{4,2},{5,3},{6,0},{7,1},{8,14},{9,15},{10,... | collective-permute-start | bytes 196616 | tf_op jit(solution)/shard_map/ppermute | solution.py:325
  68.3 6.8 %collective-permute-start.15 = (f32[192,128]{1,0:T(8,128)S(1)}, f32[192,128]{1,0:T(8,128)S(1)}, u32[]{:S(2)}, u32[]{:S(2)}) collective-permute-start(f32[192,128]{1,0:T(8,128)S(1)} %get-tuple-element.31), channel_id=1, source_target_pairs={{0,8},{8,0},{16,24},{24,16},{32,40},{40,32},{48,56},{56,48},{64,72... | collective-permute-start | bytes 294920 | tf_op jit(solution)/shard_map/ppermute | solution.py:325
  72.4 6.2 %collective-permute-start.16 = (f32[192,128]{1,0:T(8,128)S(1)}, f32[192,128]{1,0:T(8,128)S(1)}, u32[]{:S(2)}, u32[]{:S(2)}) collective-permute-start(f32[192,128]{1,0:T(8,128)S(1)} %get-tuple-element.31), channel_id=1, source_target_pairs={{0,16},{8,24},{16,0},{24,8},{32,48},{40,56},{48,32},{56,40},{64,80... | collective-permute-start | bytes 294920 | tf_op jit(solution)/shard_map/ppermute | solution.py:325
  74.2 5.3 %collective-permute-start.17 = (f32[192,128]{1,0:T(8,128)S(1)}, f32[192,128]{1,0:T(8,128)S(1)}, u32[]{:S(2)}, u32[]{:S(2)}) collective-permute-start(f32[192,128]{1,0:T(8,128)S(1)} %get-tuple-element.31), channel_id=1, source_target_pairs={{0,24},{8,16},{16,8},{24,0},{32,56},{40,48},{48,40},{56,32},{64,88... | collective-permute-start | bytes 294920 | tf_op jit(solution)/shard_map/ppermute | solution.py:325
  79.6 6.3 %collective-permute-start.18 = (f32[192,128]{1,0:T(8,128)S(1)}, f32[192,128]{1,0:T(8,128)S(1)}, u32[]{:S(2)}, u32[]{:S(2)}) collective-permute-start(f32[192,128]{1,0:T(8,128)S(1)} %multiply_add_fusion.3), channel_id=1, source_target_pairs={{0,32},{8,40},{16,48},{24,56},{32,0},{40,8},{48,16},{56,24},{64,96... | collective-permute-start | bytes 294920 | tf_op jit(solution)/shard_map/ppermute | solution.py:325
  83.4 10.3 %collective-permute-start.19 = (f32[192,128]{1,0:T(8,128)S(1)}, f32[192,128]{1,0:T(8,128)S(1)}, u32[]{:S(2)}, u32[]{:S(2)}) collective-permute-start(f32[192,128]{1,0:T(8,128)S(1)} %multiply_add_fusion.3), channel_id=1, source_target_pairs={{0,64},{8,72},{16,80},{24,88},{32,96},{40,104},{48,112},{56,120},{... | collective-permute-start | bytes 294920 | tf_op jit(solution)/shard_map/ppermute | solution.py:325
  85.0 8.7 %collective-permute-start.20 = (f32[192,128]{1,0:T(8,128)S(1)}, f32[192,128]{1,0:T(8,128)S(1)}, u32[]{:S(2)}, u32[]{:S(2)}) collective-permute-start(f32[192,128]{1,0:T(8,128)S(1)} %multiply_add_fusion.3), channel_id=1, source_target_pairs={{0,96},{8,104},{16,112},{24,120},{32,64},{40,72},{48,80},{56,88},{... | collective-permute-start | bytes 294920 | tf_op jit(solution)/shard_map/ppermute | solution.py:325
  93.8 6.7 %collective-permute-start.21 = (f32[192,128]{1,0:T(8,128)S(1)}, f32[192,128]{1,0:T(8,128)S(1)}, u32[]{:S(2)}, u32[]{:S(2)}) collective-permute-start(f32[192,128]{1,0:T(8,128)S(1)} %multiply_add_fusion.2.refs_1_), channel_id=1, source_target_pairs={{0,224},{8,232},{16,240},{24,248},{32,192},{40,200},{48,208},{56,2... | collective-permute-start | bytes 294920 | tf_op jit(solution)/shard_map/ppermute | solution.py:330
  102.8 5.6 %collective-permute-start.23 = (f32[128,128]{1,0:T(8,128)S(1)}, f32[128,128]{1,0:T(8,128)S(1)}, u32[]{:S(2)}, u32[]{:S(2)}) collective-permute-start(f32[128,128]{1,0:T(8,128)S(1)} %multiply_add_fusion.6.refs_1_), channel_id=1, source_target_pairs={{0,2},{1,3},{2,0},{3,1},{4,6},{5,7},{6,4},{7,5},{8,10},{9,11},{10,... | collective-permute-start | bytes 196616 | tf_op jit(solution)/shard_map/ppermute | solution.py:325
  105.0 6.7 %collective-permute-start.24 = (f32[128,128]{1,0:T(8,128)S(1)}, f32[128,128]{1,0:T(8,128)S(1)}, u32[]{:S(2)}, u32[]{:S(2)}) collective-permute-start(f32[128,128]{1,0:T(8,128)S(1)} %multiply_add_fusion.6.refs_1_), channel_id=1, source_target_pairs={{0,4},{1,5},{2,6},{3,7},{4,0},{5,1},{6,2},{7,3},{8,12},{9,13},{10,... | collective-permute-start | bytes 196616 | tf_op jit(solution)/shard_map/ppermute | solution.py:325
  108.0 5.5 %collective-permute-start.25 = (f32[128,128]{1,0:T(8,128)S(1)}, f32[128,128]{1,0:T(8,128)S(1)}, u32[]{:S(2)}, u32[]{:S(2)}) collective-permute-start(f32[128,128]{1,0:T(8,128)S(1)} %multiply_add_fusion.6.refs_1_), channel_id=1, source_target_pairs={{0,6},{1,7},{2,4},{3,5},{4,2},{5,3},{6,0},{7,1},{8,14},{9,15},{10,... | collective-permute-start | bytes 196616 | tf_op jit(solution)/shard_map/ppermute | solution.py:325
  116.2 8.5 %collective-permute-start.26 = (f32[192,128]{1,0:T(8,128)S(1)}, f32[192,128]{1,0:T(8,128)S(1)}, u32[]{:S(2)}, u32[]{:S(2)}) collective-permute-start(f32[192,128]{1,0:T(8,128)S(1)} %get-tuple-element.35), channel_id=1, source_target_pairs={{0,8},{8,0},{16,24},{24,16},{32,40},{40,32},{48,56},{56,48},{64,72... | collective-permute-start | bytes 294920 | tf_op jit(solution)/shard_map/ppermute | solution.py:325
  118.9 8.9 %collective-permute-start.27 = (f32[192,128]{1,0:T(8,128)S(1)}, f32[192,128]{1,0:T(8,128)S(1)}, u32[]{:S(2)}, u32[]{:S(2)}) collective-permute-start(f32[192,128]{1,0:T(8,128)S(1)} %get-tuple-element.35), channel_id=1, source_target_pairs={{0,16},{8,24},{16,0},{24,8},{32,48},{40,56},{48,32},{56,40},{64,80... | collective-permute-start | bytes 294920 | tf_op jit(solution)/shard_map/ppermute | solution.py:325
  124.2 4.6 %collective-permute-start.28 = (f32[192,128]{1,0:T(8,128)S(1)}, f32[192,128]{1,0:T(8,128)S(1)}, u32[]{:S(2)}, u32[]{:S(2)}) collective-permute-start(f32[192,128]{1,0:T(8,128)S(1)} %get-tuple-element.35), channel_id=1, source_target_pairs={{0,24},{8,16},{16,8},{24,0},{32,56},{40,48},{48,40},{56,32},{64,88... | collective-permute-start | bytes 294920 | tf_op jit(solution)/shard_map/ppermute | solution.py:325
  128.9 6.9 %collective-permute-start.29 = (f32[192,128]{1,0:T(8,128)S(1)}, f32[192,128]{1,0:T(8,128)S(1)}, u32[]{:S(2)}, u32[]{:S(2)}) collective-permute-start(f32[192,128]{1,0:T(8,128)S(1)} %multiply_add_fusion.1), channel_id=1, source_target_pairs={{0,32},{8,40},{16,48},{24,56},{32,0},{40,8},{48,16},{56,24},{64,96... | collective-permute-start | bytes 294920 | tf_op jit(solution)/shard_map/ppermute | solution.py:325
  133.3 10.4 %collective-permute-start.30 = (f32[192,128]{1,0:T(8,128)S(1)}, f32[192,128]{1,0:T(8,128)S(1)}, u32[]{:S(2)}, u32[]{:S(2)}) collective-permute-start(f32[192,128]{1,0:T(8,128)S(1)} %multiply_add_fusion.1), channel_id=1, source_target_pairs={{0,64},{8,72},{16,80},{24,88},{32,96},{40,104},{48,112},{56,120},{... | collective-permute-start | bytes 294920 | tf_op jit(solution)/shard_map/ppermute | solution.py:325
  134.1 9.6 %collective-permute-start.31 = (f32[192,128]{1,0:T(8,128)S(1)}, f32[192,128]{1,0:T(8,128)S(1)}, u32[]{:S(2)}, u32[]{:S(2)}) collective-permute-start(f32[192,128]{1,0:T(8,128)S(1)} %multiply_add_fusion.1), channel_id=1, source_target_pairs={{0,96},{8,104},{16,112},{24,120},{32,64},{40,72},{48,80},{56,88},{... | collective-permute-start | bytes 294920 | tf_op jit(solution)/shard_map/ppermute | solution.py:325
  143.8 6.5 %collective-permute-start.32 = (f32[192,128]{1,0:T(8,128)S(1)}, f32[192,128]{1,0:T(8,128)S(1)}, u32[]{:S(2)}, u32[]{:S(2)}) collective-permute-start(f32[192,128]{1,0:T(8,128)S(1)} %multiply_add_fusion), channel_id=1, source_target_pairs={{0,224},{8,232},{16,240},{24,248},{32,192},{40,200},{48,208},{56,2... | collective-permute-start | bytes 294920 | tf_op jit(solution)/shard_map/ppermute | solution.py:330
  (1 other events, 1.3 us)

commit v5 on v4

--- a/solution.py
+++ b/solution.py
@@ -315,36 +315,30 @@
     )(tiles, counts, cost, *operands)
 
 
-def fan(value, axis, size, stride, count):
-    got = [value]
-    for turn in range(1, count):
-        pairs = []
-        for k in range(size):
-            place = (k // stride) % count
-            pairs.append((k, k + ((place ^ turn) - place) * stride))
-        got.append(lax.ppermute(value, axis, pairs))
-    return got
-
-
-def pair(value, axis, size, flip):
-    return [value, lax.ppermute(value, axis, [(k, flip(k)) for k in range(size)])]
+def swap(value, axis, flip):
+    size = lax.axis_size(axis)
+    return lax.ppermute(value, axis, [(k, k ^ flip) for k in range(size)])
+
+
+def fan(value, axis, flips):
+    total = value
+    for flip in flips[:-1]:
+        total = lax.optimization_barrier(lse2_many([total, swap(value, axis, flip)]))
+    return lax.optimization_barrier([total, swap(value, axis, flips[-1])])
 
 
 def over_core(value):
-    size = lax.axis_size("tgt")
-    return lse2_many(pair(value, "tgt", size, lambda k: k ^ 1))
+    return lse2_many([value, swap(value, "tgt", 1)])
 
 
 def over_y(value):
-    size = lax.axis_size("tgt")
-    return fan(value, "tgt", size, 2, size // 2)
+    return fan(value, "tgt", (6, 4, 2))
 
 
 def over_src(value):
-    size = lax.axis_size("src")
-    value = lse2_many(fan(value, "src", size, 1, 4))
-    value = lse2_many(fan(value, "src", size, 4, 4))
-    return pair(value, "src", size, lambda k: k ^ 28)
+    value = lse2_many([value, swap(value, "src", 28)])
+    value = lax.optimization_barrier(lse2_many(fan(value, "src", (4, 12, 8))))
+    return fan(value, "src", (3, 2, 1))
 
 
 def body(src_points, tgt_points, tiles, counts):

time: 154 us -> 151 us (0.981); the launches traced: 151 us -> 151 us
  waiting for transfers between devices: 65.7 us -> 57.8 us
  Pallas kernels: 15.6 us -> 19.5 us
  starting transfers between devices: 66.9 us -> 70 us
    ppermute x33, waiting for transfers between devices: 65.7 us -> 57.8 us  [swap(): return lax.ppermute(value, axis, [(k, k ^ flip) for k in range(size)])]
    pallas_call x5, Pallas kernels: 9.96 us -> 13.8 us  [sweep(): pl.pallas_call(kernel, out_shape=(jax.ShapeDtypeStruct((2 * blocks_out, H...]
    ppermute x33, starting transfers between devices: 66.9 us -> 70 us  [swap(): return lax.ppermute(value, axis, [(k, k ^ flip) for k in range(size)])]
  transfers between devices with their start and end apart: 33 -> 33, of which waited for: 24 -> 30; matrix products, arithmetic and copies ran while one was open for 0% -> 1% of each run, Pallas kernels for 1% -> 1%
where the time goes in v5:
time: 151 us
  starting transfers between devices  70 us (46%)
  waiting for transfers between devices  57.8 us (38%)
  Pallas kernels  19.5 us (13%)
  other arithmetic  2.2 us (1%)
  between operations  1.51 us (1%)
    ppermute x33, starting transfers between devices, swap(): return lax.ppermute(value, axis, [(k, k ^ flip) for k in range(size)])  70 us
    ppermute x33, waiting for transfers between devices, swap(): return lax.ppermute(value, axis, [(k, k ^ flip) for k in range(size)])  57.8 us
    pallas_call x5, Pallas kernels, sweep(): pl.pallas_call(kernel, out_shape=(jax.ShapeDtypeStruct((2 * blocks_out, H...  13.8 us
    pallas_call x1, Pallas kernels, costs(): pl.pallas_call(functools.partial(cost_kernel, blocks_in, blocks_out), out...  4.74 us
  transfers between devices with their start and end apart: 33, of which 30 were waited for; matrix products, arithmetic and copies ran while one was open for 1% of the time, Pallas kernels for 1%

profile of v5, /device:TPU:2, one launch (start us, length us, event | category | flops | bytes accessed | tf_op | source)
XLA Modules:
  0.0 151.0 jit_solution(786273265517144321)
XLA Ops:
  1.3 4.7 %shard_map.59 = (f32[32,256,256]{2,1,0:T(8,128)S(1)}, f32[128,128]{1,0:T(8,128)S(1)}, bf16[32,128,256]{2,1,0:T(8,128)(2,1)S(1)}, bf16[32,128,256]{2,1,0:T(8,128)(2,1)S(1)}, s32[2,32]{1,0:T(2,128)S(4)}) custom-call(s32[2,32]{1,0:T(2,128)} %bitcast.4, s32[1,1]{1,0:T(1,128)S(6)} %copy.6.counts, f32[50,16384]{1,0:T(8,128)} %src.1, f32[50,24576]{1,0:T(8,128)} %tgt.1), custom_call_target="tpu_custom_call" | custom-call | tf_op jit(solution)/shard_map/pallas_call | solution.py:255
  7.4 5.5 %collective-permute-start.2 = (f32[128,128]{1,0:T(8,128)S(1)}, f32[128,128]{1,0:T(8,128)S(1)}, u32[]{:S(2)}, u32[]{:S(2)}) collective-permute-start(f32[128,128]{1,0:T(8,128)S(1)} %multiply_add_fusion.26), channel_id=1, source_target_pairs={{0,4},{1,5},{2,6},{3,7},{4,0},{5,1},{6,2},{7,3},{8,12},{9,13},{10,... | collective-permute-start | bytes 196616 | tf_op jit(solution)/shard_map/ppermute | solution.py:320
  13.9 4.5 %collective-permute-done.1 = f32[128,128]{1,0:T(8,128)S(1)} collective-permute-done((f32[128,128]{1,0:T(8,128)S(1)}, f32[128,128]{1,0:T(8,128)S(1)}, u32[]{:S(2)}, u32[]{:S(2)}) %collective-permute-start.1) | collective-permute-done | bytes 65568 | tf_op jit(solution)/shard_map/ppermute | solution.py:320
  18.6 4.0 %shard_map.61 = (f32[192,128]{1,0:T(8,128)S(1)}, f32[128,128]{1,0:T(8,128)S(1)}) custom-call(s32[2,32]{1,0:T(2,128)S(4)} %get-tuple-element.37.tiles, s32[1,1]{1,0:T(1,128)S(6)} %copy.6.counts, f32[32,256,256]{2,1,0:T(8,128)S(1)} %shard_map.60.cost, f32[128,128]{1,0:T(8,128)S(1)} %multiply_add_fusion.24.refs_0_, f32[128,128]{1,0:T(8,128)S(1)} %collective-permute-done.3.refs_1_), custom_call_target="tpu_custom_call" | custom-call | tf_op jit(solution)/shard_map/pallas_call | solution.py:300
  22.6 4.3 %collective-permute-start.4 = (f32[192,128]{1,0:T(8,128)S(1)}, f32[192,128]{1,0:T(8,128)S(1)}, u32[]{:S(2)}, u32[]{:S(2)}) collective-permute-start(f32[192,128]{1,0:T(8,128)S(1)} %get-tuple-element.47), channel_id=1, source_target_pairs={{0,224},{8,232},{16,240},{24,248},{32,192},{40,200},{48,208},{56,2... | collective-permute-start | bytes 294920 | tf_op jit(solution)/shard_map/ppermute | solution.py:320
  26.9 3.2 %collective-permute-done.4 = f32[192,128]{1,0:T(8,128)S(1)} collective-permute-done((f32[192,128]{1,0:T(8,128)S(1)}, f32[192,128]{1,0:T(8,128)S(1)}, u32[]{:S(2)}, u32[]{:S(2)}) %collective-permute-start.4) | collective-permute-done | bytes 98336 | tf_op jit(solution)/shard_map/ppermute | solution.py:320
  30.2 5.8 %collective-permute-start.5 = (f32[192,128]{1,0:T(8,128)S(1)}, f32[192,128]{1,0:T(8,128)S(1)}, u32[]{:S(2)}, u32[]{:S(2)}) collective-permute-start(f32[192,128]{1,0:T(8,128)S(1)} %multiply_add_fusion.17), channel_id=1, source_target_pairs={{0,32},{8,40},{16,48},{24,56},{32,0},{40,8},{48,16},{56,24},{64,96... | collective-permute-start | bytes 294920 | tf_op jit(solution)/shard_map/ppermute | solution.py:320
  36.0 4.2 %collective-permute-start.6 = (f32[192,128]{1,0:T(8,128)S(1)}, f32[192,128]{1,0:T(8,128)S(1)}, u32[]{:S(2)}, u32[]{:S(2)}) collective-permute-start(f32[192,128]{1,0:T(8,128)S(1)} %multiply_add_fusion.17), channel_id=1, source_target_pairs={{0,96},{8,104},{16,112},{24,120},{32,64},{40,72},{48,80},{56,88},{... | collective-permute-start | bytes 294920 | tf_op jit(solution)/shard_map/ppermute | solution.py:320
  40.6 3.3 %collective-permute-done.6 = f32[192,128]{1,0:T(8,128)S(1)} collective-permute-done((f32[192,128]{1,0:T(8,128)S(1)}, f32[192,128]{1,0:T(8,128)S(1)}, u32[]{:S(2)}, u32[]{:S(2)}) %collective-permute-start.6) | collective-permute-done | bytes 98336 | tf_op jit(solution)/shard_map/ppermute | solution.py:320
  43.9 2.0 %collective-permute-done.7 = f32[192,128]{1,0:T(8,128)S(1)} collective-permute-done((f32[192,128]{1,0:T(8,128)S(1)}, f32[192,128]{1,0:T(8,128)S(1)}, u32[]{:S(2)}, u32[]{:S(2)}) %collective-permute-start.7) | collective-permute-done | bytes 98336 | tf_op jit(solution)/shard_map/ppermute | solution.py:320
  46.2 4.0 %collective-permute-start.10 = (f32[192,128]{1,0:T(8,128)S(1)}, f32[192,128]{1,0:T(8,128)S(1)}, u32[]{:S(2)}, u32[]{:S(2)}) collective-permute-start(f32[192,128]{1,0:T(8,128)S(1)} %multiply_add_fusion.14), channel_id=1, source_target_pairs={{0,8},{8,0},{16,24},{24,16},{32,40},{40,32},{48,56},{56,48},{64,72... | collective-permute-start | bytes 294920 | tf_op jit(solution)/shard_map/ppermute | solution.py:320
  56.1 2.9 %collective-permute-start.12 = (f32[128,128]{1,0:T(8,128)S(1)}, f32[128,128]{1,0:T(8,128)S(1)}, u32[]{:S(2)}, u32[]{:S(2)}) collective-permute-start(f32[128,128]{1,0:T(8,128)S(1)} %multiply_add_fusion.23), channel_id=1, source_target_pairs={{0,6},{1,7},{2,4},{3,5},{4,2},{5,3},{6,0},{7,1},{8,14},{9,15},{10,... | collective-permute-start | bytes 196616 | tf_op jit(solution)/shard_map/ppermute | solution.py:320
  60.2 1.8 %collective-permute-done.12 = f32[128,128]{1,0:T(8,128)S(1)} collective-permute-done((f32[128,128]{1,0:T(8,128)S(1)}, f32[128,128]{1,0:T(8,128)S(1)}, u32[]{:S(2)}, u32[]{:S(2)}) %collective-permute-start.12) | collective-permute-done | bytes 65568 | tf_op jit(solution)/shard_map/ppermute | solution.py:320
  62.1 2.9 %collective-permute-done.13 = f32[128,128]{1,0:T(8,128)S(1)} collective-permute-done((f32[128,128]{1,0:T(8,128)S(1)}, f32[128,128]{1,0:T(8,128)S(1)}, u32[]{:S(2)}, u32[]{:S(2)}) %collective-permute-start.13) | collective-permute-done | bytes 65568 | tf_op jit(solution)/shard_map/ppermute | solution.py:320
  65.1 4.0 %shard_map.63 = (f32[192,128]{1,0:T(8,128)S(1)}, f32[128,128]{1,0:T(8,128)S(1)}) custom-call(s32[2,32]{1,0:T(2,128)S(4)} %get-tuple-element.37.tiles, s32[1,1]{1,0:T(1,128)S(6)} %copy.6.counts, f32[32,256,256]{2,1,0:T(8,128)S(1)} %shard_map.60.cost, f32[192,128]{1,0:T(8,128)S(1)} %get-tuple-element.52.refs_0_, f32[128,128]{1,0:T(8,128)S(1)} %multiply_add_fusion.21.refs_1_, ...), custom_call_target="tpu_custom_call" | custom-call | tf_op jit(solution)/shard_map/pallas_call | solution.py:300
  69.1 2.2 %collective-permute-start.15 = (f32[192,128]{1,0:T(8,128)S(1)}, f32[192,128]{1,0:T(8,128)S(1)}, u32[]{:S(2)}, u32[]{:S(2)}) collective-permute-start(f32[192,128]{1,0:T(8,128)S(1)} %get-tuple-element.57), channel_id=1, source_target_pairs={{0,224},{8,232},{16,240},{24,248},{32,192},{40,200},{48,208},{56,2... | collective-permute-start | bytes 294920 | tf_op jit(solution)/shard_map/ppermute | solution.py:320
  71.3 3.7 %collective-permute-done.15 = f32[192,128]{1,0:T(8,128)S(1)} collective-permute-done((f32[192,128]{1,0:T(8,128)S(1)}, f32[192,128]{1,0:T(8,128)S(1)}, u32[]{:S(2)}, u32[]{:S(2)}) %collective-permute-start.15) | collective-permute-done | bytes 98336 | tf_op jit(solution)/shard_map/ppermute | solution.py:320
  75.1 10.7 %collective-permute-start.16 = (f32[192,128]{1,0:T(8,128)S(1)}, f32[192,128]{1,0:T(8,128)S(1)}, u32[]{:S(2)}, u32[]{:S(2)}) collective-permute-start(f32[192,128]{1,0:T(8,128)S(1)} %multiply_add_fusion.11), channel_id=1, source_target_pairs={{0,32},{8,40},{16,48},{24,56},{32,0},{40,8},{48,16},{56,24},{64,96... | collective-permute-start | bytes 294920 | tf_op jit(solution)/shard_map/ppermute | solution.py:320
  85.8 1.6 %collective-permute-start.18 = (f32[192,128]{1,0:T(8,128)S(1)}, f32[192,128]{1,0:T(8,128)S(1)}, u32[]{:S(2)}, u32[]{:S(2)}) collective-permute-start(f32[192,128]{1,0:T(8,128)S(1)} %multiply_add_fusion.11), channel_id=1, source_target_pairs={{0,64},{8,72},{16,80},{24,88},{32,96},{40,104},{48,112},{56,120},{... | collective-permute-start | bytes 294920 | tf_op jit(solution)/shard_map/ppermute | solution.py:320
  88.9 3.4 %collective-permute-done.17 = f32[192,128]{1,0:T(8,128)S(1)} collective-permute-done((f32[192,128]{1,0:T(8,128)S(1)}, f32[192,128]{1,0:T(8,128)S(1)}, u32[]{:S(2)}, u32[]{:S(2)}) %collective-permute-start.17) | collective-permute-done | bytes 98336 | tf_op jit(solution)/shard_map/ppermute | solution.py:320
  93.7 4.0 %collective-permute-start.21 = (f32[192,128]{1,0:T(8,128)S(1)}, f32[192,128]{1,0:T(8,128)S(1)}, u32[]{:S(2)}, u32[]{:S(2)}) collective-permute-start(f32[192,128]{1,0:T(8,128)S(1)} %multiply_add_fusion.8), channel_id=1, source_target_pairs={{0,8},{8,0},{16,24},{24,16},{32,40},{40,32},{48,56},{56,48},{64,72... | collective-permute-start | bytes 294920 | tf_op jit(solution)/shard_map/ppermute | solution.py:320
  103.6 2.2 %collective-permute-start.23 = (f32[128,128]{1,0:T(8,128)S(1)}, f32[128,128]{1,0:T(8,128)S(1)}, u32[]{:S(2)}, u32[]{:S(2)}) collective-permute-start(f32[128,128]{1,0:T(8,128)S(1)} %multiply_add_fusion.20), channel_id=1, source_target_pairs={{0,6},{1,7},{2,4},{3,5},{4,2},{5,3},{6,0},{7,1},{8,14},{9,15},{10,... | collective-permute-start | bytes 196616 | tf_op jit(solution)/shard_map/ppermute | solution.py:320
  105.7 3.0 %collective-permute-start.24 = (f32[128,128]{1,0:T(8,128)S(1)}, f32[128,128]{1,0:T(8,128)S(1)}, u32[]{:S(2)}, u32[]{:S(2)}) collective-permute-start(f32[128,128]{1,0:T(8,128)S(1)} %multiply_add_fusion.20), channel_id=1, source_target_pairs={{0,4},{1,5},{2,6},{3,7},{4,0},{5,1},{6,2},{7,3},{8,12},{9,13},{10,... | collective-permute-start | bytes 196616 | tf_op jit(solution)/shard_map/ppermute | solution.py:320
  109.2 2.6 %collective-permute-done.24 = f32[128,128]{1,0:T(8,128)S(1)} collective-permute-done((f32[128,128]{1,0:T(8,128)S(1)}, f32[128,128]{1,0:T(8,128)S(1)}, u32[]{:S(2)}, u32[]{:S(2)}) %collective-permute-start.24) | collective-permute-done | bytes 65568 | tf_op jit(solution)/shard_map/ppermute | solution.py:320
  113.0 4.0 %shard_map.65 = (f32[192,128]{1,0:T(8,128)S(1)}, f32[128,128]{1,0:T(8,128)}) custom-call(s32[2,32]{1,0:T(2,128)S(4)} %get-tuple-element.37.tiles, s32[1,1]{1,0:T(1,128)S(6)} %copy.6.counts, f32[32,256,256]{2,1,0:T(8,128)S(1)} %shard_map.60.cost, f32[192,128]{1,0:T(8,128)S(1)} %get-tuple-element.62.refs_0_, f32[128,128]{1,0:T(8,128)S(1)} %multiply_add_fusion.18.refs_1_, ...), custom_call_target="tpu_custom_call" | custom-call | tf_op jit(solution)/shard_map/pallas_call | solution.py:300
  117.8 5.1 %collective-permute-done.26 = f32[192,128]{1,0:T(8,128)S(1)} collective-permute-done((f32[192,128]{1,0:T(8,128)S(1)}, f32[192,128]{1,0:T(8,128)S(1)}, u32[]{:S(2)}, u32[]{:S(2)}) %collective-permute-start.26) | collective-permute-done | bytes 98336 | tf_op jit(solution)/shard_map/ppermute | solution.py:320
  123.0 11.2 %collective-permute-start.27 = (f32[192,128]{1,0:T(8,128)S(1)}, f32[192,128]{1,0:T(8,128)S(1)}, u32[]{:S(2)}, u32[]{:S(2)}) collective-permute-start(f32[192,128]{1,0:T(8,128)S(1)} %multiply_add_fusion.5), channel_id=1, source_target_pairs={{0,32},{8,40},{16,48},{24,56},{32,0},{40,8},{48,16},{56,24},{64,96... | collective-permute-start | bytes 294920 | tf_op jit(solution)/shard_map/ppermute | solution.py:320
  134.2 1.6 %collective-permute-start.29 = (f32[192,128]{1,0:T(8,128)S(1)}, f32[192,128]{1,0:T(8,128)S(1)}, u32[]{:S(2)}, u32[]{:S(2)}) collective-permute-start(f32[192,128]{1,0:T(8,128)S(1)} %multiply_add_fusion.5), channel_id=1, source_target_pairs={{0,64},{8,72},{16,80},{24,88},{32,96},{40,104},{48,112},{56,120},{... | collective-permute-start | bytes 294920 | tf_op jit(solution)/shard_map/ppermute | solution.py:320
  135.8 2.4 %collective-permute-done.27 = f32[192,128]{1,0:T(8,128)S(1)} collective-permute-done((f32[192,128]{1,0:T(8,128)S(1)}, f32[192,128]{1,0:T(8,128)S(1)}, u32[]{:S(2)}, u32[]{:S(2)}) %collective-permute-start.27) | collective-permute-done | bytes 98336 | tf_op jit(solution)/shard_map/ppermute | solution.py:320
  138.2 2.5 %collective-permute-done.28 = f32[192,128]{1,0:T(8,128)S(1)} collective-permute-done((f32[192,128]{1,0:T(8,128)S(1)}, f32[192,128]{1,0:T(8,128)S(1)}, u32[]{:S(2)}, u32[]{:S(2)}) %collective-permute-start.28) | collective-permute-done | bytes 98336 | tf_op jit(solution)/shard_map/ppermute | solution.py:320
  140.8 1.6 %collective-permute-done.29 = f32[192,128]{1,0:T(8,128)S(1)} collective-permute-done((f32[192,128]{1,0:T(8,128)S(1)}, f32[192,128]{1,0:T(8,128)S(1)}, u32[]{:S(2)}, u32[]{:S(2)}) %collective-permute-start.29) | collective-permute-done | bytes 98336 | tf_op jit(solution)/shard_map/ppermute | solution.py:320
  142.7 4.0 %collective-permute-start.32 = (f32[192,128]{1,0:T(8,128)S(1)}, f32[192,128]{1,0:T(8,128)S(1)}, u32[]{:S(2)}, u32[]{:S(2)}) collective-permute-start(f32[192,128]{1,0:T(8,128)S(1)} %multiply_add_fusion.2), channel_id=1, source_target_pairs={{0,8},{8,0},{16,24},{24,16},{32,40},{40,32},{48,56},{56,48},{64,72... | collective-permute-start | bytes 294920 | tf_op jit(solution)/shard_map/ppermute | solution.py:320
  (69 shorter events, 26.6 us)
Async XLA Ops:
  6.0 1.3 collective-permute-start
  7.4 11.1 %collective-permute-start.2 = (f32[128,128]{1,0:T(8,128)S(1)}, f32[128,128]{1,0:T(8,128)S(1)}, u32[]{:S(2)}, u32[]{:S(2)}) collective-permute-start(f32[128,128]{1,0:T(8,128)S(1)} %multiply_add_fusion.26), channel_id=1, source_target_pairs={{0,4},{1,5},{2,6},{3,7},{4,0},{5,1},{6,2},{7,3},{8,12},{9,13},{10,... | collective-permute-start | bytes 196616 | tf_op jit(solution)/shard_map/ppermute | solution.py:320
  13.0 5.5 %collective-permute-start.1 = (f32[128,128]{1,0:T(8,128)S(1)}, f32[128,128]{1,0:T(8,128)S(1)}, u32[]{:S(2)}, u32[]{:S(2)}) collective-permute-start(f32[128,128]{1,0:T(8,128)S(1)} %multiply_add_fusion.26), channel_id=1, source_target_pairs={{0,6},{1,7},{2,4},{3,5},{4,2},{5,3},{6,0},{7,1},{8,14},{9,15},{10,... | collective-permute-start | bytes 196616 | tf_op jit(solution)/shard_map/ppermute | solution.py:320
  13.0 5.6 %collective-permute-start.3 = (f32[128,128]{1,0:T(8,128)S(1)}, f32[128,128]{1,0:T(8,128)S(1)}, u32[]{:S(2)}, u32[]{:S(2)}) collective-permute-start(f32[128,128]{1,0:T(8,128)S(1)} %multiply_add_fusion.26), channel_id=1, source_target_pairs={{0,2},{1,3},{2,0},{3,1},{4,6},{5,7},{6,4},{7,5},{8,10},{9,11},{10,... | collective-permute-start | bytes 196616 | tf_op jit(solution)/shard_map/ppermute | solution.py:320
  22.6 7.5 %collective-permute-start.4 = (f32[192,128]{1,0:T(8,128)S(1)}, f32[192,128]{1,0:T(8,128)S(1)}, u32[]{:S(2)}, u32[]{:S(2)}) collective-permute-start(f32[192,128]{1,0:T(8,128)S(1)} %get-tuple-element.47), channel_id=1, source_target_pairs={{0,224},{8,232},{16,240},{24,248},{32,192},{40,200},{48,208},{56,2... | collective-permute-start | bytes 294920 | tf_op jit(solution)/shard_map/ppermute | solution.py:320
  30.2 10.3 %collective-permute-start.5 = (f32[192,128]{1,0:T(8,128)S(1)}, f32[192,128]{1,0:T(8,128)S(1)}, u32[]{:S(2)}, u32[]{:S(2)}) collective-permute-start(f32[192,128]{1,0:T(8,128)S(1)} %multiply_add_fusion.17), channel_id=1, source_target_pairs={{0,32},{8,40},{16,48},{24,56},{32,0},{40,8},{48,16},{56,24},{64,96... | collective-permute-start | bytes 294920 | tf_op jit(solution)/shard_map/ppermute | solution.py:320
  36.0 7.8 %collective-permute-start.6 = (f32[192,128]{1,0:T(8,128)S(1)}, f32[192,128]{1,0:T(8,128)S(1)}, u32[]{:S(2)}, u32[]{:S(2)}) collective-permute-start(f32[192,128]{1,0:T(8,128)S(1)} %multiply_add_fusion.17), channel_id=1, source_target_pairs={{0,96},{8,104},{16,112},{24,120},{32,64},{40,72},{48,80},{56,88},{... | collective-permute-start | bytes 294920 | tf_op jit(solution)/shard_map/ppermute | solution.py:320
  40.2 5.8 %collective-permute-start.7 = (f32[192,128]{1,0:T(8,128)S(1)}, f32[192,128]{1,0:T(8,128)S(1)}, u32[]{:S(2)}, u32[]{:S(2)}) collective-permute-start(f32[192,128]{1,0:T(8,128)S(1)} %multiply_add_fusion.17), channel_id=1, source_target_pairs={{0,64},{8,72},{16,80},{24,88},{32,96},{40,104},{48,112},{56,120},{... | collective-permute-start | bytes 294920 | tf_op jit(solution)/shard_map/ppermute | solution.py:320
  46.0 4.7 %collective-permute-start.8 = (f32[192,128]{1,0:T(8,128)S(1)}, f32[192,128]{1,0:T(8,128)S(1)}, u32[]{:S(2)}, u32[]{:S(2)}) collective-permute-start(f32[192,128]{1,0:T(8,128)S(1)} %multiply_add_fusion.14), channel_id=1, source_target_pairs={{0,24},{8,16},{16,8},{24,0},{32,56},{40,48},{48,40},{56,32},{64,88... | collective-permute-start | bytes 294920 | tf_op jit(solution)/shard_map/ppermute | solution.py:320
  46.1 6.2 %collective-permute-start.9 = (f32[192,128]{1,0:T(8,128)S(1)}, f32[192,128]{1,0:T(8,128)S(1)}, u32[]{:S(2)}, u32[]{:S(2)}) collective-permute-start(f32[192,128]{1,0:T(8,128)S(1)} %multiply_add_fusion.14), channel_id=1, source_target_pairs={{0,16},{8,24},{16,0},{24,8},{32,48},{40,56},{48,32},{56,40},{64,80... | collective-permute-start | bytes 294920 | tf_op jit(solution)/shard_map/ppermute | solution.py:320
  46.2 7.6 %collective-permute-start.10 = (f32[192,128]{1,0:T(8,128)S(1)}, f32[192,128]{1,0:T(8,128)S(1)}, u32[]{:S(2)}, u32[]{:S(2)}) collective-permute-start(f32[192,128]{1,0:T(8,128)S(1)} %multiply_add_fusion.14), channel_id=1, source_target_pairs={{0,8},{8,0},{16,24},{24,16},{32,40},{40,32},{48,56},{56,48},{64,72... | collective-permute-start | bytes 294920 | tf_op jit(solution)/shard_map/ppermute | solution.py:320
  54.7 1.3 collective-permute-start.11
  56.1 6.0 %collective-permute-start.12 = (f32[128,128]{1,0:T(8,128)S(1)}, f32[128,128]{1,0:T(8,128)S(1)}, u32[]{:S(2)}, u32[]{:S(2)}) collective-permute-start(f32[128,128]{1,0:T(8,128)S(1)} %multiply_add_fusion.23), channel_id=1, source_target_pairs={{0,6},{1,7},{2,4},{3,5},{4,2},{5,3},{6,0},{7,1},{8,14},{9,15},{10,... | collective-permute-start | bytes 196616 | tf_op jit(solution)/shard_map/ppermute | solution.py:320
  59.0 6.1 %collective-permute-start.13 = (f32[128,128]{1,0:T(8,128)S(1)}, f32[128,128]{1,0:T(8,128)S(1)}, u32[]{:S(2)}, u32[]{:S(2)}) collective-permute-start(f32[128,128]{1,0:T(8,128)S(1)} %multiply_add_fusion.23), channel_id=1, source_target_pairs={{0,4},{1,5},{2,6},{3,7},{4,0},{5,1},{6,2},{7,3},{8,12},{9,13},{10,... | collective-permute-start | bytes 196616 | tf_op jit(solution)/shard_map/ppermute | solution.py:320
  59.0 6.1 %collective-permute-start.14 = (f32[128,128]{1,0:T(8,128)S(1)}, f32[128,128]{1,0:T(8,128)S(1)}, u32[]{:S(2)}, u32[]{:S(2)}) collective-permute-start(f32[128,128]{1,0:T(8,128)S(1)} %multiply_add_fusion.23), channel_id=1, source_target_pairs={{0,2},{1,3},{2,0},{3,1},{4,6},{5,7},{6,4},{7,5},{8,10},{9,11},{10,... | collective-permute-start | bytes 196616 | tf_op jit(solution)/shard_map/ppermute | solution.py:320
  69.1 5.9 %collective-permute-start.15 = (f32[192,128]{1,0:T(8,128)S(1)}, f32[192,128]{1,0:T(8,128)S(1)}, u32[]{:S(2)}, u32[]{:S(2)}) collective-permute-start(f32[192,128]{1,0:T(8,128)S(1)} %get-tuple-element.57), channel_id=1, source_target_pairs={{0,224},{8,232},{16,240},{24,248},{32,192},{40,200},{48,208},{56,2... | collective-permute-start | bytes 294920 | tf_op jit(solution)/shard_map/ppermute | solution.py:320
  75.1 13.7 %collective-permute-start.16 = (f32[192,128]{1,0:T(8,128)S(1)}, f32[192,128]{1,0:T(8,128)S(1)}, u32[]{:S(2)}, u32[]{:S(2)}) collective-permute-start(f32[192,128]{1,0:T(8,128)S(1)} %multiply_add_fusion.11), channel_id=1, source_target_pairs={{0,32},{8,40},{16,48},{24,56},{32,0},{40,8},{48,16},{56,24},{64,96... | collective-permute-start | bytes 294920 | tf_op jit(solution)/shard_map/ppermute | solution.py:320
  85.8 6.5 %collective-permute-start.17 = (f32[192,128]{1,0:T(8,128)S(1)}, f32[192,128]{1,0:T(8,128)S(1)}, u32[]{:S(2)}, u32[]{:S(2)}) collective-permute-start(f32[192,128]{1,0:T(8,128)S(1)} %multiply_add_fusion.11), channel_id=1, source_target_pairs={{0,96},{8,104},{16,112},{24,120},{32,64},{40,72},{48,80},{56,88},{... | collective-permute-start | bytes 294920 | tf_op jit(solution)/shard_map/ppermute | solution.py:320
  85.8 7.6 %collective-permute-start.18 = (f32[192,128]{1,0:T(8,128)S(1)}, f32[192,128]{1,0:T(8,128)S(1)}, u32[]{:S(2)}, u32[]{:S(2)}) collective-permute-start(f32[192,128]{1,0:T(8,128)S(1)} %multiply_add_fusion.11), channel_id=1, source_target_pairs={{0,64},{8,72},{16,80},{24,88},{32,96},{40,104},{48,112},{56,120},{... | collective-permute-start | bytes 294920 | tf_op jit(solution)/shard_map/ppermute | solution.py:320
  93.5 4.7 %collective-permute-start.19 = (f32[192,128]{1,0:T(8,128)S(1)}, f32[192,128]{1,0:T(8,128)S(1)}, u32[]{:S(2)}, u32[]{:S(2)}) collective-permute-start(f32[192,128]{1,0:T(8,128)S(1)} %multiply_add_fusion.8), channel_id=1, source_target_pairs={{0,24},{8,16},{16,8},{24,0},{32,56},{40,48},{48,40},{56,32},{64,88... | collective-permute-start | bytes 294920 | tf_op jit(solution)/shard_map/ppermute | solution.py:320
  93.6 6.2 %collective-permute-start.20 = (f32[192,128]{1,0:T(8,128)S(1)}, f32[192,128]{1,0:T(8,128)S(1)}, u32[]{:S(2)}, u32[]{:S(2)}) collective-permute-start(f32[192,128]{1,0:T(8,128)S(1)} %multiply_add_fusion.8), channel_id=1, source_target_pairs={{0,16},{8,24},{16,0},{24,8},{32,48},{40,56},{48,32},{56,40},{64,80... | collective-permute-start | bytes 294920 | tf_op jit(solution)/shard_map/ppermute | solution.py:320
  93.7 7.6 %collective-permute-start.21 = (f32[192,128]{1,0:T(8,128)S(1)}, f32[192,128]{1,0:T(8,128)S(1)}, u32[]{:S(2)}, u32[]{:S(2)}) collective-permute-start(f32[192,128]{1,0:T(8,128)S(1)} %multiply_add_fusion.8), channel_id=1, source_target_pairs={{0,8},{8,0},{16,24},{24,16},{32,40},{40,32},{48,56},{56,48},{64,72... | collective-permute-start | bytes 294920 | tf_op jit(solution)/shard_map/ppermute | solution.py:320
  103.6 5.6 %collective-permute-start.23 = (f32[128,128]{1,0:T(8,128)S(1)}, f32[128,128]{1,0:T(8,128)S(1)}, u32[]{:S(2)}, u32[]{:S(2)}) collective-permute-start(f32[128,128]{1,0:T(8,128)S(1)} %multiply_add_fusion.20), channel_id=1, source_target_pairs={{0,6},{1,7},{2,4},{3,5},{4,2},{5,3},{6,0},{7,1},{8,14},{9,15},{10,... | collective-permute-start | bytes 196616 | tf_op jit(solution)/shard_map/ppermute | solution.py:320
  105.7 6.0 %collective-permute-start.24 = (f32[128,128]{1,0:T(8,128)S(1)}, f32[128,128]{1,0:T(8,128)S(1)}, u32[]{:S(2)}, u32[]{:S(2)}) collective-permute-start(f32[128,128]{1,0:T(8,128)S(1)} %multiply_add_fusion.20), channel_id=1, source_target_pairs={{0,4},{1,5},{2,6},{3,7},{4,0},{5,1},{6,2},{7,3},{8,12},{9,13},{10,... | collective-permute-start | bytes 196616 | tf_op jit(solution)/shard_map/ppermute | solution.py:320
  108.7 4.3 %collective-permute-start.25 = (f32[128,128]{1,0:T(8,128)S(1)}, f32[128,128]{1,0:T(8,128)S(1)}, u32[]{:S(2)}, u32[]{:S(2)}) collective-permute-start(f32[128,128]{1,0:T(8,128)S(1)} %multiply_add_fusion.20), channel_id=1, source_target_pairs={{0,2},{1,3},{2,0},{3,1},{4,6},{5,7},{6,4},{7,5},{8,10},{9,11},{10,... | collective-permute-start | bytes 196616 | tf_op jit(solution)/shard_map/ppermute | solution.py:320
  117.0 5.9 %collective-permute-start.26 = (f32[192,128]{1,0:T(8,128)S(1)}, f32[192,128]{1,0:T(8,128)S(1)}, u32[]{:S(2)}, u32[]{:S(2)}) collective-permute-start(f32[192,128]{1,0:T(8,128)S(1)} %get-tuple-element.67), channel_id=1, source_target_pairs={{0,224},{8,232},{16,240},{24,248},{32,192},{40,200},{48,208},{56,2... | collective-permute-start | bytes 294920 | tf_op jit(solution)/shard_map/ppermute | solution.py:320
  123.0 15.2 %collective-permute-start.27 = (f32[192,128]{1,0:T(8,128)S(1)}, f32[192,128]{1,0:T(8,128)S(1)}, u32[]{:S(2)}, u32[]{:S(2)}) collective-permute-start(f32[192,128]{1,0:T(8,128)S(1)} %multiply_add_fusion.5), channel_id=1, source_target_pairs={{0,32},{8,40},{16,48},{24,56},{32,0},{40,8},{48,16},{56,24},{64,96... | collective-permute-start | bytes 294920 | tf_op jit(solution)/shard_map/ppermute | solution.py:320
  134.2 6.5 %collective-permute-start.28 = (f32[192,128]{1,0:T(8,128)S(1)}, f32[192,128]{1,0:T(8,128)S(1)}, u32[]{:S(2)}, u32[]{:S(2)}) collective-permute-start(f32[192,128]{1,0:T(8,128)S(1)} %multiply_add_fusion.5), channel_id=1, source_target_pairs={{0,96},{8,104},{16,112},{24,120},{32,64},{40,72},{48,80},{56,88},{... | collective-permute-start | bytes 294920 | tf_op jit(solution)/shard_map/ppermute | solution.py:320
  134.2 8.2 %collective-permute-start.29 = (f32[192,128]{1,0:T(8,128)S(1)}, f32[192,128]{1,0:T(8,128)S(1)}, u32[]{:S(2)}, u32[]{:S(2)}) collective-permute-start(f32[192,128]{1,0:T(8,128)S(1)} %multiply_add_fusion.5), channel_id=1, source_target_pairs={{0,64},{8,72},{16,80},{24,88},{32,96},{40,104},{48,112},{56,120},{... | collective-permute-start | bytes 294920 | tf_op jit(solution)/shard_map/ppermute | solution.py:320
  142.5 4.7 %collective-permute-start.30 = (f32[192,128]{1,0:T(8,128)S(1)}, f32[192,128]{1,0:T(8,128)S(1)}, u32[]{:S(2)}, u32[]{:S(2)}) collective-permute-start(f32[192,128]{1,0:T(8,128)S(1)} %multiply_add_fusion.2), channel_id=1, source_target_pairs={{0,24},{8,16},{16,8},{24,0},{32,56},{40,48},{48,40},{56,32},{64,88... | collective-permute-start | bytes 294920 | tf_op jit(solution)/shard_map/ppermute | solution.py:320
  142.6 6.2 %collective-permute-start.31 = (f32[192,128]{1,0:T(8,128)S(1)}, f32[192,128]{1,0:T(8,128)S(1)}, u32[]{:S(2)}, u32[]{:S(2)}) collective-permute-start(f32[192,128]{1,0:T(8,128)S(1)} %multiply_add_fusion.2), channel_id=1, source_target_pairs={{0,16},{8,24},{16,0},{24,8},{32,48},{40,56},{48,32},{56,40},{64,80... | collective-permute-start | bytes 294920 | tf_op jit(solution)/shard_map/ppermute | solution.py:320
  142.7 7.6 %collective-permute-start.32 = (f32[192,128]{1,0:T(8,128)S(1)}, f32[192,128]{1,0:T(8,128)S(1)}, u32[]{:S(2)}, u32[]{:S(2)}) collective-permute-start(f32[192,128]{1,0:T(8,128)S(1)} %multiply_add_fusion.2), channel_id=1, source_target_pairs={{0,8},{8,0},{16,24},{24,16},{32,40},{40,32},{48,56},{56,48},{64,72... | collective-permute-start | bytes 294920 | tf_op jit(solution)/shard_map/ppermute | solution.py:320
  (1 other events, 1.3 us)

commit v6 on v5

--- a/solution.py
+++ b/solution.py
@@ -321,14 +321,11 @@
 
 
 def fan(value, axis, flips):
-    total = value
-    for flip in flips[:-1]:
-        total = lax.optimization_barrier(lse2_many([total, swap(value, axis, flip)]))
-    return lax.optimization_barrier([total, swap(value, axis, flips[-1])])
+    return [value, *[swap(value, axis, flip) for flip in flips]]
 
 
 def over_core(value):
-    return lse2_many([value, swap(value, "tgt", 1)])
+    return lse2_many(fan(value, "tgt", (1,)))
 
 
 def over_y(value):
@@ -336,9 +333,10 @@
 
 
 def over_src(value):
-    value = lse2_many([value, swap(value, "src", 28)])
-    value = lax.optimization_barrier(lse2_many(fan(value, "src", (4, 12, 8))))
-    return fan(value, "src", (3, 2, 1))
+    value = lse2_many(fan(value, "src", (3, 2, 1)))
+    value = lse2_many(fan(value, "src", (4,)))
+    value = lse2_many(fan(value, "src", (12,)))
+    return fan(value, "src", (28,))
 
 
 def body(src_points, tgt_points, tiles, counts):

time: 151 us -> 155 us (1.026); the launches traced: 151 us -> 153 us
  starting transfers between devices: 70 us -> 40.7 us
  Pallas kernels: 19.5 us -> 45.8 us
  waiting for transfers between devices: 57.8 us -> 63.9 us
    ppermute x33 -> x30, starting transfers between devices: 70 us -> 40.7 us  [swap(): return lax.ppermute(value, axis, [(k, k ^ flip) for k in range(size)])]
    pallas_call x5, Pallas kernels: 13.8 us -> 36.9 us  [sweep(): pl.pallas_call(kernel, out_shape=(jax.ShapeDtypeStruct((2 * blocks_out, H...]
    ppermute x33 -> x30, waiting for transfers between devices: 57.8 us -> 63.9 us  [swap(): return lax.ppermute(value, axis, [(k, k ^ flip) for k in range(size)])]
    pallas_call x1, Pallas kernels: 4.74 us -> 7 us  [costs(): pl.pallas_call(functools.partial(cost_kernel, blocks_in, blocks_out), out...]
  transfers between devices with their start and end apart: 33 -> 30, of which waited for: 30 -> 28; matrix products, arithmetic and copies ran while one was open for 1% -> 0% of each run, Pallas kernels for 1% -> 1%
where the time goes in v6:
time: 155 us; the launch traced here: 153 us
  waiting for transfers between devices  63.9 us (41%)
  Pallas kernels  45.8 us (30%)
  starting transfers between devices  40.7 us (26%)
    ppermute x30, waiting for transfers between devices, swap(): return lax.ppermute(value, axis, [(k, k ^ flip) for k in range(size)])  63.9 us
    ppermute x30, starting transfers between devices, swap(): return lax.ppermute(value, axis, [(k, k ^ flip) for k in range(size)])  40.7 us
    pallas_call x5, Pallas kernels, sweep(): pl.pallas_call(kernel, out_shape=(jax.ShapeDtypeStruct((2 * blocks_out, H...  36.9 us
    pallas_call x1, Pallas kernels, costs(): pl.pallas_call(functools.partial(cost_kernel, blocks_in, blocks_out), out...  7 us
  transfers between devices with their start and end apart: 30, of which 28 were waited for; matrix products, arithmetic and copies ran while one was open for 0% of the time, Pallas kernels for 1%

profile of v6, /device:TPU:2, one launch (start us, length us, event | category | flops | bytes accessed | tf_op | source)
XLA Modules:
  0.0 153.4 jit_solution(16949615737488931803)
XLA Ops:
  1.3 7.0 %shard_map.59 = (f32[32,256,256]{2,1,0:T(8,128)S(1)}, f32[128,128]{1,0:T(8,128)S(1)}, bf16[32,128,256]{2,1,0:T(8,128)(2,1)S(1)}, bf16[32,128,256]{2,1,0:T(8,128)(2,1)S(1)}, s32[2,32]{1,0:T(2,128)S(4)}) custom-call(s32[2,32]{1,0:T(2,128)} %bitcast.4, s32[1,1]{1,0:T(1,128)S(6)} %copy.6.counts, f32[50,16384]{1,0:T(8,128)} %src.1, f32[50,24576]{1,0:T(8,128)} %tgt.1), custom_call_target="tpu_custom_call" | custom-call | tf_op jit(solution)/shard_map/pallas_call | solution.py:255
  10.8 3.1 %collective-permute-start.3 = (f32[128,128]{1,0:T(8,128)S(1)}, f32[128,128]{1,0:T(8,128)S(1)}, u32[]{:S(2)}, u32[]{:S(2)}) collective-permute-start(f32[128,128]{1,0:T(8,128)S(1)} %multiply_add_fusion.11.refs_0_), channel_id=1, source_target_pairs={{0,2},{1,3},{2,0},{3,1},{4,6},{5,7},{6,4},{7,5},{8,10},{9,11},{10,... | collective-permute-start | bytes 196616 | tf_op jit(solution)/shard_map/ppermute | solution.py:320
  13.9 1.9 %shard_map.60.cost = f32[32,256,256]{2,1,0:T(8,128)S(1)} custom-call(s32[1,1]{1,0:T(1,128)S(6)} %copy.6.counts, bf16[32,128,256]{2,1,0:T(8,128)(2,1)S(1)} %get-tuple-element.22.lefts, bf16[32,128,256]{2,1,0:T(8,128)(2,1)S(1)} %get-tuple-element.23.rights), custom_call_target="tpu_custom_call" | custom-call | flops 1073741824 | bytes 16777216 | tf_op jit(solution)/shard_map/pallas_call | solution.py:282
  17.1 7.3 %shard_map.61 = (f32[192,128]{1,0:T(8,128)S(1)}, f32[128,128]{1,0:T(8,128)S(1)}) custom-call(s32[2,32]{1,0:T(2,128)S(4)} %get-tuple-element.19.tiles, s32[1,1]{1,0:T(1,128)S(6)} %copy.6.counts, f32[32,256,256]{2,1,0:T(8,128)S(1)} %shard_map.60.cost, f32[128,128]{1,0:T(8,128)S(1)} %multiply_add_fusion.11.refs_0_, ...), custom_call_target="tpu_custom_call" | custom-call | tf_op jit(solution)/shard_map/pallas_call | solution.py:300
  24.6 2.9 %collective-permute-start.5 = (f32[192,128]{1,0:T(8,128)S(1)}, f32[192,128]{1,0:T(8,128)S(1)}, u32[]{:S(2)}, u32[]{:S(2)}) collective-permute-start(f32[192,128]{1,0:T(8,128)S(1)} %get-tuple-element.27), channel_id=1, source_target_pairs={{0,16},{8,24},{16,0},{24,8},{32,48},{40,56},{48,32},{56,40},{64,80... | collective-permute-start | bytes 294920 | tf_op jit(solution)/shard_map/ppermute | solution.py:320
  32.8 4.3 %collective-permute-done.7 = f32[192,128]{1,0:T(8,128)S(1)} collective-permute-done((f32[192,128]{1,0:T(8,128)S(1)}, f32[192,128]{1,0:T(8,128)S(1)}, u32[]{:S(2)}, u32[]{:S(2)}) %collective-permute-start.7) | collective-permute-done | bytes 98336 | tf_op jit(solution)/shard_map/ppermute | solution.py:320
  37.2 4.4 %collective-permute-start.8 = (f32[192,128]{1,0:T(8,128)S(1)}, f32[192,128]{1,0:T(8,128)S(1)}, u32[]{:S(2)}, u32[]{:S(2)}) collective-permute-start(f32[192,128]{1,0:T(8,128)S(1)} %multiply_add_fusion.7), channel_id=1, source_target_pairs={{0,96},{8,104},{16,112},{24,120},{32,64},{40,72},{48,80},{56,88},{... | collective-permute-start | bytes 294920 | tf_op jit(solution)/shard_map/ppermute | solution.py:320
  41.5 2.6 %collective-permute-done.8 = f32[192,128]{1,0:T(8,128)S(1)} collective-permute-done((f32[192,128]{1,0:T(8,128)S(1)}, f32[192,128]{1,0:T(8,128)S(1)}, u32[]{:S(2)}, u32[]{:S(2)}) %collective-permute-start.8) | collective-permute-done | bytes 98336 | tf_op jit(solution)/shard_map/ppermute | solution.py:320
  44.2 6.4 %collective-permute-start.9 = (f32[192,128]{1,0:T(8,128)S(1)}, f32[192,128]{1,0:T(8,128)S(1)}, u32[]{:S(2)}, u32[]{:S(2)}) collective-permute-start(f32[192,128]{1,0:T(8,128)S(1)} %multiply_add_fusion.6.refs_1_), channel_id=1, source_target_pairs={{0,224},{8,232},{16,240},{24,248},{32,192},{40,200},{48,208},{56,2... | collective-permute-start | bytes 294920 | tf_op jit(solution)/shard_map/ppermute | solution.py:320
  50.6 2.6 %collective-permute-done.9.refs_2_ = f32[192,128]{1,0:T(8,128)S(1)} collective-permute-done((f32[192,128]{1,0:T(8,128)S(1)}, f32[192,128]{1,0:T(8,128)S(1)}, u32[]{:S(2)}, u32[]{:S(2)}) %collective-permute-start.9) | collective-permute-done | bytes 98336 | tf_op jit(solution)/shard_map/ppermute | solution.py:320
  53.2 7.4 %shard_map.62 = (f32[128,128]{1,0:T(8,128)S(1)}, f32[192,128]{1,0:T(8,128)S(1)}) custom-call(s32[2,32]{1,0:T(2,128)S(4)} %get-tuple-element.19.tiles, s32[1,1]{1,0:T(1,128)S(6)} %copy.6.counts, f32[32,256,256]{2,1,0:T(8,128)S(1)} %get-tuple-element.24.cost, f32[128,128]{1,0:T(8,128)S(1)} %get-tuple-element.26.refs_0_, ...), custom_call_target="tpu_custom_call" | custom-call | tf_op jit(solution)/shard_map/pallas_call | solution.py:300
  62.1 4.0 %collective-permute-start.13 = (f32[128,128]{1,0:T(8,128)S(1)}, f32[128,128]{1,0:T(8,128)S(1)}, u32[]{:S(2)}, u32[]{:S(2)}) collective-permute-start(f32[128,128]{1,0:T(8,128)S(1)} %multiply_add_fusion.10.refs_1_), channel_id=1, source_target_pairs={{0,2},{1,3},{2,0},{3,1},{4,6},{5,7},{6,4},{7,5},{8,10},{9,11},{10,... | collective-permute-start | bytes 196616 | tf_op jit(solution)/shard_map/ppermute | solution.py:320
  66.1 2.7 %collective-permute-done.11.refs_2_ = f32[128,128]{1,0:T(8,128)S(1)} collective-permute-done((f32[128,128]{1,0:T(8,128)S(1)}, f32[128,128]{1,0:T(8,128)S(1)}, u32[]{:S(2)}, u32[]{:S(2)}) %collective-permute-start.11) | collective-permute-done | bytes 65568 | tf_op jit(solution)/shard_map/ppermute | solution.py:320
  69.3 7.5 %shard_map.63 = (f32[192,128]{1,0:T(8,128)S(1)}, f32[128,128]{1,0:T(8,128)S(1)}) custom-call(s32[2,32]{1,0:T(2,128)S(4)} %get-tuple-element.19.tiles, s32[1,1]{1,0:T(1,128)S(6)} %copy.6.counts, f32[32,256,256]{2,1,0:T(8,128)S(1)} %shard_map.60.cost, f32[192,128]{1,0:T(8,128)S(1)} %get-tuple-element.28.refs_0_, f32[128,128]{1,0:T(8,128)S(1)} %multiply_add_fusion.10.refs_1_, ...), custom_call_target="tpu_custom_call" | custom-call | tf_op jit(solution)/shard_map/pallas_call | solution.py:300
  77.0 2.2 %collective-permute-start.15 = (f32[192,128]{1,0:T(8,128)S(1)}, f32[192,128]{1,0:T(8,128)S(1)}, u32[]{:S(2)}, u32[]{:S(2)}) collective-permute-start(f32[192,128]{1,0:T(8,128)S(1)} %get-tuple-element.31), channel_id=1, source_target_pairs={{0,16},{8,24},{16,0},{24,8},{32,48},{40,56},{48,32},{56,40},{64,80... | collective-permute-start | bytes 294920 | tf_op jit(solution)/shard_map/ppermute | solution.py:320
  79.2 1.8 %collective-permute-start.16 = (f32[192,128]{1,0:T(8,128)S(1)}, f32[192,128]{1,0:T(8,128)S(1)}, u32[]{:S(2)}, u32[]{:S(2)}) collective-permute-start(f32[192,128]{1,0:T(8,128)S(1)} %get-tuple-element.31), channel_id=1, source_target_pairs={{0,8},{8,0},{16,24},{24,16},{32,40},{40,32},{48,56},{56,48},{64,72... | collective-permute-start | bytes 294920 | tf_op jit(solution)/shard_map/ppermute | solution.py:320
  81.6 1.6 %collective-permute-done.15 = f32[192,128]{1,0:T(8,128)S(1)} collective-permute-done((f32[192,128]{1,0:T(8,128)S(1)}, f32[192,128]{1,0:T(8,128)S(1)}, u32[]{:S(2)}, u32[]{:S(2)}) %collective-permute-start.15) | collective-permute-done | bytes 98336 | tf_op jit(solution)/shard_map/ppermute | solution.py:320
  83.2 1.5 collective-permute-done.16
  84.9 4.6 %collective-permute-done.17 = f32[192,128]{1,0:T(8,128)S(1)} collective-permute-done((f32[192,128]{1,0:T(8,128)S(1)}, f32[192,128]{1,0:T(8,128)S(1)}, u32[]{:S(2)}, u32[]{:S(2)}) %collective-permute-start.17) | collective-permute-done | bytes 98336 | tf_op jit(solution)/shard_map/ppermute | solution.py:320
  89.7 6.9 %collective-permute-done.18 = f32[192,128]{1,0:T(8,128)S(1)} collective-permute-done((f32[192,128]{1,0:T(8,128)S(1)}, f32[192,128]{1,0:T(8,128)S(1)}, u32[]{:S(2)}, u32[]{:S(2)}) %collective-permute-start.18) | collective-permute-done | bytes 98336 | tf_op jit(solution)/shard_map/ppermute | solution.py:320
  96.7 3.7 %collective-permute-start.19 = (f32[192,128]{1,0:T(8,128)S(1)}, f32[192,128]{1,0:T(8,128)S(1)}, u32[]{:S(2)}, u32[]{:S(2)}) collective-permute-start(f32[192,128]{1,0:T(8,128)S(1)} %multiply_add_fusion.3.refs_1_), channel_id=1, source_target_pairs={{0,224},{8,232},{16,240},{24,248},{32,192},{40,200},{48,208},{56,2... | collective-permute-start | bytes 294920 | tf_op jit(solution)/shard_map/ppermute | solution.py:320
  100.4 3.2 %collective-permute-done.19.refs_2_ = f32[192,128]{1,0:T(8,128)S(1)} collective-permute-done((f32[192,128]{1,0:T(8,128)S(1)}, f32[192,128]{1,0:T(8,128)S(1)}, u32[]{:S(2)}, u32[]{:S(2)}) %collective-permute-start.19) | collective-permute-done | bytes 98336 | tf_op jit(solution)/shard_map/ppermute | solution.py:320
  103.5 7.4 %shard_map.64 = (f32[128,128]{1,0:T(8,128)S(1)}, f32[192,128]{1,0:T(8,128)S(1)}) custom-call(s32[2,32]{1,0:T(2,128)S(4)} %get-tuple-element.19.tiles, s32[1,1]{1,0:T(1,128)S(6)} %copy.6.counts, f32[32,256,256]{2,1,0:T(8,128)S(1)} %get-tuple-element.24.cost, f32[128,128]{1,0:T(8,128)S(1)} %get-tuple-element.30.refs_0_, ...), custom_call_target="tpu_custom_call" | custom-call | tf_op jit(solution)/shard_map/pallas_call | solution.py:300
  112.5 4.0 %collective-permute-start.23 = (f32[128,128]{1,0:T(8,128)S(1)}, f32[128,128]{1,0:T(8,128)S(1)}, u32[]{:S(2)}, u32[]{:S(2)}) collective-permute-start(f32[128,128]{1,0:T(8,128)S(1)} %multiply_add_fusion.9.refs_1_), channel_id=1, source_target_pairs={{0,2},{1,3},{2,0},{3,1},{4,6},{5,7},{6,4},{7,5},{8,10},{9,11},{10,... | collective-permute-start | bytes 196616 | tf_op jit(solution)/shard_map/ppermute | solution.py:320
  116.5 2.7 %collective-permute-done.21.refs_2_ = f32[128,128]{1,0:T(8,128)S(1)} collective-permute-done((f32[128,128]{1,0:T(8,128)S(1)}, f32[128,128]{1,0:T(8,128)S(1)}, u32[]{:S(2)}, u32[]{:S(2)}) %collective-permute-start.21) | collective-permute-done | bytes 65568 | tf_op jit(solution)/shard_map/ppermute | solution.py:320
  119.7 7.3 %shard_map.65 = (f32[192,128]{1,0:T(8,128)S(1)}, f32[128,128]{1,0:T(8,128)}) custom-call(s32[2,32]{1,0:T(2,128)S(4)} %get-tuple-element.19.tiles, s32[1,1]{1,0:T(1,128)S(6)} %copy.6.counts, f32[32,256,256]{2,1,0:T(8,128)S(1)} %shard_map.60.cost, f32[192,128]{1,0:T(8,128)S(1)} %get-tuple-element.32.refs_0_, f32[128,128]{1,0:T(8,128)S(1)} %multiply_add_fusion.9.refs_1_, ...), custom_call_target="tpu_custom_call" | custom-call | tf_op jit(solution)/shard_map/pallas_call | solution.py:300
  127.9 3.3 %collective-permute-start.26 = (f32[192,128]{1,0:T(8,128)S(1)}, f32[192,128]{1,0:T(8,128)S(1)}, u32[]{:S(2)}, u32[]{:S(2)}) collective-permute-start(f32[192,128]{1,0:T(8,128)S(1)} %get-tuple-element.35), channel_id=1, source_target_pairs={{0,8},{8,0},{16,24},{24,16},{32,40},{40,32},{48,56},{56,48},{64,72... | collective-permute-start | bytes 294920 | tf_op jit(solution)/shard_map/ppermute | solution.py:320
  131.8 1.6 %collective-permute-done.25 = f32[192,128]{1,0:T(8,128)S(1)} collective-permute-done((f32[192,128]{1,0:T(8,128)S(1)}, f32[192,128]{1,0:T(8,128)S(1)}, u32[]{:S(2)}, u32[]{:S(2)}) %collective-permute-start.25) | collective-permute-done | bytes 98336 | tf_op jit(solution)/shard_map/ppermute | solution.py:320
  133.4 1.5 collective-permute-done.26
  135.1 4.6 %collective-permute-done.27 = f32[192,128]{1,0:T(8,128)S(1)} collective-permute-done((f32[192,128]{1,0:T(8,128)S(1)}, f32[192,128]{1,0:T(8,128)S(1)}, u32[]{:S(2)}, u32[]{:S(2)}) %collective-permute-start.27) | collective-permute-done | bytes 98336 | tf_op jit(solution)/shard_map/ppermute | solution.py:320
  139.9 6.5 %collective-permute-done.28 = f32[192,128]{1,0:T(8,128)S(1)} collective-permute-done((f32[192,128]{1,0:T(8,128)S(1)}, f32[192,128]{1,0:T(8,128)S(1)}, u32[]{:S(2)}, u32[]{:S(2)}) %collective-permute-start.28) | collective-permute-done | bytes 98336 | tf_op jit(solution)/shard_map/ppermute | solution.py:320
  146.5 6.2 %collective-permute-done.29 = f32[192,128]{1,0:T(8,128)S(1)} collective-permute-done((f32[192,128]{1,0:T(8,128)S(1)}, f32[192,128]{1,0:T(8,128)S(1)}, u32[]{:S(2)}, u32[]{:S(2)}) %collective-permute-start.29) | collective-permute-done | bytes 98336 | tf_op jit(solution)/shard_map/ppermute | solution.py:320
  (48 shorter events, 17.3 us)
Async XLA Ops:
  8.3 1.3 collective-permute-start
  9.7 6.5 %collective-permute-start.1 = (f32[128,128]{1,0:T(8,128)S(1)}, f32[128,128]{1,0:T(8,128)S(1)}, u32[]{:S(2)}, u32[]{:S(2)}) collective-permute-start(f32[128,128]{1,0:T(8,128)S(1)} %multiply_add_fusion.11.refs_0_), channel_id=1, source_target_pairs={{0,6},{1,7},{2,4},{3,5},{4,2},{5,3},{6,0},{7,1},{8,14},{9,15},{10,... | collective-permute-start | bytes 196616 | tf_op jit(solution)/shard_map/ppermute | solution.py:320
  10.5 6.1 %collective-permute-start.2 = (f32[128,128]{1,0:T(8,128)S(1)}, f32[128,128]{1,0:T(8,128)S(1)}, u32[]{:S(2)}, u32[]{:S(2)}) collective-permute-start(f32[128,128]{1,0:T(8,128)S(1)} %multiply_add_fusion.11.refs_0_), channel_id=1, source_target_pairs={{0,4},{1,5},{2,6},{3,7},{4,0},{5,1},{6,2},{7,3},{8,12},{9,13},{10,... | collective-permute-start | bytes 196616 | tf_op jit(solution)/shard_map/ppermute | solution.py:320
  10.8 6.4 %collective-permute-start.3 = (f32[128,128]{1,0:T(8,128)S(1)}, f32[128,128]{1,0:T(8,128)S(1)}, u32[]{:S(2)}, u32[]{:S(2)}) collective-permute-start(f32[128,128]{1,0:T(8,128)S(1)} %multiply_add_fusion.11.refs_0_), channel_id=1, source_target_pairs={{0,2},{1,3},{2,0},{3,1},{4,6},{5,7},{6,4},{7,5},{8,10},{9,11},{10,... | collective-permute-start | bytes 196616 | tf_op jit(solution)/shard_map/ppermute | solution.py:320
  24.5 5.6 %collective-permute-start.4 = (f32[192,128]{1,0:T(8,128)S(1)}, f32[192,128]{1,0:T(8,128)S(1)}, u32[]{:S(2)}, u32[]{:S(2)}) collective-permute-start(f32[192,128]{1,0:T(8,128)S(1)} %get-tuple-element.27), channel_id=1, source_target_pairs={{0,24},{8,16},{16,8},{24,0},{32,56},{40,48},{48,40},{56,32},{64,88... | collective-permute-start | bytes 294920 | tf_op jit(solution)/shard_map/ppermute | solution.py:320
  24.6 6.4 %collective-permute-start.5 = (f32[192,128]{1,0:T(8,128)S(1)}, f32[192,128]{1,0:T(8,128)S(1)}, u32[]{:S(2)}, u32[]{:S(2)}) collective-permute-start(f32[192,128]{1,0:T(8,128)S(1)} %get-tuple-element.27), channel_id=1, source_target_pairs={{0,16},{8,24},{16,0},{24,8},{32,48},{40,56},{48,32},{56,40},{64,80... | collective-permute-start | bytes 294920 | tf_op jit(solution)/shard_map/ppermute | solution.py:320
  27.5 4.8 %collective-permute-start.6 = (f32[192,128]{1,0:T(8,128)S(1)}, f32[192,128]{1,0:T(8,128)S(1)}, u32[]{:S(2)}, u32[]{:S(2)}) collective-permute-start(f32[192,128]{1,0:T(8,128)S(1)} %get-tuple-element.27), channel_id=1, source_target_pairs={{0,8},{8,0},{16,24},{24,16},{32,40},{40,32},{48,56},{56,48},{64,72... | collective-permute-start | bytes 294920 | tf_op jit(solution)/shard_map/ppermute | solution.py:320
  32.4 4.7 %collective-permute-start.7 = (f32[192,128]{1,0:T(8,128)S(1)}, f32[192,128]{1,0:T(8,128)S(1)}, u32[]{:S(2)}, u32[]{:S(2)}) collective-permute-start(f32[192,128]{1,0:T(8,128)S(1)} %multiply_add_fusion.8), channel_id=1, source_target_pairs={{0,32},{8,40},{16,48},{24,56},{32,0},{40,8},{48,16},{56,24},{64,96... | collective-permute-start | bytes 294920 | tf_op jit(solution)/shard_map/ppermute | solution.py:320
  37.2 7.0 %collective-permute-start.8 = (f32[192,128]{1,0:T(8,128)S(1)}, f32[192,128]{1,0:T(8,128)S(1)}, u32[]{:S(2)}, u32[]{:S(2)}) collective-permute-start(f32[192,128]{1,0:T(8,128)S(1)} %multiply_add_fusion.7), channel_id=1, source_target_pairs={{0,96},{8,104},{16,112},{24,120},{32,64},{40,72},{48,80},{56,88},{... | collective-permute-start | bytes 294920 | tf_op jit(solution)/shard_map/ppermute | solution.py:320
  44.2 9.0 %collective-permute-start.9 = (f32[192,128]{1,0:T(8,128)S(1)}, f32[192,128]{1,0:T(8,128)S(1)}, u32[]{:S(2)}, u32[]{:S(2)}) collective-permute-start(f32[192,128]{1,0:T(8,128)S(1)} %multiply_add_fusion.6.refs_1_), channel_id=1, source_target_pairs={{0,224},{8,232},{16,240},{24,248},{32,192},{40,200},{48,208},{56,2... | collective-permute-start | bytes 294920 | tf_op jit(solution)/shard_map/ppermute | solution.py:320
  60.5 1.3 collective-permute-start.10
  61.9 6.9 %collective-permute-start.11 = (f32[128,128]{1,0:T(8,128)S(1)}, f32[128,128]{1,0:T(8,128)S(1)}, u32[]{:S(2)}, u32[]{:S(2)}) collective-permute-start(f32[128,128]{1,0:T(8,128)S(1)} %multiply_add_fusion.10.refs_1_), channel_id=1, source_target_pairs={{0,6},{1,7},{2,4},{3,5},{4,2},{5,3},{6,0},{7,1},{8,14},{9,15},{10,... | collective-permute-start | bytes 196616 | tf_op jit(solution)/shard_map/ppermute | solution.py:320
  62.0 6.8 %collective-permute-start.12 = (f32[128,128]{1,0:T(8,128)S(1)}, f32[128,128]{1,0:T(8,128)S(1)}, u32[]{:S(2)}, u32[]{:S(2)}) collective-permute-start(f32[128,128]{1,0:T(8,128)S(1)} %multiply_add_fusion.10.refs_1_), channel_id=1, source_target_pairs={{0,4},{1,5},{2,6},{3,7},{4,0},{5,1},{6,2},{7,3},{8,12},{9,13},{10,... | collective-permute-start | bytes 196616 | tf_op jit(solution)/shard_map/ppermute | solution.py:320
  62.1 7.2 %collective-permute-start.13 = (f32[128,128]{1,0:T(8,128)S(1)}, f32[128,128]{1,0:T(8,128)S(1)}, u32[]{:S(2)}, u32[]{:S(2)}) collective-permute-start(f32[128,128]{1,0:T(8,128)S(1)} %multiply_add_fusion.10.refs_1_), channel_id=1, source_target_pairs={{0,2},{1,3},{2,0},{3,1},{4,6},{5,7},{6,4},{7,5},{8,10},{9,11},{10,... | collective-permute-start | bytes 196616 | tf_op jit(solution)/shard_map/ppermute | solution.py:320
  76.9 4.7 %collective-permute-start.14 = (f32[192,128]{1,0:T(8,128)S(1)}, f32[192,128]{1,0:T(8,128)S(1)}, u32[]{:S(2)}, u32[]{:S(2)}) collective-permute-start(f32[192,128]{1,0:T(8,128)S(1)} %get-tuple-element.31), channel_id=1, source_target_pairs={{0,24},{8,16},{16,8},{24,0},{32,56},{40,48},{48,40},{56,32},{64,88... | collective-permute-start | bytes 294920 | tf_op jit(solution)/shard_map/ppermute | solution.py:320
  77.0 6.2 %collective-permute-start.15 = (f32[192,128]{1,0:T(8,128)S(1)}, f32[192,128]{1,0:T(8,128)S(1)}, u32[]{:S(2)}, u32[]{:S(2)}) collective-permute-start(f32[192,128]{1,0:T(8,128)S(1)} %get-tuple-element.31), channel_id=1, source_target_pairs={{0,16},{8,24},{16,0},{24,8},{32,48},{40,56},{48,32},{56,40},{64,80... | collective-permute-start | bytes 294920 | tf_op jit(solution)/shard_map/ppermute | solution.py:320
  79.2 5.5 %collective-permute-start.16 = (f32[192,128]{1,0:T(8,128)S(1)}, f32[192,128]{1,0:T(8,128)S(1)}, u32[]{:S(2)}, u32[]{:S(2)}) collective-permute-start(f32[192,128]{1,0:T(8,128)S(1)} %get-tuple-element.31), channel_id=1, source_target_pairs={{0,8},{8,0},{16,24},{24,16},{32,40},{40,32},{48,56},{56,48},{64,72... | collective-permute-start | bytes 294920 | tf_op jit(solution)/shard_map/ppermute | solution.py:320
  84.8 4.7 %collective-permute-start.17 = (f32[192,128]{1,0:T(8,128)S(1)}, f32[192,128]{1,0:T(8,128)S(1)}, u32[]{:S(2)}, u32[]{:S(2)}) collective-permute-start(f32[192,128]{1,0:T(8,128)S(1)} %multiply_add_fusion.5), channel_id=1, source_target_pairs={{0,32},{8,40},{16,48},{24,56},{32,0},{40,8},{48,16},{56,24},{64,96... | collective-permute-start | bytes 294920 | tf_op jit(solution)/shard_map/ppermute | solution.py:320
  89.6 7.0 %collective-permute-start.18 = (f32[192,128]{1,0:T(8,128)S(1)}, f32[192,128]{1,0:T(8,128)S(1)}, u32[]{:S(2)}, u32[]{:S(2)}) collective-permute-start(f32[192,128]{1,0:T(8,128)S(1)} %multiply_add_fusion.4), channel_id=1, source_target_pairs={{0,96},{8,104},{16,112},{24,120},{32,64},{40,72},{48,80},{56,88},{... | collective-permute-start | bytes 294920 | tf_op jit(solution)/shard_map/ppermute | solution.py:320
  96.7 6.9 %collective-permute-start.19 = (f32[192,128]{1,0:T(8,128)S(1)}, f32[192,128]{1,0:T(8,128)S(1)}, u32[]{:S(2)}, u32[]{:S(2)}) collective-permute-start(f32[192,128]{1,0:T(8,128)S(1)} %multiply_add_fusion.3.refs_1_), channel_id=1, source_target_pairs={{0,224},{8,232},{16,240},{24,248},{32,192},{40,200},{48,208},{56,2... | collective-permute-start | bytes 294920 | tf_op jit(solution)/shard_map/ppermute | solution.py:320
  110.9 1.3 collective-permute-start.20
  112.3 6.9 %collective-permute-start.21 = (f32[128,128]{1,0:T(8,128)S(1)}, f32[128,128]{1,0:T(8,128)S(1)}, u32[]{:S(2)}, u32[]{:S(2)}) collective-permute-start(f32[128,128]{1,0:T(8,128)S(1)} %multiply_add_fusion.9.refs_1_), channel_id=1, source_target_pairs={{0,6},{1,7},{2,4},{3,5},{4,2},{5,3},{6,0},{7,1},{8,14},{9,15},{10,... | collective-permute-start | bytes 196616 | tf_op jit(solution)/shard_map/ppermute | solution.py:320
  112.4 6.8 %collective-permute-start.22 = (f32[128,128]{1,0:T(8,128)S(1)}, f32[128,128]{1,0:T(8,128)S(1)}, u32[]{:S(2)}, u32[]{:S(2)}) collective-permute-start(f32[128,128]{1,0:T(8,128)S(1)} %multiply_add_fusion.9.refs_1_), channel_id=1, source_target_pairs={{0,4},{1,5},{2,6},{3,7},{4,0},{5,1},{6,2},{7,3},{8,12},{9,13},{10,... | collective-permute-start | bytes 196616 | tf_op jit(solution)/shard_map/ppermute | solution.py:320
  112.5 7.2 %collective-permute-start.23 = (f32[128,128]{1,0:T(8,128)S(1)}, f32[128,128]{1,0:T(8,128)S(1)}, u32[]{:S(2)}, u32[]{:S(2)}) collective-permute-start(f32[128,128]{1,0:T(8,128)S(1)} %multiply_add_fusion.9.refs_1_), channel_id=1, source_target_pairs={{0,2},{1,3},{2,0},{3,1},{4,6},{5,7},{6,4},{7,5},{8,10},{9,11},{10,... | collective-permute-start | bytes 196616 | tf_op jit(solution)/shard_map/ppermute | solution.py:320
  127.1 4.7 %collective-permute-start.24 = (f32[192,128]{1,0:T(8,128)S(1)}, f32[192,128]{1,0:T(8,128)S(1)}, u32[]{:S(2)}, u32[]{:S(2)}) collective-permute-start(f32[192,128]{1,0:T(8,128)S(1)} %get-tuple-element.35), channel_id=1, source_target_pairs={{0,24},{8,16},{16,8},{24,0},{32,56},{40,48},{48,40},{56,32},{64,88... | collective-permute-start | bytes 294920 | tf_op jit(solution)/shard_map/ppermute | solution.py:320
  127.2 6.2 %collective-permute-start.25 = (f32[192,128]{1,0:T(8,128)S(1)}, f32[192,128]{1,0:T(8,128)S(1)}, u32[]{:S(2)}, u32[]{:S(2)}) collective-permute-start(f32[192,128]{1,0:T(8,128)S(1)} %get-tuple-element.35), channel_id=1, source_target_pairs={{0,16},{8,24},{16,0},{24,8},{32,48},{40,56},{48,32},{56,40},{64,80... | collective-permute-start | bytes 294920 | tf_op jit(solution)/shard_map/ppermute | solution.py:320
  127.9 7.0 %collective-permute-start.26 = (f32[192,128]{1,0:T(8,128)S(1)}, f32[192,128]{1,0:T(8,128)S(1)}, u32[]{:S(2)}, u32[]{:S(2)}) collective-permute-start(f32[192,128]{1,0:T(8,128)S(1)} %get-tuple-element.35), channel_id=1, source_target_pairs={{0,8},{8,0},{16,24},{24,16},{32,40},{40,32},{48,56},{56,48},{64,72... | collective-permute-start | bytes 294920 | tf_op jit(solution)/shard_map/ppermute | solution.py:320
  135.0 4.7 %collective-permute-start.27 = (f32[192,128]{1,0:T(8,128)S(1)}, f32[192,128]{1,0:T(8,128)S(1)}, u32[]{:S(2)}, u32[]{:S(2)}) collective-permute-start(f32[192,128]{1,0:T(8,128)S(1)} %multiply_add_fusion.2), channel_id=1, source_target_pairs={{0,32},{8,40},{16,48},{24,56},{32,0},{40,8},{48,16},{56,24},{64,96... | collective-permute-start | bytes 294920 | tf_op jit(solution)/shard_map/ppermute | solution.py:320
  139.8 6.6 %collective-permute-start.28 = (f32[192,128]{1,0:T(8,128)S(1)}, f32[192,128]{1,0:T(8,128)S(1)}, u32[]{:S(2)}, u32[]{:S(2)}) collective-permute-start(f32[192,128]{1,0:T(8,128)S(1)} %multiply_add_fusion.1), channel_id=1, source_target_pairs={{0,96},{8,104},{16,112},{24,120},{32,64},{40,72},{48,80},{56,88},{... | collective-permute-start | bytes 294920 | tf_op jit(solution)/shard_map/ppermute | solution.py:320
  146.4 6.3 %collective-permute-start.29 = (f32[192,128]{1,0:T(8,128)S(1)}, f32[192,128]{1,0:T(8,128)S(1)}, u32[]{:S(2)}, u32[]{:S(2)}) collective-permute-start(f32[192,128]{1,0:T(8,128)S(1)} %multiply_add_fusion), channel_id=1, source_target_pairs={{0,224},{8,232},{16,240},{24,248},{32,192},{40,200},{48,208},{56,2... | collective-permute-start | bytes 294920 | tf_op jit(solution)/shard_map/ppermute | solution.py:320

commit v7 on v6

--- a/solution.py
+++ b/solution.py
@@ -114,9 +114,15 @@
 ):
     table = pltpu.make_async_copy(tiles_in, tiles, tsem)
     table.start()
+    width = src.shape[0]
+    ext[...] = jnp.zeros_like(ext)
+    for u in range(GROUP):
+        for side, place in ((0, 1), (0, 3), (1, 0), (1, 2)):
+            ext[u, side, pl.ds(width + place, 1), :] = jnp.ones((1, TILE), jnp.float32)
+    top[...] = jnp.full_like(top, FLOOR)
+    total[...] = jnp.zeros_like(total)
     table.wait()
     live = counts[0, 0]
-    width = src.shape[0]
 
     def copies(k):
         first = pl.multiple_of(block(tiles, 0, k, blocks_out) * TILE, TILE)
@@ -137,12 +143,6 @@
         return carry
 
     lax.fori_loop(0, live, begin, 0)
-    ext[...] = jnp.zeros_like(ext)
-    for u in range(GROUP):
-        for side, place in ((0, 1), (0, 3), (1, 0), (1, 2)):
-            ext[u, side, pl.ds(width + place, 1), :] = jnp.ones((1, TILE), jnp.float32)
-    top[...] = jnp.full_like(top, FLOOR)
-    total[...] = jnp.zeros_like(total)
 
     def extend(u, side, points, scale):
         square = jnp.sum(points * points, axis=0, keepdims=True) * SCALE
@@ -174,7 +174,7 @@
         return carry
 
     lax.fori_loop(0, (live + GROUP - 1) // GROUP, group, 0)
-    add_up(GROUP, live, tiles, 0, blocks_out, cost, lambda k: None, top, total)
+    add_up(WIDE, live, tiles, 0, blocks_out, cost, lambda k: None, top, total)
     finish(out, top, total)
 
 
@@ -333,10 +333,9 @@
 
 
 def over_src(value):
-    value = lse2_many(fan(value, "src", (3, 2, 1)))
-    value = lse2_many(fan(value, "src", (4,)))
-    value = lse2_many(fan(value, "src", (12,)))
-    return fan(value, "src", (28,))
+    for flip in (28, 12, 4):
+        value = lse2_many(fan(value, "src", (flip,)))
+    return fan(value, "src", (3, 2, 1))
 
 
 def body(src_points, tgt_points, tiles, counts):

time: 155 us -> 153 us (0.987)
  waiting for transfers between devices: 63.9 us -> 75.7 us
  Pallas kernels: 45.8 us -> 34.3 us
    ppermute x30, waiting for transfers between devices: 63.9 us -> 75.7 us  [swap(): return lax.ppermute(value, axis, [(k, k ^ flip) for k in range(size)])]
    pallas_call x5, Pallas kernels: 36.9 us -> 26.7 us  [sweep(): pl.pallas_call(kernel, out_shape=(jax.ShapeDtypeStruct((2 * blocks_out, H...]
  transfers between devices with their start and end apart: 30 -> 30, of which waited for: 28 -> 25; matrix products, arithmetic and copies ran while one was open for 0% -> 0% of each run, Pallas kernels for 1% -> 1%
where the time goes in v7:
time: 153 us
  waiting for transfers between devices  75.7 us (49%)
  starting transfers between devices  40 us (26%)
  Pallas kernels  34.3 us (22%)
    ppermute x30, waiting for transfers between devices, swap(): return lax.ppermute(value, axis, [(k, k ^ flip) for k in range(size)])  75.7 us
    ppermute x30, starting transfers between devices, swap(): return lax.ppermute(value, axis, [(k, k ^ flip) for k in range(size)])  40 us
    pallas_call x5, Pallas kernels, sweep(): pl.pallas_call(kernel, out_shape=(jax.ShapeDtypeStruct((2 * blocks_out, H...  26.7 us
    pallas_call x1, Pallas kernels, costs(): pl.pallas_call(functools.partial(cost_kernel, blocks_in, blocks_out), out...  6.19 us
  transfers between devices with their start and end apart: 30, of which 25 were waited for; matrix products, arithmetic and copies ran while one was open for 0% of the time, Pallas kernels for 1%

profile of v7, /device:TPU:2, one launch (start us, length us, event | category | flops | bytes accessed | tf_op | source)
XLA Modules:
  0.0 152.9 jit_solution(8140664082276640386)
XLA Ops:
  1.3 6.2 %shard_map.59 = (f32[32,256,256]{2,1,0:T(8,128)S(1)}, f32[128,128]{1,0:T(8,128)S(1)}, bf16[32,128,256]{2,1,0:T(8,128)(2,1)S(1)}, bf16[32,128,256]{2,1,0:T(8,128)(2,1)S(1)}, s32[2,32]{1,0:T(2,128)S(4)}) custom-call(s32[2,32]{1,0:T(2,128)} %bitcast.4, s32[1,1]{1,0:T(1,128)S(6)} %copy.6.counts, f32[50,16384]{1,0:T(8,128)} %src.1, f32[50,24576]{1,0:T(8,128)} %tgt.1), custom_call_target="tpu_custom_call" | custom-call | tf_op jit(solution)/shard_map/pallas_call | solution.py:255
  9.9 3.1 %collective-permute-start.2 = (f32[128,128]{1,0:T(8,128)S(1)}, f32[128,128]{1,0:T(8,128)S(1)}, u32[]{:S(2)}, u32[]{:S(2)}) collective-permute-start(f32[128,128]{1,0:T(8,128)S(1)} %multiply_add_fusion.11.refs_0_), channel_id=1, source_target_pairs={{0,4},{1,5},{2,6},{3,7},{4,0},{5,1},{6,2},{7,3},{8,12},{9,13},{10,... | collective-permute-start | bytes 196616 | tf_op jit(solution)/shard_map/ppermute | solution.py:320
  15.8 1.5 collective-permute-done.3.refs_3_
  17.3 6.3 %shard_map.61 = (f32[192,128]{1,0:T(8,128)S(1)}, f32[128,128]{1,0:T(8,128)S(1)}) custom-call(s32[2,32]{1,0:T(2,128)S(4)} %get-tuple-element.19.tiles, s32[1,1]{1,0:T(1,128)S(6)} %copy.6.counts, f32[32,256,256]{2,1,0:T(8,128)S(1)} %shard_map.60.cost, f32[128,128]{1,0:T(8,128)S(1)} %multiply_add_fusion.11.refs_0_, ...), custom_call_target="tpu_custom_call" | custom-call | tf_op jit(solution)/shard_map/pallas_call | solution.py:300
  23.6 5.5 %collective-permute-start.4 = (f32[192,128]{1,0:T(8,128)S(1)}, f32[192,128]{1,0:T(8,128)S(1)}, u32[]{:S(2)}, u32[]{:S(2)}) collective-permute-start(f32[192,128]{1,0:T(8,128)S(1)} %get-tuple-element.27), channel_id=1, source_target_pairs={{0,224},{8,232},{16,240},{24,248},{32,192},{40,200},{48,208},{56,2... | collective-permute-start | bytes 294920 | tf_op jit(solution)/shard_map/ppermute | solution.py:320
  29.1 4.4 %collective-permute-done.4 = f32[192,128]{1,0:T(8,128)S(1)} collective-permute-done((f32[192,128]{1,0:T(8,128)S(1)}, f32[192,128]{1,0:T(8,128)S(1)}, u32[]{:S(2)}, u32[]{:S(2)}) %collective-permute-start.4) | collective-permute-done | bytes 98336 | tf_op jit(solution)/shard_map/ppermute | solution.py:320
  33.7 6.5 %collective-permute-done.5 = f32[192,128]{1,0:T(8,128)S(1)} collective-permute-done((f32[192,128]{1,0:T(8,128)S(1)}, f32[192,128]{1,0:T(8,128)S(1)}, u32[]{:S(2)}, u32[]{:S(2)}) %collective-permute-start.5) | collective-permute-done | bytes 98336 | tf_op jit(solution)/shard_map/ppermute | solution.py:320
  40.4 4.6 %collective-permute-done.6 = f32[192,128]{1,0:T(8,128)S(1)} collective-permute-done((f32[192,128]{1,0:T(8,128)S(1)}, f32[192,128]{1,0:T(8,128)S(1)}, u32[]{:S(2)}, u32[]{:S(2)}) %collective-permute-start.6) | collective-permute-done | bytes 98336 | tf_op jit(solution)/shard_map/ppermute | solution.py:320
  46.6 2.6 %collective-permute-start.9 = (f32[192,128]{1,0:T(8,128)S(1)}, f32[192,128]{1,0:T(8,128)S(1)}, u32[]{:S(2)}, u32[]{:S(2)}) collective-permute-start(f32[192,128]{1,0:T(8,128)S(1)} %multiply_add_fusion.6.refs_1_), channel_id=1, source_target_pairs={{0,8},{8,0},{16,24},{24,16},{32,40},{40,32},{48,56},{56,48},{64,72... | collective-permute-start | bytes 294920 | tf_op jit(solution)/shard_map/ppermute | solution.py:320
  49.7 1.6 %collective-permute-done.8.refs_3_ = f32[192,128]{1,0:T(8,128)S(1)} collective-permute-done((f32[192,128]{1,0:T(8,128)S(1)}, f32[192,128]{1,0:T(8,128)S(1)}, u32[]{:S(2)}, u32[]{:S(2)}) %collective-permute-start.8) | collective-permute-done | bytes 98336 | tf_op jit(solution)/shard_map/ppermute | solution.py:320
  51.3 1.5 collective-permute-done.9.refs_4_
  52.8 6.3 %shard_map.62 = (f32[128,128]{1,0:T(8,128)S(1)}, f32[192,128]{1,0:T(8,128)S(1)}) custom-call(s32[2,32]{1,0:T(2,128)S(4)} %get-tuple-element.19.tiles, s32[1,1]{1,0:T(1,128)S(6)} %copy.6.counts, f32[32,256,256]{2,1,0:T(8,128)S(1)} %get-tuple-element.24.cost, f32[128,128]{1,0:T(8,128)S(1)} %get-tuple-element.26.refs_0_, ...), custom_call_target="tpu_custom_call" | custom-call | tf_op jit(solution)/shard_map/pallas_call | solution.py:300
  60.8 4.0 %collective-permute-start.13 = (f32[128,128]{1,0:T(8,128)S(1)}, f32[128,128]{1,0:T(8,128)S(1)}, u32[]{:S(2)}, u32[]{:S(2)}) collective-permute-start(f32[128,128]{1,0:T(8,128)S(1)} %multiply_add_fusion.10.refs_1_), channel_id=1, source_target_pairs={{0,2},{1,3},{2,0},{3,1},{4,6},{5,7},{6,4},{7,5},{8,10},{9,11},{10,... | collective-permute-start | bytes 196616 | tf_op jit(solution)/shard_map/ppermute | solution.py:320
  64.7 2.7 %collective-permute-done.11.refs_2_ = f32[128,128]{1,0:T(8,128)S(1)} collective-permute-done((f32[128,128]{1,0:T(8,128)S(1)}, f32[128,128]{1,0:T(8,128)S(1)}, u32[]{:S(2)}, u32[]{:S(2)}) %collective-permute-start.11) | collective-permute-done | bytes 65568 | tf_op jit(solution)/shard_map/ppermute | solution.py:320
  68.0 6.3 %shard_map.63 = (f32[192,128]{1,0:T(8,128)S(1)}, f32[128,128]{1,0:T(8,128)S(1)}) custom-call(s32[2,32]{1,0:T(2,128)S(4)} %get-tuple-element.19.tiles, s32[1,1]{1,0:T(1,128)S(6)} %copy.6.counts, f32[32,256,256]{2,1,0:T(8,128)S(1)} %shard_map.60.cost, f32[192,128]{1,0:T(8,128)S(1)} %get-tuple-element.28.refs_0_, f32[128,128]{1,0:T(8,128)S(1)} %multiply_add_fusion.10.refs_1_, ...), custom_call_target="tpu_custom_call" | custom-call | tf_op jit(solution)/shard_map/pallas_call | solution.py:300
  74.4 5.8 %collective-permute-done.14 = f32[192,128]{1,0:T(8,128)S(1)} collective-permute-done((f32[192,128]{1,0:T(8,128)S(1)}, f32[192,128]{1,0:T(8,128)S(1)}, u32[]{:S(2)}, u32[]{:S(2)}) %collective-permute-start.14) | collective-permute-done | bytes 98336 | tf_op jit(solution)/shard_map/ppermute | solution.py:320
  80.4 6.5 %collective-permute-done.15 = f32[192,128]{1,0:T(8,128)S(1)} collective-permute-done((f32[192,128]{1,0:T(8,128)S(1)}, f32[192,128]{1,0:T(8,128)S(1)}, u32[]{:S(2)}, u32[]{:S(2)}) %collective-permute-start.15) | collective-permute-done | bytes 98336 | tf_op jit(solution)/shard_map/ppermute | solution.py:320
  87.0 4.6 %collective-permute-done.16 = f32[192,128]{1,0:T(8,128)S(1)} collective-permute-done((f32[192,128]{1,0:T(8,128)S(1)}, f32[192,128]{1,0:T(8,128)S(1)}, u32[]{:S(2)}, u32[]{:S(2)}) %collective-permute-start.16) | collective-permute-done | bytes 98336 | tf_op jit(solution)/shard_map/ppermute | solution.py:320
  91.7 4.6 %collective-permute-start.17 = (f32[192,128]{1,0:T(8,128)S(1)}, f32[192,128]{1,0:T(8,128)S(1)}, u32[]{:S(2)}, u32[]{:S(2)}) collective-permute-start(f32[192,128]{1,0:T(8,128)S(1)} %multiply_add_fusion.3.refs_1_), channel_id=1, source_target_pairs={{0,24},{8,16},{16,8},{24,0},{32,56},{40,48},{48,40},{56,32},{64,88... | collective-permute-start | bytes 294920 | tf_op jit(solution)/shard_map/ppermute | solution.py:320
  96.3 2.2 %collective-permute-start.19 = (f32[192,128]{1,0:T(8,128)S(1)}, f32[192,128]{1,0:T(8,128)S(1)}, u32[]{:S(2)}, u32[]{:S(2)}) collective-permute-start(f32[192,128]{1,0:T(8,128)S(1)} %multiply_add_fusion.3.refs_1_), channel_id=1, source_target_pairs={{0,8},{8,0},{16,24},{24,16},{32,40},{40,32},{48,56},{56,48},{64,72... | collective-permute-start | bytes 294920 | tf_op jit(solution)/shard_map/ppermute | solution.py:320
  98.9 3.5 %collective-permute-done.18.refs_3_ = f32[192,128]{1,0:T(8,128)S(1)} collective-permute-done((f32[192,128]{1,0:T(8,128)S(1)}, f32[192,128]{1,0:T(8,128)S(1)}, u32[]{:S(2)}, u32[]{:S(2)}) %collective-permute-start.18) | collective-permute-done | bytes 98336 | tf_op jit(solution)/shard_map/ppermute | solution.py:320
  102.4 1.6 %shard_map.64 = (f32[128,128]{1,0:T(8,128)S(1)}, f32[192,128]{1,0:T(8,128)S(1)}) custom-call(s32[2,32]{1,0:T(2,128)S(4)} %get-tuple-element.19.tiles, s32[1,1]{1,0:T(1,128)S(6)} %copy.6.counts, f32[32,256,256]{2,1,0:T(8,128)S(1)} %get-tuple-element.24.cost, f32[128,128]{1,0:T(8,128)S(1)} %get-tuple-element.30.refs_0_, ...), custom_call_target="tpu_custom_call" | custom-call | tf_op jit(solution)/shard_map/pallas_call | solution.py:300
  105.4 1.9 %collective-permute-start.21 = (f32[128,128]{1,0:T(8,128)S(1)}, f32[128,128]{1,0:T(8,128)S(1)}, u32[]{:S(2)}, u32[]{:S(2)}) collective-permute-start(f32[128,128]{1,0:T(8,128)S(1)} %multiply_add_fusion.9.refs_1_), channel_id=1, source_target_pairs={{0,6},{1,7},{2,4},{3,5},{4,2},{5,3},{6,0},{7,1},{8,14},{9,15},{10,... | collective-permute-start | bytes 196616 | tf_op jit(solution)/shard_map/ppermute | solution.py:320
  107.2 2.3 %collective-permute-start.23 = (f32[128,128]{1,0:T(8,128)S(1)}, f32[128,128]{1,0:T(8,128)S(1)}, u32[]{:S(2)}, u32[]{:S(2)}) collective-permute-start(f32[128,128]{1,0:T(8,128)S(1)} %multiply_add_fusion.9.refs_1_), channel_id=1, source_target_pairs={{0,2},{1,3},{2,0},{3,1},{4,6},{5,7},{6,4},{7,5},{8,10},{9,11},{10,... | collective-permute-start | bytes 196616 | tf_op jit(solution)/shard_map/ppermute | solution.py:320
  110.9 2.4 %collective-permute-done.22.refs_3_ = f32[128,128]{1,0:T(8,128)S(1)} collective-permute-done((f32[128,128]{1,0:T(8,128)S(1)}, f32[128,128]{1,0:T(8,128)S(1)}, u32[]{:S(2)}, u32[]{:S(2)}) %collective-permute-start.22) | collective-permute-done | bytes 65568 | tf_op jit(solution)/shard_map/ppermute | solution.py:320
  113.3 6.3 %shard_map.65 = (f32[192,128]{1,0:T(8,128)S(1)}, f32[128,128]{1,0:T(8,128)}) custom-call(s32[2,32]{1,0:T(2,128)S(4)} %get-tuple-element.19.tiles, s32[1,1]{1,0:T(1,128)S(6)} %copy.6.counts, f32[32,256,256]{2,1,0:T(8,128)S(1)} %shard_map.60.cost, f32[192,128]{1,0:T(8,128)S(1)} %get-tuple-element.32.refs_0_, f32[128,128]{1,0:T(8,128)S(1)} %multiply_add_fusion.9.refs_1_, ...), custom_call_target="tpu_custom_call" | custom-call | tf_op jit(solution)/shard_map/pallas_call | solution.py:300
  119.7 6.1 %collective-permute-done.24 = f32[192,128]{1,0:T(8,128)S(1)} collective-permute-done((f32[192,128]{1,0:T(8,128)S(1)}, f32[192,128]{1,0:T(8,128)S(1)}, u32[]{:S(2)}, u32[]{:S(2)}) %collective-permute-start.24) | collective-permute-done | bytes 98336 | tf_op jit(solution)/shard_map/ppermute | solution.py:320
  125.9 7.5 %collective-permute-done.25 = f32[192,128]{1,0:T(8,128)S(1)} collective-permute-done((f32[192,128]{1,0:T(8,128)S(1)}, f32[192,128]{1,0:T(8,128)S(1)}, u32[]{:S(2)}, u32[]{:S(2)}) %collective-permute-start.25) | collective-permute-done | bytes 98336 | tf_op jit(solution)/shard_map/ppermute | solution.py:320
  133.6 4.6 %collective-permute-done.26 = f32[192,128]{1,0:T(8,128)S(1)} collective-permute-done((f32[192,128]{1,0:T(8,128)S(1)}, f32[192,128]{1,0:T(8,128)S(1)}, u32[]{:S(2)}, u32[]{:S(2)}) %collective-permute-start.26) | collective-permute-done | bytes 98336 | tf_op jit(solution)/shard_map/ppermute | solution.py:320
  138.2 7.8 %collective-permute-start.27 = (f32[192,128]{1,0:T(8,128)S(1)}, f32[192,128]{1,0:T(8,128)S(1)}, u32[]{:S(2)}, u32[]{:S(2)}) collective-permute-start(f32[192,128]{1,0:T(8,128)S(1)} %multiply_add_fusion), channel_id=1, source_target_pairs={{0,24},{8,16},{16,8},{24,0},{32,56},{40,48},{48,40},{56,32},{64,88... | collective-permute-start | bytes 294920 | tf_op jit(solution)/shard_map/ppermute | solution.py:320
  146.0 2.2 %collective-permute-start.29 = (f32[192,128]{1,0:T(8,128)S(1)}, f32[192,128]{1,0:T(8,128)S(1)}, u32[]{:S(2)}, u32[]{:S(2)}) collective-permute-start(f32[192,128]{1,0:T(8,128)S(1)} %multiply_add_fusion), channel_id=1, source_target_pairs={{0,8},{8,0},{16,24},{24,16},{32,40},{40,32},{48,56},{56,48},{64,72... | collective-permute-start | bytes 294920 | tf_op jit(solution)/shard_map/ppermute | solution.py:320
  148.6 3.5 %collective-permute-done.28 = f32[192,128]{1,0:T(8,128)S(1)} collective-permute-done((f32[192,128]{1,0:T(8,128)S(1)}, f32[192,128]{1,0:T(8,128)S(1)}, u32[]{:S(2)}, u32[]{:S(2)}) %collective-permute-start.28) | collective-permute-done | bytes 98336 | tf_op jit(solution)/shard_map/ppermute | solution.py:320
  (48 shorter events, 15.2 us)
Async XLA Ops:
  7.5 1.3 collective-permute-start
  8.9 7.0 %collective-permute-start.1 = (f32[128,128]{1,0:T(8,128)S(1)}, f32[128,128]{1,0:T(8,128)S(1)}, u32[]{:S(2)}, u32[]{:S(2)}) collective-permute-start(f32[128,128]{1,0:T(8,128)S(1)} %multiply_add_fusion.11.refs_0_), channel_id=1, source_target_pairs={{0,6},{1,7},{2,4},{3,5},{4,2},{5,3},{6,0},{7,1},{8,14},{9,15},{10,... | collective-permute-start | bytes 196616 | tf_op jit(solution)/shard_map/ppermute | solution.py:320
  9.9 5.9 %collective-permute-start.2 = (f32[128,128]{1,0:T(8,128)S(1)}, f32[128,128]{1,0:T(8,128)S(1)}, u32[]{:S(2)}, u32[]{:S(2)}) collective-permute-start(f32[128,128]{1,0:T(8,128)S(1)} %multiply_add_fusion.11.refs_0_), channel_id=1, source_target_pairs={{0,4},{1,5},{2,6},{3,7},{4,0},{5,1},{6,2},{7,3},{8,12},{9,13},{10,... | collective-permute-start | bytes 196616 | tf_op jit(solution)/shard_map/ppermute | solution.py:320
  13.0 4.3 %collective-permute-start.3 = (f32[128,128]{1,0:T(8,128)S(1)}, f32[128,128]{1,0:T(8,128)S(1)}, u32[]{:S(2)}, u32[]{:S(2)}) collective-permute-start(f32[128,128]{1,0:T(8,128)S(1)} %multiply_add_fusion.11.refs_0_), channel_id=1, source_target_pairs={{0,2},{1,3},{2,0},{3,1},{4,6},{5,7},{6,4},{7,5},{8,10},{9,11},{10,... | collective-permute-start | bytes 196616 | tf_op jit(solution)/shard_map/ppermute | solution.py:320
  23.6 9.9 %collective-permute-start.4 = (f32[192,128]{1,0:T(8,128)S(1)}, f32[192,128]{1,0:T(8,128)S(1)}, u32[]{:S(2)}, u32[]{:S(2)}) collective-permute-start(f32[192,128]{1,0:T(8,128)S(1)} %get-tuple-element.27), channel_id=1, source_target_pairs={{0,224},{8,232},{16,240},{24,248},{32,192},{40,200},{48,208},{56,2... | collective-permute-start | bytes 294920 | tf_op jit(solution)/shard_map/ppermute | solution.py:320
  33.5 6.7 %collective-permute-start.5 = (f32[192,128]{1,0:T(8,128)S(1)}, f32[192,128]{1,0:T(8,128)S(1)}, u32[]{:S(2)}, u32[]{:S(2)}) collective-permute-start(f32[192,128]{1,0:T(8,128)S(1)} %multiply_add_fusion.8), channel_id=1, source_target_pairs={{0,96},{8,104},{16,112},{24,120},{32,64},{40,72},{48,80},{56,88},{... | collective-permute-start | bytes 294920 | tf_op jit(solution)/shard_map/ppermute | solution.py:320
  40.3 4.7 %collective-permute-start.6 = (f32[192,128]{1,0:T(8,128)S(1)}, f32[192,128]{1,0:T(8,128)S(1)}, u32[]{:S(2)}, u32[]{:S(2)}) collective-permute-start(f32[192,128]{1,0:T(8,128)S(1)} %multiply_add_fusion.7), channel_id=1, source_target_pairs={{0,32},{8,40},{16,48},{24,56},{32,0},{40,8},{48,16},{56,24},{64,96... | collective-permute-start | bytes 294920 | tf_op jit(solution)/shard_map/ppermute | solution.py:320
  45.0 4.7 %collective-permute-start.7 = (f32[192,128]{1,0:T(8,128)S(1)}, f32[192,128]{1,0:T(8,128)S(1)}, u32[]{:S(2)}, u32[]{:S(2)}) collective-permute-start(f32[192,128]{1,0:T(8,128)S(1)} %multiply_add_fusion.6.refs_1_), channel_id=1, source_target_pairs={{0,24},{8,16},{16,8},{24,0},{32,56},{40,48},{48,40},{56,32},{64,88... | collective-permute-start | bytes 294920 | tf_op jit(solution)/shard_map/ppermute | solution.py:320
  45.1 6.2 %collective-permute-start.8 = (f32[192,128]{1,0:T(8,128)S(1)}, f32[192,128]{1,0:T(8,128)S(1)}, u32[]{:S(2)}, u32[]{:S(2)}) collective-permute-start(f32[192,128]{1,0:T(8,128)S(1)} %multiply_add_fusion.6.refs_1_), channel_id=1, source_target_pairs={{0,16},{8,24},{16,0},{24,8},{32,48},{40,56},{48,32},{56,40},{64,80... | collective-permute-start | bytes 294920 | tf_op jit(solution)/shard_map/ppermute | solution.py:320
  46.6 6.3 %collective-permute-start.9 = (f32[192,128]{1,0:T(8,128)S(1)}, f32[192,128]{1,0:T(8,128)S(1)}, u32[]{:S(2)}, u32[]{:S(2)}) collective-permute-start(f32[192,128]{1,0:T(8,128)S(1)} %multiply_add_fusion.6.refs_1_), channel_id=1, source_target_pairs={{0,8},{8,0},{16,24},{24,16},{32,40},{40,32},{48,56},{56,48},{64,72... | collective-permute-start | bytes 294920 | tf_op jit(solution)/shard_map/ppermute | solution.py:320
  59.2 1.3 collective-permute-start.10
  60.6 6.9 %collective-permute-start.11 = (f32[128,128]{1,0:T(8,128)S(1)}, f32[128,128]{1,0:T(8,128)S(1)}, u32[]{:S(2)}, u32[]{:S(2)}) collective-permute-start(f32[128,128]{1,0:T(8,128)S(1)} %multiply_add_fusion.10.refs_1_), channel_id=1, source_target_pairs={{0,6},{1,7},{2,4},{3,5},{4,2},{5,3},{6,0},{7,1},{8,14},{9,15},{10,... | collective-permute-start | bytes 196616 | tf_op jit(solution)/shard_map/ppermute | solution.py:320
  60.7 6.8 %collective-permute-start.12 = (f32[128,128]{1,0:T(8,128)S(1)}, f32[128,128]{1,0:T(8,128)S(1)}, u32[]{:S(2)}, u32[]{:S(2)}) collective-permute-start(f32[128,128]{1,0:T(8,128)S(1)} %multiply_add_fusion.10.refs_1_), channel_id=1, source_target_pairs={{0,4},{1,5},{2,6},{3,7},{4,0},{5,1},{6,2},{7,3},{8,12},{9,13},{10,... | collective-permute-start | bytes 196616 | tf_op jit(solution)/shard_map/ppermute | solution.py:320
  60.8 7.2 %collective-permute-start.13 = (f32[128,128]{1,0:T(8,128)S(1)}, f32[128,128]{1,0:T(8,128)S(1)}, u32[]{:S(2)}, u32[]{:S(2)}) collective-permute-start(f32[128,128]{1,0:T(8,128)S(1)} %multiply_add_fusion.10.refs_1_), channel_id=1, source_target_pairs={{0,2},{1,3},{2,0},{3,1},{4,6},{5,7},{6,4},{7,5},{8,10},{9,11},{10,... | collective-permute-start | bytes 196616 | tf_op jit(solution)/shard_map/ppermute | solution.py:320
  74.3 5.9 %collective-permute-start.14 = (f32[192,128]{1,0:T(8,128)S(1)}, f32[192,128]{1,0:T(8,128)S(1)}, u32[]{:S(2)}, u32[]{:S(2)}) collective-permute-start(f32[192,128]{1,0:T(8,128)S(1)} %get-tuple-element.31), channel_id=1, source_target_pairs={{0,224},{8,232},{16,240},{24,248},{32,192},{40,200},{48,208},{56,2... | collective-permute-start | bytes 294920 | tf_op jit(solution)/shard_map/ppermute | solution.py:320
  80.3 6.6 %collective-permute-start.15 = (f32[192,128]{1,0:T(8,128)S(1)}, f32[192,128]{1,0:T(8,128)S(1)}, u32[]{:S(2)}, u32[]{:S(2)}) collective-permute-start(f32[192,128]{1,0:T(8,128)S(1)} %multiply_add_fusion.5), channel_id=1, source_target_pairs={{0,96},{8,104},{16,112},{24,120},{32,64},{40,72},{48,80},{56,88},{... | collective-permute-start | bytes 294920 | tf_op jit(solution)/shard_map/ppermute | solution.py:320
  86.9 4.7 %collective-permute-start.16 = (f32[192,128]{1,0:T(8,128)S(1)}, f32[192,128]{1,0:T(8,128)S(1)}, u32[]{:S(2)}, u32[]{:S(2)}) collective-permute-start(f32[192,128]{1,0:T(8,128)S(1)} %multiply_add_fusion.4), channel_id=1, source_target_pairs={{0,32},{8,40},{16,48},{24,56},{32,0},{40,8},{48,16},{56,24},{64,96... | collective-permute-start | bytes 294920 | tf_op jit(solution)/shard_map/ppermute | solution.py:320
  91.7 7.2 %collective-permute-start.17 = (f32[192,128]{1,0:T(8,128)S(1)}, f32[192,128]{1,0:T(8,128)S(1)}, u32[]{:S(2)}, u32[]{:S(2)}) collective-permute-start(f32[192,128]{1,0:T(8,128)S(1)} %multiply_add_fusion.3.refs_1_), channel_id=1, source_target_pairs={{0,24},{8,16},{16,8},{24,0},{32,56},{40,48},{48,40},{56,32},{64,88... | collective-permute-start | bytes 294920 | tf_op jit(solution)/shard_map/ppermute | solution.py:320
  96.3 6.1 %collective-permute-start.18 = (f32[192,128]{1,0:T(8,128)S(1)}, f32[192,128]{1,0:T(8,128)S(1)}, u32[]{:S(2)}, u32[]{:S(2)}) collective-permute-start(f32[192,128]{1,0:T(8,128)S(1)} %multiply_add_fusion.3.refs_1_), channel_id=1, source_target_pairs={{0,16},{8,24},{16,0},{24,8},{32,48},{40,56},{48,32},{56,40},{64,80... | collective-permute-start | bytes 294920 | tf_op jit(solution)/shard_map/ppermute | solution.py:320
  96.3 6.1 %collective-permute-start.19 = (f32[192,128]{1,0:T(8,128)S(1)}, f32[192,128]{1,0:T(8,128)S(1)}, u32[]{:S(2)}, u32[]{:S(2)}) collective-permute-start(f32[192,128]{1,0:T(8,128)S(1)} %multiply_add_fusion.3.refs_1_), channel_id=1, source_target_pairs={{0,8},{8,0},{16,24},{24,16},{32,40},{40,32},{48,56},{56,48},{64,72... | collective-permute-start | bytes 294920 | tf_op jit(solution)/shard_map/ppermute | solution.py:320
  104.0 1.3 collective-permute-start.20
  105.4 5.6 %collective-permute-start.21 = (f32[128,128]{1,0:T(8,128)S(1)}, f32[128,128]{1,0:T(8,128)S(1)}, u32[]{:S(2)}, u32[]{:S(2)}) collective-permute-start(f32[128,128]{1,0:T(8,128)S(1)} %multiply_add_fusion.9.refs_1_), channel_id=1, source_target_pairs={{0,6},{1,7},{2,4},{3,5},{4,2},{5,3},{6,0},{7,1},{8,14},{9,15},{10,... | collective-permute-start | bytes 196616 | tf_op jit(solution)/shard_map/ppermute | solution.py:320
  107.2 6.1 %collective-permute-start.22 = (f32[128,128]{1,0:T(8,128)S(1)}, f32[128,128]{1,0:T(8,128)S(1)}, u32[]{:S(2)}, u32[]{:S(2)}) collective-permute-start(f32[128,128]{1,0:T(8,128)S(1)} %multiply_add_fusion.9.refs_1_), channel_id=1, source_target_pairs={{0,4},{1,5},{2,6},{3,7},{4,0},{5,1},{6,2},{7,3},{8,12},{9,13},{10,... | collective-permute-start | bytes 196616 | tf_op jit(solution)/shard_map/ppermute | solution.py:320
  107.2 6.1 %collective-permute-start.23 = (f32[128,128]{1,0:T(8,128)S(1)}, f32[128,128]{1,0:T(8,128)S(1)}, u32[]{:S(2)}, u32[]{:S(2)}) collective-permute-start(f32[128,128]{1,0:T(8,128)S(1)} %multiply_add_fusion.9.refs_1_), channel_id=1, source_target_pairs={{0,2},{1,3},{2,0},{3,1},{4,6},{5,7},{6,4},{7,5},{8,10},{9,11},{10,... | collective-permute-start | bytes 196616 | tf_op jit(solution)/shard_map/ppermute | solution.py:320
  119.6 6.2 %collective-permute-start.24 = (f32[192,128]{1,0:T(8,128)S(1)}, f32[192,128]{1,0:T(8,128)S(1)}, u32[]{:S(2)}, u32[]{:S(2)}) collective-permute-start(f32[192,128]{1,0:T(8,128)S(1)} %get-tuple-element.35), channel_id=1, source_target_pairs={{0,224},{8,232},{16,240},{24,248},{32,192},{40,200},{48,208},{56,2... | collective-permute-start | bytes 294920 | tf_op jit(solution)/shard_map/ppermute | solution.py:320
  125.8 7.6 %collective-permute-start.25 = (f32[192,128]{1,0:T(8,128)S(1)}, f32[192,128]{1,0:T(8,128)S(1)}, u32[]{:S(2)}, u32[]{:S(2)}) collective-permute-start(f32[192,128]{1,0:T(8,128)S(1)} %multiply_add_fusion.2), channel_id=1, source_target_pairs={{0,96},{8,104},{16,112},{24,120},{32,64},{40,72},{48,80},{56,88},{... | collective-permute-start | bytes 294920 | tf_op jit(solution)/shard_map/ppermute | solution.py:320
  133.5 4.7 %collective-permute-start.26 = (f32[192,128]{1,0:T(8,128)S(1)}, f32[192,128]{1,0:T(8,128)S(1)}, u32[]{:S(2)}, u32[]{:S(2)}) collective-permute-start(f32[192,128]{1,0:T(8,128)S(1)} %multiply_add_fusion.1), channel_id=1, source_target_pairs={{0,32},{8,40},{16,48},{24,56},{32,0},{40,8},{48,16},{56,24},{64,96... | collective-permute-start | bytes 294920 | tf_op jit(solution)/shard_map/ppermute | solution.py:320
  138.2 10.4 %collective-permute-start.27 = (f32[192,128]{1,0:T(8,128)S(1)}, f32[192,128]{1,0:T(8,128)S(1)}, u32[]{:S(2)}, u32[]{:S(2)}) collective-permute-start(f32[192,128]{1,0:T(8,128)S(1)} %multiply_add_fusion), channel_id=1, source_target_pairs={{0,24},{8,16},{16,8},{24,0},{32,56},{40,48},{48,40},{56,32},{64,88... | collective-permute-start | bytes 294920 | tf_op jit(solution)/shard_map/ppermute | solution.py:320
  146.0 6.1 %collective-permute-start.28 = (f32[192,128]{1,0:T(8,128)S(1)}, f32[192,128]{1,0:T(8,128)S(1)}, u32[]{:S(2)}, u32[]{:S(2)}) collective-permute-start(f32[192,128]{1,0:T(8,128)S(1)} %multiply_add_fusion), channel_id=1, source_target_pairs={{0,16},{8,24},{16,0},{24,8},{32,48},{40,56},{48,32},{56,40},{64,80... | collective-permute-start | bytes 294920 | tf_op jit(solution)/shard_map/ppermute | solution.py:320
  146.0 6.1 %collective-permute-start.29 = (f32[192,128]{1,0:T(8,128)S(1)}, f32[192,128]{1,0:T(8,128)S(1)}, u32[]{:S(2)}, u32[]{:S(2)}) collective-permute-start(f32[192,128]{1,0:T(8,128)S(1)} %multiply_add_fusion), channel_id=1, source_target_pairs={{0,8},{8,0},{16,24},{24,16},{32,40},{40,32},{48,56},{56,48},{64,72... | collective-permute-start | bytes 294920 | tf_op jit(solution)/shard_map/ppermute | solution.py:320

commit v8 on v7

--- a/solution.py
+++ b/solution.py
@@ -315,27 +315,33 @@
     )(tiles, counts, cost, *operands)
 
 
-def swap(value, axis, flip):
-    size = lax.axis_size(axis)
-    return lax.ppermute(value, axis, [(k, k ^ flip) for k in range(size)])
-
-
-def fan(value, axis, flips):
-    return [value, *[swap(value, axis, flip) for flip in flips]]
+def swap(value, axis, flips):
+    src, tgt = lax.axis_size("src"), lax.axis_size("tgt")
+    pairs = []
+    for s in range(src):
+        for t in range(tgt):
+            flip = flips[t % 2]
+            other = (s ^ flip, t) if axis == "src" else (s, t ^ flip)
+            pairs.append((s * tgt + t, other[0] * tgt + other[1]))
+    return lax.ppermute(value, ("src", "tgt"), pairs)
+
+
+def fan(value, axis, *flips):
+    return [value, *[swap(value, axis, each) for each in flips]]
 
 
 def over_core(value):
-    return lse2_many(fan(value, "tgt", (1,)))
+    return lse2_many(fan(value, "tgt", (1, 1)))
 
 
 def over_y(value):
-    return fan(value, "tgt", (6, 4, 2))
+    return fan(value, "tgt", (6, 4), (4, 6), (2, 2))
 
 
 def over_src(value):
-    for flip in (28, 12, 4):
-        value = lse2_many(fan(value, "src", (flip,)))
-    return fan(value, "src", (3, 2, 1))
+    for flips in ((28, 12), (12, 28), (4, 4)):
+        value = lse2_many(fan(value, "src", flips))
+    return fan(value, "src", (3, 2), (2, 3), (1, 1))
 
 
 def body(src_points, tgt_points, tiles, counts):

time: 153 us -> 153 us (level)
  the two profiles are of different devices: /device:TPU:2 before, /device:TPU:40 now
where the time goes in v8:
time: 153 us; the launch traced here: 154 us
  starting transfers between devices  69.4 us (45%)
  waiting for transfers between devices  62.4 us (41%)
  Pallas kernels  19.3 us (13%)
    ppermute x30, starting transfers between devices, swap(): return lax.ppermute(value, ('src', 'tgt'), pairs)  69.4 us
    ppermute x30, waiting for transfers between devices, swap(): return lax.ppermute(value, ('src', 'tgt'), pairs)  62.4 us
    pallas_call x5, Pallas kernels, sweep(): pl.pallas_call(kernel, out_shape=(jax.ShapeDtypeStruct((2 * blocks_out, H...  13.5 us
    pallas_call x1, Pallas kernels, costs(): pl.pallas_call(functools.partial(cost_kernel, blocks_in, blocks_out), out...  4.78 us
  transfers between devices with their start and end apart: 30, of which 27 were waited for; matrix products, arithmetic and copies ran while one was open for 0% of the time, Pallas kernels for 1%

profile of v8, /device:TPU:40, one launch (start us, length us, event | category | flops | bytes accessed | tf_op | source)
XLA Modules:
  0.0 154.0 jit_solution(5517370601411442981)
XLA Ops:
  1.3 4.8 %shard_map.59 = (f32[32,256,256]{2,1,0:T(8,128)S(1)}, f32[128,128]{1,0:T(8,128)S(1)}, bf16[32,128,256]{2,1,0:T(8,128)(2,1)S(1)}, bf16[32,128,256]{2,1,0:T(8,128)(2,1)S(1)}, s32[2,32]{1,0:T(2,128)S(4)}) custom-call(s32[2,32]{1,0:T(2,128)} %bitcast.4, s32[1,1]{1,0:T(1,128)S(6)} %copy.6.counts, f32[50,16384]{1,0:T(8,128)} %src.1, f32[50,24576]{1,0:T(8,128)} %tgt.1), custom_call_target="tpu_custom_call" | custom-call | tf_op jit(solution)/shard_map/pallas_call | solution.py:255
  8.5 3.2 %collective-permute-start.2 = (f32[128,128]{1,0:T(8,128)S(1)}, f32[128,128]{1,0:T(8,128)S(1)}, u32[]{:S(2)}, u32[]{:S(2)}) collective-permute-start(f32[128,128]{1,0:T(8,128)S(1)} %multiply_add_fusion.11.refs_0_), channel_id=1, source_target_pairs={{0,4},{1,7},{2,6},{3,5},{4,0},{5,3},{6,2},{7,1},{8,12},{9,15},{10,... | collective-permute-start | bytes 196616 | tf_op jit(solution)/shard_map/ppermute | solution.py:326
  14.3 2.1 %collective-permute-done.3.refs_3_ = f32[128,128]{1,0:T(8,128)S(1)} collective-permute-done((f32[128,128]{1,0:T(8,128)S(1)}, f32[128,128]{1,0:T(8,128)S(1)}, u32[]{:S(2)}, u32[]{:S(2)}) %collective-permute-start.3) | collective-permute-done | bytes 65568 | tf_op jit(solution)/shard_map/ppermute | solution.py:326
  16.3 3.9 %shard_map.61 = (f32[192,128]{1,0:T(8,128)S(1)}, f32[128,128]{1,0:T(8,128)S(1)}) custom-call(s32[2,32]{1,0:T(2,128)S(4)} %get-tuple-element.19.tiles, s32[1,1]{1,0:T(1,128)S(6)} %copy.6.counts, f32[32,256,256]{2,1,0:T(8,128)S(1)} %shard_map.60.cost, f32[128,128]{1,0:T(8,128)S(1)} %multiply_add_fusion.11.refs_0_, ...), custom_call_target="tpu_custom_call" | custom-call | tf_op jit(solution)/shard_map/pallas_call | solution.py:300
  20.3 10.6 %collective-permute-start.4 = (f32[192,128]{1,0:T(8,128)S(1)}, f32[192,128]{1,0:T(8,128)S(1)}, u32[]{:S(2)}, u32[]{:S(2)}) collective-permute-start(f32[192,128]{1,0:T(8,128)S(1)} %get-tuple-element.27), channel_id=1, source_target_pairs={{0,224},{1,97},{2,226},{3,99},{4,228},{5,101},{6,230},{7,103},{8,2... | collective-permute-start | bytes 294920 | tf_op jit(solution)/shard_map/ppermute | solution.py:326
  30.8 3.2 %collective-permute-done.4 = f32[192,128]{1,0:T(8,128)S(1)} collective-permute-done((f32[192,128]{1,0:T(8,128)S(1)}, f32[192,128]{1,0:T(8,128)S(1)}, u32[]{:S(2)}, u32[]{:S(2)}) %collective-permute-start.4) | collective-permute-done | bytes 98336 | tf_op jit(solution)/shard_map/ppermute | solution.py:326
  34.1 4.6 %collective-permute-done.5 = f32[192,128]{1,0:T(8,128)S(1)} collective-permute-done((f32[192,128]{1,0:T(8,128)S(1)}, f32[192,128]{1,0:T(8,128)S(1)}, u32[]{:S(2)}, u32[]{:S(2)}) %collective-permute-start.5) | collective-permute-done | bytes 98336 | tf_op jit(solution)/shard_map/ppermute | solution.py:326
  38.9 4.6 %collective-permute-done.6 = f32[192,128]{1,0:T(8,128)S(1)} collective-permute-done((f32[192,128]{1,0:T(8,128)S(1)}, f32[192,128]{1,0:T(8,128)S(1)}, u32[]{:S(2)}, u32[]{:S(2)}) %collective-permute-start.6) | collective-permute-done | bytes 98336 | tf_op jit(solution)/shard_map/ppermute | solution.py:326
  43.6 2.0 %collective-permute-start.7 = (f32[192,128]{1,0:T(8,128)S(1)}, f32[192,128]{1,0:T(8,128)S(1)}, u32[]{:S(2)}, u32[]{:S(2)}) collective-permute-start(f32[192,128]{1,0:T(8,128)S(1)} %multiply_add_fusion.6.refs_1_), channel_id=1, source_target_pairs={{0,24},{1,17},{2,26},{3,19},{4,28},{5,21},{6,30},{7,23},{8,16},{9,... | collective-permute-start | bytes 294920 | tf_op jit(solution)/shard_map/ppermute | solution.py:326
  45.6 2.4 %collective-permute-start.8 = (f32[192,128]{1,0:T(8,128)S(1)}, f32[192,128]{1,0:T(8,128)S(1)}, u32[]{:S(2)}, u32[]{:S(2)}) collective-permute-start(f32[192,128]{1,0:T(8,128)S(1)} %multiply_add_fusion.6.refs_1_), channel_id=1, source_target_pairs={{0,16},{1,25},{2,18},{3,27},{4,20},{5,29},{6,22},{7,31},{8,24},{9,... | collective-permute-start | bytes 294920 | tf_op jit(solution)/shard_map/ppermute | solution.py:326
  48.0 1.4 collective-permute-done.7.refs_2_
  49.5 2.2 %collective-permute-done.8.refs_3_ = f32[192,128]{1,0:T(8,128)S(1)} collective-permute-done((f32[192,128]{1,0:T(8,128)S(1)}, f32[192,128]{1,0:T(8,128)S(1)}, u32[]{:S(2)}, u32[]{:S(2)}) %collective-permute-start.8) | collective-permute-done | bytes 98336 | tf_op jit(solution)/shard_map/ppermute | solution.py:326
  55.0 1.5 collective-permute-start.12
  56.5 2.6 %collective-permute-start.13 = (f32[128,128]{1,0:T(8,128)S(1)}, f32[128,128]{1,0:T(8,128)S(1)}, u32[]{:S(2)}, u32[]{:S(2)}) collective-permute-start(f32[128,128]{1,0:T(8,128)S(1)} %multiply_add_fusion.10.refs_1_), channel_id=1, source_target_pairs={{0,2},{1,3},{2,0},{3,1},{4,6},{5,7},{6,4},{7,5},{8,10},{9,11},{10,... | collective-permute-start | bytes 196616 | tf_op jit(solution)/shard_map/ppermute | solution.py:326
  59.1 1.3 collective-permute-done.11.refs_2_
  62.3 3.9 %shard_map.63 = (f32[192,128]{1,0:T(8,128)S(1)}, f32[128,128]{1,0:T(8,128)S(1)}) custom-call(s32[2,32]{1,0:T(2,128)S(4)} %get-tuple-element.19.tiles, s32[1,1]{1,0:T(1,128)S(6)} %copy.6.counts, f32[32,256,256]{2,1,0:T(8,128)S(1)} %shard_map.60.cost, f32[192,128]{1,0:T(8,128)S(1)} %get-tuple-element.28.refs_0_, f32[128,128]{1,0:T(8,128)S(1)} %multiply_add_fusion.10.refs_1_, ...), custom_call_target="tpu_custom_call" | custom-call | tf_op jit(solution)/shard_map/pallas_call | solution.py:300
  66.2 15.6 %collective-permute-start.14 = (f32[192,128]{1,0:T(8,128)S(1)}, f32[192,128]{1,0:T(8,128)S(1)}, u32[]{:S(2)}, u32[]{:S(2)}) collective-permute-start(f32[192,128]{1,0:T(8,128)S(1)} %get-tuple-element.31), channel_id=1, source_target_pairs={{0,224},{1,97},{2,226},{3,99},{4,228},{5,101},{6,230},{7,103},{8,2... | collective-permute-start | bytes 294920 | tf_op jit(solution)/shard_map/ppermute | solution.py:326
  81.8 3.6 %collective-permute-done.14 = f32[192,128]{1,0:T(8,128)S(1)} collective-permute-done((f32[192,128]{1,0:T(8,128)S(1)}, f32[192,128]{1,0:T(8,128)S(1)}, u32[]{:S(2)}, u32[]{:S(2)}) %collective-permute-start.14) | collective-permute-done | bytes 98336 | tf_op jit(solution)/shard_map/ppermute | solution.py:326
  85.6 4.6 %collective-permute-done.15 = f32[192,128]{1,0:T(8,128)S(1)} collective-permute-done((f32[192,128]{1,0:T(8,128)S(1)}, f32[192,128]{1,0:T(8,128)S(1)}, u32[]{:S(2)}, u32[]{:S(2)}) %collective-permute-start.15) | collective-permute-done | bytes 98336 | tf_op jit(solution)/shard_map/ppermute | solution.py:326
  90.3 4.6 %collective-permute-done.16 = f32[192,128]{1,0:T(8,128)S(1)} collective-permute-done((f32[192,128]{1,0:T(8,128)S(1)}, f32[192,128]{1,0:T(8,128)S(1)}, u32[]{:S(2)}, u32[]{:S(2)}) %collective-permute-start.16) | collective-permute-done | bytes 98336 | tf_op jit(solution)/shard_map/ppermute | solution.py:326
  95.2 4.0 %collective-permute-start.19 = (f32[192,128]{1,0:T(8,128)S(1)}, f32[192,128]{1,0:T(8,128)S(1)}, u32[]{:S(2)}, u32[]{:S(2)}) collective-permute-start(f32[192,128]{1,0:T(8,128)S(1)} %multiply_add_fusion.3.refs_1_), channel_id=1, source_target_pairs={{0,8},{1,9},{2,10},{3,11},{4,12},{5,13},{6,14},{7,15},{8,0},{9,1},... | collective-permute-start | bytes 294920 | tf_op jit(solution)/shard_map/ppermute | solution.py:326
  99.2 2.8 %collective-permute-done.17.refs_2_ = f32[192,128]{1,0:T(8,128)S(1)} collective-permute-done((f32[192,128]{1,0:T(8,128)S(1)}, f32[192,128]{1,0:T(8,128)S(1)}, u32[]{:S(2)}, u32[]{:S(2)}) %collective-permute-start.17) | collective-permute-done | bytes 98336 | tf_op jit(solution)/shard_map/ppermute | solution.py:326
  105.2 1.3 collective-permute-start.22
  106.5 2.8 %collective-permute-start.23 = (f32[128,128]{1,0:T(8,128)S(1)}, f32[128,128]{1,0:T(8,128)S(1)}, u32[]{:S(2)}, u32[]{:S(2)}) collective-permute-start(f32[128,128]{1,0:T(8,128)S(1)} %multiply_add_fusion.9.refs_1_), channel_id=1, source_target_pairs={{0,2},{1,3},{2,0},{3,1},{4,6},{5,7},{6,4},{7,5},{8,10},{9,11},{10,... | collective-permute-start | bytes 196616 | tf_op jit(solution)/shard_map/ppermute | solution.py:326
  109.3 1.9 %collective-permute-done.21.refs_2_ = f32[128,128]{1,0:T(8,128)S(1)} collective-permute-done((f32[128,128]{1,0:T(8,128)S(1)}, f32[128,128]{1,0:T(8,128)S(1)}, u32[]{:S(2)}, u32[]{:S(2)}) %collective-permute-start.21) | collective-permute-done | bytes 65568 | tf_op jit(solution)/shard_map/ppermute | solution.py:326
  112.4 3.9 %shard_map.65 = (f32[192,128]{1,0:T(8,128)S(1)}, f32[128,128]{1,0:T(8,128)}) custom-call(s32[2,32]{1,0:T(2,128)S(4)} %get-tuple-element.19.tiles, s32[1,1]{1,0:T(1,128)S(6)} %copy.6.counts, f32[32,256,256]{2,1,0:T(8,128)S(1)} %shard_map.60.cost, f32[192,128]{1,0:T(8,128)S(1)} %get-tuple-element.32.refs_0_, f32[128,128]{1,0:T(8,128)S(1)} %multiply_add_fusion.9.refs_1_, ...), custom_call_target="tpu_custom_call" | custom-call | tf_op jit(solution)/shard_map/pallas_call | solution.py:300
  116.4 16.0 %collective-permute-start.24 = (f32[192,128]{1,0:T(8,128)S(1)}, f32[192,128]{1,0:T(8,128)S(1)}, u32[]{:S(2)}, u32[]{:S(2)}) collective-permute-start(f32[192,128]{1,0:T(8,128)S(1)} %get-tuple-element.35), channel_id=1, source_target_pairs={{0,224},{1,97},{2,226},{3,99},{4,228},{5,101},{6,230},{7,103},{8,2... | collective-permute-start | bytes 294920 | tf_op jit(solution)/shard_map/ppermute | solution.py:326
  132.4 3.4 %collective-permute-done.24 = f32[192,128]{1,0:T(8,128)S(1)} collective-permute-done((f32[192,128]{1,0:T(8,128)S(1)}, f32[192,128]{1,0:T(8,128)S(1)}, u32[]{:S(2)}, u32[]{:S(2)}) %collective-permute-start.24) | collective-permute-done | bytes 98336 | tf_op jit(solution)/shard_map/ppermute | solution.py:326
  136.0 4.6 %collective-permute-done.25 = f32[192,128]{1,0:T(8,128)S(1)} collective-permute-done((f32[192,128]{1,0:T(8,128)S(1)}, f32[192,128]{1,0:T(8,128)S(1)}, u32[]{:S(2)}, u32[]{:S(2)}) %collective-permute-start.25) | collective-permute-done | bytes 98336 | tf_op jit(solution)/shard_map/ppermute | solution.py:326
  140.8 4.6 %collective-permute-done.26 = f32[192,128]{1,0:T(8,128)S(1)} collective-permute-done((f32[192,128]{1,0:T(8,128)S(1)}, f32[192,128]{1,0:T(8,128)S(1)}, u32[]{:S(2)}, u32[]{:S(2)}) %collective-permute-start.26) | collective-permute-done | bytes 98336 | tf_op jit(solution)/shard_map/ppermute | solution.py:326
  145.6 4.0 %collective-permute-start.29 = (f32[192,128]{1,0:T(8,128)S(1)}, f32[192,128]{1,0:T(8,128)S(1)}, u32[]{:S(2)}, u32[]{:S(2)}) collective-permute-start(f32[192,128]{1,0:T(8,128)S(1)} %multiply_add_fusion), channel_id=1, source_target_pairs={{0,8},{1,9},{2,10},{3,11},{4,12},{5,13},{6,14},{7,15},{8,0},{9,1},... | collective-permute-start | bytes 294920 | tf_op jit(solution)/shard_map/ppermute | solution.py:326
  149.6 2.8 %collective-permute-done.27 = f32[192,128]{1,0:T(8,128)S(1)} collective-permute-done((f32[192,128]{1,0:T(8,128)S(1)}, f32[192,128]{1,0:T(8,128)S(1)}, u32[]{:S(2)}, u32[]{:S(2)}) %collective-permute-start.27) | collective-permute-done | bytes 98336 | tf_op jit(solution)/shard_map/ppermute | solution.py:326
  (48 shorter events, 17.7 us)
Async XLA Ops:
  6.1 1.3 collective-permute-start
  7.5 6.2 %collective-permute-start.1 = (f32[128,128]{1,0:T(8,128)S(1)}, f32[128,128]{1,0:T(8,128)S(1)}, u32[]{:S(2)}, u32[]{:S(2)}) collective-permute-start(f32[128,128]{1,0:T(8,128)S(1)} %multiply_add_fusion.11.refs_0_), channel_id=1, source_target_pairs={{0,6},{1,5},{2,4},{3,7},{4,2},{5,1},{6,0},{7,3},{8,14},{9,13},{10,... | collective-permute-start | bytes 196616 | tf_op jit(solution)/shard_map/ppermute | solution.py:326
  8.5 5.8 %collective-permute-start.2 = (f32[128,128]{1,0:T(8,128)S(1)}, f32[128,128]{1,0:T(8,128)S(1)}, u32[]{:S(2)}, u32[]{:S(2)}) collective-permute-start(f32[128,128]{1,0:T(8,128)S(1)} %multiply_add_fusion.11.refs_0_), channel_id=1, source_target_pairs={{0,4},{1,7},{2,6},{3,5},{4,0},{5,3},{6,2},{7,1},{8,12},{9,15},{10,... | collective-permute-start | bytes 196616 | tf_op jit(solution)/shard_map/ppermute | solution.py:326
  11.7 4.7 %collective-permute-start.3 = (f32[128,128]{1,0:T(8,128)S(1)}, f32[128,128]{1,0:T(8,128)S(1)}, u32[]{:S(2)}, u32[]{:S(2)}) collective-permute-start(f32[128,128]{1,0:T(8,128)S(1)} %multiply_add_fusion.11.refs_0_), channel_id=1, source_target_pairs={{0,2},{1,3},{2,0},{3,1},{4,6},{5,7},{6,4},{7,5},{8,10},{9,11},{10,... | collective-permute-start | bytes 196616 | tf_op jit(solution)/shard_map/ppermute | solution.py:326
  20.3 13.7 %collective-permute-start.4 = (f32[192,128]{1,0:T(8,128)S(1)}, f32[192,128]{1,0:T(8,128)S(1)}, u32[]{:S(2)}, u32[]{:S(2)}) collective-permute-start(f32[192,128]{1,0:T(8,128)S(1)} %get-tuple-element.27), channel_id=1, source_target_pairs={{0,224},{1,97},{2,226},{3,99},{4,228},{5,101},{6,230},{7,103},{8,2... | collective-permute-start | bytes 294920 | tf_op jit(solution)/shard_map/ppermute | solution.py:326
  34.0 4.7 %collective-permute-start.5 = (f32[192,128]{1,0:T(8,128)S(1)}, f32[192,128]{1,0:T(8,128)S(1)}, u32[]{:S(2)}, u32[]{:S(2)}) collective-permute-start(f32[192,128]{1,0:T(8,128)S(1)} %multiply_add_fusion.8), channel_id=1, source_target_pairs={{0,96},{1,225},{2,98},{3,227},{4,100},{5,229},{6,102},{7,231},{8,1... | collective-permute-start | bytes 294920 | tf_op jit(solution)/shard_map/ppermute | solution.py:326
  38.8 4.7 %collective-permute-start.6 = (f32[192,128]{1,0:T(8,128)S(1)}, f32[192,128]{1,0:T(8,128)S(1)}, u32[]{:S(2)}, u32[]{:S(2)}) collective-permute-start(f32[192,128]{1,0:T(8,128)S(1)} %multiply_add_fusion.7), channel_id=1, source_target_pairs={{0,32},{1,33},{2,34},{3,35},{4,36},{5,37},{6,38},{7,39},{8,40},{9,... | collective-permute-start | bytes 294920 | tf_op jit(solution)/shard_map/ppermute | solution.py:326
  43.6 5.9 %collective-permute-start.7 = (f32[192,128]{1,0:T(8,128)S(1)}, f32[192,128]{1,0:T(8,128)S(1)}, u32[]{:S(2)}, u32[]{:S(2)}) collective-permute-start(f32[192,128]{1,0:T(8,128)S(1)} %multiply_add_fusion.6.refs_1_), channel_id=1, source_target_pairs={{0,24},{1,17},{2,26},{3,19},{4,28},{5,21},{6,30},{7,23},{8,16},{9,... | collective-permute-start | bytes 294920 | tf_op jit(solution)/shard_map/ppermute | solution.py:326
  45.6 6.1 %collective-permute-start.8 = (f32[192,128]{1,0:T(8,128)S(1)}, f32[192,128]{1,0:T(8,128)S(1)}, u32[]{:S(2)}, u32[]{:S(2)}) collective-permute-start(f32[192,128]{1,0:T(8,128)S(1)} %multiply_add_fusion.6.refs_1_), channel_id=1, source_target_pairs={{0,16},{1,25},{2,18},{3,27},{4,20},{5,29},{6,22},{7,31},{8,24},{9,... | collective-permute-start | bytes 294920 | tf_op jit(solution)/shard_map/ppermute | solution.py:326
  48.0 4.6 %collective-permute-start.9 = (f32[192,128]{1,0:T(8,128)S(1)}, f32[192,128]{1,0:T(8,128)S(1)}, u32[]{:S(2)}, u32[]{:S(2)}) collective-permute-start(f32[192,128]{1,0:T(8,128)S(1)} %multiply_add_fusion.6.refs_1_), channel_id=1, source_target_pairs={{0,8},{1,9},{2,10},{3,11},{4,12},{5,13},{6,14},{7,15},{8,0},{9,1},... | collective-permute-start | bytes 294920 | tf_op jit(solution)/shard_map/ppermute | solution.py:326
  53.6 1.3 collective-permute-start.10
  54.9 5.5 %collective-permute-start.11 = (f32[128,128]{1,0:T(8,128)S(1)}, f32[128,128]{1,0:T(8,128)S(1)}, u32[]{:S(2)}, u32[]{:S(2)}) collective-permute-start(f32[128,128]{1,0:T(8,128)S(1)} %multiply_add_fusion.10.refs_1_), channel_id=1, source_target_pairs={{0,6},{1,5},{2,4},{3,7},{4,2},{5,1},{6,0},{7,3},{8,14},{9,13},{10,... | collective-permute-start | bytes 196616 | tf_op jit(solution)/shard_map/ppermute | solution.py:326
  55.0 6.3 %collective-permute-start.12 = (f32[128,128]{1,0:T(8,128)S(1)}, f32[128,128]{1,0:T(8,128)S(1)}, u32[]{:S(2)}, u32[]{:S(2)}) collective-permute-start(f32[128,128]{1,0:T(8,128)S(1)} %multiply_add_fusion.10.refs_1_), channel_id=1, source_target_pairs={{0,4},{1,7},{2,6},{3,5},{4,0},{5,3},{6,2},{7,1},{8,12},{9,15},{10,... | collective-permute-start | bytes 196616 | tf_op jit(solution)/shard_map/ppermute | solution.py:326
  56.5 5.8 %collective-permute-start.13 = (f32[128,128]{1,0:T(8,128)S(1)}, f32[128,128]{1,0:T(8,128)S(1)}, u32[]{:S(2)}, u32[]{:S(2)}) collective-permute-start(f32[128,128]{1,0:T(8,128)S(1)} %multiply_add_fusion.10.refs_1_), channel_id=1, source_target_pairs={{0,2},{1,3},{2,0},{3,1},{4,6},{5,7},{6,4},{7,5},{8,10},{9,11},{10,... | collective-permute-start | bytes 196616 | tf_op jit(solution)/shard_map/ppermute | solution.py:326
  66.2 19.2 %collective-permute-start.14 = (f32[192,128]{1,0:T(8,128)S(1)}, f32[192,128]{1,0:T(8,128)S(1)}, u32[]{:S(2)}, u32[]{:S(2)}) collective-permute-start(f32[192,128]{1,0:T(8,128)S(1)} %get-tuple-element.31), channel_id=1, source_target_pairs={{0,224},{1,97},{2,226},{3,99},{4,228},{5,101},{6,230},{7,103},{8,2... | collective-permute-start | bytes 294920 | tf_op jit(solution)/shard_map/ppermute | solution.py:326
  85.5 4.7 %collective-permute-start.15 = (f32[192,128]{1,0:T(8,128)S(1)}, f32[192,128]{1,0:T(8,128)S(1)}, u32[]{:S(2)}, u32[]{:S(2)}) collective-permute-start(f32[192,128]{1,0:T(8,128)S(1)} %multiply_add_fusion.5), channel_id=1, source_target_pairs={{0,96},{1,225},{2,98},{3,227},{4,100},{5,229},{6,102},{7,231},{8,1... | collective-permute-start | bytes 294920 | tf_op jit(solution)/shard_map/ppermute | solution.py:326
  90.2 4.7 %collective-permute-start.16 = (f32[192,128]{1,0:T(8,128)S(1)}, f32[192,128]{1,0:T(8,128)S(1)}, u32[]{:S(2)}, u32[]{:S(2)}) collective-permute-start(f32[192,128]{1,0:T(8,128)S(1)} %multiply_add_fusion.4), channel_id=1, source_target_pairs={{0,32},{1,33},{2,34},{3,35},{4,36},{5,37},{6,38},{7,39},{8,40},{9,... | collective-permute-start | bytes 294920 | tf_op jit(solution)/shard_map/ppermute | solution.py:326
  95.0 7.0 %collective-permute-start.17 = (f32[192,128]{1,0:T(8,128)S(1)}, f32[192,128]{1,0:T(8,128)S(1)}, u32[]{:S(2)}, u32[]{:S(2)}) collective-permute-start(f32[192,128]{1,0:T(8,128)S(1)} %multiply_add_fusion.3.refs_1_), channel_id=1, source_target_pairs={{0,24},{1,17},{2,26},{3,19},{4,28},{5,21},{6,30},{7,23},{8,16},{9,... | collective-permute-start | bytes 294920 | tf_op jit(solution)/shard_map/ppermute | solution.py:326
  95.1 6.9 %collective-permute-start.18 = (f32[192,128]{1,0:T(8,128)S(1)}, f32[192,128]{1,0:T(8,128)S(1)}, u32[]{:S(2)}, u32[]{:S(2)}) collective-permute-start(f32[192,128]{1,0:T(8,128)S(1)} %multiply_add_fusion.3.refs_1_), channel_id=1, source_target_pairs={{0,16},{1,25},{2,18},{3,27},{4,20},{5,29},{6,22},{7,31},{8,24},{9,... | collective-permute-start | bytes 294920 | tf_op jit(solution)/shard_map/ppermute | solution.py:326
  95.2 7.6 %collective-permute-start.19 = (f32[192,128]{1,0:T(8,128)S(1)}, f32[192,128]{1,0:T(8,128)S(1)}, u32[]{:S(2)}, u32[]{:S(2)}) collective-permute-start(f32[192,128]{1,0:T(8,128)S(1)} %multiply_add_fusion.3.refs_1_), channel_id=1, source_target_pairs={{0,8},{1,9},{2,10},{3,11},{4,12},{5,13},{6,14},{7,15},{8,0},{9,1},... | collective-permute-start | bytes 294920 | tf_op jit(solution)/shard_map/ppermute | solution.py:326
  103.7 1.3 collective-permute-start.20
  105.1 6.1 %collective-permute-start.21 = (f32[128,128]{1,0:T(8,128)S(1)}, f32[128,128]{1,0:T(8,128)S(1)}, u32[]{:S(2)}, u32[]{:S(2)}) collective-permute-start(f32[128,128]{1,0:T(8,128)S(1)} %multiply_add_fusion.9.refs_1_), channel_id=1, source_target_pairs={{0,6},{1,5},{2,4},{3,7},{4,2},{5,1},{6,0},{7,3},{8,14},{9,13},{10,... | collective-permute-start | bytes 196616 | tf_op jit(solution)/shard_map/ppermute | solution.py:326
  105.2 6.4 %collective-permute-start.22 = (f32[128,128]{1,0:T(8,128)S(1)}, f32[128,128]{1,0:T(8,128)S(1)}, u32[]{:S(2)}, u32[]{:S(2)}) collective-permute-start(f32[128,128]{1,0:T(8,128)S(1)} %multiply_add_fusion.9.refs_1_), channel_id=1, source_target_pairs={{0,4},{1,7},{2,6},{3,5},{4,0},{5,3},{6,2},{7,1},{8,12},{9,15},{10,... | collective-permute-start | bytes 196616 | tf_op jit(solution)/shard_map/ppermute | solution.py:326
  106.5 6.0 %collective-permute-start.23 = (f32[128,128]{1,0:T(8,128)S(1)}, f32[128,128]{1,0:T(8,128)S(1)}, u32[]{:S(2)}, u32[]{:S(2)}) collective-permute-start(f32[128,128]{1,0:T(8,128)S(1)} %multiply_add_fusion.9.refs_1_), channel_id=1, source_target_pairs={{0,2},{1,3},{2,0},{3,1},{4,6},{5,7},{6,4},{7,5},{8,10},{9,11},{10,... | collective-permute-start | bytes 196616 | tf_op jit(solution)/shard_map/ppermute | solution.py:326
  116.4 19.5 %collective-permute-start.24 = (f32[192,128]{1,0:T(8,128)S(1)}, f32[192,128]{1,0:T(8,128)S(1)}, u32[]{:S(2)}, u32[]{:S(2)}) collective-permute-start(f32[192,128]{1,0:T(8,128)S(1)} %get-tuple-element.35), channel_id=1, source_target_pairs={{0,224},{1,97},{2,226},{3,99},{4,228},{5,101},{6,230},{7,103},{8,2... | collective-permute-start | bytes 294920 | tf_op jit(solution)/shard_map/ppermute | solution.py:326
  135.9 4.7 %collective-permute-start.25 = (f32[192,128]{1,0:T(8,128)S(1)}, f32[192,128]{1,0:T(8,128)S(1)}, u32[]{:S(2)}, u32[]{:S(2)}) collective-permute-start(f32[192,128]{1,0:T(8,128)S(1)} %multiply_add_fusion.2), channel_id=1, source_target_pairs={{0,96},{1,225},{2,98},{3,227},{4,100},{5,229},{6,102},{7,231},{8,1... | collective-permute-start | bytes 294920 | tf_op jit(solution)/shard_map/ppermute | solution.py:326
  140.7 4.7 %collective-permute-start.26 = (f32[192,128]{1,0:T(8,128)S(1)}, f32[192,128]{1,0:T(8,128)S(1)}, u32[]{:S(2)}, u32[]{:S(2)}) collective-permute-start(f32[192,128]{1,0:T(8,128)S(1)} %multiply_add_fusion.1), channel_id=1, source_target_pairs={{0,32},{1,33},{2,34},{3,35},{4,36},{5,37},{6,38},{7,39},{8,40},{9,... | collective-permute-start | bytes 294920 | tf_op jit(solution)/shard_map/ppermute | solution.py:326
  145.4 7.0 %collective-permute-start.27 = (f32[192,128]{1,0:T(8,128)S(1)}, f32[192,128]{1,0:T(8,128)S(1)}, u32[]{:S(2)}, u32[]{:S(2)}) collective-permute-start(f32[192,128]{1,0:T(8,128)S(1)} %multiply_add_fusion), channel_id=1, source_target_pairs={{0,24},{1,17},{2,26},{3,19},{4,28},{5,21},{6,30},{7,23},{8,16},{9,... | collective-permute-start | bytes 294920 | tf_op jit(solution)/shard_map/ppermute | solution.py:326
  145.5 6.9 %collective-permute-start.28 = (f32[192,128]{1,0:T(8,128)S(1)}, f32[192,128]{1,0:T(8,128)S(1)}, u32[]{:S(2)}, u32[]{:S(2)}) collective-permute-start(f32[192,128]{1,0:T(8,128)S(1)} %multiply_add_fusion), channel_id=1, source_target_pairs={{0,16},{1,25},{2,18},{3,27},{4,20},{5,29},{6,22},{7,31},{8,24},{9,... | collective-permute-start | bytes 294920 | tf_op jit(solution)/shard_map/ppermute | solution.py:326
  145.6 7.6 %collective-permute-start.29 = (f32[192,128]{1,0:T(8,128)S(1)}, f32[192,128]{1,0:T(8,128)S(1)}, u32[]{:S(2)}, u32[]{:S(2)}) collective-permute-start(f32[192,128]{1,0:T(8,128)S(1)} %multiply_add_fusion), channel_id=1, source_target_pairs={{0,8},{1,9},{2,10},{3,11},{4,12},{5,13},{6,14},{7,15},{8,0},{9,1},... | collective-permute-start | bytes 294920 | tf_op jit(solution)/shard_map/ppermute | solution.py:326

commit v9 on v8

--- a/solution.py
+++ b/solution.py
@@ -339,9 +339,10 @@
 
 
 def over_src(value):
-    for flips in ((28, 12), (12, 28), (4, 4)):
+    value = lse2_many(fan(value, "src", (3, 2), (2, 3), (1, 1)))
+    for flips in ((4, 4), (12, 28)):
         value = lse2_many(fan(value, "src", flips))
-    return fan(value, "src", (3, 2), (2, 3), (1, 1))
+    return fan(value, "src", (28, 12))
 
 
 def body(src_points, tgt_points, tiles, counts):

time: 153 us -> 159 us (1.039)
  the two profiles are of different devices: /device:TPU:40 before, /device:TPU:176 now
where the time goes in v9:
time: 159 us; the launch traced here: 158 us
  waiting for transfers between devices  84.5 us (53%)
  starting transfers between devices  57.1 us (36%)
  Pallas kernels  13.5 us (8%)
    ppermute x30, waiting for transfers between devices, swap(): return lax.ppermute(value, ('src', 'tgt'), pairs)  84.5 us
    ppermute x30, starting transfers between devices, swap(): return lax.ppermute(value, ('src', 'tgt'), pairs)  57.1 us
    pallas_call x5, Pallas kernels, sweep(): pl.pallas_call(kernel, out_shape=(jax.ShapeDtypeStruct((2 * blocks_out, H...  9.15 us
    pallas_call x1, Pallas kernels, costs(): pl.pallas_call(functools.partial(cost_kernel, blocks_in, blocks_out), out...  3.9 us
  transfers between devices with their start and end apart: 30, of which 25 were waited for; matrix products, arithmetic and copies ran while one was open for 0% of the time, Pallas kernels for 0%

profile of v9, /device:TPU:176, one launch (start us, length us, event | category | flops | bytes accessed | tf_op | source)
XLA Modules:
  0.0 158.1 jit_solution(6767080598133634532)
XLA Ops:
  1.3 3.9 %shard_map.59 = (f32[32,256,256]{2,1,0:T(8,128)S(1)}, f32[128,128]{1,0:T(8,128)S(1)}, bf16[32,128,256]{2,1,0:T(8,128)(2,1)S(1)}, bf16[32,128,256]{2,1,0:T(8,128)(2,1)S(1)}, s32[2,32]{1,0:T(2,128)S(4)}) custom-call(s32[2,32]{1,0:T(2,128)} %bitcast.4, s32[1,1]{1,0:T(1,128)S(6)} %copy.6.counts, f32[50,16384]{1,0:T(8,128)} %src.1, f32[50,24576]{1,0:T(8,128)} %tgt.1), custom_call_target="tpu_custom_call" | custom-call | tf_op jit(solution)/shard_map/pallas_call | solution.py:255
  5.2 2.2 %collective-permute-start = (f32[128,128]{1,0:T(8,128)S(1)}, f32[128,128]{1,0:T(8,128)S(1)}, u32[]{:S(2)}, u32[]{:S(2)}) collective-permute-start(f32[128,128]{1,0:T(8,128)S(1)} %get-tuple-element.20), channel_id=1, source_target_pairs={{0,1},{1,0},{2,3},{3,2},{4,5},{5,4},{6,7},{7,6},{8,9},{9,8},{10,11... | collective-permute-start | bytes 196616 | tf_op jit(solution)/shard_map/ppermute | solution.py:326
  8.4 1.9 %collective-permute-start.2 = (f32[128,128]{1,0:T(8,128)S(1)}, f32[128,128]{1,0:T(8,128)S(1)}, u32[]{:S(2)}, u32[]{:S(2)}) collective-permute-start(f32[128,128]{1,0:T(8,128)S(1)} %multiply_add_fusion.11.refs_0_), channel_id=1, source_target_pairs={{0,4},{1,7},{2,6},{3,5},{4,0},{5,3},{6,2},{7,1},{8,12},{9,15},{10,... | collective-permute-start | bytes 196616 | tf_op jit(solution)/shard_map/ppermute | solution.py:326
  10.3 2.2 %collective-permute-start.3 = (f32[128,128]{1,0:T(8,128)S(1)}, f32[128,128]{1,0:T(8,128)S(1)}, u32[]{:S(2)}, u32[]{:S(2)}) collective-permute-start(f32[128,128]{1,0:T(8,128)S(1)} %multiply_add_fusion.11.refs_0_), channel_id=1, source_target_pairs={{0,2},{1,3},{2,0},{3,1},{4,6},{5,7},{6,4},{7,5},{8,10},{9,11},{10,... | collective-permute-start | bytes 196616 | tf_op jit(solution)/shard_map/ppermute | solution.py:326
  13.0 1.8 %collective-permute-done.2.refs_2_ = f32[128,128]{1,0:T(8,128)S(1)} collective-permute-done((f32[128,128]{1,0:T(8,128)S(1)}, f32[128,128]{1,0:T(8,128)S(1)}, u32[]{:S(2)}, u32[]{:S(2)}) %collective-permute-start.2) | collective-permute-done | bytes 65568 | tf_op jit(solution)/shard_map/ppermute | solution.py:326
  15.8 2.5 %shard_map.61 = (f32[192,128]{1,0:T(8,128)S(1)}, f32[128,128]{1,0:T(8,128)S(1)}) custom-call(s32[2,32]{1,0:T(2,128)S(4)} %get-tuple-element.19.tiles, s32[1,1]{1,0:T(1,128)S(6)} %copy.6.counts, f32[32,256,256]{2,1,0:T(8,128)S(1)} %shard_map.60.cost, f32[128,128]{1,0:T(8,128)S(1)} %multiply_add_fusion.11.refs_0_, ...), custom_call_target="tpu_custom_call" | custom-call | tf_op jit(solution)/shard_map/pallas_call | solution.py:300
  18.3 3.5 %collective-permute-start.4 = (f32[192,128]{1,0:T(8,128)S(1)}, f32[192,128]{1,0:T(8,128)S(1)}, u32[]{:S(2)}, u32[]{:S(2)}) collective-permute-start(f32[192,128]{1,0:T(8,128)S(1)} %get-tuple-element.27), channel_id=1, source_target_pairs={{0,24},{1,17},{2,26},{3,19},{4,28},{5,21},{6,30},{7,23},{8,16},{9,... | collective-permute-start | bytes 294920 | tf_op jit(solution)/shard_map/ppermute | solution.py:326
  21.8 7.0 %collective-permute-start.5 = (f32[192,128]{1,0:T(8,128)S(1)}, f32[192,128]{1,0:T(8,128)S(1)}, u32[]{:S(2)}, u32[]{:S(2)}) collective-permute-start(f32[192,128]{1,0:T(8,128)S(1)} %get-tuple-element.27), channel_id=1, source_target_pairs={{0,16},{1,25},{2,18},{3,27},{4,20},{5,29},{6,22},{7,31},{8,24},{9,... | collective-permute-start | bytes 294920 | tf_op jit(solution)/shard_map/ppermute | solution.py:326
  28.9 2.6 %collective-permute-done.5 = f32[192,128]{1,0:T(8,128)S(1)} collective-permute-done((f32[192,128]{1,0:T(8,128)S(1)}, f32[192,128]{1,0:T(8,128)S(1)}, u32[]{:S(2)}, u32[]{:S(2)}) %collective-permute-start.5) | collective-permute-done | bytes 98336 | tf_op jit(solution)/shard_map/ppermute | solution.py:326
  31.5 2.0 %collective-permute-done.6 = f32[192,128]{1,0:T(8,128)S(1)} collective-permute-done((f32[192,128]{1,0:T(8,128)S(1)}, f32[192,128]{1,0:T(8,128)S(1)}, u32[]{:S(2)}, u32[]{:S(2)}) %collective-permute-start.6) | collective-permute-done | bytes 98336 | tf_op jit(solution)/shard_map/ppermute | solution.py:326
  33.7 4.6 %collective-permute-done.7 = f32[192,128]{1,0:T(8,128)S(1)} collective-permute-done((f32[192,128]{1,0:T(8,128)S(1)}, f32[192,128]{1,0:T(8,128)S(1)}, u32[]{:S(2)}, u32[]{:S(2)}) %collective-permute-start.7) | collective-permute-done | bytes 98336 | tf_op jit(solution)/shard_map/ppermute | solution.py:326
  38.7 6.9 %collective-permute-done.8 = f32[192,128]{1,0:T(8,128)S(1)} collective-permute-done((f32[192,128]{1,0:T(8,128)S(1)}, f32[192,128]{1,0:T(8,128)S(1)}, u32[]{:S(2)}, u32[]{:S(2)}) %collective-permute-start.8) | collective-permute-done | bytes 98336 | tf_op jit(solution)/shard_map/ppermute | solution.py:326
  45.8 7.6 %collective-permute-done.9.refs_2_ = f32[192,128]{1,0:T(8,128)S(1)} collective-permute-done((f32[192,128]{1,0:T(8,128)S(1)}, f32[192,128]{1,0:T(8,128)S(1)}, u32[]{:S(2)}, u32[]{:S(2)}) %collective-permute-start.9) | collective-permute-done | bytes 98336 | tf_op jit(solution)/shard_map/ppermute | solution.py:326
  55.7 3.7 %collective-permute-start.12 = (f32[128,128]{1,0:T(8,128)S(1)}, f32[128,128]{1,0:T(8,128)S(1)}, u32[]{:S(2)}, u32[]{:S(2)}) collective-permute-start(f32[128,128]{1,0:T(8,128)S(1)} %multiply_add_fusion.10.refs_1_), channel_id=1, source_target_pairs={{0,4},{1,7},{2,6},{3,5},{4,0},{5,3},{6,2},{7,1},{8,12},{9,15},{10,... | collective-permute-start | bytes 196616 | tf_op jit(solution)/shard_map/ppermute | solution.py:326
  61.9 2.1 %collective-permute-done.13.refs_4_ = f32[128,128]{1,0:T(8,128)S(1)} collective-permute-done((f32[128,128]{1,0:T(8,128)S(1)}, f32[128,128]{1,0:T(8,128)S(1)}, u32[]{:S(2)}, u32[]{:S(2)}) %collective-permute-start.13) | collective-permute-done | bytes 65568 | tf_op jit(solution)/shard_map/ppermute | solution.py:326
  63.9 2.5 %shard_map.63 = (f32[192,128]{1,0:T(8,128)S(1)}, f32[128,128]{1,0:T(8,128)S(1)}) custom-call(s32[2,32]{1,0:T(2,128)S(4)} %get-tuple-element.19.tiles, s32[1,1]{1,0:T(1,128)S(6)} %copy.6.counts, f32[32,256,256]{2,1,0:T(8,128)S(1)} %shard_map.60.cost, f32[192,128]{1,0:T(8,128)S(1)} %get-tuple-element.28.refs_0_, f32[128,128]{1,0:T(8,128)S(1)} %multiply_add_fusion.10.refs_1_, ...), custom_call_target="tpu_custom_call" | custom-call | tf_op jit(solution)/shard_map/pallas_call | solution.py:300
  67.4 13.5 %collective-permute-start.15 = (f32[192,128]{1,0:T(8,128)S(1)}, f32[192,128]{1,0:T(8,128)S(1)}, u32[]{:S(2)}, u32[]{:S(2)}) collective-permute-start(f32[192,128]{1,0:T(8,128)S(1)} %get-tuple-element.31), channel_id=1, source_target_pairs={{0,16},{1,25},{2,18},{3,27},{4,20},{5,29},{6,22},{7,31},{8,24},{9,... | collective-permute-start | bytes 294920 | tf_op jit(solution)/shard_map/ppermute | solution.py:326
  80.9 2.6 %collective-permute-done.15 = f32[192,128]{1,0:T(8,128)S(1)} collective-permute-done((f32[192,128]{1,0:T(8,128)S(1)}, f32[192,128]{1,0:T(8,128)S(1)}, u32[]{:S(2)}, u32[]{:S(2)}) %collective-permute-start.15) | collective-permute-done | bytes 98336 | tf_op jit(solution)/shard_map/ppermute | solution.py:326
  83.5 2.0 %collective-permute-done.16 = f32[192,128]{1,0:T(8,128)S(1)} collective-permute-done((f32[192,128]{1,0:T(8,128)S(1)}, f32[192,128]{1,0:T(8,128)S(1)}, u32[]{:S(2)}, u32[]{:S(2)}) %collective-permute-start.16) | collective-permute-done | bytes 98336 | tf_op jit(solution)/shard_map/ppermute | solution.py:326
  85.7 4.6 %collective-permute-done.17 = f32[192,128]{1,0:T(8,128)S(1)} collective-permute-done((f32[192,128]{1,0:T(8,128)S(1)}, f32[192,128]{1,0:T(8,128)S(1)}, u32[]{:S(2)}, u32[]{:S(2)}) %collective-permute-start.17) | collective-permute-done | bytes 98336 | tf_op jit(solution)/shard_map/ppermute | solution.py:326
  90.5 7.4 %collective-permute-done.18 = f32[192,128]{1,0:T(8,128)S(1)} collective-permute-done((f32[192,128]{1,0:T(8,128)S(1)}, f32[192,128]{1,0:T(8,128)S(1)}, u32[]{:S(2)}, u32[]{:S(2)}) %collective-permute-start.18) | collective-permute-done | bytes 98336 | tf_op jit(solution)/shard_map/ppermute | solution.py:326
  98.1 7.6 %collective-permute-done.19.refs_2_ = f32[192,128]{1,0:T(8,128)S(1)} collective-permute-done((f32[192,128]{1,0:T(8,128)S(1)}, f32[192,128]{1,0:T(8,128)S(1)}, u32[]{:S(2)}, u32[]{:S(2)}) %collective-permute-start.19) | collective-permute-done | bytes 98336 | tf_op jit(solution)/shard_map/ppermute | solution.py:326
  108.1 1.7 %collective-permute-start.22 = (f32[128,128]{1,0:T(8,128)S(1)}, f32[128,128]{1,0:T(8,128)S(1)}, u32[]{:S(2)}, u32[]{:S(2)}) collective-permute-start(f32[128,128]{1,0:T(8,128)S(1)} %multiply_add_fusion.9.refs_1_), channel_id=1, source_target_pairs={{0,4},{1,7},{2,6},{3,5},{4,0},{5,3},{6,2},{7,1},{8,12},{9,15},{10,... | collective-permute-start | bytes 196616 | tf_op jit(solution)/shard_map/ppermute | solution.py:326
  109.7 2.4 %collective-permute-start.23 = (f32[128,128]{1,0:T(8,128)S(1)}, f32[128,128]{1,0:T(8,128)S(1)}, u32[]{:S(2)}, u32[]{:S(2)}) collective-permute-start(f32[128,128]{1,0:T(8,128)S(1)} %multiply_add_fusion.9.refs_1_), channel_id=1, source_target_pairs={{0,2},{1,3},{2,0},{3,1},{4,6},{5,7},{6,4},{7,5},{8,10},{9,11},{10,... | collective-permute-start | bytes 196616 | tf_op jit(solution)/shard_map/ppermute | solution.py:326
  115.3 2.5 %shard_map.65 = (f32[192,128]{1,0:T(8,128)S(1)}, f32[128,128]{1,0:T(8,128)}) custom-call(s32[2,32]{1,0:T(2,128)S(4)} %get-tuple-element.19.tiles, s32[1,1]{1,0:T(1,128)S(6)} %copy.6.counts, f32[32,256,256]{2,1,0:T(8,128)S(1)} %shard_map.60.cost, f32[192,128]{1,0:T(8,128)S(1)} %get-tuple-element.32.refs_0_, f32[128,128]{1,0:T(8,128)S(1)} %multiply_add_fusion.9.refs_1_, ...), custom_call_target="tpu_custom_call" | custom-call | tf_op jit(solution)/shard_map/pallas_call | solution.py:300
  117.8 2.2 %collective-permute-start.24 = (f32[192,128]{1,0:T(8,128)S(1)}, f32[192,128]{1,0:T(8,128)S(1)}, u32[]{:S(2)}, u32[]{:S(2)}) collective-permute-start(f32[192,128]{1,0:T(8,128)S(1)} %get-tuple-element.35), channel_id=1, source_target_pairs={{0,24},{1,17},{2,26},{3,19},{4,28},{5,21},{6,30},{7,23},{8,16},{9,... | collective-permute-start | bytes 294920 | tf_op jit(solution)/shard_map/ppermute | solution.py:326
  120.0 13.1 %collective-permute-start.25 = (f32[192,128]{1,0:T(8,128)S(1)}, f32[192,128]{1,0:T(8,128)S(1)}, u32[]{:S(2)}, u32[]{:S(2)}) collective-permute-start(f32[192,128]{1,0:T(8,128)S(1)} %get-tuple-element.35), channel_id=1, source_target_pairs={{0,16},{1,25},{2,18},{3,27},{4,20},{5,29},{6,22},{7,31},{8,24},{9,... | collective-permute-start | bytes 294920 | tf_op jit(solution)/shard_map/ppermute | solution.py:326
  133.2 2.6 %collective-permute-done.25 = f32[192,128]{1,0:T(8,128)S(1)} collective-permute-done((f32[192,128]{1,0:T(8,128)S(1)}, f32[192,128]{1,0:T(8,128)S(1)}, u32[]{:S(2)}, u32[]{:S(2)}) %collective-permute-start.25) | collective-permute-done | bytes 98336 | tf_op jit(solution)/shard_map/ppermute | solution.py:326
  135.8 2.0 %collective-permute-done.26 = f32[192,128]{1,0:T(8,128)S(1)} collective-permute-done((f32[192,128]{1,0:T(8,128)S(1)}, f32[192,128]{1,0:T(8,128)S(1)}, u32[]{:S(2)}, u32[]{:S(2)}) %collective-permute-start.26) | collective-permute-done | bytes 98336 | tf_op jit(solution)/shard_map/ppermute | solution.py:326
  138.0 4.6 %collective-permute-done.27 = f32[192,128]{1,0:T(8,128)S(1)} collective-permute-done((f32[192,128]{1,0:T(8,128)S(1)}, f32[192,128]{1,0:T(8,128)S(1)}, u32[]{:S(2)}, u32[]{:S(2)}) %collective-permute-start.27) | collective-permute-done | bytes 98336 | tf_op jit(solution)/shard_map/ppermute | solution.py:326
  142.8 6.8 %collective-permute-done.28 = f32[192,128]{1,0:T(8,128)S(1)} collective-permute-done((f32[192,128]{1,0:T(8,128)S(1)}, f32[192,128]{1,0:T(8,128)S(1)}, u32[]{:S(2)}, u32[]{:S(2)}) %collective-permute-start.28) | collective-permute-done | bytes 98336 | tf_op jit(solution)/shard_map/ppermute | solution.py:326
  149.7 7.6 %collective-permute-done.29 = f32[192,128]{1,0:T(8,128)S(1)} collective-permute-done((f32[192,128]{1,0:T(8,128)S(1)}, f32[192,128]{1,0:T(8,128)S(1)}, u32[]{:S(2)}, u32[]{:S(2)}) %collective-permute-start.29) | collective-permute-done | bytes 98336 | tf_op jit(solution)/shard_map/ppermute | solution.py:326
  (48 shorter events, 16.2 us)
Async XLA Ops:
  5.2 3.1 %collective-permute-start = (f32[128,128]{1,0:T(8,128)S(1)}, f32[128,128]{1,0:T(8,128)S(1)}, u32[]{:S(2)}, u32[]{:S(2)}) collective-permute-start(f32[128,128]{1,0:T(8,128)S(1)} %get-tuple-element.20), channel_id=1, source_target_pairs={{0,1},{1,0},{2,3},{3,2},{4,5},{5,4},{6,7},{7,6},{8,9},{9,8},{10,11... | collective-permute-start | bytes 196616 | tf_op jit(solution)/shard_map/ppermute | solution.py:326
  8.3 4.7 %collective-permute-start.1 = (f32[128,128]{1,0:T(8,128)S(1)}, f32[128,128]{1,0:T(8,128)S(1)}, u32[]{:S(2)}, u32[]{:S(2)}) collective-permute-start(f32[128,128]{1,0:T(8,128)S(1)} %multiply_add_fusion.11.refs_0_), channel_id=1, source_target_pairs={{0,6},{1,5},{2,4},{3,7},{4,2},{5,1},{6,0},{7,3},{8,14},{9,13},{10,... | collective-permute-start | bytes 196616 | tf_op jit(solution)/shard_map/ppermute | solution.py:326
  8.4 6.4 %collective-permute-start.2 = (f32[128,128]{1,0:T(8,128)S(1)}, f32[128,128]{1,0:T(8,128)S(1)}, u32[]{:S(2)}, u32[]{:S(2)}) collective-permute-start(f32[128,128]{1,0:T(8,128)S(1)} %multiply_add_fusion.11.refs_0_), channel_id=1, source_target_pairs={{0,4},{1,7},{2,6},{3,5},{4,0},{5,3},{6,2},{7,1},{8,12},{9,15},{10,... | collective-permute-start | bytes 196616 | tf_op jit(solution)/shard_map/ppermute | solution.py:326
  10.3 5.5 %collective-permute-start.3 = (f32[128,128]{1,0:T(8,128)S(1)}, f32[128,128]{1,0:T(8,128)S(1)}, u32[]{:S(2)}, u32[]{:S(2)}) collective-permute-start(f32[128,128]{1,0:T(8,128)S(1)} %multiply_add_fusion.11.refs_0_), channel_id=1, source_target_pairs={{0,2},{1,3},{2,0},{3,1},{4,6},{5,7},{6,4},{7,5},{8,10},{9,11},{10,... | collective-permute-start | bytes 196616 | tf_op jit(solution)/shard_map/ppermute | solution.py:326
  18.3 10.6 %collective-permute-start.4 = (f32[192,128]{1,0:T(8,128)S(1)}, f32[192,128]{1,0:T(8,128)S(1)}, u32[]{:S(2)}, u32[]{:S(2)}) collective-permute-start(f32[192,128]{1,0:T(8,128)S(1)} %get-tuple-element.27), channel_id=1, source_target_pairs={{0,24},{1,17},{2,26},{3,19},{4,28},{5,21},{6,30},{7,23},{8,16},{9,... | collective-permute-start | bytes 294920 | tf_op jit(solution)/shard_map/ppermute | solution.py:326
  21.8 9.6 %collective-permute-start.5 = (f32[192,128]{1,0:T(8,128)S(1)}, f32[192,128]{1,0:T(8,128)S(1)}, u32[]{:S(2)}, u32[]{:S(2)}) collective-permute-start(f32[192,128]{1,0:T(8,128)S(1)} %get-tuple-element.27), channel_id=1, source_target_pairs={{0,16},{1,25},{2,18},{3,27},{4,20},{5,29},{6,22},{7,31},{8,24},{9,... | collective-permute-start | bytes 294920 | tf_op jit(solution)/shard_map/ppermute | solution.py:326
  28.9 4.6 %collective-permute-start.6 = (f32[192,128]{1,0:T(8,128)S(1)}, f32[192,128]{1,0:T(8,128)S(1)}, u32[]{:S(2)}, u32[]{:S(2)}) collective-permute-start(f32[192,128]{1,0:T(8,128)S(1)} %get-tuple-element.27), channel_id=1, source_target_pairs={{0,8},{1,9},{2,10},{3,11},{4,12},{5,13},{6,14},{7,15},{8,0},{9,1},... | collective-permute-start | bytes 294920 | tf_op jit(solution)/shard_map/ppermute | solution.py:326
  33.6 4.7 %collective-permute-start.7 = (f32[192,128]{1,0:T(8,128)S(1)}, f32[192,128]{1,0:T(8,128)S(1)}, u32[]{:S(2)}, u32[]{:S(2)}) collective-permute-start(f32[192,128]{1,0:T(8,128)S(1)} %multiply_add_fusion.8), channel_id=1, source_target_pairs={{0,32},{1,33},{2,34},{3,35},{4,36},{5,37},{6,38},{7,39},{8,40},{9,... | collective-permute-start | bytes 294920 | tf_op jit(solution)/shard_map/ppermute | solution.py:326
  38.4 7.2 %collective-permute-start.8 = (f32[192,128]{1,0:T(8,128)S(1)}, f32[192,128]{1,0:T(8,128)S(1)}, u32[]{:S(2)}, u32[]{:S(2)}) collective-permute-start(f32[192,128]{1,0:T(8,128)S(1)} %multiply_add_fusion.7), channel_id=1, source_target_pairs={{0,96},{1,225},{2,98},{3,227},{4,100},{5,229},{6,102},{7,231},{8,1... | collective-permute-start | bytes 294920 | tf_op jit(solution)/shard_map/ppermute | solution.py:326
  45.7 7.7 %collective-permute-start.9 = (f32[192,128]{1,0:T(8,128)S(1)}, f32[192,128]{1,0:T(8,128)S(1)}, u32[]{:S(2)}, u32[]{:S(2)}) collective-permute-start(f32[192,128]{1,0:T(8,128)S(1)} %multiply_add_fusion.6.refs_1_), channel_id=1, source_target_pairs={{0,224},{1,97},{2,226},{3,99},{4,228},{5,101},{6,230},{7,103},{8,2... | collective-permute-start | bytes 294920 | tf_op jit(solution)/shard_map/ppermute | solution.py:326
  54.3 1.3 collective-permute-start.10
  55.6 4.9 %collective-permute-start.11 = (f32[128,128]{1,0:T(8,128)S(1)}, f32[128,128]{1,0:T(8,128)S(1)}, u32[]{:S(2)}, u32[]{:S(2)}) collective-permute-start(f32[128,128]{1,0:T(8,128)S(1)} %multiply_add_fusion.10.refs_1_), channel_id=1, source_target_pairs={{0,6},{1,5},{2,4},{3,7},{4,2},{5,1},{6,0},{7,3},{8,14},{9,13},{10,... | collective-permute-start | bytes 196616 | tf_op jit(solution)/shard_map/ppermute | solution.py:326
  55.7 6.1 %collective-permute-start.12 = (f32[128,128]{1,0:T(8,128)S(1)}, f32[128,128]{1,0:T(8,128)S(1)}, u32[]{:S(2)}, u32[]{:S(2)}) collective-permute-start(f32[128,128]{1,0:T(8,128)S(1)} %multiply_add_fusion.10.refs_1_), channel_id=1, source_target_pairs={{0,4},{1,7},{2,6},{3,5},{4,0},{5,3},{6,2},{7,1},{8,12},{9,15},{10,... | collective-permute-start | bytes 196616 | tf_op jit(solution)/shard_map/ppermute | solution.py:326
  59.5 4.5 %collective-permute-start.13 = (f32[128,128]{1,0:T(8,128)S(1)}, f32[128,128]{1,0:T(8,128)S(1)}, u32[]{:S(2)}, u32[]{:S(2)}) collective-permute-start(f32[128,128]{1,0:T(8,128)S(1)} %multiply_add_fusion.10.refs_1_), channel_id=1, source_target_pairs={{0,2},{1,3},{2,0},{3,1},{4,6},{5,7},{6,4},{7,5},{8,10},{9,11},{10,... | collective-permute-start | bytes 196616 | tf_op jit(solution)/shard_map/ppermute | solution.py:326
  66.4 14.5 %collective-permute-start.14 = (f32[192,128]{1,0:T(8,128)S(1)}, f32[192,128]{1,0:T(8,128)S(1)}, u32[]{:S(2)}, u32[]{:S(2)}) collective-permute-start(f32[192,128]{1,0:T(8,128)S(1)} %get-tuple-element.31), channel_id=1, source_target_pairs={{0,24},{1,17},{2,26},{3,19},{4,28},{5,21},{6,30},{7,23},{8,16},{9,... | collective-permute-start | bytes 294920 | tf_op jit(solution)/shard_map/ppermute | solution.py:326
  67.4 16.1 %collective-permute-start.15 = (f32[192,128]{1,0:T(8,128)S(1)}, f32[192,128]{1,0:T(8,128)S(1)}, u32[]{:S(2)}, u32[]{:S(2)}) collective-permute-start(f32[192,128]{1,0:T(8,128)S(1)} %get-tuple-element.31), channel_id=1, source_target_pairs={{0,16},{1,25},{2,18},{3,27},{4,20},{5,29},{6,22},{7,31},{8,24},{9,... | collective-permute-start | bytes 294920 | tf_op jit(solution)/shard_map/ppermute | solution.py:326
  80.9 4.6 %collective-permute-start.16 = (f32[192,128]{1,0:T(8,128)S(1)}, f32[192,128]{1,0:T(8,128)S(1)}, u32[]{:S(2)}, u32[]{:S(2)}) collective-permute-start(f32[192,128]{1,0:T(8,128)S(1)} %get-tuple-element.31), channel_id=1, source_target_pairs={{0,8},{1,9},{2,10},{3,11},{4,12},{5,13},{6,14},{7,15},{8,0},{9,1},... | collective-permute-start | bytes 294920 | tf_op jit(solution)/shard_map/ppermute | solution.py:326
  85.6 4.7 %collective-permute-start.17 = (f32[192,128]{1,0:T(8,128)S(1)}, f32[192,128]{1,0:T(8,128)S(1)}, u32[]{:S(2)}, u32[]{:S(2)}) collective-permute-start(f32[192,128]{1,0:T(8,128)S(1)} %multiply_add_fusion.5), channel_id=1, source_target_pairs={{0,32},{1,33},{2,34},{3,35},{4,36},{5,37},{6,38},{7,39},{8,40},{9,... | collective-permute-start | bytes 294920 | tf_op jit(solution)/shard_map/ppermute | solution.py:326
  90.4 7.5 %collective-permute-start.18 = (f32[192,128]{1,0:T(8,128)S(1)}, f32[192,128]{1,0:T(8,128)S(1)}, u32[]{:S(2)}, u32[]{:S(2)}) collective-permute-start(f32[192,128]{1,0:T(8,128)S(1)} %multiply_add_fusion.4), channel_id=1, source_target_pairs={{0,96},{1,225},{2,98},{3,227},{4,100},{5,229},{6,102},{7,231},{8,1... | collective-permute-start | bytes 294920 | tf_op jit(solution)/shard_map/ppermute | solution.py:326
  98.0 7.7 %collective-permute-start.19 = (f32[192,128]{1,0:T(8,128)S(1)}, f32[192,128]{1,0:T(8,128)S(1)}, u32[]{:S(2)}, u32[]{:S(2)}) collective-permute-start(f32[192,128]{1,0:T(8,128)S(1)} %multiply_add_fusion.3.refs_1_), channel_id=1, source_target_pairs={{0,224},{1,97},{2,226},{3,99},{4,228},{5,101},{6,230},{7,103},{8,2... | collective-permute-start | bytes 294920 | tf_op jit(solution)/shard_map/ppermute | solution.py:326
  106.6 1.3 collective-permute-start.20
  108.0 5.5 %collective-permute-start.21 = (f32[128,128]{1,0:T(8,128)S(1)}, f32[128,128]{1,0:T(8,128)S(1)}, u32[]{:S(2)}, u32[]{:S(2)}) collective-permute-start(f32[128,128]{1,0:T(8,128)S(1)} %multiply_add_fusion.9.refs_1_), channel_id=1, source_target_pairs={{0,6},{1,5},{2,4},{3,7},{4,2},{5,1},{6,0},{7,3},{8,14},{9,13},{10,... | collective-permute-start | bytes 196616 | tf_op jit(solution)/shard_map/ppermute | solution.py:326
  108.1 6.5 %collective-permute-start.22 = (f32[128,128]{1,0:T(8,128)S(1)}, f32[128,128]{1,0:T(8,128)S(1)}, u32[]{:S(2)}, u32[]{:S(2)}) collective-permute-start(f32[128,128]{1,0:T(8,128)S(1)} %multiply_add_fusion.9.refs_1_), channel_id=1, source_target_pairs={{0,4},{1,7},{2,6},{3,5},{4,0},{5,3},{6,2},{7,1},{8,12},{9,15},{10,... | collective-permute-start | bytes 196616 | tf_op jit(solution)/shard_map/ppermute | solution.py:326
  109.7 5.6 %collective-permute-start.23 = (f32[128,128]{1,0:T(8,128)S(1)}, f32[128,128]{1,0:T(8,128)S(1)}, u32[]{:S(2)}, u32[]{:S(2)}) collective-permute-start(f32[128,128]{1,0:T(8,128)S(1)} %multiply_add_fusion.9.refs_1_), channel_id=1, source_target_pairs={{0,2},{1,3},{2,0},{3,1},{4,6},{5,7},{6,4},{7,5},{8,10},{9,11},{10,... | collective-permute-start | bytes 196616 | tf_op jit(solution)/shard_map/ppermute | solution.py:326
  117.8 15.4 %collective-permute-start.24 = (f32[192,128]{1,0:T(8,128)S(1)}, f32[192,128]{1,0:T(8,128)S(1)}, u32[]{:S(2)}, u32[]{:S(2)}) collective-permute-start(f32[192,128]{1,0:T(8,128)S(1)} %get-tuple-element.35), channel_id=1, source_target_pairs={{0,24},{1,17},{2,26},{3,19},{4,28},{5,21},{6,30},{7,23},{8,16},{9,... | collective-permute-start | bytes 294920 | tf_op jit(solution)/shard_map/ppermute | solution.py:326
  120.0 15.7 %collective-permute-start.25 = (f32[192,128]{1,0:T(8,128)S(1)}, f32[192,128]{1,0:T(8,128)S(1)}, u32[]{:S(2)}, u32[]{:S(2)}) collective-permute-start(f32[192,128]{1,0:T(8,128)S(1)} %get-tuple-element.35), channel_id=1, source_target_pairs={{0,16},{1,25},{2,18},{3,27},{4,20},{5,29},{6,22},{7,31},{8,24},{9,... | collective-permute-start | bytes 294920 | tf_op jit(solution)/shard_map/ppermute | solution.py:326
  133.2 4.6 %collective-permute-start.26 = (f32[192,128]{1,0:T(8,128)S(1)}, f32[192,128]{1,0:T(8,128)S(1)}, u32[]{:S(2)}, u32[]{:S(2)}) collective-permute-start(f32[192,128]{1,0:T(8,128)S(1)} %get-tuple-element.35), channel_id=1, source_target_pairs={{0,8},{1,9},{2,10},{3,11},{4,12},{5,13},{6,14},{7,15},{8,0},{9,1},... | collective-permute-start | bytes 294920 | tf_op jit(solution)/shard_map/ppermute | solution.py:326
  137.9 4.7 %collective-permute-start.27 = (f32[192,128]{1,0:T(8,128)S(1)}, f32[192,128]{1,0:T(8,128)S(1)}, u32[]{:S(2)}, u32[]{:S(2)}) collective-permute-start(f32[192,128]{1,0:T(8,128)S(1)} %multiply_add_fusion.2), channel_id=1, source_target_pairs={{0,32},{1,33},{2,34},{3,35},{4,36},{5,37},{6,38},{7,39},{8,40},{9,... | collective-permute-start | bytes 294920 | tf_op jit(solution)/shard_map/ppermute | solution.py:326
  142.7 6.9 %collective-permute-start.28 = (f32[192,128]{1,0:T(8,128)S(1)}, f32[192,128]{1,0:T(8,128)S(1)}, u32[]{:S(2)}, u32[]{:S(2)}) collective-permute-start(f32[192,128]{1,0:T(8,128)S(1)} %multiply_add_fusion.1), channel_id=1, source_target_pairs={{0,96},{1,225},{2,98},{3,227},{4,100},{5,229},{6,102},{7,231},{8,1... | collective-permute-start | bytes 294920 | tf_op jit(solution)/shard_map/ppermute | solution.py:326
  149.6 7.7 %collective-permute-start.29 = (f32[192,128]{1,0:T(8,128)S(1)}, f32[192,128]{1,0:T(8,128)S(1)}, u32[]{:S(2)}, u32[]{:S(2)}) collective-permute-start(f32[192,128]{1,0:T(8,128)S(1)} %multiply_add_fusion), channel_id=1, source_target_pairs={{0,224},{1,97},{2,226},{3,99},{4,228},{5,101},{6,230},{7,103},{8,2... | collective-permute-start | bytes 294920 | tf_op jit(solution)/shard_map/ppermute | solution.py:326

commit v10 on v9

--- a/solution.py
+++ b/solution.py
@@ -330,16 +330,16 @@
     return [value, *[swap(value, axis, each) for each in flips]]
 
 
+def over_y(value):
+    return lse2_many(fan(value, "tgt", (2, 2), (4, 4), (6, 6)))
+
+
 def over_core(value):
-    return lse2_many(fan(value, "tgt", (1, 1)))
-
-
-def over_y(value):
-    return fan(value, "tgt", (6, 4), (4, 6), (2, 2))
+    return fan(value, "tgt", (1, 1))
 
 
 def over_src(value):
-    value = lse2_many(fan(value, "src", (3, 2), (2, 3), (1, 1)))
+    value = lse2_many(fan(value, "src", (1, 1), (2, 2), (3, 3)))
     for flips in ((4, 4), (12, 28)):
         value = lse2_many(fan(value, "src", flips))
     return fan(value, "src", (28, 12))
@@ -360,12 +360,12 @@
     target = None
     for turn in range(ITERS):
         last = turn == ITERS - 1
-        rows = over_core(rows)
+        rows = over_y(rows)
         if turn == 0:
-            rows, lefts = lax.optimization_barrier((rows, lefts))
             cost_ab = turned(counts, lefts, rights)
+            rows, cost_ab = lax.optimization_barrier((rows, cost_ab))
         cols, source = sweep(
-            tiles, counts, cost_ab, target, over_y(rows), src_cells, tgt_cells, 0, 1,
+            tiles, counts, cost_ab, target, over_core(rows), src_cells, tgt_cells, 0, 1,
             row_blocks, col_blocks, last,
         )
         parts = over_src(cols)

time: 159 us -> 155 us (0.975)
  the two profiles are of different devices: /device:TPU:176 before, /device:TPU:2 now
where the time goes in v10:
time: 155 us; the launch traced here: 157 us
  starting transfers between devices  83.4 us (54%)
  waiting for transfers between devices  56.9 us (37%)
  Pallas kernels  13.4 us (9%)
  other arithmetic  1.6 us (1%)
    ppermute x30, starting transfers between devices, swap(): return lax.ppermute(value, ('src', 'tgt'), pairs)  83.4 us
    ppermute x30, waiting for transfers between devices, swap(): return lax.ppermute(value, ('src', 'tgt'), pairs)  56.9 us
    pallas_call x5, Pallas kernels, sweep(): pl.pallas_call(kernel, out_shape=(jax.ShapeDtypeStruct((2 * blocks_out, H...  9.07 us
    pallas_call x1, Pallas kernels, costs(): pl.pallas_call(functools.partial(cost_kernel, blocks_in, blocks_out), out...  3.91 us
  transfers between devices with their start and end apart: 30, of which 26 were waited for; matrix products, arithmetic and copies ran while one was open for 0% of the time, Pallas kernels for 0%

profile of v10, /device:TPU:2, one launch (start us, length us, event | category | flops | bytes accessed | tf_op | source)
XLA Modules:
  0.0 156.7 jit_solution(2574180833245288502)
XLA Ops:
  1.3 3.9 %shard_map.59 = (f32[32,256,256]{2,1,0:T(8,128)S(1)}, f32[128,128]{1,0:T(8,128)S(1)}, bf16[32,128,256]{2,1,0:T(8,128)(2,1)S(1)}, bf16[32,128,256]{2,1,0:T(8,128)(2,1)S(1)}, s32[2,32]{1,0:T(2,128)S(4)}) custom-call(s32[2,32]{1,0:T(2,128)} %bitcast.4, s32[1,1]{1,0:T(1,128)S(6)} %copy.6.counts, f32[50,16384]{1,0:T(8,128)} %src.1, f32[50,24576]{1,0:T(8,128)} %tgt.1), custom_call_target="tpu_custom_call" | custom-call | tf_op jit(solution)/shard_map/pallas_call | solution.py:255
  5.2 3.9 %collective-permute-start.2 = (f32[128,128]{1,0:T(8,128)S(1)}, f32[128,128]{1,0:T(8,128)S(1)}, u32[]{:S(2)}, u32[]{:S(2)}) collective-permute-start(f32[128,128]{1,0:T(8,128)S(1)} %get-tuple-element.20), channel_id=1, source_target_pairs={{0,6},{1,7},{2,4},{3,5},{4,2},{5,3},{6,0},{7,1},{8,14},{9,15},{10,... | collective-permute-start | bytes 196616 | tf_op jit(solution)/shard_map/ppermute | solution.py:326
  12.5 3.0 %collective-permute-done.1 = f32[128,128]{1,0:T(8,128)S(1)} collective-permute-done((f32[128,128]{1,0:T(8,128)S(1)}, f32[128,128]{1,0:T(8,128)S(1)}, u32[]{:S(2)}, u32[]{:S(2)}) %collective-permute-start.1) | collective-permute-done | bytes 65568 | tf_op jit(solution)/shard_map/ppermute | solution.py:326
  16.9 2.4 %shard_map.61 = (f32[192,128]{1,0:T(8,128)S(1)}, f32[128,128]{1,0:T(8,128)S(1)}) custom-call(s32[2,32]{1,0:T(2,128)S(4)} %get-tuple-element.19.tiles, s32[1,1]{1,0:T(1,128)S(6)} %copy.6.counts, f32[32,256,256]{2,1,0:T(8,128)S(1)} %shard_map.60.cost, f32[128,128]{1,0:T(8,128)S(1)} %multiply_add_fusion.11.refs_0_, f32[128,128]{1,0:T(8,128)S(1)} %collective-permute-done.3.refs_1_), custom_call_target="tpu_custom_call" | custom-call | tf_op jit(solution)/shard_map/pallas_call | solution.py:300
  19.4 3.0 %collective-permute-start.6 = (f32[192,128]{1,0:T(8,128)S(1)}, f32[192,128]{1,0:T(8,128)S(1)}, u32[]{:S(2)}, u32[]{:S(2)}) collective-permute-start(f32[192,128]{1,0:T(8,128)S(1)} %get-tuple-element.27), channel_id=1, source_target_pairs={{0,24},{1,25},{2,26},{3,27},{4,28},{5,29},{6,30},{7,31},{8,16},{9,... | collective-permute-start | bytes 294920 | tf_op jit(solution)/shard_map/ppermute | solution.py:326
  25.0 3.6 %collective-permute-done.5 = f32[192,128]{1,0:T(8,128)S(1)} collective-permute-done((f32[192,128]{1,0:T(8,128)S(1)}, f32[192,128]{1,0:T(8,128)S(1)}, u32[]{:S(2)}, u32[]{:S(2)}) %collective-permute-start.5) | collective-permute-done | bytes 98336 | tf_op jit(solution)/shard_map/ppermute | solution.py:326
  28.7 3.6 %collective-permute-start.7 = (f32[192,128]{1,0:T(8,128)S(1)}, f32[192,128]{1,0:T(8,128)S(1)}, u32[]{:S(2)}, u32[]{:S(2)}) collective-permute-start(f32[192,128]{1,0:T(8,128)S(1)} %multiply_add_fusion.8), channel_id=1, source_target_pairs={{0,32},{1,33},{2,34},{3,35},{4,36},{5,37},{6,38},{7,39},{8,40},{9,... | collective-permute-start | bytes 294920 | tf_op jit(solution)/shard_map/ppermute | solution.py:326
  32.3 2.7 %collective-permute-done.7 = f32[192,128]{1,0:T(8,128)S(1)} collective-permute-done((f32[192,128]{1,0:T(8,128)S(1)}, f32[192,128]{1,0:T(8,128)S(1)}, u32[]{:S(2)}, u32[]{:S(2)}) %collective-permute-start.7) | collective-permute-done | bytes 98336 | tf_op jit(solution)/shard_map/ppermute | solution.py:326
  35.0 6.8 %collective-permute-start.8 = (f32[192,128]{1,0:T(8,128)S(1)}, f32[192,128]{1,0:T(8,128)S(1)}, u32[]{:S(2)}, u32[]{:S(2)}) collective-permute-start(f32[192,128]{1,0:T(8,128)S(1)} %multiply_add_fusion.7), channel_id=1, source_target_pairs={{0,96},{1,225},{2,98},{3,227},{4,100},{5,229},{6,102},{7,231},{8,1... | collective-permute-start | bytes 294920 | tf_op jit(solution)/shard_map/ppermute | solution.py:326
  41.8 2.7 %collective-permute-done.8 = f32[192,128]{1,0:T(8,128)S(1)} collective-permute-done((f32[192,128]{1,0:T(8,128)S(1)}, f32[192,128]{1,0:T(8,128)S(1)}, u32[]{:S(2)}, u32[]{:S(2)}) %collective-permute-start.8) | collective-permute-done | bytes 98336 | tf_op jit(solution)/shard_map/ppermute | solution.py:326
  44.6 7.0 %collective-permute-start.9 = (f32[192,128]{1,0:T(8,128)S(1)}, f32[192,128]{1,0:T(8,128)S(1)}, u32[]{:S(2)}, u32[]{:S(2)}) collective-permute-start(f32[192,128]{1,0:T(8,128)S(1)} %multiply_add_fusion.6.refs_1_), channel_id=1, source_target_pairs={{0,224},{1,97},{2,226},{3,99},{4,228},{5,101},{6,230},{7,103},{8,2... | collective-permute-start | bytes 294920 | tf_op jit(solution)/shard_map/ppermute | solution.py:326
  51.5 2.6 %collective-permute-done.9.refs_2_ = f32[192,128]{1,0:T(8,128)S(1)} collective-permute-done((f32[192,128]{1,0:T(8,128)S(1)}, f32[192,128]{1,0:T(8,128)S(1)}, u32[]{:S(2)}, u32[]{:S(2)}) %collective-permute-start.9) | collective-permute-done | bytes 98336 | tf_op jit(solution)/shard_map/ppermute | solution.py:326
  56.8 2.4 %collective-permute-start.10 = (f32[128,128]{1,0:T(8,128)S(1)}, f32[128,128]{1,0:T(8,128)S(1)}, u32[]{:S(2)}, u32[]{:S(2)}) collective-permute-start(f32[128,128]{1,0:T(8,128)S(1)} %get-tuple-element.29), channel_id=1, source_target_pairs={{0,2},{1,3},{2,0},{3,1},{4,6},{5,7},{6,4},{7,5},{8,10},{9,11},{10,... | collective-permute-start | bytes 196616 | tf_op jit(solution)/shard_map/ppermute | solution.py:326
  64.2 2.5 %shard_map.63 = (f32[192,128]{1,0:T(8,128)S(1)}, f32[128,128]{1,0:T(8,128)S(1)}) custom-call(s32[2,32]{1,0:T(2,128)S(4)} %get-tuple-element.19.tiles, s32[1,1]{1,0:T(1,128)S(6)} %copy.6.counts, f32[32,256,256]{2,1,0:T(8,128)S(1)} %shard_map.60.cost, f32[192,128]{1,0:T(8,128)S(1)} %get-tuple-element.28.refs_0_, f32[128,128]{1,0:T(8,128)S(1)} %multiply_add_fusion.10.refs_1_, ...), custom_call_target="tpu_custom_call" | custom-call | tf_op jit(solution)/shard_map/pallas_call | solution.py:300
  66.6 2.8 %collective-permute-start.16 = (f32[192,128]{1,0:T(8,128)S(1)}, f32[192,128]{1,0:T(8,128)S(1)}, u32[]{:S(2)}, u32[]{:S(2)}) collective-permute-start(f32[192,128]{1,0:T(8,128)S(1)} %get-tuple-element.31), channel_id=1, source_target_pairs={{0,24},{1,25},{2,26},{3,27},{4,28},{5,29},{6,30},{7,31},{8,16},{9,... | collective-permute-start | bytes 294920 | tf_op jit(solution)/shard_map/ppermute | solution.py:326
  69.4 2.3 %collective-permute-start.15 = (f32[192,128]{1,0:T(8,128)S(1)}, f32[192,128]{1,0:T(8,128)S(1)}, u32[]{:S(2)}, u32[]{:S(2)}) collective-permute-start(f32[192,128]{1,0:T(8,128)S(1)} %get-tuple-element.31), channel_id=1, source_target_pairs={{0,16},{1,17},{2,18},{3,19},{4,20},{5,21},{6,22},{7,23},{8,24},{9,... | collective-permute-start | bytes 294920 | tf_op jit(solution)/shard_map/ppermute | solution.py:326
  72.0 3.6 %collective-permute-done.15 = f32[192,128]{1,0:T(8,128)S(1)} collective-permute-done((f32[192,128]{1,0:T(8,128)S(1)}, f32[192,128]{1,0:T(8,128)S(1)}, u32[]{:S(2)}, u32[]{:S(2)}) %collective-permute-start.15) | collective-permute-done | bytes 98336 | tf_op jit(solution)/shard_map/ppermute | solution.py:326
  76.4 6.5 %collective-permute-start.17 = (f32[192,128]{1,0:T(8,128)S(1)}, f32[192,128]{1,0:T(8,128)S(1)}, u32[]{:S(2)}, u32[]{:S(2)}) collective-permute-start(f32[192,128]{1,0:T(8,128)S(1)} %multiply_add_fusion.5), channel_id=1, source_target_pairs={{0,32},{1,33},{2,34},{3,35},{4,36},{5,37},{6,38},{7,39},{8,40},{9,... | collective-permute-start | bytes 294920 | tf_op jit(solution)/shard_map/ppermute | solution.py:326
  82.9 3.0 %collective-permute-done.17 = f32[192,128]{1,0:T(8,128)S(1)} collective-permute-done((f32[192,128]{1,0:T(8,128)S(1)}, f32[192,128]{1,0:T(8,128)S(1)}, u32[]{:S(2)}, u32[]{:S(2)}) %collective-permute-start.17) | collective-permute-done | bytes 98336 | tf_op jit(solution)/shard_map/ppermute | solution.py:326
  85.9 6.6 %collective-permute-start.18 = (f32[192,128]{1,0:T(8,128)S(1)}, f32[192,128]{1,0:T(8,128)S(1)}, u32[]{:S(2)}, u32[]{:S(2)}) collective-permute-start(f32[192,128]{1,0:T(8,128)S(1)} %multiply_add_fusion.4), channel_id=1, source_target_pairs={{0,96},{1,225},{2,98},{3,227},{4,100},{5,229},{6,102},{7,231},{8,1... | collective-permute-start | bytes 294920 | tf_op jit(solution)/shard_map/ppermute | solution.py:326
  92.5 2.6 %collective-permute-done.18 = f32[192,128]{1,0:T(8,128)S(1)} collective-permute-done((f32[192,128]{1,0:T(8,128)S(1)}, f32[192,128]{1,0:T(8,128)S(1)}, u32[]{:S(2)}, u32[]{:S(2)}) %collective-permute-start.18) | collective-permute-done | bytes 98336 | tf_op jit(solution)/shard_map/ppermute | solution.py:326
  95.2 7.6 %collective-permute-start.19 = (f32[192,128]{1,0:T(8,128)S(1)}, f32[192,128]{1,0:T(8,128)S(1)}, u32[]{:S(2)}, u32[]{:S(2)}) collective-permute-start(f32[192,128]{1,0:T(8,128)S(1)} %multiply_add_fusion.3.refs_1_), channel_id=1, source_target_pairs={{0,224},{1,97},{2,226},{3,99},{4,228},{5,101},{6,230},{7,103},{8,2... | collective-permute-start | bytes 294920 | tf_op jit(solution)/shard_map/ppermute | solution.py:326
  102.8 3.0 %collective-permute-done.19.refs_2_ = f32[192,128]{1,0:T(8,128)S(1)} collective-permute-done((f32[192,128]{1,0:T(8,128)S(1)}, f32[192,128]{1,0:T(8,128)S(1)}, u32[]{:S(2)}, u32[]{:S(2)}) %collective-permute-start.19) | collective-permute-done | bytes 98336 | tf_op jit(solution)/shard_map/ppermute | solution.py:326
  106.7 2.7 %collective-permute-start.21 = (f32[128,128]{1,0:T(8,128)S(1)}, f32[128,128]{1,0:T(8,128)S(1)}, u32[]{:S(2)}, u32[]{:S(2)}) collective-permute-start(f32[128,128]{1,0:T(8,128)S(1)} %get-tuple-element.33), channel_id=1, source_target_pairs={{0,4},{1,5},{2,6},{3,7},{4,0},{5,1},{6,2},{7,3},{8,12},{9,13},{10,... | collective-permute-start | bytes 196616 | tf_op jit(solution)/shard_map/ppermute | solution.py:326
  115.2 2.4 %shard_map.65 = (f32[192,128]{1,0:T(8,128)S(1)}, f32[128,128]{1,0:T(8,128)}) custom-call(s32[2,32]{1,0:T(2,128)S(4)} %get-tuple-element.19.tiles, s32[1,1]{1,0:T(1,128)S(6)} %copy.6.counts, f32[32,256,256]{2,1,0:T(8,128)S(1)} %shard_map.60.cost, f32[192,128]{1,0:T(8,128)S(1)} %get-tuple-element.32.refs_0_, f32[128,128]{1,0:T(8,128)S(1)} %multiply_add_fusion.9.refs_1_, ...), custom_call_target="tpu_custom_call" | custom-call | tf_op jit(solution)/shard_map/pallas_call | solution.py:300
  117.6 2.4 %collective-permute-start.26 = (f32[192,128]{1,0:T(8,128)S(1)}, f32[192,128]{1,0:T(8,128)S(1)}, u32[]{:S(2)}, u32[]{:S(2)}) collective-permute-start(f32[192,128]{1,0:T(8,128)S(1)} %get-tuple-element.35), channel_id=1, source_target_pairs={{0,24},{1,25},{2,26},{3,27},{4,28},{5,29},{6,30},{7,31},{8,16},{9,... | collective-permute-start | bytes 294920 | tf_op jit(solution)/shard_map/ppermute | solution.py:326
  122.6 3.6 %collective-permute-done.25 = f32[192,128]{1,0:T(8,128)S(1)} collective-permute-done((f32[192,128]{1,0:T(8,128)S(1)}, f32[192,128]{1,0:T(8,128)S(1)}, u32[]{:S(2)}, u32[]{:S(2)}) %collective-permute-start.25) | collective-permute-done | bytes 98336 | tf_op jit(solution)/shard_map/ppermute | solution.py:326
  127.0 7.8 %collective-permute-start.27 = (f32[192,128]{1,0:T(8,128)S(1)}, f32[192,128]{1,0:T(8,128)S(1)}, u32[]{:S(2)}, u32[]{:S(2)}) collective-permute-start(f32[192,128]{1,0:T(8,128)S(1)} %multiply_add_fusion.2), channel_id=1, source_target_pairs={{0,32},{1,33},{2,34},{3,35},{4,36},{5,37},{6,38},{7,39},{8,40},{9,... | collective-permute-start | bytes 294920 | tf_op jit(solution)/shard_map/ppermute | solution.py:326
  134.8 3.0 %collective-permute-done.27 = f32[192,128]{1,0:T(8,128)S(1)} collective-permute-done((f32[192,128]{1,0:T(8,128)S(1)}, f32[192,128]{1,0:T(8,128)S(1)}, u32[]{:S(2)}, u32[]{:S(2)}) %collective-permute-start.27) | collective-permute-done | bytes 98336 | tf_op jit(solution)/shard_map/ppermute | solution.py:326
  137.9 6.6 %collective-permute-done.28 = f32[192,128]{1,0:T(8,128)S(1)} collective-permute-done((f32[192,128]{1,0:T(8,128)S(1)}, f32[192,128]{1,0:T(8,128)S(1)}, u32[]{:S(2)}, u32[]{:S(2)}) %collective-permute-start.28) | collective-permute-done | bytes 98336 | tf_op jit(solution)/shard_map/ppermute | solution.py:326
  144.6 8.8 %collective-permute-start.29 = (f32[192,128]{1,0:T(8,128)S(1)}, f32[192,128]{1,0:T(8,128)S(1)}, u32[]{:S(2)}, u32[]{:S(2)}) collective-permute-start(f32[192,128]{1,0:T(8,128)S(1)} %multiply_add_fusion), channel_id=1, source_target_pairs={{0,224},{1,97},{2,226},{3,99},{4,228},{5,101},{6,230},{7,103},{8,2... | collective-permute-start | bytes 294920 | tf_op jit(solution)/shard_map/ppermute | solution.py:326
  153.4 2.6 %collective-permute-done.29 = f32[192,128]{1,0:T(8,128)S(1)} collective-permute-done((f32[192,128]{1,0:T(8,128)S(1)}, f32[192,128]{1,0:T(8,128)S(1)}, u32[]{:S(2)}, u32[]{:S(2)}) %collective-permute-start.29) | collective-permute-done | bytes 98336 | tf_op jit(solution)/shard_map/ppermute | solution.py:326
  (48 shorter events, 27.6 us)
Async XLA Ops:
  5.2 7.3 %collective-permute-start.2 = (f32[128,128]{1,0:T(8,128)S(1)}, f32[128,128]{1,0:T(8,128)S(1)}, u32[]{:S(2)}, u32[]{:S(2)}) collective-permute-start(f32[128,128]{1,0:T(8,128)S(1)} %get-tuple-element.20), channel_id=1, source_target_pairs={{0,6},{1,7},{2,4},{3,5},{4,2},{5,3},{6,0},{7,1},{8,14},{9,15},{10,... | collective-permute-start | bytes 196616 | tf_op jit(solution)/shard_map/ppermute | solution.py:326
  9.1 6.4 %collective-permute-start.1 = (f32[128,128]{1,0:T(8,128)S(1)}, f32[128,128]{1,0:T(8,128)S(1)}, u32[]{:S(2)}, u32[]{:S(2)}) collective-permute-start(f32[128,128]{1,0:T(8,128)S(1)} %get-tuple-element.20), channel_id=1, source_target_pairs={{0,4},{1,5},{2,6},{3,7},{4,0},{5,1},{6,2},{7,3},{8,12},{9,13},{10,... | collective-permute-start | bytes 196616 | tf_op jit(solution)/shard_map/ppermute | solution.py:326
  9.7 5.8 %collective-permute-start = (f32[128,128]{1,0:T(8,128)S(1)}, f32[128,128]{1,0:T(8,128)S(1)}, u32[]{:S(2)}, u32[]{:S(2)}) collective-permute-start(f32[128,128]{1,0:T(8,128)S(1)} %get-tuple-element.20), channel_id=1, source_target_pairs={{0,2},{1,3},{2,0},{3,1},{4,6},{5,7},{6,4},{7,5},{8,10},{9,11},{10,... | collective-permute-start | bytes 196616 | tf_op jit(solution)/shard_map/ppermute | solution.py:326
  15.6 1.3 collective-permute-start.3
  19.4 5.6 %collective-permute-start.6 = (f32[192,128]{1,0:T(8,128)S(1)}, f32[192,128]{1,0:T(8,128)S(1)}, u32[]{:S(2)}, u32[]{:S(2)}) collective-permute-start(f32[192,128]{1,0:T(8,128)S(1)} %get-tuple-element.27), channel_id=1, source_target_pairs={{0,24},{1,25},{2,26},{3,27},{4,28},{5,29},{6,30},{7,31},{8,16},{9,... | collective-permute-start | bytes 294920 | tf_op jit(solution)/shard_map/ppermute | solution.py:326
  22.4 6.2 %collective-permute-start.5 = (f32[192,128]{1,0:T(8,128)S(1)}, f32[192,128]{1,0:T(8,128)S(1)}, u32[]{:S(2)}, u32[]{:S(2)}) collective-permute-start(f32[192,128]{1,0:T(8,128)S(1)} %get-tuple-element.27), channel_id=1, source_target_pairs={{0,16},{1,17},{2,18},{3,19},{4,20},{5,21},{6,22},{7,23},{8,24},{9,... | collective-permute-start | bytes 294920 | tf_op jit(solution)/shard_map/ppermute | solution.py:326
  22.4 6.2 %collective-permute-start.4 = (f32[192,128]{1,0:T(8,128)S(1)}, f32[192,128]{1,0:T(8,128)S(1)}, u32[]{:S(2)}, u32[]{:S(2)}) collective-permute-start(f32[192,128]{1,0:T(8,128)S(1)} %get-tuple-element.27), channel_id=1, source_target_pairs={{0,8},{1,9},{2,10},{3,11},{4,12},{5,13},{6,14},{7,15},{8,0},{9,1},... | collective-permute-start | bytes 294920 | tf_op jit(solution)/shard_map/ppermute | solution.py:326
  28.7 6.3 %collective-permute-start.7 = (f32[192,128]{1,0:T(8,128)S(1)}, f32[192,128]{1,0:T(8,128)S(1)}, u32[]{:S(2)}, u32[]{:S(2)}) collective-permute-start(f32[192,128]{1,0:T(8,128)S(1)} %multiply_add_fusion.8), channel_id=1, source_target_pairs={{0,32},{1,33},{2,34},{3,35},{4,36},{5,37},{6,38},{7,39},{8,40},{9,... | collective-permute-start | bytes 294920 | tf_op jit(solution)/shard_map/ppermute | solution.py:326
  35.0 9.5 %collective-permute-start.8 = (f32[192,128]{1,0:T(8,128)S(1)}, f32[192,128]{1,0:T(8,128)S(1)}, u32[]{:S(2)}, u32[]{:S(2)}) collective-permute-start(f32[192,128]{1,0:T(8,128)S(1)} %multiply_add_fusion.7), channel_id=1, source_target_pairs={{0,96},{1,225},{2,98},{3,227},{4,100},{5,229},{6,102},{7,231},{8,1... | collective-permute-start | bytes 294920 | tf_op jit(solution)/shard_map/ppermute | solution.py:326
  44.6 9.6 %collective-permute-start.9 = (f32[192,128]{1,0:T(8,128)S(1)}, f32[192,128]{1,0:T(8,128)S(1)}, u32[]{:S(2)}, u32[]{:S(2)}) collective-permute-start(f32[192,128]{1,0:T(8,128)S(1)} %multiply_add_fusion.6.refs_1_), channel_id=1, source_target_pairs={{0,224},{1,97},{2,226},{3,99},{4,228},{5,101},{6,230},{7,103},{8,2... | collective-permute-start | bytes 294920 | tf_op jit(solution)/shard_map/ppermute | solution.py:326
  55.0 5.6 %collective-permute-start.12 = (f32[128,128]{1,0:T(8,128)S(1)}, f32[128,128]{1,0:T(8,128)S(1)}, u32[]{:S(2)}, u32[]{:S(2)}) collective-permute-start(f32[128,128]{1,0:T(8,128)S(1)} %get-tuple-element.29), channel_id=1, source_target_pairs={{0,6},{1,7},{2,4},{3,5},{4,2},{5,3},{6,0},{7,1},{8,14},{9,15},{10,... | collective-permute-start | bytes 196616 | tf_op jit(solution)/shard_map/ppermute | solution.py:326
  56.8 5.8 %collective-permute-start.11 = (f32[128,128]{1,0:T(8,128)S(1)}, f32[128,128]{1,0:T(8,128)S(1)}, u32[]{:S(2)}, u32[]{:S(2)}) collective-permute-start(f32[128,128]{1,0:T(8,128)S(1)} %get-tuple-element.29), channel_id=1, source_target_pairs={{0,4},{1,5},{2,6},{3,7},{4,0},{5,1},{6,2},{7,3},{8,12},{9,13},{10,... | collective-permute-start | bytes 196616 | tf_op jit(solution)/shard_map/ppermute | solution.py:326
  56.8 5.8 %collective-permute-start.10 = (f32[128,128]{1,0:T(8,128)S(1)}, f32[128,128]{1,0:T(8,128)S(1)}, u32[]{:S(2)}, u32[]{:S(2)}) collective-permute-start(f32[128,128]{1,0:T(8,128)S(1)} %get-tuple-element.29), channel_id=1, source_target_pairs={{0,2},{1,3},{2,0},{3,1},{4,6},{5,7},{6,4},{7,5},{8,10},{9,11},{10,... | collective-permute-start | bytes 196616 | tf_op jit(solution)/shard_map/ppermute | solution.py:326
  62.7 1.5 collective-permute-start.13
  66.6 5.4 %collective-permute-start.16 = (f32[192,128]{1,0:T(8,128)S(1)}, f32[192,128]{1,0:T(8,128)S(1)}, u32[]{:S(2)}, u32[]{:S(2)}) collective-permute-start(f32[192,128]{1,0:T(8,128)S(1)} %get-tuple-element.31), channel_id=1, source_target_pairs={{0,24},{1,25},{2,26},{3,27},{4,28},{5,29},{6,30},{7,31},{8,16},{9,... | collective-permute-start | bytes 294920 | tf_op jit(solution)/shard_map/ppermute | solution.py:326
  69.4 6.2 %collective-permute-start.15 = (f32[192,128]{1,0:T(8,128)S(1)}, f32[192,128]{1,0:T(8,128)S(1)}, u32[]{:S(2)}, u32[]{:S(2)}) collective-permute-start(f32[192,128]{1,0:T(8,128)S(1)} %get-tuple-element.31), channel_id=1, source_target_pairs={{0,16},{1,17},{2,18},{3,19},{4,20},{5,21},{6,22},{7,23},{8,24},{9,... | collective-permute-start | bytes 294920 | tf_op jit(solution)/shard_map/ppermute | solution.py:326
  71.7 4.6 %collective-permute-start.14 = (f32[192,128]{1,0:T(8,128)S(1)}, f32[192,128]{1,0:T(8,128)S(1)}, u32[]{:S(2)}, u32[]{:S(2)}) collective-permute-start(f32[192,128]{1,0:T(8,128)S(1)} %get-tuple-element.31), channel_id=1, source_target_pairs={{0,8},{1,9},{2,10},{3,11},{4,12},{5,13},{6,14},{7,15},{8,0},{9,1},... | collective-permute-start | bytes 294920 | tf_op jit(solution)/shard_map/ppermute | solution.py:326
  76.4 9.5 %collective-permute-start.17 = (f32[192,128]{1,0:T(8,128)S(1)}, f32[192,128]{1,0:T(8,128)S(1)}, u32[]{:S(2)}, u32[]{:S(2)}) collective-permute-start(f32[192,128]{1,0:T(8,128)S(1)} %multiply_add_fusion.5), channel_id=1, source_target_pairs={{0,32},{1,33},{2,34},{3,35},{4,36},{5,37},{6,38},{7,39},{8,40},{9,... | collective-permute-start | bytes 294920 | tf_op jit(solution)/shard_map/ppermute | solution.py:326
  85.9 9.1 %collective-permute-start.18 = (f32[192,128]{1,0:T(8,128)S(1)}, f32[192,128]{1,0:T(8,128)S(1)}, u32[]{:S(2)}, u32[]{:S(2)}) collective-permute-start(f32[192,128]{1,0:T(8,128)S(1)} %multiply_add_fusion.4), channel_id=1, source_target_pairs={{0,96},{1,225},{2,98},{3,227},{4,100},{5,229},{6,102},{7,231},{8,1... | collective-permute-start | bytes 294920 | tf_op jit(solution)/shard_map/ppermute | solution.py:326
  95.2 10.6 %collective-permute-start.19 = (f32[192,128]{1,0:T(8,128)S(1)}, f32[192,128]{1,0:T(8,128)S(1)}, u32[]{:S(2)}, u32[]{:S(2)}) collective-permute-start(f32[192,128]{1,0:T(8,128)S(1)} %multiply_add_fusion.3.refs_1_), channel_id=1, source_target_pairs={{0,224},{1,97},{2,226},{3,99},{4,228},{5,101},{6,230},{7,103},{8,2... | collective-permute-start | bytes 294920 | tf_op jit(solution)/shard_map/ppermute | solution.py:326
  106.6 6.3 %collective-permute-start.22 = (f32[128,128]{1,0:T(8,128)S(1)}, f32[128,128]{1,0:T(8,128)S(1)}, u32[]{:S(2)}, u32[]{:S(2)}) collective-permute-start(f32[128,128]{1,0:T(8,128)S(1)} %get-tuple-element.33), channel_id=1, source_target_pairs={{0,6},{1,7},{2,4},{3,5},{4,2},{5,3},{6,0},{7,1},{8,14},{9,15},{10,... | collective-permute-start | bytes 196616 | tf_op jit(solution)/shard_map/ppermute | solution.py:326
  106.7 6.2 %collective-permute-start.21 = (f32[128,128]{1,0:T(8,128)S(1)}, f32[128,128]{1,0:T(8,128)S(1)}, u32[]{:S(2)}, u32[]{:S(2)}) collective-permute-start(f32[128,128]{1,0:T(8,128)S(1)} %get-tuple-element.33), channel_id=1, source_target_pairs={{0,4},{1,5},{2,6},{3,7},{4,0},{5,1},{6,2},{7,3},{8,12},{9,13},{10,... | collective-permute-start | bytes 196616 | tf_op jit(solution)/shard_map/ppermute | solution.py:326
  109.4 4.3 %collective-permute-start.20 = (f32[128,128]{1,0:T(8,128)S(1)}, f32[128,128]{1,0:T(8,128)S(1)}, u32[]{:S(2)}, u32[]{:S(2)}) collective-permute-start(f32[128,128]{1,0:T(8,128)S(1)} %get-tuple-element.33), channel_id=1, source_target_pairs={{0,2},{1,3},{2,0},{3,1},{4,6},{5,7},{6,4},{7,5},{8,10},{9,11},{10,... | collective-permute-start | bytes 196616 | tf_op jit(solution)/shard_map/ppermute | solution.py:326
  113.8 1.3 collective-permute-start.23
  117.6 5.0 %collective-permute-start.26 = (f32[192,128]{1,0:T(8,128)S(1)}, f32[192,128]{1,0:T(8,128)S(1)}, u32[]{:S(2)}, u32[]{:S(2)}) collective-permute-start(f32[192,128]{1,0:T(8,128)S(1)} %get-tuple-element.35), channel_id=1, source_target_pairs={{0,24},{1,25},{2,26},{3,27},{4,28},{5,29},{6,30},{7,31},{8,16},{9,... | collective-permute-start | bytes 294920 | tf_op jit(solution)/shard_map/ppermute | solution.py:326
  120.0 6.2 %collective-permute-start.25 = (f32[192,128]{1,0:T(8,128)S(1)}, f32[192,128]{1,0:T(8,128)S(1)}, u32[]{:S(2)}, u32[]{:S(2)}) collective-permute-start(f32[192,128]{1,0:T(8,128)S(1)} %get-tuple-element.35), channel_id=1, source_target_pairs={{0,16},{1,17},{2,18},{3,19},{4,20},{5,21},{6,22},{7,23},{8,24},{9,... | collective-permute-start | bytes 294920 | tf_op jit(solution)/shard_map/ppermute | solution.py:326
  122.3 4.6 %collective-permute-start.24 = (f32[192,128]{1,0:T(8,128)S(1)}, f32[192,128]{1,0:T(8,128)S(1)}, u32[]{:S(2)}, u32[]{:S(2)}) collective-permute-start(f32[192,128]{1,0:T(8,128)S(1)} %get-tuple-element.35), channel_id=1, source_target_pairs={{0,8},{1,9},{2,10},{3,11},{4,12},{5,13},{6,14},{7,15},{8,0},{9,1},... | collective-permute-start | bytes 294920 | tf_op jit(solution)/shard_map/ppermute | solution.py:326
  127.0 10.7 %collective-permute-start.27 = (f32[192,128]{1,0:T(8,128)S(1)}, f32[192,128]{1,0:T(8,128)S(1)}, u32[]{:S(2)}, u32[]{:S(2)}) collective-permute-start(f32[192,128]{1,0:T(8,128)S(1)} %multiply_add_fusion.2), channel_id=1, source_target_pairs={{0,32},{1,33},{2,34},{3,35},{4,36},{5,37},{6,38},{7,39},{8,40},{9,... | collective-permute-start | bytes 294920 | tf_op jit(solution)/shard_map/ppermute | solution.py:326
  137.8 6.7 %collective-permute-start.28 = (f32[192,128]{1,0:T(8,128)S(1)}, f32[192,128]{1,0:T(8,128)S(1)}, u32[]{:S(2)}, u32[]{:S(2)}) collective-permute-start(f32[192,128]{1,0:T(8,128)S(1)} %multiply_add_fusion.1), channel_id=1, source_target_pairs={{0,96},{1,225},{2,98},{3,227},{4,100},{5,229},{6,102},{7,231},{8,1... | collective-permute-start | bytes 294920 | tf_op jit(solution)/shard_map/ppermute | solution.py:326
  144.6 11.4 %collective-permute-start.29 = (f32[192,128]{1,0:T(8,128)S(1)}, f32[192,128]{1,0:T(8,128)S(1)}, u32[]{:S(2)}, u32[]{:S(2)}) collective-permute-start(f32[192,128]{1,0:T(8,128)S(1)} %multiply_add_fusion), channel_id=1, source_target_pairs={{0,224},{1,97},{2,226},{3,99},{4,228},{5,101},{6,230},{7,103},{8,2... | collective-permute-start | bytes 294920 | tf_op jit(solution)/shard_map/ppermute | solution.py:326

commit v11 on v8

--- a/solution.py
+++ b/solution.py
@@ -338,10 +338,31 @@
     return fan(value, "tgt", (6, 4), (4, 6), (2, 2))
 
 
+def hand(value, giver):
+    src, tgt = lax.axis_size("src"), lax.axis_size("tgt")
+    pairs = [(s * tgt + t, s * tgt + (t ^ 1)) for s in range(src) for t in range(giver, tgt, 2)]
+    return lax.ppermute(value, ("src", "tgt"), pairs)
+
+
+def among(value, *flips):
+    src, tgt = lax.axis_size("src"), lax.axis_size("tgt")
+    got = [value]
+    for flip in flips:
+        pairs = [(s * tgt + t, (s ^ flip) * tgt + t) for s in range(src) for t in range(1, tgt, 2)]
+        got.append(lax.ppermute(value, ("src", "tgt"), pairs))
+    return got
+
+
 def over_src(value):
-    for flips in ((28, 12), (12, 28), (4, 4)):
-        value = lse2_many(fan(value, "src", flips))
-    return fan(value, "src", (3, 2), (2, 3), (1, 1))
+    rows = value.shape[0]
+    second = lax.axis_index("tgt") % 2 == 1
+    both = jnp.concatenate([value, hand(value, 0)], axis=0)
+    for flips in ((3, 2, 1), (4,), (12,)):
+        both = lse2_many(among(both, *flips))
+    parts = among(both, 28)
+    own = lse2_many([part[:rows] for part in parts])
+    other = hand(lse2_many([part[rows:] for part in parts]), 1)
+    return [jnp.where(second, own, other)]
 
 
 def body(src_points, tgt_points, tiles, counts):

time: 153 us -> 210 us (1.37)
  the two profiles are of different devices: /device:TPU:40 before, /device:TPU:2 now
where the time goes in v11:
time: 210 us; the launch traced here: 208 us
  waiting for transfers between devices  138 us (66%)
  starting transfers between devices  42.8 us (20%)
  Pallas kernels  15.6 us (7%)
  local copies, waits for them, and re-layouts  6.68 us (3%)
  other arithmetic  2.39 us (1%)
    ppermute x6, waiting for transfers between devices, hand(): return lax.ppermute(value, ('src', 'tgt'), pairs)  126 us
    ppermute x12, starting transfers between devices, swap(): return lax.ppermute(value, ('src', 'tgt'), pairs)  16.1 us
    ppermute x6, starting transfers between devices, hand(): return lax.ppermute(value, ('src', 'tgt'), pairs)  14.5 us
    ppermute x18, starting transfers between devices, among(): got.append(lax.ppermute(value, ('src', 'tgt'), pairs))  12.1 us
    ppermute x12, waiting for transfers between devices, swap(): return lax.ppermute(value, ('src', 'tgt'), pairs)  12 us
    pallas_call x5, Pallas kernels, sweep(): pl.pallas_call(kernel, out_shape=(jax.ShapeDtypeStruct((2 * blocks_out, H...  9.93 us
    unnamed x11, local copies, waits for them, and re-layouts  6.65 us
    pallas_call x1, Pallas kernels, costs(): pl.pallas_call(functools.partial(cost_kernel, blocks_in, blocks_out), out...  4.7 us
  transfers between devices with their start and end apart: 36, of which 16 were waited for; matrix products, arithmetic and copies ran while one was open for 0% of the time, Pallas kernels for 0%

profile of v11, /device:TPU:2, one launch (start us, length us, event | category | flops | bytes accessed | tf_op | source)
XLA Modules:
  0.0 207.6 jit_solution(4376851858766278917)
XLA Ops:
  1.3 4.7 %shard_map.59 = (f32[32,256,256]{2,1,0:T(8,128)S(1)}, f32[128,128]{1,0:T(8,128)S(1)}, bf16[32,128,256]{2,1,0:T(8,128)(2,1)S(1)}, bf16[32,128,256]{2,1,0:T(8,128)(2,1)S(1)}, s32[2,32]{1,0:T(2,128)S(4)}) custom-call(s32[2,32]{1,0:T(2,128)} %bitcast.4, s32[1,1]{1,0:T(1,128)S(6)} %copy.9.counts, f32[50,16384]{1,0:T(8,128)} %src.1, f32[50,24576]{1,0:T(8,128)} %tgt.1), custom_call_target="tpu_custom_call" | custom-call | tf_op jit(solution)/shard_map/pallas_call | solution.py:255
  6.0 3.2 %copy-done.2 = f32[32,256,256]{2,1,0:T(8,128)} copy-done((f32[32,256,256]{2,1,0:T(8,128)}, f32[32,256,256]{2,1,0:T(8,128)S(1)}, u32[]{:S(2)}) %copy-start.2) | copy-done | bytes 8388632
  9.2 1.3 collective-permute-start
  11.5 1.3 collective-permute-start.1
  12.8 2.4 %collective-permute-start.2 = (f32[128,128]{1,0:T(8,128)S(1)}, f32[128,128]{1,0:T(8,128)S(1)}, u32[]{:S(2)}, u32[]{:S(2)}) collective-permute-start(f32[128,128]{1,0:T(8,128)S(1)} %multiply_add_fusion.14.refs_0_), channel_id=1, source_target_pairs={{0,4},{1,7},{2,6},{3,5},{4,0},{5,3},{6,2},{7,1},{8,12},{9,15},{10,... | collective-permute-start | bytes 196616 | tf_op jit(solution)/shard_map/ppermute | solution.py:326
  15.7 0.9 shard_map.60.cost
  16.7 1.7 collective-permute-done.1.refs_1_
  18.4 0.9 collective-permute-done.2.refs_2_
  19.6 2.7 %shard_map.61 = (f32[192,128]{1,0:T(8,128)S(1)}, f32[128,128]{1,0:T(8,128)S(1)}) custom-call(s32[2,32]{1,0:T(2,128)S(4)} %get-tuple-element.19.tiles, s32[1,1]{1,0:T(1,128)S(6)} %copy.9.counts, f32[32,256,256]{2,1,0:T(8,128)S(1)} %shard_map.60.cost, f32[128,128]{1,0:T(8,128)S(1)} %multiply_add_fusion.14.refs_0_, ...), custom_call_target="tpu_custom_call" | custom-call | tf_op jit(solution)/shard_map/pallas_call | solution.py:300
  22.4 3.9 %collective-permute-start.4 = (f32[192,128]{1,0:T(8,128)S(1)}, f32[192,128]{1,0:T(8,128)S(1)}, u32[]{:S(2)}, u32[]{:S(2)}) collective-permute-start(f32[192,128]{1,0:T(8,128)S(1)} %get-tuple-element.27), channel_id=1, source_target_pairs={{0,1},{2,3},{4,5},{6,7},{8,9},{10,11},{12,13},{14,15},{16,17},{18,... | collective-permute-start | bytes 294920 | tf_op jit(solution)/shard_map/ppermute | solution.py:344
  26.3 0.9 collective-permute-done.4
  31.9 1.3 collective-permute-start.11
  33.2 39.9 %collective-permute-done.11 = f32[192,128]{1,0:T(8,128)S(1)} collective-permute-done((f32[192,128]{1,0:T(8,128)S(1)}, f32[192,128]{1,0:T(8,128)S(1)}, u32[]{:S(2)}, u32[]{:S(2)}) %collective-permute-start.11) | collective-permute-done | bytes 98336 | tf_op jit(solution)/shard_map/ppermute | solution.py:344
  73.2 3.4 %copy-done.3 = f32[32,256,256]{2,1,0:T(8,128)S(1)} copy-done((f32[32,256,256]{2,1,0:T(8,128)S(1)}, f32[32,256,256]{2,1,0:T(8,128)}, u32[]{:S(2)}) %copy-start.3) | copy-done | bytes 8388632
  77.4 1.3 collective-permute-start.12
  79.7 1.5 collective-permute-start.13
  81.2 2.7 %collective-permute-start.15 = (f32[128,128]{1,0:T(8,128)S(1)}, f32[128,128]{1,0:T(8,128)S(1)}, u32[]{:S(2)}, u32[]{:S(2)}) collective-permute-start(f32[128,128]{1,0:T(8,128)S(1)} %multiply_add_fusion.13.refs_1_), channel_id=1, source_target_pairs={{0,2},{1,3},{2,0},{3,1},{4,6},{5,7},{6,4},{7,5},{8,10},{9,11},{10,... | collective-permute-start | bytes 196616 | tf_op jit(solution)/shard_map/ppermute | solution.py:326
  83.9 2.3 %collective-permute-done.13.refs_2_ = f32[128,128]{1,0:T(8,128)S(1)} collective-permute-done((f32[128,128]{1,0:T(8,128)S(1)}, f32[128,128]{1,0:T(8,128)S(1)}, u32[]{:S(2)}, u32[]{:S(2)}) %collective-permute-start.13) | collective-permute-done | bytes 65568 | tf_op jit(solution)/shard_map/ppermute | solution.py:326
  87.0 2.7 %shard_map.63 = (f32[192,128]{1,0:T(8,128)S(1)}, f32[128,128]{1,0:T(8,128)S(1)}) custom-call(s32[2,32]{1,0:T(2,128)S(4)} %get-tuple-element.19.tiles, s32[1,1]{1,0:T(1,128)S(6)} %copy.9.counts, f32[32,256,256]{2,1,0:T(8,128)S(1)} %copy-done.1, f32[192,128]{1,0:T(8,128)S(1)} %get-tuple-element.28.refs_0_, f32[128,128]{1,0:T(8,128)S(1)} %multiply_add_fusion.13.refs_1_, ...), custom_call_target="tpu_custom_call" | custom-call | tf_op jit(solution)/shard_map/pallas_call | solution.py:300
  89.8 3.3 %collective-permute-start.16 = (f32[192,128]{1,0:T(8,128)S(1)}, f32[192,128]{1,0:T(8,128)S(1)}, u32[]{:S(2)}, u32[]{:S(2)}) collective-permute-start(f32[192,128]{1,0:T(8,128)S(1)} %get-tuple-element.31), channel_id=1, source_target_pairs={{0,1},{2,3},{4,5},{6,7},{8,9},{10,11},{12,13},{14,15},{16,17},{18,... | collective-permute-start | bytes 294920 | tf_op jit(solution)/shard_map/ppermute | solution.py:344
  93.0 0.9 collective-permute-done.16
  98.6 1.5 collective-permute-start.23
  100.1 41.4 %collective-permute-done.23 = f32[192,128]{1,0:T(8,128)S(1)} collective-permute-done((f32[192,128]{1,0:T(8,128)S(1)}, f32[192,128]{1,0:T(8,128)S(1)}, u32[]{:S(2)}, u32[]{:S(2)}) %collective-permute-start.23) | collective-permute-done | bytes 98336 | tf_op jit(solution)/shard_map/ppermute | solution.py:344
  142.4 0.9 collective-permute-start.24
  144.3 1.6 collective-permute-start.25
  145.9 2.5 %collective-permute-start.27 = (f32[128,128]{1,0:T(8,128)S(1)}, f32[128,128]{1,0:T(8,128)S(1)}, u32[]{:S(2)}, u32[]{:S(2)}) collective-permute-start(f32[128,128]{1,0:T(8,128)S(1)} %multiply_add_fusion.12.refs_1_), channel_id=1, source_target_pairs={{0,2},{1,3},{2,0},{3,1},{4,6},{5,7},{6,4},{7,5},{8,10},{9,11},{10,... | collective-permute-start | bytes 196616 | tf_op jit(solution)/shard_map/ppermute | solution.py:326
  148.5 2.4 %collective-permute-done.25.refs_2_ = f32[128,128]{1,0:T(8,128)S(1)} collective-permute-done((f32[128,128]{1,0:T(8,128)S(1)}, f32[128,128]{1,0:T(8,128)S(1)}, u32[]{:S(2)}, u32[]{:S(2)}) %collective-permute-start.25) | collective-permute-done | bytes 65568 | tf_op jit(solution)/shard_map/ppermute | solution.py:326
  151.7 2.7 %shard_map.65 = (f32[192,128]{1,0:T(8,128)S(1)}, f32[128,128]{1,0:T(8,128)}) custom-call(s32[2,32]{1,0:T(2,128)S(4)} %get-tuple-element.19.tiles, s32[1,1]{1,0:T(1,128)S(6)} %copy.9.counts, f32[32,256,256]{2,1,0:T(8,128)S(1)} %copy-done.1, f32[192,128]{1,0:T(8,128)S(1)} %get-tuple-element.32.refs_0_, f32[128,128]{1,0:T(8,128)S(1)} %multiply_add_fusion.12.refs_1_, ...), custom_call_target="tpu_custom_call" | custom-call | tf_op jit(solution)/shard_map/pallas_call | solution.py:300
  154.5 3.3 %collective-permute-start.28 = (f32[192,128]{1,0:T(8,128)S(1)}, f32[192,128]{1,0:T(8,128)S(1)}, u32[]{:S(2)}, u32[]{:S(2)}) collective-permute-start(f32[192,128]{1,0:T(8,128)S(1)} %get-tuple-element.35), channel_id=1, source_target_pairs={{0,1},{2,3},{4,5},{6,7},{8,9},{10,11},{12,13},{14,15},{16,17},{18,... | collective-permute-start | bytes 294920 | tf_op jit(solution)/shard_map/ppermute | solution.py:344
  157.8 0.9 collective-permute-done.28
  163.3 1.3 collective-permute-start.35
  164.6 42.2 %collective-permute-done.35 = f32[192,128]{1,0:T(8,128)S(1)} collective-permute-done((f32[192,128]{1,0:T(8,128)S(1)}, f32[192,128]{1,0:T(8,128)S(1)}, u32[]{:S(2)}, u32[]{:S(2)}) %collective-permute-start.35) | collective-permute-done | bytes 98336 | tf_op jit(solution)/shard_map/ppermute | solution.py:344
  (79 shorter events, 21.6 us)
Async XLA Ops:
  9.2 2.2 %collective-permute-start = (f32[128,128]{1,0:T(8,128)S(1)}, f32[128,128]{1,0:T(8,128)S(1)}, u32[]{:S(2)}, u32[]{:S(2)}) collective-permute-start(f32[128,128]{1,0:T(8,128)S(1)} %get-tuple-element.20), channel_id=1, source_target_pairs={{0,1},{1,0},{2,3},{3,2},{4,5},{5,4},{6,7},{7,6},{8,9},{9,8},{10,11... | collective-permute-start | bytes 196616 | tf_op jit(solution)/shard_map/ppermute | solution.py:326
  11.5 6.9 %collective-permute-start.1 = (f32[128,128]{1,0:T(8,128)S(1)}, f32[128,128]{1,0:T(8,128)S(1)}, u32[]{:S(2)}, u32[]{:S(2)}) collective-permute-start(f32[128,128]{1,0:T(8,128)S(1)} %multiply_add_fusion.14.refs_0_), channel_id=1, source_target_pairs={{0,6},{1,5},{2,4},{3,7},{4,2},{5,1},{6,0},{7,3},{8,14},{9,13},{10,... | collective-permute-start | bytes 196616 | tf_op jit(solution)/shard_map/ppermute | solution.py:326
  12.8 6.5 %collective-permute-start.2 = (f32[128,128]{1,0:T(8,128)S(1)}, f32[128,128]{1,0:T(8,128)S(1)}, u32[]{:S(2)}, u32[]{:S(2)}) collective-permute-start(f32[128,128]{1,0:T(8,128)S(1)} %multiply_add_fusion.14.refs_0_), channel_id=1, source_target_pairs={{0,4},{1,7},{2,6},{3,5},{4,0},{5,3},{6,2},{7,1},{8,12},{9,15},{10,... | collective-permute-start | bytes 196616 | tf_op jit(solution)/shard_map/ppermute | solution.py:326
  15.2 4.4 %collective-permute-start.3 = (f32[128,128]{1,0:T(8,128)S(1)}, f32[128,128]{1,0:T(8,128)S(1)}, u32[]{:S(2)}, u32[]{:S(2)}) collective-permute-start(f32[128,128]{1,0:T(8,128)S(1)} %multiply_add_fusion.14.refs_0_), channel_id=1, source_target_pairs={{0,2},{1,3},{2,0},{3,1},{4,6},{5,7},{6,4},{7,5},{8,10},{9,11},{10,... | collective-permute-start | bytes 196616 | tf_op jit(solution)/shard_map/ppermute | solution.py:326
  22.4 4.8 %collective-permute-start.4 = (f32[192,128]{1,0:T(8,128)S(1)}, f32[192,128]{1,0:T(8,128)S(1)}, u32[]{:S(2)}, u32[]{:S(2)}) collective-permute-start(f32[192,128]{1,0:T(8,128)S(1)} %get-tuple-element.27), channel_id=1, source_target_pairs={{0,1},{2,3},{4,5},{6,7},{8,9},{10,11},{12,13},{14,15},{16,17},{18,... | collective-permute-start | bytes 294920 | tf_op jit(solution)/shard_map/ppermute | solution.py:344
  27.2 2.0 collective-permute-start.5
  27.9 1.4 collective-permute-start.6
  28.6 0.7 collective-permute-start.7
  29.5 0.7 collective-permute-start.8
  30.3 0.7 collective-permute-start.9
  31.1 0.7 collective-permute-start.10
  31.9 41.3 %collective-permute-start.11 = (f32[192,128]{1,0:T(8,128)S(1)}, f32[192,128]{1,0:T(8,128)S(1)}, u32[]{:S(2)}, u32[]{:S(2)}) collective-permute-start(f32[192,128]{1,0:T(8,128)S(1)} %multiply_add_fusion.11), channel_id=1, source_target_pairs={{1,0},{3,2},{5,4},{7,6},{9,8},{11,10},{13,12},{15,14},{17,16},{19,... | collective-permute-start | bytes 294920 | tf_op jit(solution)/shard_map/ppermute | solution.py:344
  77.4 2.2 %collective-permute-start.12 = (f32[128,128]{1,0:T(8,128)S(1)}, f32[128,128]{1,0:T(8,128)S(1)}, u32[]{:S(2)}, u32[]{:S(2)}) collective-permute-start(f32[128,128]{1,0:T(8,128)S(1)} %get-tuple-element.29), channel_id=1, source_target_pairs={{0,1},{1,0},{2,3},{3,2},{4,5},{5,4},{6,7},{7,6},{8,9},{9,8},{10,11... | collective-permute-start | bytes 196616 | tf_op jit(solution)/shard_map/ppermute | solution.py:326
  79.7 6.5 %collective-permute-start.13 = (f32[128,128]{1,0:T(8,128)S(1)}, f32[128,128]{1,0:T(8,128)S(1)}, u32[]{:S(2)}, u32[]{:S(2)}) collective-permute-start(f32[128,128]{1,0:T(8,128)S(1)} %multiply_add_fusion.13.refs_1_), channel_id=1, source_target_pairs={{0,6},{1,5},{2,4},{3,7},{4,2},{5,1},{6,0},{7,3},{8,14},{9,13},{10,... | collective-permute-start | bytes 196616 | tf_op jit(solution)/shard_map/ppermute | solution.py:326
  81.2 5.8 %collective-permute-start.14 = (f32[128,128]{1,0:T(8,128)S(1)}, f32[128,128]{1,0:T(8,128)S(1)}, u32[]{:S(2)}, u32[]{:S(2)}) collective-permute-start(f32[128,128]{1,0:T(8,128)S(1)} %multiply_add_fusion.13.refs_1_), channel_id=1, source_target_pairs={{0,4},{1,7},{2,6},{3,5},{4,0},{5,3},{6,2},{7,1},{8,12},{9,15},{10,... | collective-permute-start | bytes 196616 | tf_op jit(solution)/shard_map/ppermute | solution.py:326
  81.2 5.8 %collective-permute-start.15 = (f32[128,128]{1,0:T(8,128)S(1)}, f32[128,128]{1,0:T(8,128)S(1)}, u32[]{:S(2)}, u32[]{:S(2)}) collective-permute-start(f32[128,128]{1,0:T(8,128)S(1)} %multiply_add_fusion.13.refs_1_), channel_id=1, source_target_pairs={{0,2},{1,3},{2,0},{3,1},{4,6},{5,7},{6,4},{7,5},{8,10},{9,11},{10,... | collective-permute-start | bytes 196616 | tf_op jit(solution)/shard_map/ppermute | solution.py:326
  89.8 4.2 %collective-permute-start.16 = (f32[192,128]{1,0:T(8,128)S(1)}, f32[192,128]{1,0:T(8,128)S(1)}, u32[]{:S(2)}, u32[]{:S(2)}) collective-permute-start(f32[192,128]{1,0:T(8,128)S(1)} %get-tuple-element.31), channel_id=1, source_target_pairs={{0,1},{2,3},{4,5},{6,7},{8,9},{10,11},{12,13},{14,15},{16,17},{18,... | collective-permute-start | bytes 294920 | tf_op jit(solution)/shard_map/ppermute | solution.py:344
  93.9 2.0 collective-permute-start.17
  94.6 1.4 collective-permute-start.18
  95.3 0.7 collective-permute-start.19
  97.0 0.7 collective-permute-start.21
  97.8 0.7 collective-permute-start.22
  98.6 42.9 %collective-permute-start.23 = (f32[192,128]{1,0:T(8,128)S(1)}, f32[192,128]{1,0:T(8,128)S(1)}, u32[]{:S(2)}, u32[]{:S(2)}) collective-permute-start(f32[192,128]{1,0:T(8,128)S(1)} %multiply_add_fusion.10), channel_id=1, source_target_pairs={{1,0},{3,2},{5,4},{7,6},{9,8},{11,10},{13,12},{15,14},{17,16},{19,... | collective-permute-start | bytes 294920 | tf_op jit(solution)/shard_map/ppermute | solution.py:344
  142.4 1.8 collective-permute-start.24
  144.3 6.6 %collective-permute-start.25 = (f32[128,128]{1,0:T(8,128)S(1)}, f32[128,128]{1,0:T(8,128)S(1)}, u32[]{:S(2)}, u32[]{:S(2)}) collective-permute-start(f32[128,128]{1,0:T(8,128)S(1)} %multiply_add_fusion.12.refs_1_), channel_id=1, source_target_pairs={{0,6},{1,5},{2,4},{3,7},{4,2},{5,1},{6,0},{7,3},{8,14},{9,13},{10,... | collective-permute-start | bytes 196616 | tf_op jit(solution)/shard_map/ppermute | solution.py:326
  145.9 5.8 %collective-permute-start.26 = (f32[128,128]{1,0:T(8,128)S(1)}, f32[128,128]{1,0:T(8,128)S(1)}, u32[]{:S(2)}, u32[]{:S(2)}) collective-permute-start(f32[128,128]{1,0:T(8,128)S(1)} %multiply_add_fusion.12.refs_1_), channel_id=1, source_target_pairs={{0,4},{1,7},{2,6},{3,5},{4,0},{5,3},{6,2},{7,1},{8,12},{9,15},{10,... | collective-permute-start | bytes 196616 | tf_op jit(solution)/shard_map/ppermute | solution.py:326
  145.9 5.8 %collective-permute-start.27 = (f32[128,128]{1,0:T(8,128)S(1)}, f32[128,128]{1,0:T(8,128)S(1)}, u32[]{:S(2)}, u32[]{:S(2)}) collective-permute-start(f32[128,128]{1,0:T(8,128)S(1)} %multiply_add_fusion.12.refs_1_), channel_id=1, source_target_pairs={{0,2},{1,3},{2,0},{3,1},{4,6},{5,7},{6,4},{7,5},{8,10},{9,11},{10,... | collective-permute-start | bytes 196616 | tf_op jit(solution)/shard_map/ppermute | solution.py:326
  154.5 4.3 %collective-permute-start.28 = (f32[192,128]{1,0:T(8,128)S(1)}, f32[192,128]{1,0:T(8,128)S(1)}, u32[]{:S(2)}, u32[]{:S(2)}) collective-permute-start(f32[192,128]{1,0:T(8,128)S(1)} %get-tuple-element.35), channel_id=1, source_target_pairs={{0,1},{2,3},{4,5},{6,7},{8,9},{10,11},{12,13},{14,15},{16,17},{18,... | collective-permute-start | bytes 294920 | tf_op jit(solution)/shard_map/ppermute | solution.py:344
  158.7 2.0 collective-permute-start.29
  159.4 1.4 collective-permute-start.30
  160.1 0.7 collective-permute-start.31
  163.3 43.5 %collective-permute-start.35 = (f32[192,128]{1,0:T(8,128)S(1)}, f32[192,128]{1,0:T(8,128)S(1)}, u32[]{:S(2)}, u32[]{:S(2)}) collective-permute-start(f32[192,128]{1,0:T(8,128)S(1)} %multiply_add_fusion.9), channel_id=1, source_target_pairs={{1,0},{3,2},{5,4},{7,6},{9,8},{11,10},{13,12},{15,14},{17,16},{19,... | collective-permute-start | bytes 294920 | tf_op jit(solution)/shard_map/ppermute | solution.py:344
  (8 other events, 77.6 us)

commit v12 on v9

--- a/solution.py
+++ b/solution.py
@@ -335,11 +335,19 @@
 
 
 def over_y(value):
-    return fan(value, "tgt", (6, 4), (4, 6), (2, 2))
+    src, tgt = lax.axis_size("src"), lax.axis_size("tgt")
+    parts = [value]
+    for flip in (2, 4, 6):
+        pairs = [(s * tgt + t, s * tgt + (t ^ flip)) for s in range(src) for t in range(1, tgt, 2)]
+        parts.append(lax.ppermute(value, ("src", "tgt"), pairs))
+    total = lse2_many(parts)
+    pairs = [(s * tgt + t, s * tgt + t - 1) for s in range(src) for t in range(1, tgt, 2)]
+    other = lax.ppermute(total, ("src", "tgt"), pairs)
+    return [jnp.where(lax.axis_index("tgt") % 2 == 1, total, other)]
 
 
 def over_src(value):
-    value = lse2_many(fan(value, "src", (3, 2), (2, 3), (1, 1)))
+    value = lse2_many(fan(value, "src", (1, 1), (2, 3), (3, 2)))
     for flips in ((4, 4), (12, 28)):
         value = lse2_many(fan(value, "src", flips))
     return fan(value, "src", (28, 12))

time: 159 us -> 178 us (1.12)
  the two profiles are of different devices: /device:TPU:176 before, /device:TPU:2 now
where the time goes in v12:
time: 178 us; the launch traced here: 175 us
  waiting for transfers between devices  83.9 us (47%)
  starting transfers between devices  56.2 us (32%)
  Pallas kernels  25.2 us (14%)
  local copies, waits for them, and re-layouts  6.34 us (4%)
    ppermute x21, waiting for transfers between devices, swap(): return lax.ppermute(value, ('src', 'tgt'), pairs)  54.9 us
    ppermute x21, starting transfers between devices, swap(): return lax.ppermute(value, ('src', 'tgt'), pairs)  46.3 us
    ppermute x3, waiting for transfers between devices, over_y(): other = lax.ppermute(total, ('src', 'tgt'), pairs)  29 us
    pallas_call x5, Pallas kernels, sweep(): pl.pallas_call(kernel, out_shape=(jax.ShapeDtypeStruct((2 * blocks_out, H...  19.5 us
    unnamed x10, local copies, waits for them, and re-layouts  6.34 us
    ppermute x9, starting transfers between devices, over_y(): parts.append(lax.ppermute(value, ('src', 'tgt'), pairs))  5.98 us
    pallas_call x1, Pallas kernels, costs(): pl.pallas_call(functools.partial(cost_kernel, blocks_in, blocks_out), out...  4.73 us
    ppermute x3, starting transfers between devices, over_y(): other = lax.ppermute(total, ('src', 'tgt'), pairs)  3.88 us
  transfers between devices with their start and end apart: 33, of which 23 were waited for; matrix products, arithmetic and copies ran while one was open for 0% of the time, Pallas kernels for 1%

profile of v12, /device:TPU:2, one launch (start us, length us, event | category | flops | bytes accessed | tf_op | source)
XLA Modules:
  0.0 175.0 jit_solution(17247549248805832397)
XLA Ops:
  1.3 4.7 %shard_map.59 = (f32[32,256,256]{2,1,0:T(8,128)S(1)}, f32[128,128]{1,0:T(8,128)S(1)}, bf16[32,128,256]{2,1,0:T(8,128)(2,1)S(1)}, bf16[32,128,256]{2,1,0:T(8,128)(2,1)S(1)}, s32[2,32]{1,0:T(2,128)S(4)}) custom-call(s32[2,32]{1,0:T(2,128)} %bitcast.6, s32[1,1]{1,0:T(1,128)S(6)} %copy.6.counts, f32[50,16384]{1,0:T(8,128)} %src.1, f32[50,24576]{1,0:T(8,128)} %tgt.1), custom_call_target="tpu_custom_call" | custom-call | tf_op jit(solution)/shard_map/pallas_call | solution.py:255
  6.0 3.3 %copy-done = f32[32,256,256]{2,1,0:T(8,128)} copy-done((f32[32,256,256]{2,1,0:T(8,128)}, f32[32,256,256]{2,1,0:T(8,128)S(1)}, u32[]{:S(2)}) %copy-start) | copy-done | bytes 8388632
  18.1 10.0 %collective-permute-done.4 = f32[128,128]{1,0:T(8,128)S(1)} collective-permute-done((f32[128,128]{1,0:T(8,128)S(1)}, f32[128,128]{1,0:T(8,128)S(1)}, u32[]{:S(2)}, u32[]{:S(2)}) %collective-permute-start.4) | collective-permute-done | bytes 65568 | tf_op jit(solution)/shard_map/ppermute | solution.py:345
  28.1 3.9 %shard_map.61 = (f32[192,128]{1,0:T(8,128)S(1)}, f32[128,128]{1,0:T(8,128)S(1)}) custom-call(s32[2,32]{1,0:T(2,128)S(4)} %get-tuple-element.19.tiles, s32[1,1]{1,0:T(1,128)S(6)} %copy.6.counts, f32[32,256,256]{2,1,0:T(8,128)S(1)} %shard_map.60.cost, f32[128,128]{1,0:T(8,128)S(1)} %broadcast_select_fusion.2.refs_0_), custom_call_target="tpu_custom_call" | custom-call | tf_op jit(solution)/shard_map/pallas_call | solution.py:300
  32.3 2.1 %collective-permute-start.6 = (f32[192,128]{1,0:T(8,128)S(1)}, f32[192,128]{1,0:T(8,128)S(1)}, u32[]{:S(2)}, u32[]{:S(2)}) collective-permute-start(f32[192,128]{1,0:T(8,128)S(1)} %get-tuple-element.27), channel_id=1, source_target_pairs={{0,16},{1,25},{2,18},{3,27},{4,20},{5,29},{6,22},{7,31},{8,24},{9,... | collective-permute-start | bytes 294920 | tf_op jit(solution)/shard_map/ppermute | solution.py:326
  34.4 1.7 collective-permute-start.5
  36.7 2.6 %collective-permute-done.6 = f32[192,128]{1,0:T(8,128)S(1)} collective-permute-done((f32[192,128]{1,0:T(8,128)S(1)}, f32[192,128]{1,0:T(8,128)S(1)}, u32[]{:S(2)}, u32[]{:S(2)}) %collective-permute-start.6) | collective-permute-done | bytes 98336 | tf_op jit(solution)/shard_map/ppermute | solution.py:326
  39.3 2.1 %collective-permute-done.5 = f32[192,128]{1,0:T(8,128)S(1)} collective-permute-done((f32[192,128]{1,0:T(8,128)S(1)}, f32[192,128]{1,0:T(8,128)S(1)}, u32[]{:S(2)}, u32[]{:S(2)}) %collective-permute-start.5) | collective-permute-done | bytes 98336 | tf_op jit(solution)/shard_map/ppermute | solution.py:326
  42.0 5.1 %collective-permute-done.8 = f32[192,128]{1,0:T(8,128)S(1)} collective-permute-done((f32[192,128]{1,0:T(8,128)S(1)}, f32[192,128]{1,0:T(8,128)S(1)}, u32[]{:S(2)}, u32[]{:S(2)}) %collective-permute-start.8) | collective-permute-done | bytes 98336 | tf_op jit(solution)/shard_map/ppermute | solution.py:326
  47.8 5.9 %collective-permute-done.9 = f32[192,128]{1,0:T(8,128)S(1)} collective-permute-done((f32[192,128]{1,0:T(8,128)S(1)}, f32[192,128]{1,0:T(8,128)S(1)}, u32[]{:S(2)}, u32[]{:S(2)}) %collective-permute-start.9) | collective-permute-done | bytes 98336 | tf_op jit(solution)/shard_map/ppermute | solution.py:326
  53.7 10.2 %collective-permute-start.10 = (f32[192,128]{1,0:T(8,128)S(1)}, f32[192,128]{1,0:T(8,128)S(1)}, u32[]{:S(2)}, u32[]{:S(2)}) collective-permute-start(f32[192,128]{1,0:T(8,128)S(1)} %multiply_add_fusion.6.refs_1_), channel_id=1, source_target_pairs={{0,224},{1,97},{2,226},{3,99},{4,228},{5,101},{6,230},{7,103},{8,2... | collective-permute-start | bytes 294920 | tf_op jit(solution)/shard_map/ppermute | solution.py:326
  63.9 2.6 %collective-permute-done.10.refs_2_ = f32[192,128]{1,0:T(8,128)S(1)} collective-permute-done((f32[192,128]{1,0:T(8,128)S(1)}, f32[192,128]{1,0:T(8,128)S(1)}, u32[]{:S(2)}, u32[]{:S(2)}) %collective-permute-start.10) | collective-permute-done | bytes 98336 | tf_op jit(solution)/shard_map/ppermute | solution.py:326
  66.5 3.9 %shard_map.62 = (f32[128,128]{1,0:T(8,128)S(1)}, f32[192,128]{1,0:T(8,128)S(1)}) custom-call(s32[2,32]{1,0:T(2,128)S(4)} %get-tuple-element.19.tiles, s32[1,1]{1,0:T(1,128)S(6)} %copy.6.counts, f32[32,256,256]{2,1,0:T(8,128)S(1)} %bitcast.5, f32[128,128]{1,0:T(8,128)S(1)} %get-tuple-element.26.refs_0_, f32[192,128]{1,0:T(8,128)S(1)} %multiply_add_fusion.6.refs_1_, ...), custom_call_target="tpu_custom_call" | custom-call | tf_op jit(solution)/shard_map/pallas_call | solution.py:300
  75.3 9.5 %collective-permute-done.15 = f32[128,128]{1,0:T(8,128)S(1)} collective-permute-done((f32[128,128]{1,0:T(8,128)S(1)}, f32[128,128]{1,0:T(8,128)S(1)}, u32[]{:S(2)}, u32[]{:S(2)}) %collective-permute-start.15) | collective-permute-done | bytes 65568 | tf_op jit(solution)/shard_map/ppermute | solution.py:345
  84.8 3.9 %shard_map.63 = (f32[192,128]{1,0:T(8,128)S(1)}, f32[128,128]{1,0:T(8,128)S(1)}) custom-call(s32[2,32]{1,0:T(2,128)S(4)} %get-tuple-element.19.tiles, s32[1,1]{1,0:T(1,128)S(6)} %copy.6.counts, f32[32,256,256]{2,1,0:T(8,128)S(1)} %shard_map.60.cost, f32[192,128]{1,0:T(8,128)S(1)} %get-tuple-element.28.refs_0_, f32[128,128]{1,0:T(8,128)S(1)} %broadcast_select_fusion.1.refs_1_), custom_call_target="tpu_custom_call" | custom-call | tf_op jit(solution)/shard_map/pallas_call | solution.py:300
  88.8 1.8 %collective-permute-start.17 = (f32[192,128]{1,0:T(8,128)S(1)}, f32[192,128]{1,0:T(8,128)S(1)}, u32[]{:S(2)}, u32[]{:S(2)}) collective-permute-start(f32[192,128]{1,0:T(8,128)S(1)} %get-tuple-element.31), channel_id=1, source_target_pairs={{0,16},{1,25},{2,18},{3,27},{4,20},{5,29},{6,22},{7,31},{8,24},{9,... | collective-permute-start | bytes 294920 | tf_op jit(solution)/shard_map/ppermute | solution.py:326
  90.6 2.3 %collective-permute-start.16 = (f32[192,128]{1,0:T(8,128)S(1)}, f32[192,128]{1,0:T(8,128)S(1)}, u32[]{:S(2)}, u32[]{:S(2)}) collective-permute-start(f32[192,128]{1,0:T(8,128)S(1)} %get-tuple-element.31), channel_id=1, source_target_pairs={{0,8},{1,9},{2,10},{3,11},{4,12},{5,13},{6,14},{7,15},{8,0},{9,1},... | collective-permute-start | bytes 294920 | tf_op jit(solution)/shard_map/ppermute | solution.py:326
  92.9 2.2 %collective-permute-done.18 = f32[192,128]{1,0:T(8,128)S(1)} collective-permute-done((f32[192,128]{1,0:T(8,128)S(1)}, f32[192,128]{1,0:T(8,128)S(1)}, u32[]{:S(2)}, u32[]{:S(2)}) %collective-permute-start.18) | collective-permute-done | bytes 98336 | tf_op jit(solution)/shard_map/ppermute | solution.py:326
  97.4 3.9 %collective-permute-done.19 = f32[192,128]{1,0:T(8,128)S(1)} collective-permute-done((f32[192,128]{1,0:T(8,128)S(1)}, f32[192,128]{1,0:T(8,128)S(1)}, u32[]{:S(2)}, u32[]{:S(2)}) %collective-permute-start.19) | collective-permute-done | bytes 98336 | tf_op jit(solution)/shard_map/ppermute | solution.py:326
  102.2 5.7 %collective-permute-done.20 = f32[192,128]{1,0:T(8,128)S(1)} collective-permute-done((f32[192,128]{1,0:T(8,128)S(1)}, f32[192,128]{1,0:T(8,128)S(1)}, u32[]{:S(2)}, u32[]{:S(2)}) %collective-permute-start.20) | collective-permute-done | bytes 98336 | tf_op jit(solution)/shard_map/ppermute | solution.py:326
  107.9 8.1 %collective-permute-start.21 = (f32[192,128]{1,0:T(8,128)S(1)}, f32[192,128]{1,0:T(8,128)S(1)}, u32[]{:S(2)}, u32[]{:S(2)}) collective-permute-start(f32[192,128]{1,0:T(8,128)S(1)} %multiply_add_fusion.3.refs_1_), channel_id=1, source_target_pairs={{0,224},{1,97},{2,226},{3,99},{4,228},{5,101},{6,230},{7,103},{8,2... | collective-permute-start | bytes 294920 | tf_op jit(solution)/shard_map/ppermute | solution.py:326
  116.1 3.6 %collective-permute-done.21.refs_2_ = f32[192,128]{1,0:T(8,128)S(1)} collective-permute-done((f32[192,128]{1,0:T(8,128)S(1)}, f32[192,128]{1,0:T(8,128)S(1)}, u32[]{:S(2)}, u32[]{:S(2)}) %collective-permute-start.21) | collective-permute-done | bytes 98336 | tf_op jit(solution)/shard_map/ppermute | solution.py:326
  119.7 3.9 %shard_map.64 = (f32[128,128]{1,0:T(8,128)S(1)}, f32[192,128]{1,0:T(8,128)S(1)}) custom-call(s32[2,32]{1,0:T(2,128)S(4)} %get-tuple-element.19.tiles, s32[1,1]{1,0:T(1,128)S(6)} %copy.6.counts, f32[32,256,256]{2,1,0:T(8,128)S(1)} %bitcast.5, f32[128,128]{1,0:T(8,128)S(1)} %get-tuple-element.30.refs_0_, f32[192,128]{1,0:T(8,128)S(1)} %multiply_add_fusion.3.refs_1_, ...), custom_call_target="tpu_custom_call" | custom-call | tf_op jit(solution)/shard_map/pallas_call | solution.py:300
  128.5 9.5 %collective-permute-done.26 = f32[128,128]{1,0:T(8,128)S(1)} collective-permute-done((f32[128,128]{1,0:T(8,128)S(1)}, f32[128,128]{1,0:T(8,128)S(1)}, u32[]{:S(2)}, u32[]{:S(2)}) %collective-permute-start.26) | collective-permute-done | bytes 65568 | tf_op jit(solution)/shard_map/ppermute | solution.py:345
  138.0 3.9 %shard_map.65 = (f32[192,128]{1,0:T(8,128)S(1)}, f32[128,128]{1,0:T(8,128)}) custom-call(s32[2,32]{1,0:T(2,128)S(4)} %get-tuple-element.19.tiles, s32[1,1]{1,0:T(1,128)S(6)} %copy.6.counts, f32[32,256,256]{2,1,0:T(8,128)S(1)} %shard_map.60.cost, f32[192,128]{1,0:T(8,128)S(1)} %get-tuple-element.32.refs_0_, f32[128,128]{1,0:T(8,128)S(1)} %broadcast_select_fusion.refs_1_), custom_call_target="tpu_custom_call" | custom-call | tf_op jit(solution)/shard_map/pallas_call | solution.py:300
  142.9 3.1 %collective-permute-start.27 = (f32[192,128]{1,0:T(8,128)S(1)}, f32[192,128]{1,0:T(8,128)S(1)}, u32[]{:S(2)}, u32[]{:S(2)}) collective-permute-start(f32[192,128]{1,0:T(8,128)S(1)} %get-tuple-element.35), channel_id=1, source_target_pairs={{0,8},{1,9},{2,10},{3,11},{4,12},{5,13},{6,14},{7,15},{8,0},{9,1},... | collective-permute-start | bytes 294920 | tf_op jit(solution)/shard_map/ppermute | solution.py:326
  146.0 2.9 %collective-permute-done.29 = f32[192,128]{1,0:T(8,128)S(1)} collective-permute-done((f32[192,128]{1,0:T(8,128)S(1)}, f32[192,128]{1,0:T(8,128)S(1)}, u32[]{:S(2)}, u32[]{:S(2)}) %collective-permute-start.29) | collective-permute-done | bytes 98336 | tf_op jit(solution)/shard_map/ppermute | solution.py:326
  149.8 5.4 %collective-permute-start.30 = (f32[192,128]{1,0:T(8,128)S(1)}, f32[192,128]{1,0:T(8,128)S(1)}, u32[]{:S(2)}, u32[]{:S(2)}) collective-permute-start(f32[192,128]{1,0:T(8,128)S(1)} %multiply_add_fusion.2), channel_id=1, source_target_pairs={{0,32},{1,33},{2,34},{3,35},{4,36},{5,37},{6,38},{7,39},{8,40},{9,... | collective-permute-start | bytes 294920 | tf_op jit(solution)/shard_map/ppermute | solution.py:326
  155.1 2.6 %collective-permute-done.30 = f32[192,128]{1,0:T(8,128)S(1)} collective-permute-done((f32[192,128]{1,0:T(8,128)S(1)}, f32[192,128]{1,0:T(8,128)S(1)}, u32[]{:S(2)}, u32[]{:S(2)}) %collective-permute-start.30) | collective-permute-done | bytes 98336 | tf_op jit(solution)/shard_map/ppermute | solution.py:326
  157.9 6.6 %collective-permute-done.31 = f32[192,128]{1,0:T(8,128)S(1)} collective-permute-done((f32[192,128]{1,0:T(8,128)S(1)}, f32[192,128]{1,0:T(8,128)S(1)}, u32[]{:S(2)}, u32[]{:S(2)}) %collective-permute-start.31) | collective-permute-done | bytes 98336 | tf_op jit(solution)/shard_map/ppermute | solution.py:326
  164.6 7.2 %collective-permute-start.32 = (f32[192,128]{1,0:T(8,128)S(1)}, f32[192,128]{1,0:T(8,128)S(1)}, u32[]{:S(2)}, u32[]{:S(2)}) collective-permute-start(f32[192,128]{1,0:T(8,128)S(1)} %multiply_add_fusion), channel_id=1, source_target_pairs={{0,224},{1,97},{2,226},{3,99},{4,228},{5,101},{6,230},{7,103},{8,2... | collective-permute-start | bytes 294920 | tf_op jit(solution)/shard_map/ppermute | solution.py:326
  171.7 2.6 %collective-permute-done.32 = f32[192,128]{1,0:T(8,128)S(1)} collective-permute-done((f32[192,128]{1,0:T(8,128)S(1)}, f32[192,128]{1,0:T(8,128)S(1)}, u32[]{:S(2)}, u32[]{:S(2)}) %collective-permute-start.32) | collective-permute-done | bytes 98336 | tf_op jit(solution)/shard_map/ppermute | solution.py:326
  (71 shorter events, 26.6 us)
Async XLA Ops:
  10.6 1.3 collective-permute-start
  11.9 2.0 %collective-permute-start.3 = (f32[128,128]{1,0:T(8,128)S(1)}, f32[128,128]{1,0:T(8,128)S(1)}, u32[]{:S(2)}, u32[]{:S(2)}) collective-permute-start(f32[128,128]{1,0:T(8,128)S(1)} %multiply_add_fusion.14), channel_id=1, source_target_pairs={{1,7},{3,5},{5,3},{7,1},{9,15},{11,13},{13,11},{15,9},{17,23},{19,... | collective-permute-start | bytes 196616 | tf_op jit(solution)/shard_map/ppermute | solution.py:342
  12.6 1.4 collective-permute-start.2
  13.3 0.7 collective-permute-start.1
  14.1 14.0 %collective-permute-start.4 = (f32[128,128]{1,0:T(8,128)S(1)}, f32[128,128]{1,0:T(8,128)S(1)}, u32[]{:S(2)}, u32[]{:S(2)}) collective-permute-start(f32[128,128]{1,0:T(8,128)S(1)} %multiply_add_fusion.13), channel_id=1, source_target_pairs={{1,0},{3,2},{5,4},{7,6},{9,8},{11,10},{13,12},{15,14},{17,16},{19,... | collective-permute-start | bytes 196616 | tf_op jit(solution)/shard_map/ppermute | solution.py:345
  32.0 4.7 %collective-permute-start.7 = (f32[192,128]{1,0:T(8,128)S(1)}, f32[192,128]{1,0:T(8,128)S(1)}, u32[]{:S(2)}, u32[]{:S(2)}) collective-permute-start(f32[192,128]{1,0:T(8,128)S(1)} %get-tuple-element.27), channel_id=1, source_target_pairs={{0,24},{1,17},{2,26},{3,19},{4,28},{5,21},{6,30},{7,23},{8,16},{9,... | collective-permute-start | bytes 294920 | tf_op jit(solution)/shard_map/ppermute | solution.py:326
  32.3 7.0 %collective-permute-start.6 = (f32[192,128]{1,0:T(8,128)S(1)}, f32[192,128]{1,0:T(8,128)S(1)}, u32[]{:S(2)}, u32[]{:S(2)}) collective-permute-start(f32[192,128]{1,0:T(8,128)S(1)} %get-tuple-element.27), channel_id=1, source_target_pairs={{0,16},{1,25},{2,18},{3,27},{4,20},{5,29},{6,22},{7,31},{8,24},{9,... | collective-permute-start | bytes 294920 | tf_op jit(solution)/shard_map/ppermute | solution.py:326
  34.4 7.0 %collective-permute-start.5 = (f32[192,128]{1,0:T(8,128)S(1)}, f32[192,128]{1,0:T(8,128)S(1)}, u32[]{:S(2)}, u32[]{:S(2)}) collective-permute-start(f32[192,128]{1,0:T(8,128)S(1)} %get-tuple-element.27), channel_id=1, source_target_pairs={{0,8},{1,9},{2,10},{3,11},{4,12},{5,13},{6,14},{7,15},{8,0},{9,1},... | collective-permute-start | bytes 294920 | tf_op jit(solution)/shard_map/ppermute | solution.py:326
  41.6 5.5 %collective-permute-start.8 = (f32[192,128]{1,0:T(8,128)S(1)}, f32[192,128]{1,0:T(8,128)S(1)}, u32[]{:S(2)}, u32[]{:S(2)}) collective-permute-start(f32[192,128]{1,0:T(8,128)S(1)} %multiply_add_fusion.8), channel_id=1, source_target_pairs={{0,32},{1,33},{2,34},{3,35},{4,36},{5,37},{6,38},{7,39},{8,40},{9,... | collective-permute-start | bytes 294920 | tf_op jit(solution)/shard_map/ppermute | solution.py:326
  47.2 6.5 %collective-permute-start.9 = (f32[192,128]{1,0:T(8,128)S(1)}, f32[192,128]{1,0:T(8,128)S(1)}, u32[]{:S(2)}, u32[]{:S(2)}) collective-permute-start(f32[192,128]{1,0:T(8,128)S(1)} %multiply_add_fusion.7), channel_id=1, source_target_pairs={{0,96},{1,225},{2,98},{3,227},{4,100},{5,229},{6,102},{7,231},{8,1... | collective-permute-start | bytes 294920 | tf_op jit(solution)/shard_map/ppermute | solution.py:326
  53.7 12.8 %collective-permute-start.10 = (f32[192,128]{1,0:T(8,128)S(1)}, f32[192,128]{1,0:T(8,128)S(1)}, u32[]{:S(2)}, u32[]{:S(2)}) collective-permute-start(f32[192,128]{1,0:T(8,128)S(1)} %multiply_add_fusion.6.refs_1_), channel_id=1, source_target_pairs={{0,224},{1,97},{2,226},{3,99},{4,228},{5,101},{6,230},{7,103},{8,2... | collective-permute-start | bytes 294920 | tf_op jit(solution)/shard_map/ppermute | solution.py:326
  70.5 1.3 collective-permute-start.11
  71.9 2.0 %collective-permute-start.14 = (f32[128,128]{1,0:T(8,128)S(1)}, f32[128,128]{1,0:T(8,128)S(1)}, u32[]{:S(2)}, u32[]{:S(2)}) collective-permute-start(f32[128,128]{1,0:T(8,128)S(1)} %multiply_add_fusion.12), channel_id=1, source_target_pairs={{1,7},{3,5},{5,3},{7,1},{9,15},{11,13},{13,11},{15,9},{17,23},{19,... | collective-permute-start | bytes 196616 | tf_op jit(solution)/shard_map/ppermute | solution.py:342
  72.5 1.4 collective-permute-start.13
  73.2 0.7 collective-permute-start.12
  74.0 10.8 %collective-permute-start.15 = (f32[128,128]{1,0:T(8,128)S(1)}, f32[128,128]{1,0:T(8,128)S(1)}, u32[]{:S(2)}, u32[]{:S(2)}) collective-permute-start(f32[128,128]{1,0:T(8,128)S(1)} %multiply_add_fusion.11), channel_id=1, source_target_pairs={{1,0},{3,2},{5,4},{7,6},{9,8},{11,10},{13,12},{15,14},{17,16},{19,... | collective-permute-start | bytes 196616 | tf_op jit(solution)/shard_map/ppermute | solution.py:345
  88.7 6.4 %collective-permute-start.18 = (f32[192,128]{1,0:T(8,128)S(1)}, f32[192,128]{1,0:T(8,128)S(1)}, u32[]{:S(2)}, u32[]{:S(2)}) collective-permute-start(f32[192,128]{1,0:T(8,128)S(1)} %get-tuple-element.31), channel_id=1, source_target_pairs={{0,24},{1,17},{2,26},{3,19},{4,28},{5,21},{6,30},{7,23},{8,16},{9,... | collective-permute-start | bytes 294920 | tf_op jit(solution)/shard_map/ppermute | solution.py:326
  88.8 7.1 %collective-permute-start.17 = (f32[192,128]{1,0:T(8,128)S(1)}, f32[192,128]{1,0:T(8,128)S(1)}, u32[]{:S(2)}, u32[]{:S(2)}) collective-permute-start(f32[192,128]{1,0:T(8,128)S(1)} %get-tuple-element.31), channel_id=1, source_target_pairs={{0,16},{1,25},{2,18},{3,27},{4,20},{5,29},{6,22},{7,31},{8,24},{9,... | collective-permute-start | bytes 294920 | tf_op jit(solution)/shard_map/ppermute | solution.py:326
  90.6 5.9 %collective-permute-start.16 = (f32[192,128]{1,0:T(8,128)S(1)}, f32[192,128]{1,0:T(8,128)S(1)}, u32[]{:S(2)}, u32[]{:S(2)}) collective-permute-start(f32[192,128]{1,0:T(8,128)S(1)} %get-tuple-element.31), channel_id=1, source_target_pairs={{0,8},{1,9},{2,10},{3,11},{4,12},{5,13},{6,14},{7,15},{8,0},{9,1},... | collective-permute-start | bytes 294920 | tf_op jit(solution)/shard_map/ppermute | solution.py:326
  96.6 4.7 %collective-permute-start.19 = (f32[192,128]{1,0:T(8,128)S(1)}, f32[192,128]{1,0:T(8,128)S(1)}, u32[]{:S(2)}, u32[]{:S(2)}) collective-permute-start(f32[192,128]{1,0:T(8,128)S(1)} %multiply_add_fusion.5), channel_id=1, source_target_pairs={{0,32},{1,33},{2,34},{3,35},{4,36},{5,37},{6,38},{7,39},{8,40},{9,... | collective-permute-start | bytes 294920 | tf_op jit(solution)/shard_map/ppermute | solution.py:326
  101.4 6.5 %collective-permute-start.20 = (f32[192,128]{1,0:T(8,128)S(1)}, f32[192,128]{1,0:T(8,128)S(1)}, u32[]{:S(2)}, u32[]{:S(2)}) collective-permute-start(f32[192,128]{1,0:T(8,128)S(1)} %multiply_add_fusion.4), channel_id=1, source_target_pairs={{0,96},{1,225},{2,98},{3,227},{4,100},{5,229},{6,102},{7,231},{8,1... | collective-permute-start | bytes 294920 | tf_op jit(solution)/shard_map/ppermute | solution.py:326
  107.9 11.8 %collective-permute-start.21 = (f32[192,128]{1,0:T(8,128)S(1)}, f32[192,128]{1,0:T(8,128)S(1)}, u32[]{:S(2)}, u32[]{:S(2)}) collective-permute-start(f32[192,128]{1,0:T(8,128)S(1)} %multiply_add_fusion.3.refs_1_), channel_id=1, source_target_pairs={{0,224},{1,97},{2,226},{3,99},{4,228},{5,101},{6,230},{7,103},{8,2... | collective-permute-start | bytes 294920 | tf_op jit(solution)/shard_map/ppermute | solution.py:326
  123.6 1.3 collective-permute-start.22
  125.0 2.0 %collective-permute-start.25 = (f32[128,128]{1,0:T(8,128)S(1)}, f32[128,128]{1,0:T(8,128)S(1)}, u32[]{:S(2)}, u32[]{:S(2)}) collective-permute-start(f32[128,128]{1,0:T(8,128)S(1)} %multiply_add_fusion.10), channel_id=1, source_target_pairs={{1,7},{3,5},{5,3},{7,1},{9,15},{11,13},{13,11},{15,9},{17,23},{19,... | collective-permute-start | bytes 196616 | tf_op jit(solution)/shard_map/ppermute | solution.py:342
  125.7 1.4 collective-permute-start.24
  127.2 10.8 %collective-permute-start.26 = (f32[128,128]{1,0:T(8,128)S(1)}, f32[128,128]{1,0:T(8,128)S(1)}, u32[]{:S(2)}, u32[]{:S(2)}) collective-permute-start(f32[128,128]{1,0:T(8,128)S(1)} %multiply_add_fusion.9), channel_id=1, source_target_pairs={{1,0},{3,2},{5,4},{7,6},{9,8},{11,10},{13,12},{15,14},{17,16},{19,... | collective-permute-start | bytes 196616 | tf_op jit(solution)/shard_map/ppermute | solution.py:345
  141.9 7.1 %collective-permute-start.29 = (f32[192,128]{1,0:T(8,128)S(1)}, f32[192,128]{1,0:T(8,128)S(1)}, u32[]{:S(2)}, u32[]{:S(2)}) collective-permute-start(f32[192,128]{1,0:T(8,128)S(1)} %get-tuple-element.35), channel_id=1, source_target_pairs={{0,24},{1,17},{2,26},{3,19},{4,28},{5,21},{6,30},{7,23},{8,16},{9,... | collective-permute-start | bytes 294920 | tf_op jit(solution)/shard_map/ppermute | solution.py:326
  142.0 7.0 %collective-permute-start.28 = (f32[192,128]{1,0:T(8,128)S(1)}, f32[192,128]{1,0:T(8,128)S(1)}, u32[]{:S(2)}, u32[]{:S(2)}) collective-permute-start(f32[192,128]{1,0:T(8,128)S(1)} %get-tuple-element.35), channel_id=1, source_target_pairs={{0,16},{1,25},{2,18},{3,27},{4,20},{5,29},{6,22},{7,31},{8,24},{9,... | collective-permute-start | bytes 294920 | tf_op jit(solution)/shard_map/ppermute | solution.py:326
  142.9 6.7 %collective-permute-start.27 = (f32[192,128]{1,0:T(8,128)S(1)}, f32[192,128]{1,0:T(8,128)S(1)}, u32[]{:S(2)}, u32[]{:S(2)}) collective-permute-start(f32[192,128]{1,0:T(8,128)S(1)} %get-tuple-element.35), channel_id=1, source_target_pairs={{0,8},{1,9},{2,10},{3,11},{4,12},{5,13},{6,14},{7,15},{8,0},{9,1},... | collective-permute-start | bytes 294920 | tf_op jit(solution)/shard_map/ppermute | solution.py:326
  149.8 8.0 %collective-permute-start.30 = (f32[192,128]{1,0:T(8,128)S(1)}, f32[192,128]{1,0:T(8,128)S(1)}, u32[]{:S(2)}, u32[]{:S(2)}) collective-permute-start(f32[192,128]{1,0:T(8,128)S(1)} %multiply_add_fusion.2), channel_id=1, source_target_pairs={{0,32},{1,33},{2,34},{3,35},{4,36},{5,37},{6,38},{7,39},{8,40},{9,... | collective-permute-start | bytes 294920 | tf_op jit(solution)/shard_map/ppermute | solution.py:326
  157.8 6.7 %collective-permute-start.31 = (f32[192,128]{1,0:T(8,128)S(1)}, f32[192,128]{1,0:T(8,128)S(1)}, u32[]{:S(2)}, u32[]{:S(2)}) collective-permute-start(f32[192,128]{1,0:T(8,128)S(1)} %multiply_add_fusion.1), channel_id=1, source_target_pairs={{0,96},{1,225},{2,98},{3,227},{4,100},{5,229},{6,102},{7,231},{8,1... | collective-permute-start | bytes 294920 | tf_op jit(solution)/shard_map/ppermute | solution.py:326
  164.6 9.8 %collective-permute-start.32 = (f32[192,128]{1,0:T(8,128)S(1)}, f32[192,128]{1,0:T(8,128)S(1)}, u32[]{:S(2)}, u32[]{:S(2)}) collective-permute-start(f32[192,128]{1,0:T(8,128)S(1)} %multiply_add_fusion), channel_id=1, source_target_pairs={{0,224},{1,97},{2,226},{3,99},{4,228},{5,101},{6,230},{7,103},{8,2... | collective-permute-start | bytes 294920 | tf_op jit(solution)/shard_map/ppermute | solution.py:326
  (6 other events, 107.6 us)

commit v13 on v9

--- a/solution.py
+++ b/solution.py
@@ -339,7 +339,7 @@
 
 
 def over_src(value):
-    value = lse2_many(fan(value, "src", (3, 2), (2, 3), (1, 1)))
+    value = lse2_many(fan(value, "src", (3, 3), (2, 2), (1, 1)))
     for flips in ((4, 4), (12, 28)):
         value = lse2_many(fan(value, "src", flips))
     return fan(value, "src", (28, 12))

time: 159 us -> 158 us (level)
  the two profiles are of different devices: /device:TPU:176 before, /device:TPU:56 now
where the time goes in v13:
time: 158 us; the launch traced here: 157 us
  waiting for transfers between devices  73 us (46%)
  starting transfers between devices  64 us (41%)
  Pallas kernels  17.1 us (11%)
    ppermute x30, waiting for transfers between devices, swap(): return lax.ppermute(value, ('src', 'tgt'), pairs)  73 us
    ppermute x30, starting transfers between devices, swap(): return lax.ppermute(value, ('src', 'tgt'), pairs)  64 us
    pallas_call x5, Pallas kernels, sweep(): pl.pallas_call(kernel, out_shape=(jax.ShapeDtypeStruct((2 * blocks_out, H...  11.5 us
    pallas_call x1, Pallas kernels, costs(): pl.pallas_call(functools.partial(cost_kernel, blocks_in, blocks_out), out...  4.71 us
  transfers between devices with their start and end apart: 30, of which 26 were waited for; matrix products, arithmetic and copies ran while one was open for 0% of the time, Pallas kernels for 1%

profile of v13, /device:TPU:56, one launch (start us, length us, event | category | flops | bytes accessed | tf_op | source)
XLA Modules:
  0.0 157.0 jit_solution(18057657204504385323)
XLA Ops:
  1.3 4.7 %shard_map.59 = (f32[32,256,256]{2,1,0:T(8,128)S(1)}, f32[128,128]{1,0:T(8,128)S(1)}, bf16[32,128,256]{2,1,0:T(8,128)(2,1)S(1)}, bf16[32,128,256]{2,1,0:T(8,128)(2,1)S(1)}, s32[2,32]{1,0:T(2,128)S(4)}) custom-call(s32[2,32]{1,0:T(2,128)} %bitcast.4, s32[1,1]{1,0:T(1,128)S(6)} %copy.6.counts, f32[50,16384]{1,0:T(8,128)} %src.1, f32[50,24576]{1,0:T(8,128)} %tgt.1), custom_call_target="tpu_custom_call" | custom-call | tf_op jit(solution)/shard_map/pallas_call | solution.py:255
  7.5 2.3 %collective-permute-start.2 = (f32[128,128]{1,0:T(8,128)S(1)}, f32[128,128]{1,0:T(8,128)S(1)}, u32[]{:S(2)}, u32[]{:S(2)}) collective-permute-start(f32[128,128]{1,0:T(8,128)S(1)} %multiply_add_fusion.11.refs_0_), channel_id=1, source_target_pairs={{0,4},{1,7},{2,6},{3,5},{4,0},{5,3},{6,2},{7,1},{8,12},{9,15},{10,... | collective-permute-start | bytes 196616 | tf_op jit(solution)/shard_map/ppermute | solution.py:326
  14.9 3.2 %shard_map.61 = (f32[192,128]{1,0:T(8,128)S(1)}, f32[128,128]{1,0:T(8,128)S(1)}) custom-call(s32[2,32]{1,0:T(2,128)S(4)} %get-tuple-element.19.tiles, s32[1,1]{1,0:T(1,128)S(6)} %copy.6.counts, f32[32,256,256]{2,1,0:T(8,128)S(1)} %shard_map.60.cost, f32[128,128]{1,0:T(8,128)S(1)} %multiply_add_fusion.11.refs_0_, ...), custom_call_target="tpu_custom_call" | custom-call | tf_op jit(solution)/shard_map/pallas_call | solution.py:300
  18.2 3.4 %collective-permute-start.4 = (f32[192,128]{1,0:T(8,128)S(1)}, f32[192,128]{1,0:T(8,128)S(1)}, u32[]{:S(2)}, u32[]{:S(2)}) collective-permute-start(f32[192,128]{1,0:T(8,128)S(1)} %get-tuple-element.27), channel_id=1, source_target_pairs={{0,24},{1,25},{2,26},{3,27},{4,28},{5,29},{6,30},{7,31},{8,16},{9,... | collective-permute-start | bytes 294920 | tf_op jit(solution)/shard_map/ppermute | solution.py:326
  21.6 2.9 %collective-permute-start.5 = (f32[192,128]{1,0:T(8,128)S(1)}, f32[192,128]{1,0:T(8,128)S(1)}, u32[]{:S(2)}, u32[]{:S(2)}) collective-permute-start(f32[192,128]{1,0:T(8,128)S(1)} %get-tuple-element.27), channel_id=1, source_target_pairs={{0,16},{1,17},{2,18},{3,19},{4,20},{5,21},{6,22},{7,23},{8,24},{9,... | collective-permute-start | bytes 294920 | tf_op jit(solution)/shard_map/ppermute | solution.py:326
  24.5 3.2 %collective-permute-done.5 = f32[192,128]{1,0:T(8,128)S(1)} collective-permute-done((f32[192,128]{1,0:T(8,128)S(1)}, f32[192,128]{1,0:T(8,128)S(1)}, u32[]{:S(2)}, u32[]{:S(2)}) %collective-permute-start.5) | collective-permute-done | bytes 98336 | tf_op jit(solution)/shard_map/ppermute | solution.py:326
  27.7 2.1 %collective-permute-done.6 = f32[192,128]{1,0:T(8,128)S(1)} collective-permute-done((f32[192,128]{1,0:T(8,128)S(1)}, f32[192,128]{1,0:T(8,128)S(1)}, u32[]{:S(2)}, u32[]{:S(2)}) %collective-permute-start.6) | collective-permute-done | bytes 98336 | tf_op jit(solution)/shard_map/ppermute | solution.py:326
  31.6 3.0 %collective-permute-done.7 = f32[192,128]{1,0:T(8,128)S(1)} collective-permute-done((f32[192,128]{1,0:T(8,128)S(1)}, f32[192,128]{1,0:T(8,128)S(1)}, u32[]{:S(2)}, u32[]{:S(2)}) %collective-permute-start.7) | collective-permute-done | bytes 98336 | tf_op jit(solution)/shard_map/ppermute | solution.py:326
  34.7 5.9 %collective-permute-start.8 = (f32[192,128]{1,0:T(8,128)S(1)}, f32[192,128]{1,0:T(8,128)S(1)}, u32[]{:S(2)}, u32[]{:S(2)}) collective-permute-start(f32[192,128]{1,0:T(8,128)S(1)} %multiply_add_fusion.7), channel_id=1, source_target_pairs={{0,96},{1,225},{2,98},{3,227},{4,100},{5,229},{6,102},{7,231},{8,1... | collective-permute-start | bytes 294920 | tf_op jit(solution)/shard_map/ppermute | solution.py:326
  40.6 3.6 %collective-permute-done.8 = f32[192,128]{1,0:T(8,128)S(1)} collective-permute-done((f32[192,128]{1,0:T(8,128)S(1)}, f32[192,128]{1,0:T(8,128)S(1)}, u32[]{:S(2)}, u32[]{:S(2)}) %collective-permute-start.8) | collective-permute-done | bytes 98336 | tf_op jit(solution)/shard_map/ppermute | solution.py:326
  44.3 3.3 %collective-permute-start.9 = (f32[192,128]{1,0:T(8,128)S(1)}, f32[192,128]{1,0:T(8,128)S(1)}, u32[]{:S(2)}, u32[]{:S(2)}) collective-permute-start(f32[192,128]{1,0:T(8,128)S(1)} %multiply_add_fusion.6.refs_1_), channel_id=1, source_target_pairs={{0,224},{1,97},{2,226},{3,99},{4,228},{5,101},{6,230},{7,103},{8,2... | collective-permute-start | bytes 294920 | tf_op jit(solution)/shard_map/ppermute | solution.py:326
  47.6 4.5 %collective-permute-done.9.refs_2_ = f32[192,128]{1,0:T(8,128)S(1)} collective-permute-done((f32[192,128]{1,0:T(8,128)S(1)}, f32[192,128]{1,0:T(8,128)S(1)}, u32[]{:S(2)}, u32[]{:S(2)}) %collective-permute-start.9) | collective-permute-done | bytes 98336 | tf_op jit(solution)/shard_map/ppermute | solution.py:326
  54.5 4.5 %collective-permute-start.12 = (f32[128,128]{1,0:T(8,128)S(1)}, f32[128,128]{1,0:T(8,128)S(1)}, u32[]{:S(2)}, u32[]{:S(2)}) collective-permute-start(f32[128,128]{1,0:T(8,128)S(1)} %multiply_add_fusion.10.refs_1_), channel_id=1, source_target_pairs={{0,4},{1,7},{2,6},{3,5},{4,0},{5,3},{6,2},{7,1},{8,12},{9,15},{10,... | collective-permute-start | bytes 196616 | tf_op jit(solution)/shard_map/ppermute | solution.py:326
  61.4 1.9 %collective-permute-done.13.refs_4_ = f32[128,128]{1,0:T(8,128)S(1)} collective-permute-done((f32[128,128]{1,0:T(8,128)S(1)}, f32[128,128]{1,0:T(8,128)S(1)}, u32[]{:S(2)}, u32[]{:S(2)}) %collective-permute-start.13) | collective-permute-done | bytes 65568 | tf_op jit(solution)/shard_map/ppermute | solution.py:326
  63.3 3.3 %shard_map.63 = (f32[192,128]{1,0:T(8,128)S(1)}, f32[128,128]{1,0:T(8,128)S(1)}) custom-call(s32[2,32]{1,0:T(2,128)S(4)} %get-tuple-element.19.tiles, s32[1,1]{1,0:T(1,128)S(6)} %copy.6.counts, f32[32,256,256]{2,1,0:T(8,128)S(1)} %shard_map.60.cost, f32[192,128]{1,0:T(8,128)S(1)} %get-tuple-element.28.refs_0_, f32[128,128]{1,0:T(8,128)S(1)} %multiply_add_fusion.10.refs_1_, ...), custom_call_target="tpu_custom_call" | custom-call | tf_op jit(solution)/shard_map/pallas_call | solution.py:300
  66.5 3.2 %collective-permute-start.14 = (f32[192,128]{1,0:T(8,128)S(1)}, f32[192,128]{1,0:T(8,128)S(1)}, u32[]{:S(2)}, u32[]{:S(2)}) collective-permute-start(f32[192,128]{1,0:T(8,128)S(1)} %get-tuple-element.31), channel_id=1, source_target_pairs={{0,24},{1,25},{2,26},{3,27},{4,28},{5,29},{6,30},{7,31},{8,16},{9,... | collective-permute-start | bytes 294920 | tf_op jit(solution)/shard_map/ppermute | solution.py:326
  70.9 3.4 %collective-permute-done.14 = f32[192,128]{1,0:T(8,128)S(1)} collective-permute-done((f32[192,128]{1,0:T(8,128)S(1)}, f32[192,128]{1,0:T(8,128)S(1)}, u32[]{:S(2)}, u32[]{:S(2)}) %collective-permute-start.14) | collective-permute-done | bytes 98336 | tf_op jit(solution)/shard_map/ppermute | solution.py:326
  74.3 1.9 %collective-permute-done.15 = f32[192,128]{1,0:T(8,128)S(1)} collective-permute-done((f32[192,128]{1,0:T(8,128)S(1)}, f32[192,128]{1,0:T(8,128)S(1)}, u32[]{:S(2)}, u32[]{:S(2)}) %collective-permute-start.15) | collective-permute-done | bytes 98336 | tf_op jit(solution)/shard_map/ppermute | solution.py:326
  76.7 3.2 %collective-permute-start.17 = (f32[192,128]{1,0:T(8,128)S(1)}, f32[192,128]{1,0:T(8,128)S(1)}, u32[]{:S(2)}, u32[]{:S(2)}) collective-permute-start(f32[192,128]{1,0:T(8,128)S(1)} %multiply_add_fusion.5), channel_id=1, source_target_pairs={{0,32},{1,33},{2,34},{3,35},{4,36},{5,37},{6,38},{7,39},{8,40},{9,... | collective-permute-start | bytes 294920 | tf_op jit(solution)/shard_map/ppermute | solution.py:326
  79.9 3.1 %collective-permute-done.17 = f32[192,128]{1,0:T(8,128)S(1)} collective-permute-done((f32[192,128]{1,0:T(8,128)S(1)}, f32[192,128]{1,0:T(8,128)S(1)}, u32[]{:S(2)}, u32[]{:S(2)}) %collective-permute-start.17) | collective-permute-done | bytes 98336 | tf_op jit(solution)/shard_map/ppermute | solution.py:326
  83.1 8.0 %collective-permute-start.18 = (f32[192,128]{1,0:T(8,128)S(1)}, f32[192,128]{1,0:T(8,128)S(1)}, u32[]{:S(2)}, u32[]{:S(2)}) collective-permute-start(f32[192,128]{1,0:T(8,128)S(1)} %multiply_add_fusion.4), channel_id=1, source_target_pairs={{0,96},{1,225},{2,98},{3,227},{4,100},{5,229},{6,102},{7,231},{8,1... | collective-permute-start | bytes 294920 | tf_op jit(solution)/shard_map/ppermute | solution.py:326
  91.1 5.4 %collective-permute-done.18 = f32[192,128]{1,0:T(8,128)S(1)} collective-permute-done((f32[192,128]{1,0:T(8,128)S(1)}, f32[192,128]{1,0:T(8,128)S(1)}, u32[]{:S(2)}, u32[]{:S(2)}) %collective-permute-start.18) | collective-permute-done | bytes 98336 | tf_op jit(solution)/shard_map/ppermute | solution.py:326
  96.6 7.6 %collective-permute-done.19.refs_2_ = f32[192,128]{1,0:T(8,128)S(1)} collective-permute-done((f32[192,128]{1,0:T(8,128)S(1)}, f32[192,128]{1,0:T(8,128)S(1)}, u32[]{:S(2)}, u32[]{:S(2)}) %collective-permute-start.19) | collective-permute-done | bytes 98336 | tf_op jit(solution)/shard_map/ppermute | solution.py:326
  106.8 3.9 %collective-permute-start.23 = (f32[128,128]{1,0:T(8,128)S(1)}, f32[128,128]{1,0:T(8,128)S(1)}, u32[]{:S(2)}, u32[]{:S(2)}) collective-permute-start(f32[128,128]{1,0:T(8,128)S(1)} %multiply_add_fusion.9.refs_1_), channel_id=1, source_target_pairs={{0,2},{1,3},{2,0},{3,1},{4,6},{5,7},{6,4},{7,5},{8,10},{9,11},{10,... | collective-permute-start | bytes 196616 | tf_op jit(solution)/shard_map/ppermute | solution.py:326
  110.7 2.8 %collective-permute-done.21.refs_2_ = f32[128,128]{1,0:T(8,128)S(1)} collective-permute-done((f32[128,128]{1,0:T(8,128)S(1)}, f32[128,128]{1,0:T(8,128)S(1)}, u32[]{:S(2)}, u32[]{:S(2)}) %collective-permute-start.21) | collective-permute-done | bytes 65568 | tf_op jit(solution)/shard_map/ppermute | solution.py:326
  113.6 3.3 %shard_map.65 = (f32[192,128]{1,0:T(8,128)S(1)}, f32[128,128]{1,0:T(8,128)}) custom-call(s32[2,32]{1,0:T(2,128)S(4)} %get-tuple-element.19.tiles, s32[1,1]{1,0:T(1,128)S(6)} %copy.6.counts, f32[32,256,256]{2,1,0:T(8,128)S(1)} %shard_map.60.cost, f32[192,128]{1,0:T(8,128)S(1)} %get-tuple-element.32.refs_0_, f32[128,128]{1,0:T(8,128)S(1)} %multiply_add_fusion.9.refs_1_, ...), custom_call_target="tpu_custom_call" | custom-call | tf_op jit(solution)/shard_map/pallas_call | solution.py:300
  116.9 3.9 %collective-permute-start.24 = (f32[192,128]{1,0:T(8,128)S(1)}, f32[192,128]{1,0:T(8,128)S(1)}, u32[]{:S(2)}, u32[]{:S(2)}) collective-permute-start(f32[192,128]{1,0:T(8,128)S(1)} %get-tuple-element.35), channel_id=1, source_target_pairs={{0,24},{1,25},{2,26},{3,27},{4,28},{5,29},{6,30},{7,31},{8,16},{9,... | collective-permute-start | bytes 294920 | tf_op jit(solution)/shard_map/ppermute | solution.py:326
  121.8 3.3 %collective-permute-done.24 = f32[192,128]{1,0:T(8,128)S(1)} collective-permute-done((f32[192,128]{1,0:T(8,128)S(1)}, f32[192,128]{1,0:T(8,128)S(1)}, u32[]{:S(2)}, u32[]{:S(2)}) %collective-permute-start.24) | collective-permute-done | bytes 98336 | tf_op jit(solution)/shard_map/ppermute | solution.py:326
  128.3 3.6 %collective-permute-done.27 = f32[192,128]{1,0:T(8,128)S(1)} collective-permute-done((f32[192,128]{1,0:T(8,128)S(1)}, f32[192,128]{1,0:T(8,128)S(1)}, u32[]{:S(2)}, u32[]{:S(2)}) %collective-permute-start.27) | collective-permute-done | bytes 98336 | tf_op jit(solution)/shard_map/ppermute | solution.py:326
  131.9 11.6 %collective-permute-start.28 = (f32[192,128]{1,0:T(8,128)S(1)}, f32[192,128]{1,0:T(8,128)S(1)}, u32[]{:S(2)}, u32[]{:S(2)}) collective-permute-start(f32[192,128]{1,0:T(8,128)S(1)} %multiply_add_fusion.1), channel_id=1, source_target_pairs={{0,96},{1,225},{2,98},{3,227},{4,100},{5,229},{6,102},{7,231},{8,1... | collective-permute-start | bytes 294920 | tf_op jit(solution)/shard_map/ppermute | solution.py:326
  143.6 5.0 %collective-permute-done.28 = f32[192,128]{1,0:T(8,128)S(1)} collective-permute-done((f32[192,128]{1,0:T(8,128)S(1)}, f32[192,128]{1,0:T(8,128)S(1)}, u32[]{:S(2)}, u32[]{:S(2)}) %collective-permute-start.28) | collective-permute-done | bytes 98336 | tf_op jit(solution)/shard_map/ppermute | solution.py:326
  148.7 7.6 %collective-permute-done.29 = f32[192,128]{1,0:T(8,128)S(1)} collective-permute-done((f32[192,128]{1,0:T(8,128)S(1)}, f32[192,128]{1,0:T(8,128)S(1)}, u32[]{:S(2)}, u32[]{:S(2)}) %collective-permute-start.29) | collective-permute-done | bytes 98336 | tf_op jit(solution)/shard_map/ppermute | solution.py:326
  (48 shorter events, 22.7 us)
Async XLA Ops:
  6.0 1.3 collective-permute-start
  7.4 6.7 %collective-permute-start.1 = (f32[128,128]{1,0:T(8,128)S(1)}, f32[128,128]{1,0:T(8,128)S(1)}, u32[]{:S(2)}, u32[]{:S(2)}) collective-permute-start(f32[128,128]{1,0:T(8,128)S(1)} %multiply_add_fusion.11.refs_0_), channel_id=1, source_target_pairs={{0,6},{1,5},{2,4},{3,7},{4,2},{5,1},{6,0},{7,3},{8,14},{9,13},{10,... | collective-permute-start | bytes 196616 | tf_op jit(solution)/shard_map/ppermute | solution.py:326
  7.5 6.6 %collective-permute-start.2 = (f32[128,128]{1,0:T(8,128)S(1)}, f32[128,128]{1,0:T(8,128)S(1)}, u32[]{:S(2)}, u32[]{:S(2)}) collective-permute-start(f32[128,128]{1,0:T(8,128)S(1)} %multiply_add_fusion.11.refs_0_), channel_id=1, source_target_pairs={{0,4},{1,7},{2,6},{3,5},{4,0},{5,3},{6,2},{7,1},{8,12},{9,15},{10,... | collective-permute-start | bytes 196616 | tf_op jit(solution)/shard_map/ppermute | solution.py:326
  9.8 5.1 %collective-permute-start.3 = (f32[128,128]{1,0:T(8,128)S(1)}, f32[128,128]{1,0:T(8,128)S(1)}, u32[]{:S(2)}, u32[]{:S(2)}) collective-permute-start(f32[128,128]{1,0:T(8,128)S(1)} %multiply_add_fusion.11.refs_0_), channel_id=1, source_target_pairs={{0,2},{1,3},{2,0},{3,1},{4,6},{5,7},{6,4},{7,5},{8,10},{9,11},{10,... | collective-permute-start | bytes 196616 | tf_op jit(solution)/shard_map/ppermute | solution.py:326
  18.2 6.4 %collective-permute-start.4 = (f32[192,128]{1,0:T(8,128)S(1)}, f32[192,128]{1,0:T(8,128)S(1)}, u32[]{:S(2)}, u32[]{:S(2)}) collective-permute-start(f32[192,128]{1,0:T(8,128)S(1)} %get-tuple-element.27), channel_id=1, source_target_pairs={{0,24},{1,25},{2,26},{3,27},{4,28},{5,29},{6,30},{7,31},{8,16},{9,... | collective-permute-start | bytes 294920 | tf_op jit(solution)/shard_map/ppermute | solution.py:326
  21.6 6.1 %collective-permute-start.5 = (f32[192,128]{1,0:T(8,128)S(1)}, f32[192,128]{1,0:T(8,128)S(1)}, u32[]{:S(2)}, u32[]{:S(2)}) collective-permute-start(f32[192,128]{1,0:T(8,128)S(1)} %get-tuple-element.27), channel_id=1, source_target_pairs={{0,16},{1,17},{2,18},{3,19},{4,20},{5,21},{6,22},{7,23},{8,24},{9,... | collective-permute-start | bytes 294920 | tf_op jit(solution)/shard_map/ppermute | solution.py:326
  24.5 5.3 %collective-permute-start.6 = (f32[192,128]{1,0:T(8,128)S(1)}, f32[192,128]{1,0:T(8,128)S(1)}, u32[]{:S(2)}, u32[]{:S(2)}) collective-permute-start(f32[192,128]{1,0:T(8,128)S(1)} %get-tuple-element.27), channel_id=1, source_target_pairs={{0,8},{1,9},{2,10},{3,11},{4,12},{5,13},{6,14},{7,15},{8,0},{9,1},... | collective-permute-start | bytes 294920 | tf_op jit(solution)/shard_map/ppermute | solution.py:326
  29.9 4.7 %collective-permute-start.7 = (f32[192,128]{1,0:T(8,128)S(1)}, f32[192,128]{1,0:T(8,128)S(1)}, u32[]{:S(2)}, u32[]{:S(2)}) collective-permute-start(f32[192,128]{1,0:T(8,128)S(1)} %multiply_add_fusion.8), channel_id=1, source_target_pairs={{0,32},{1,33},{2,34},{3,35},{4,36},{5,37},{6,38},{7,39},{8,40},{9,... | collective-permute-start | bytes 294920 | tf_op jit(solution)/shard_map/ppermute | solution.py:326
  34.7 9.5 %collective-permute-start.8 = (f32[192,128]{1,0:T(8,128)S(1)}, f32[192,128]{1,0:T(8,128)S(1)}, u32[]{:S(2)}, u32[]{:S(2)}) collective-permute-start(f32[192,128]{1,0:T(8,128)S(1)} %multiply_add_fusion.7), channel_id=1, source_target_pairs={{0,96},{1,225},{2,98},{3,227},{4,100},{5,229},{6,102},{7,231},{8,1... | collective-permute-start | bytes 294920 | tf_op jit(solution)/shard_map/ppermute | solution.py:326
  44.3 7.8 %collective-permute-start.9 = (f32[192,128]{1,0:T(8,128)S(1)}, f32[192,128]{1,0:T(8,128)S(1)}, u32[]{:S(2)}, u32[]{:S(2)}) collective-permute-start(f32[192,128]{1,0:T(8,128)S(1)} %multiply_add_fusion.6.refs_1_), channel_id=1, source_target_pairs={{0,224},{1,97},{2,226},{3,99},{4,228},{5,101},{6,230},{7,103},{8,2... | collective-permute-start | bytes 294920 | tf_op jit(solution)/shard_map/ppermute | solution.py:326
  53.0 1.3 collective-permute-start.10
  54.4 5.7 %collective-permute-start.11 = (f32[128,128]{1,0:T(8,128)S(1)}, f32[128,128]{1,0:T(8,128)S(1)}, u32[]{:S(2)}, u32[]{:S(2)}) collective-permute-start(f32[128,128]{1,0:T(8,128)S(1)} %multiply_add_fusion.10.refs_1_), channel_id=1, source_target_pairs={{0,6},{1,5},{2,4},{3,7},{4,2},{5,1},{6,0},{7,3},{8,14},{9,13},{10,... | collective-permute-start | bytes 196616 | tf_op jit(solution)/shard_map/ppermute | solution.py:326
  54.5 6.9 %collective-permute-start.12 = (f32[128,128]{1,0:T(8,128)S(1)}, f32[128,128]{1,0:T(8,128)S(1)}, u32[]{:S(2)}, u32[]{:S(2)}) collective-permute-start(f32[128,128]{1,0:T(8,128)S(1)} %multiply_add_fusion.10.refs_1_), channel_id=1, source_target_pairs={{0,4},{1,7},{2,6},{3,5},{4,0},{5,3},{6,2},{7,1},{8,12},{9,15},{10,... | collective-permute-start | bytes 196616 | tf_op jit(solution)/shard_map/ppermute | solution.py:326
  59.0 4.3 %collective-permute-start.13 = (f32[128,128]{1,0:T(8,128)S(1)}, f32[128,128]{1,0:T(8,128)S(1)}, u32[]{:S(2)}, u32[]{:S(2)}) collective-permute-start(f32[128,128]{1,0:T(8,128)S(1)} %multiply_add_fusion.10.refs_1_), channel_id=1, source_target_pairs={{0,2},{1,3},{2,0},{3,1},{4,6},{5,7},{6,4},{7,5},{8,10},{9,11},{10,... | collective-permute-start | bytes 196616 | tf_op jit(solution)/shard_map/ppermute | solution.py:326
  66.5 7.8 %collective-permute-start.14 = (f32[192,128]{1,0:T(8,128)S(1)}, f32[192,128]{1,0:T(8,128)S(1)}, u32[]{:S(2)}, u32[]{:S(2)}) collective-permute-start(f32[192,128]{1,0:T(8,128)S(1)} %get-tuple-element.31), channel_id=1, source_target_pairs={{0,24},{1,25},{2,26},{3,27},{4,28},{5,29},{6,30},{7,31},{8,16},{9,... | collective-permute-start | bytes 294920 | tf_op jit(solution)/shard_map/ppermute | solution.py:326
  69.7 6.5 %collective-permute-start.15 = (f32[192,128]{1,0:T(8,128)S(1)}, f32[192,128]{1,0:T(8,128)S(1)}, u32[]{:S(2)}, u32[]{:S(2)}) collective-permute-start(f32[192,128]{1,0:T(8,128)S(1)} %get-tuple-element.31), channel_id=1, source_target_pairs={{0,16},{1,17},{2,18},{3,19},{4,20},{5,21},{6,22},{7,23},{8,24},{9,... | collective-permute-start | bytes 294920 | tf_op jit(solution)/shard_map/ppermute | solution.py:326
  70.9 5.7 %collective-permute-start.16 = (f32[192,128]{1,0:T(8,128)S(1)}, f32[192,128]{1,0:T(8,128)S(1)}, u32[]{:S(2)}, u32[]{:S(2)}) collective-permute-start(f32[192,128]{1,0:T(8,128)S(1)} %get-tuple-element.31), channel_id=1, source_target_pairs={{0,8},{1,9},{2,10},{3,11},{4,12},{5,13},{6,14},{7,15},{8,0},{9,1},... | collective-permute-start | bytes 294920 | tf_op jit(solution)/shard_map/ppermute | solution.py:326
  76.7 6.3 %collective-permute-start.17 = (f32[192,128]{1,0:T(8,128)S(1)}, f32[192,128]{1,0:T(8,128)S(1)}, u32[]{:S(2)}, u32[]{:S(2)}) collective-permute-start(f32[192,128]{1,0:T(8,128)S(1)} %multiply_add_fusion.5), channel_id=1, source_target_pairs={{0,32},{1,33},{2,34},{3,35},{4,36},{5,37},{6,38},{7,39},{8,40},{9,... | collective-permute-start | bytes 294920 | tf_op jit(solution)/shard_map/ppermute | solution.py:326
  83.1 13.4 %collective-permute-start.18 = (f32[192,128]{1,0:T(8,128)S(1)}, f32[192,128]{1,0:T(8,128)S(1)}, u32[]{:S(2)}, u32[]{:S(2)}) collective-permute-start(f32[192,128]{1,0:T(8,128)S(1)} %multiply_add_fusion.4), channel_id=1, source_target_pairs={{0,96},{1,225},{2,98},{3,227},{4,100},{5,229},{6,102},{7,231},{8,1... | collective-permute-start | bytes 294920 | tf_op jit(solution)/shard_map/ppermute | solution.py:326
  96.5 7.7 %collective-permute-start.19 = (f32[192,128]{1,0:T(8,128)S(1)}, f32[192,128]{1,0:T(8,128)S(1)}, u32[]{:S(2)}, u32[]{:S(2)}) collective-permute-start(f32[192,128]{1,0:T(8,128)S(1)} %multiply_add_fusion.3.refs_1_), channel_id=1, source_target_pairs={{0,224},{1,97},{2,226},{3,99},{4,228},{5,101},{6,230},{7,103},{8,2... | collective-permute-start | bytes 294920 | tf_op jit(solution)/shard_map/ppermute | solution.py:326
  105.1 1.3 collective-permute-start.20
  106.5 7.0 %collective-permute-start.21 = (f32[128,128]{1,0:T(8,128)S(1)}, f32[128,128]{1,0:T(8,128)S(1)}, u32[]{:S(2)}, u32[]{:S(2)}) collective-permute-start(f32[128,128]{1,0:T(8,128)S(1)} %multiply_add_fusion.9.refs_1_), channel_id=1, source_target_pairs={{0,6},{1,5},{2,4},{3,7},{4,2},{5,1},{6,0},{7,3},{8,14},{9,13},{10,... | collective-permute-start | bytes 196616 | tf_op jit(solution)/shard_map/ppermute | solution.py:326
  106.6 6.9 %collective-permute-start.22 = (f32[128,128]{1,0:T(8,128)S(1)}, f32[128,128]{1,0:T(8,128)S(1)}, u32[]{:S(2)}, u32[]{:S(2)}) collective-permute-start(f32[128,128]{1,0:T(8,128)S(1)} %multiply_add_fusion.9.refs_1_), channel_id=1, source_target_pairs={{0,4},{1,7},{2,6},{3,5},{4,0},{5,3},{6,2},{7,1},{8,12},{9,15},{10,... | collective-permute-start | bytes 196616 | tf_op jit(solution)/shard_map/ppermute | solution.py:326
  106.8 6.9 %collective-permute-start.23 = (f32[128,128]{1,0:T(8,128)S(1)}, f32[128,128]{1,0:T(8,128)S(1)}, u32[]{:S(2)}, u32[]{:S(2)}) collective-permute-start(f32[128,128]{1,0:T(8,128)S(1)} %multiply_add_fusion.9.refs_1_), channel_id=1, source_target_pairs={{0,2},{1,3},{2,0},{3,1},{4,6},{5,7},{6,4},{7,5},{8,10},{9,11},{10,... | collective-permute-start | bytes 196616 | tf_op jit(solution)/shard_map/ppermute | solution.py:326
  116.9 8.2 %collective-permute-start.24 = (f32[192,128]{1,0:T(8,128)S(1)}, f32[192,128]{1,0:T(8,128)S(1)}, u32[]{:S(2)}, u32[]{:S(2)}) collective-permute-start(f32[192,128]{1,0:T(8,128)S(1)} %get-tuple-element.35), channel_id=1, source_target_pairs={{0,24},{1,25},{2,26},{3,27},{4,28},{5,29},{6,30},{7,31},{8,16},{9,... | collective-permute-start | bytes 294920 | tf_op jit(solution)/shard_map/ppermute | solution.py:326
  120.8 6.1 %collective-permute-start.25 = (f32[192,128]{1,0:T(8,128)S(1)}, f32[192,128]{1,0:T(8,128)S(1)}, u32[]{:S(2)}, u32[]{:S(2)}) collective-permute-start(f32[192,128]{1,0:T(8,128)S(1)} %get-tuple-element.35), channel_id=1, source_target_pairs={{0,16},{1,17},{2,18},{3,19},{4,20},{5,21},{6,22},{7,23},{8,24},{9,... | collective-permute-start | bytes 294920 | tf_op jit(solution)/shard_map/ppermute | solution.py:326
  121.2 5.7 %collective-permute-start.26 = (f32[192,128]{1,0:T(8,128)S(1)}, f32[192,128]{1,0:T(8,128)S(1)}, u32[]{:S(2)}, u32[]{:S(2)}) collective-permute-start(f32[192,128]{1,0:T(8,128)S(1)} %get-tuple-element.35), channel_id=1, source_target_pairs={{0,8},{1,9},{2,10},{3,11},{4,12},{5,13},{6,14},{7,15},{8,0},{9,1},... | collective-permute-start | bytes 294920 | tf_op jit(solution)/shard_map/ppermute | solution.py:326
  127.1 4.8 %collective-permute-start.27 = (f32[192,128]{1,0:T(8,128)S(1)}, f32[192,128]{1,0:T(8,128)S(1)}, u32[]{:S(2)}, u32[]{:S(2)}) collective-permute-start(f32[192,128]{1,0:T(8,128)S(1)} %multiply_add_fusion.2), channel_id=1, source_target_pairs={{0,32},{1,33},{2,34},{3,35},{4,36},{5,37},{6,38},{7,39},{8,40},{9,... | collective-permute-start | bytes 294920 | tf_op jit(solution)/shard_map/ppermute | solution.py:326
  131.9 16.6 %collective-permute-start.28 = (f32[192,128]{1,0:T(8,128)S(1)}, f32[192,128]{1,0:T(8,128)S(1)}, u32[]{:S(2)}, u32[]{:S(2)}) collective-permute-start(f32[192,128]{1,0:T(8,128)S(1)} %multiply_add_fusion.1), channel_id=1, source_target_pairs={{0,96},{1,225},{2,98},{3,227},{4,100},{5,229},{6,102},{7,231},{8,1... | collective-permute-start | bytes 294920 | tf_op jit(solution)/shard_map/ppermute | solution.py:326
  148.6 7.7 %collective-permute-start.29 = (f32[192,128]{1,0:T(8,128)S(1)}, f32[192,128]{1,0:T(8,128)S(1)}, u32[]{:S(2)}, u32[]{:S(2)}) collective-permute-start(f32[192,128]{1,0:T(8,128)S(1)} %multiply_add_fusion), channel_id=1, source_target_pairs={{0,224},{1,97},{2,226},{3,99},{4,228},{5,101},{6,230},{7,103},{8,2... | collective-permute-start | bytes 294920 | tf_op jit(solution)/shard_map/ppermute | solution.py:326
